TPU v7x, 32 devices: a whole 2x2x4 slice. The times are simulated.
32 devices in a mesh: section: 2 (over x), ctx: 16 (over z, y, core).
Axes of the slice: x: 2, y: 2, z: 4, core: 2. Of those that a mesh axis runs over, the one named last changes fastest.
Arguments:
- query_rows: bfloat16 [2, 2048, 1536], P('section', 'ctx'), may hold values from -5 to 5
- key_rows: bfloat16 [2, 2048, 1536], P('section', 'ctx'), may hold values from -5 to 5
- value_rows: bfloat16 [2, 2048, 1536], P('section', 'ctx'), may hold values from -6 to 6
- grad_output: bfloat16 [2, 2048, 1536], P('section', 'ctx'), may hold values from -6 to 6
- block_lists: int32 [16, 5], P('ctx'), may hold values from -1 to 15, as said below
Outputs:
- grad_query: bfloat16 [2, 2048, 1536], P('section', 'ctx')
- grad_key: bfloat16 [2, 2048, 1536], P('section', 'ctx')
- grad_value: bfloat16 [2, 2048, 1536], P('section', 'ctx')
- handoff: bfloat16 [2, 2048, 1536], P('section', 'ctx')
Inputs may be any that keep to these rules, and one draw needn't show every extreme that they name: `block_lists`: each list names distinct key blocks whose devices lie within 2 devices of the query block's device, always including the query block itself; -1 marks an unused entry; in every draw some query block names all 5 blocks.
All inputs are finite; a program needn't handle non-finite values.
Results may differ from a plain program's by a relative error of at most 0.011.
Values may be sent and summed in bfloat16 or wider, within the bound.
No kernel may reach another device: no remote copies, remote signals or barrier semaphores. Data moves between devices by JAX's collectives and lax.ppermute only.
A program may use at most 128 MiB of HBM per device.

v0:
```python
import jax
import jax.numpy as jnp
from jax import lax
from jax.sharding import PartitionSpec as P

H = 12
DH = 128
BLK = 128
REACH = 2


big_negative = -1e30


def from_behind(value, axis, steps):
    count = lax.axis_size(axis)
    first, last = (max(0, -steps), min(count, count - steps))
    return lax.ppermute(value, axis, [(source, source + steps) for source in range(first, last)])


def shortened(array):

    def short(part):
        return part.astype(jnp.bfloat16) if part.dtype == jnp.float32 else part

    return jax.tree.map(short, array)


def shards(query_rows, key_rows, value_rows, grad_output, block_lists):
    rows = query_rows.shape[1]
    width = query_rows.shape[2]
    per_device = block_lists.shape[0]
    scale = DH ** (-0.5)
    offsets = list(range(-REACH, REACH + 1))
    slab_count = len(offsets)
    position = lax.axis_index("ctx")
    own_query = query_rows[0].reshape(rows, H, DH)
    own_grad = grad_output[0].reshape(rows, H, DH)
    own_pair = jnp.stack([key_rows[0], value_rows[0]])
    fetched = {0: own_pair}
    lower = own_pair
    upper = own_pair
    for distance in range(1, REACH + 1):
        lower = from_behind(lower, "ctx", 1)
        upper = from_behind(upper, "ctx", -1)
        fetched[-distance] = lower
        fetched[distance] = upper
    slab_ids = jnp.stack(
        [(position + distance) * per_device + jnp.arange(per_device) for distance in offsets]
    )
    listed_ok = (block_lists >= 0)[:, :, None, None]
    needed = jnp.any(
        listed_ok & (block_lists[:, :, None, None] == slab_ids[None, None, :, :]), axis=1
    )
    row_needed = jnp.broadcast_to(
        needed[:, None, :, :, None], (per_device, BLK, slab_count, per_device, BLK)
    ).reshape(rows, slab_count * rows)
    every_pair = jnp.concatenate([fetched[distance] for distance in offsets], axis=1)
    keys_part = every_pair[0].reshape(-1, H, DH)
    scores = (
        jnp.einsum("qhd,khd->hqk", own_query, keys_part, preferred_element_type=jnp.float32) * scale
    )
    scores = jnp.where(row_needed[None], scores, big_negative)
    highest = jnp.max(scores, axis=2, keepdims=True)
    weights = jnp.exp(scores - highest)
    denom = jnp.sum(weights, axis=2, keepdims=True)
    probs = weights / denom
    probs_low = probs.astype(jnp.bfloat16)
    contribs = {}
    values_part = every_pair[1].reshape(-1, H, DH)
    attended = jnp.einsum(
        "hqk,khd->qhd", probs_low, values_part, preferred_element_type=jnp.float32
    )
    delta_heads = jnp.transpose(jnp.sum(own_grad.astype(jnp.float32) * attended, axis=2))
    keys_part = every_pair[0].reshape(-1, H, DH)
    values_part = every_pair[1].reshape(-1, H, DH)
    value_grad = jnp.einsum("hqk,qhd->khd", probs_low, own_grad, preferred_element_type=jnp.float32)
    grad_probs = jnp.einsum(
        "qhd,khd->hqk", own_grad, values_part, preferred_element_type=jnp.float32
    )
    grad_scores = probs * (grad_probs - delta_heads[:, :, None])
    scores_low = grad_scores.astype(jnp.bfloat16)
    query_grad = (
        jnp.einsum("hqk,khd->qhd", scores_low, keys_part, preferred_element_type=jnp.float32)
        * scale
    )
    key_grad = (
        jnp.einsum("hqk,qhd->khd", scores_low, own_query, preferred_element_type=jnp.float32)
        * scale
    )
    key_count = keys_part.shape[0]
    query_grad, terms_all = (
        query_grad,
        jnp.stack([key_grad.reshape(key_count, width), value_grad.reshape(key_count, width)]),
    )
    for index, distance in enumerate(offsets):
        contribs[distance] = terms_all[:, index * rows : (index + 1) * rows]
    upward = jnp.zeros((2, rows, width), jnp.float32)
    downward = jnp.zeros((2, rows, width), jnp.float32)
    for distance in range(REACH, 0, -1):
        upward = from_behind(shortened(upward + contribs[distance]), "ctx", 1)
        downward = from_behind(shortened(downward + contribs[-distance]), "ctx", -1)
    totals = contribs[0] + upward + downward
    grad_query = query_grad.reshape(rows, width).astype(jnp.bfloat16)[None]
    grad_key = totals[0].astype(jnp.bfloat16)[None]
    grad_value = totals[1].astype(jnp.bfloat16)[None]
    handoff = from_behind(grad_value, "section", -1)
    return (grad_query, grad_key, grad_value, handoff)


def solution(mesh):
    in_specs = (
        P("section", "ctx", None),
        P("section", "ctx", None),
        P("section", "ctx", None),
        P("section", "ctx", None),
        P("ctx", None),
    )
    out_specs = (
        P("section", "ctx", None),
        P("section", "ctx", None),
        P("section", "ctx", None),
        P("section", "ctx", None),
    )
    return jax.shard_map(shards, mesh=mesh, in_specs=in_specs, out_specs=out_specs, check_vma=False)
```

profile of v0, /device:TPU:12, one launch (start us, length us, event | category | flops | bytes accessed | tf_op | source)
XLA Modules:
  0.0 130.1 jit_solution(8769944384441850634)
XLA Ops:
  0.7 1.3 copy.40
  1.9 1.2 copy.41
  3.1 0.9 pad_maximum_fusion.1
  4.1 1.9 %collective-permute-start = (bf16[2,128,1536]{1,2,0:T(8,128)(2,1)}, bf16[2,128,1536]{1,2,0:T(8,128)(2,1)S(1)}, u32[]{:S(2)}, u32[]{:S(2)}) collective-permute-start(bf16[2,128,1536]{1,2,0:T(8,128)(2,1)} %pad_maximum_fusion.1), channel_id=1, source_target_pairs={{0,1},{1,2},{2,3},{3,4},{4,5},{5,6},{6,7},{7,8},{8,9},{9,10},{10,1... | collective-permute-start | bytes 2359304 | tf_op jit(solution)/shard_map/ppermute | solution.py:18
  6.0 3.6 %collective-permute-start.2 = (bf16[2,128,1536]{1,2,0:T(8,128)(2,1)}, bf16[2,128,1536]{1,2,0:T(8,128)(2,1)S(1)}, u32[]{:S(2)}, u32[]{:S(2)}) collective-permute-start(bf16[2,128,1536]{1,2,0:T(8,128)(2,1)} %pad_maximum_fusion.1), channel_id=1, source_target_pairs={{1,0},{2,1},{3,2},{4,3},{5,4},{6,5},{7,6},{8,7},{9,8},{10,9},{11,1... | collective-permute-start | bytes 2359304 | tf_op jit(solution)/shard_map/ppermute | solution.py:18
  9.7 16.4 %collective-permute-done = bf16[2,128,1536]{1,2,0:T(8,128)(2,1)S(1)} collective-permute-done((bf16[2,128,1536]{1,2,0:T(8,128)(2,1)}, bf16[2,128,1536]{1,2,0:T(8,128)(2,1)S(1)}, u32[]{:S(2)}, u32[]{:S(2)}) %collective-permute-start) | collective-permute-done | bytes 786464 | tf_op jit(solution)/shard_map/ppermute | solution.py:18
  26.0 1.9 %collective-permute-start.1 = (bf16[2,128,1536]{1,2,0:T(8,128)(2,1)S(1)}, bf16[2,128,1536]{1,2,0:T(8,128)(2,1)}, u32[]{:S(2)}, u32[]{:S(2)}) collective-permute-start(bf16[2,128,1536]{1,2,0:T(8,128)(2,1)S(1)} %collective-permute-done), channel_id=1, source_target_pairs={{0,1},{1,2},{2,3},{3,4},{4,5},{5,6},{6,7},{7,8},{8,9},{9,10},{10,1... | collective-permute-start | bytes 2359304 | tf_op jit(solution)/shard_map/ppermute | solution.py:18
  27.9 1.2 copy.42
  29.7 3.8 %collective-permute-done.2 = bf16[2,128,1536]{1,2,0:T(8,128)(2,1)S(1)} collective-permute-done((bf16[2,128,1536]{1,2,0:T(8,128)(2,1)}, bf16[2,128,1536]{1,2,0:T(8,128)(2,1)S(1)}, u32[]{:S(2)}, u32[]{:S(2)}) %collective-permute-start.2) | collective-permute-done | bytes 786464 | tf_op jit(solution)/shard_map/ppermute | solution.py:18
  33.5 3.7 %collective-permute-start.3 = (bf16[2,128,1536]{1,2,0:T(8,128)(2,1)S(1)}, bf16[2,128,1536]{1,2,0:T(8,128)(2,1)S(1)}, u32[]{:S(2)}, u32[]{:S(2)}) collective-permute-start(bf16[2,128,1536]{1,2,0:T(8,128)(2,1)S(1)} %collective-permute-done.2), channel_id=1, source_target_pairs={{1,0},{2,1},{3,2},{4,3},{5,4},{6,5},{7,6},{8,7},{9,8},{10,9},{11,1... | collective-permute-start | bytes 2359304 | tf_op jit(solution)/shard_map/ppermute | solution.py:18
  37.2 10.7 %collective-permute-done.1 = bf16[2,128,1536]{1,2,0:T(8,128)(2,1)} collective-permute-done((bf16[2,128,1536]{1,2,0:T(8,128)(2,1)S(1)}, bf16[2,128,1536]{1,2,0:T(8,128)(2,1)}, u32[]{:S(2)}, u32[]{:S(2)}) %collective-permute-start.1) | collective-permute-done | bytes 786464 | tf_op jit(solution)/shard_map/ppermute | solution.py:18
  47.9 1.3 constant_dynamic-update-slice_fusion.4
  49.9 1.7 %fusion.29 = (bf16[1,640,1536]{1,2,0:T(8,128)(2,1)}, bf16[1,640,1536]{1,2,0:T(8,128)(2,1)S(1)}) fusion(bf16[2,640,1536]{1,2,0:T(8,128)(2,1)S(1)} %constant_dynamic-update-slice_fusion), kind=kLoop, calls=%fused_computation.50 | loop fusion | bytes 7864320 | tf_op jit(solution)/shard_map/slice | solution.py:76
  51.6 3.5 %fusion.31 = (f32[12,128]{1,0:T(8,128)S(1)}, f32[12,128,640]{1,2,0:T(8,128)}) fusion(pred[640]{0:T(1024)(128)(4,1)S(1)} %broadcast_bitcast_fusion, bf16[640,12,128]{0,2,1:T(8,128)(2,1)S(1)} %bitcast.66, bf16[128,12,128]{0,2,1:T(8,128)(2,1)S(1)} %bitcast.70), kind=kOutput, calls=%fused_computation.52 | convolution fusion | flops 255591040 | bytes 6298240 | tf_op jit(solution)/shard_map/sub | solution.py:65
  55.2 2.5 %fusion.10 = bf16[12,128,640]{1,2,0:T(8,128)(2,1)S(1)} fusion(f32[12,128,640]{1,2,0:T(8,128)} %get-tuple-element.25, f32[12,128]{1,0:T(8,128)S(1)} %get-tuple-element.24), kind=kLoop, calls=%fused_computation.21 | loop fusion | flops 1966080 | bytes 5904384 | tf_op jit(solution)/shard_map/convert_element_type | solution.py:68
  57.7 2.9 %fusion.32 = f32[12,640,128]{1,2,0:T(8,128)} fusion(bf16[12,128,640]{1,2,0:T(8,128)(2,1)S(1)} %fusion.10, bf16[128,12,128]{0,2,1:T(8,128)(2,1)S(1)} %bitcast.72), kind=kOutput, calls=%fused_computation.53 | convolution fusion | flops 251658240 | bytes 6291456 | tf_op jit(solution)/shard_map/hqk,qhd->khd/dot_general | solution.py:77
  61.8 1.0 fusion.2
  62.8 2.6 %multiply_bitcast_fusion = f32[640,12,128]{2,0,1:T(8,128)} fusion(bf16[12,128,640]{1,2,0:T(8,128)(2,1)S(1)} %fusion.2, bf16[128,12,128]{0,2,1:T(8,128)(2,1)S(1)} %bitcast.71), kind=kOutput, calls=%fused_computation.15 | convolution fusion | flops 252641280 | bytes 6291456 | tf_op jit(solution)/shard_map/hqk,qhd->khd/dot_general | solution.py:88
  65.5 5.5 %copy.52 = f32[640,12,128]{0,2,1:T(8,128)} copy(f32[640,12,128]{2,0,1:T(8,128)} %multiply_bitcast_fusion) | data formatting | bytes 7864320 | tf_op jit(solution)/shard_map/mul | solution.py:88
  70.9 4.0 %fusion.1 = bf16[2,640,1536]{1,2,0:T(8,128)(2,1)S(1)} fusion(f32[1,640,1536]{1,2,0:T(8,128)} %bitcast.60, f32[1,640,1536]{1,2,0:T(8,128)} %bitcast.63), kind=kLoop, calls=%fused_computation.8 | loop fusion | flops 1966080 | bytes 11796480 | tf_op jit(solution)/shard_map/convert.3
  75.2 2.1 %collective-permute-start.4 = (bf16[2,128,1536]{1,2,0:T(8,128)(2,1)S(1)}, bf16[2,128,1536]{1,2,0:T(8,128)(2,1)S(1)}, u32[]{:S(2)}, u32[]{:S(2)}) collective-permute-start(bf16[2,128,1536]{1,2,0:T(8,128)(2,1)S(1)} %get-tuple-element.18), channel_id=1, source_target_pairs={{0,1},{1,2},{2,3},{3,4},{4,5},{5,6},{6,7},{7,8},{8,9},{9,10},{10,1... | collective-permute-start | bytes 2359304 | tf_op jit(solution)/shard_map/ppermute | solution.py:18
  77.3 3.6 %collective-permute-start.6 = (bf16[2,128,1536]{1,2,0:T(8,128)(2,1)S(1)}, bf16[2,128,1536]{1,2,0:T(8,128)(2,1)S(1)}, u32[]{:S(2)}, u32[]{:S(2)}) collective-permute-start(bf16[2,128,1536]{1,2,0:T(8,128)(2,1)S(1)} %get-tuple-element.19), channel_id=1, source_target_pairs={{1,0},{2,1},{3,2},{4,3},{5,4},{6,5},{7,6},{8,7},{9,8},{10,9},{11,1... | collective-permute-start | bytes 2359304 | tf_op jit(solution)/shard_map/ppermute | solution.py:18
  80.9 16.2 %collective-permute-done.4 = bf16[2,128,1536]{1,2,0:T(8,128)(2,1)S(1)} collective-permute-done((bf16[2,128,1536]{1,2,0:T(8,128)(2,1)S(1)}, bf16[2,128,1536]{1,2,0:T(8,128)(2,1)S(1)}, u32[]{:S(2)}, u32[]{:S(2)}) %collective-permute-start.4) | collective-permute-done | bytes 786464 | tf_op jit(solution)/shard_map/ppermute | solution.py:18
  97.4 1.9 %collective-permute-start.5 = (bf16[2,128,1536]{1,2,0:T(8,128)(2,1)S(1)}, bf16[2,128,1536]{1,2,0:T(8,128)(2,1)S(1)}, u32[]{:S(2)}, u32[]{:S(2)}) collective-permute-start(bf16[2,128,1536]{1,2,0:T(8,128)(2,1)S(1)} %get-tuple-element.16), channel_id=1, source_target_pairs={{0,1},{1,2},{2,3},{3,4},{4,5},{5,6},{6,7},{7,8},{8,9},{9,10},{10,1... | collective-permute-start | bytes 2359304 | tf_op jit(solution)/shard_map/ppermute | solution.py:18
  99.3 3.8 %collective-permute-start.7 = (bf16[2,128,1536]{1,2,0:T(8,128)(2,1)S(1)}, bf16[2,128,1536]{1,2,0:T(8,128)(2,1)S(1)}, u32[]{:S(2)}, u32[]{:S(2)}) collective-permute-start(bf16[2,128,1536]{1,2,0:T(8,128)(2,1)S(1)} %get-tuple-element.17), channel_id=1, source_target_pairs={{1,0},{2,1},{3,2},{4,3},{5,4},{6,5},{7,6},{8,7},{9,8},{10,9},{11,1... | collective-permute-start | bytes 2359304 | tf_op jit(solution)/shard_map/ppermute | solution.py:18
  103.1 16.0 %collective-permute-done.5 = bf16[2,128,1536]{1,2,0:T(8,128)(2,1)S(1)} collective-permute-done((bf16[2,128,1536]{1,2,0:T(8,128)(2,1)S(1)}, bf16[2,128,1536]{1,2,0:T(8,128)(2,1)S(1)}, u32[]{:S(2)}, u32[]{:S(2)}) %collective-permute-start.5) | collective-permute-done | bytes 786464 | tf_op jit(solution)/shard_map/ppermute | solution.py:18
  119.5 1.3 collective-permute-start.8
  121.4 0.9 copy.54
  122.4 0.9 copy.56
  123.3 0.9 copy.55
  124.2 4.9 %collective-permute-done.8 = bf16[1,128,1536]{1,2,0:T(8,128)(2,1)S(1)} collective-permute-done((bf16[1,128,1536]{1,2,0:T(8,128)(2,1)S(1)}, bf16[1,128,1536]{1,2,0:T(8,128)(2,1)S(1)}, u32[]{:S(2)}, u32[]{:S(2)}) %collective-permute-start.8) | collective-permute-done | bytes 393248 | tf_op jit(solution)/shard_map/ppermute | solution.py:18
  129.1 0.9 copy.57
  (34 shorter events, 4.1 us)
Async XLA Ops:
  0.6 28.5 %copy-start.6 = (bf16[1,128,1536]{2,1,0:T(8,128)(2,1)S(1)}, bf16[1,128,1536]{2,1,0:T(8,128)(2,1)}, u32[]{:S(2)}) copy-start(bf16[1,128,1536]{2,1,0:T(8,128)(2,1)} %param.8) | copy-start | bytes 1179652
  0.6 28.9 %copy-start.7 = (s32[1,5]{1,0:T(1,128)S(1)}, s32[1,5]{1,0:T(1,128)}, u32[]{:S(2)}) copy-start(s32[1,5]{1,0:T(1,128)} %param.9) | copy-start | bytes 64
  4.1 21.9 %collective-permute-start = (bf16[2,128,1536]{1,2,0:T(8,128)(2,1)}, bf16[2,128,1536]{1,2,0:T(8,128)(2,1)S(1)}, u32[]{:S(2)}, u32[]{:S(2)}) collective-permute-start(bf16[2,128,1536]{1,2,0:T(8,128)(2,1)} %pad_maximum_fusion.1), channel_id=1, source_target_pairs={{0,1},{1,2},{2,3},{3,4},{4,5},{5,6},{6,7},{7,8},{8,9},{9,10},{10,1... | collective-permute-start | bytes 2359304 | tf_op jit(solution)/shard_map/ppermute | solution.py:18
  6.0 27.5 %collective-permute-start.2 = (bf16[2,128,1536]{1,2,0:T(8,128)(2,1)}, bf16[2,128,1536]{1,2,0:T(8,128)(2,1)S(1)}, u32[]{:S(2)}, u32[]{:S(2)}) collective-permute-start(bf16[2,128,1536]{1,2,0:T(8,128)(2,1)} %pad_maximum_fusion.1), channel_id=1, source_target_pairs={{1,0},{2,1},{3,2},{4,3},{5,4},{6,5},{7,6},{8,7},{9,8},{10,9},{11,1... | collective-permute-start | bytes 2359304 | tf_op jit(solution)/shard_map/ppermute | solution.py:18
  26.0 21.8 %collective-permute-start.1 = (bf16[2,128,1536]{1,2,0:T(8,128)(2,1)S(1)}, bf16[2,128,1536]{1,2,0:T(8,128)(2,1)}, u32[]{:S(2)}, u32[]{:S(2)}) collective-permute-start(bf16[2,128,1536]{1,2,0:T(8,128)(2,1)S(1)} %collective-permute-done), channel_id=1, source_target_pairs={{0,1},{1,2},{2,3},{3,4},{4,5},{5,6},{6,7},{7,8},{8,9},{9,10},{10,1... | collective-permute-start | bytes 2359304 | tf_op jit(solution)/shard_map/ppermute | solution.py:18
  33.5 16.2 %collective-permute-start.3 = (bf16[2,128,1536]{1,2,0:T(8,128)(2,1)S(1)}, bf16[2,128,1536]{1,2,0:T(8,128)(2,1)S(1)}, u32[]{:S(2)}, u32[]{:S(2)}) collective-permute-start(bf16[2,128,1536]{1,2,0:T(8,128)(2,1)S(1)} %collective-permute-done.2), channel_id=1, source_target_pairs={{1,0},{2,1},{3,2},{4,3},{5,4},{6,5},{7,6},{8,7},{9,8},{10,9},{11,1... | collective-permute-start | bytes 2359304 | tf_op jit(solution)/shard_map/ppermute | solution.py:18
  51.6 3.6 %copy-start.2 = (bf16[1,640,1536]{1,2,0:T(8,128)(2,1)}, bf16[1,640,1536]{1,2,0:T(8,128)(2,1)S(1)}, u32[]{:S(2)}) copy-start(bf16[1,640,1536]{1,2,0:T(8,128)(2,1)S(1)} %get-tuple-element.21) | copy-start | bytes 5898244
  57.7 2.9 %copy-start.5 = (bf16[1,640,1536]{1,2,0:T(8,128)(2,1)S(1)}, bf16[1,640,1536]{1,2,0:T(8,128)(2,1)}, u32[]{:S(2)}) copy-start(bf16[1,640,1536]{1,2,0:T(8,128)(2,1)} %get-tuple-element.20) | copy-start | bytes 5898244
  57.7 4.1 %copy-start.4 = (f32[12,128,640]{1,2,0:T(8,128)S(1)}, f32[12,128,640]{1,2,0:T(8,128)}, u32[]{:S(2)}) copy-start(f32[12,128,640]{1,2,0:T(8,128)} %get-tuple-element.25) | copy-start | bytes 11796484
  70.9 26.2 %copy-start = (f32[12,640,128]{1,2,0:T(8,128)S(1)}, f32[12,640,128]{1,2,0:T(8,128)}, u32[]{:S(2)}) copy-start(f32[12,640,128]{1,2,0:T(8,128)} %fusion.32) | copy-start | bytes 11796484
  70.9 26.2 %copy-start.1 = (f32[640,12,128]{0,2,1:T(8,128)S(1)}, f32[640,12,128]{0,2,1:T(8,128)}, u32[]{:S(2)}) copy-start(f32[640,12,128]{0,2,1:T(8,128)} %copy.52) | copy-start | bytes 11796484
  75.2 21.9 %collective-permute-start.4 = (bf16[2,128,1536]{1,2,0:T(8,128)(2,1)S(1)}, bf16[2,128,1536]{1,2,0:T(8,128)(2,1)S(1)}, u32[]{:S(2)}, u32[]{:S(2)}) collective-permute-start(bf16[2,128,1536]{1,2,0:T(8,128)(2,1)S(1)} %get-tuple-element.18), channel_id=1, source_target_pairs={{0,1},{1,2},{2,3},{3,4},{4,5},{5,6},{6,7},{7,8},{8,9},{9,10},{10,1... | collective-permute-start | bytes 2359304 | tf_op jit(solution)/shard_map/ppermute | solution.py:18
  77.3 19.8 %collective-permute-start.6 = (bf16[2,128,1536]{1,2,0:T(8,128)(2,1)S(1)}, bf16[2,128,1536]{1,2,0:T(8,128)(2,1)S(1)}, u32[]{:S(2)}, u32[]{:S(2)}) collective-permute-start(bf16[2,128,1536]{1,2,0:T(8,128)(2,1)S(1)} %get-tuple-element.19), channel_id=1, source_target_pairs={{1,0},{2,1},{3,2},{4,3},{5,4},{6,5},{7,6},{8,7},{9,8},{10,9},{11,1... | collective-permute-start | bytes 2359304 | tf_op jit(solution)/shard_map/ppermute | solution.py:18
  97.4 21.7 %collective-permute-start.5 = (bf16[2,128,1536]{1,2,0:T(8,128)(2,1)S(1)}, bf16[2,128,1536]{1,2,0:T(8,128)(2,1)S(1)}, u32[]{:S(2)}, u32[]{:S(2)}) collective-permute-start(bf16[2,128,1536]{1,2,0:T(8,128)(2,1)S(1)} %get-tuple-element.16), channel_id=1, source_target_pairs={{0,1},{1,2},{2,3},{3,4},{4,5},{5,6},{6,7},{7,8},{8,9},{9,10},{10,1... | collective-permute-start | bytes 2359304 | tf_op jit(solution)/shard_map/ppermute | solution.py:18
  99.3 21.4 %copy-start.3 = (bf16[1,640,1536]{1,2,0:T(8,128)(2,1)S(1)}, bf16[1,640,1536]{1,2,0:T(8,128)(2,1)}, u32[]{:S(2)}) copy-start(bf16[1,640,1536]{1,2,0:T(8,128)(2,1)} %copy-done.2) | copy-start | bytes 5898244
  99.3 19.8 %collective-permute-start.7 = (bf16[2,128,1536]{1,2,0:T(8,128)(2,1)S(1)}, bf16[2,128,1536]{1,2,0:T(8,128)(2,1)S(1)}, u32[]{:S(2)}, u32[]{:S(2)}) collective-permute-start(bf16[2,128,1536]{1,2,0:T(8,128)(2,1)S(1)} %get-tuple-element.17), channel_id=1, source_target_pairs={{1,0},{2,1},{3,2},{4,3},{5,4},{6,5},{7,6},{8,7},{9,8},{10,9},{11,1... | collective-permute-start | bytes 2359304 | tf_op jit(solution)/shard_map/ppermute | solution.py:18
  119.5 9.7 %collective-permute-start.8 = (bf16[1,128,1536]{1,2,0:T(8,128)(2,1)S(1)}, bf16[1,128,1536]{1,2,0:T(8,128)(2,1)S(1)}, u32[]{:S(2)}, u32[]{:S(2)}) collective-permute-start(bf16[1,128,1536]{1,2,0:T(8,128)(2,1)S(1)} %get-tuple-element.22), channel_id=1, source_target_pairs={{16,0},{17,1},{18,2},{19,3},{20,4},{21,5},{22,6},{23,7},{24,8},{25... | collective-permute-start | bytes 1179656 | tf_op jit(solution)/shard_map/ppermute | solution.py:18
where the time goes:
time: 131 us; the launch traced here: 130 us
  waiting for transfers between devices  67.9 us (52%)
  starting transfers between devices  23.8 us (18%)
  local copies, waits for them, and re-layouts  17.7 us (14%)
  matrix products  11.4 us (9%)
  other arithmetic  8.31 us (6%)
    ppermute x9, waiting for transfers between devices, from_behind(): lax.ppermute(value, axis, [(source, source + steps) for source in range(f...  67.9 us
    ppermute x9, starting transfers between devices, from_behind(): lax.ppermute(value, axis, [(source, source + steps) for source in range(f...  23.8 us
    unnamed x27, local copies, waits for them, and re-layouts  9.83 us
    mul x1, local copies, waits for them, and re-layouts, shards(): jnp.einsum('hqk,qhd->khd', scores_low, own_query, preferred_element_type=...  5.45 us
    another operation x2, other arithmetic  4.25 us
    sub x1, matrix products, shards(): weights = jnp.exp(scores - highest)  3.55 us
    dot_general x1, matrix products, shards(): jnp.einsum('hqk,qhd->khd', probs_low, own_grad, preferred_element_type=jn...  2.86 us
    dot_general x1, matrix products, shards(): jnp.einsum('hqk,qhd->khd', scores_low, own_query, preferred_element_type=...  2.64 us
  transfers between devices with their start and end apart: 9, of which 6 were waited for; matrix products, arithmetic and copies ran while one was open for 5% of the time, Pallas kernels for 0%

commit v1 on v0

v1 whole, which is shorter than its diff:
```python
import jax
import jax.numpy as jnp
from jax import lax
from jax.experimental import pallas as pl
from jax.experimental.pallas import tpu as pltpu
from jax.sharding import PartitionSpec as P

H = 12
DH = 128
BLK = 128
REACH = 2
TEAM = 4
LOCAL = H // TEAM
SPAN = 2 * REACH + 1
SLOTS = TEAM + 2 * REACH
SCALE = DH ** (-0.5)
LOG2E = 1.4426950408889634
OFF = -1e30
MASK = 16

bf16 = jnp.bfloat16
f32 = jnp.float32


def member():
    return lax.rem(lax.axis_index("ctx"), TEAM)


def rows_of(index, count=BLK):
    return pl.ds(pl.multiple_of(index * BLK, BLK), count)


def pack_kernel(lists, q, k, v, g, own, one, kv2, kv3, qg2, qg3, edge):
    block = lax.axis_index("ctx")
    me = member()
    row = lax.broadcasted_iota(jnp.int32, (MASK, DH), 0)
    mask = jnp.full((MASK, DH), OFF, f32)
    for o in range(SPAN):
        wanted = jnp.int32(0)
        for n in range(lists.shape[1]):
            entry = lists[0, n]
            hit = (entry >= 0) & (entry == block + (o - REACH))
            wanted = jnp.maximum(wanted, hit.astype(jnp.int32))
        level = jnp.where(wanted > 0, 0.0, OFF).astype(f32)
        mask = jnp.where(row == o, level, mask)
    mask = mask.astype(bf16)

    def cut(source, group, h):
        start = pl.multiple_of(group * (LOCAL * DH) + h * DH, DH)
        return source[0, :, pl.ds(start, DH)]

    for h in range(LOCAL):
        for target, step in ((own, 0), (one, 1)):
            group = jnp.bitwise_xor(me, step)
            for n, source in enumerate((k, v, q, g)):
                piece = cut(source, group, h)
                target[h, n * BLK : (n + 1) * BLK, :] = piece
                if n < 2:
                    edge[step, h, n * BLK : (n + 1) * BLK, :] = piece
            target[h, 4 * BLK :, :] = mask
        for kv, qg, step in ((kv2, qg2, 2), (kv3, qg3, 3)):
            group = jnp.bitwise_xor(me, step)
            for n, source in enumerate((k, v)):
                kv[h, n * BLK : (n + 1) * BLK, :] = cut(source, group, h)
            for n, source in enumerate((q, g)):
                qg[h, n * BLK : (n + 1) * BLK, :] = cut(source, group, h)
            qg[h, 2 * BLK :, :] = mask


def nt(a, b):
    return lax.dot_general(a, b, (((1,), (1,)), ((), ())), preferred_element_type=f32)


def tn(a, b):
    return lax.dot_general(a, b, (((0,), (0,)), ((), ())), preferred_element_type=f32)


def nn(a, b):
    return lax.dot_general(a, b, (((1,), (0,)), ((), ())), preferred_element_type=f32)


def attend_kernel(
    own, one, kv2, kv3, qg2, qg3, edge0, edge1, late2, late3,
    dq0, dq1, dq2, dq3, dv_own, dk_own, dv_low, dv_high, dk_low, dk_high,
    ks, vs, qs, gs, bs, ps, ss, dqs,
):
    me = member()
    side = me // 2
    core = lax.rem(me, 2)
    other = 1 - core

    def put_kv(slot, source, lead=0):
        ks[rows_of(slot), :] = source[(0,) * lead + (slice(0, BLK),)]
        vs[rows_of(slot), :] = source[(0,) * lead + (slice(BLK, 2 * BLK),)]

    def put_qg(position, source, base):
        qs[rows_of(position), :] = source[0, base : base + BLK]
        gs[rows_of(position), :] = source[0, base + BLK : base + 2 * BLK]
        bs[pl.ds(pl.multiple_of(position * MASK, MASK), MASK), :] = source[
            0, base + 2 * BLK : base + 2 * BLK + MASK
        ]

    for step, source in ((0, own), (1, one), (2, kv2), (3, kv3)):
        put_kv(REACH + jnp.bitwise_xor(me, step), source, 1)
    for step, source, base in ((0, own, 2 * BLK), (1, one, 2 * BLK), (2, qg2, 0), (3, qg3, 0)):
        put_qg(jnp.bitwise_xor(me, step), source, base)
    near = (1 - side) * (REACH + TEAM)
    far = side * (REACH + TEAM)
    put_kv(near + core, edge0, 2)
    put_kv(near + other, edge1, 2)
    put_kv(far + core, late2, 1)
    put_kv(far + other, late3, 1)

    for i in range(TEAM):
        here = slice(i * BLK, (i + 1) * BLK)
        reach = slice(i * BLK, (i + SPAN) * BLK)
        keys, values = ks[reach, :], vs[reach, :]
        query, grad = qs[here, :], gs[here, :]
        bias = bs[i * MASK : (i + 1) * MASK, :].astype(f32)
        scores = nt(keys, query) * (SCALE * LOG2E)
        scores = jnp.concatenate(
            [scores[o * BLK : (o + 1) * BLK] + bias[o : o + 1] for o in range(SPAN)], axis=0
        )
        highest = jnp.max(scores, axis=0, keepdims=True)
        weights = jnp.exp2(scores - highest)
        probs = weights * (1.0 / jnp.sum(weights, axis=0, keepdims=True))
        probs_low = probs.astype(bf16)
        grad_probs = nt(values, grad)
        delta = jnp.sum(probs_low.astype(f32) * grad_probs, axis=0, keepdims=True)
        scores_low = (probs * (grad_probs - delta)).astype(bf16)
        dqs[here, :] = (tn(scores_low, keys) * SCALE).astype(bf16)
        ps[reach, here] = probs_low
        ss[reach, here] = scores_low
    for step, target in enumerate((dq0, dq1, dq2, dq3)):
        target[0] = dqs[rows_of(jnp.bitwise_xor(me, step)), :]
    for j in range(SLOTS):
        there = slice(j * BLK, (j + 1) * BLK)
        seen = slice(max(0, j - SPAN + 1) * BLK, (min(TEAM - 1, j) + 1) * BLK)
        dv = nn(ps[there, seen], gs[seen, :])
        dk = nn(ss[there, seen], qs[seen, :]) * SCALE
        if j < REACH:
            dv_low[0, there, :] = dv.astype(bf16)
            dk_low[0, there, :] = dk.astype(bf16)
        elif j < REACH + TEAM:
            at = slice((j - REACH) * BLK, (j - REACH + 1) * BLK)
            dv_own[0, at, :] = dv
            dk_own[0, at, :] = dk
        else:
            at = slice((j - REACH - TEAM) * BLK, (j - REACH - TEAM + 1) * BLK)
            dv_high[0, at, :] = dv.astype(bf16)
            dk_high[0, at, :] = dk.astype(bf16)


def total_kernel(mine, from_below, from_above, out0, out1, out2, out3):
    me = member()
    half = REACH * BLK
    for step, target in enumerate((out0, out1, out2, out3)):
        block = jnp.bitwise_xor(me, step)
        low = block < REACH
        at = rows_of(lax.rem(block, REACH))
        term = jnp.where(low, from_below[0, at, :].astype(f32), from_above[0, at, :].astype(f32))
        target[0] = (mine[0, rows_of(block), :] + term).astype(bf16)


def unpack_kernel(in0, in1, in2, in3, out):
    me = member()
    for step, source in enumerate((in0, in1, in2, in3)):
        group = jnp.bitwise_xor(me, step)
        for h in range(LOCAL):
            start = pl.multiple_of(group * (LOCAL * DH) + h * DH, DH)
            out[0, :, pl.ds(start, DH)] = source[h]


def struct(*shape, dtype=bf16):
    return jax.ShapeDtypeStruct(shape, dtype)


VM = pl.BlockSpec(memory_space=pltpu.VMEM)


def per_head(*tail):
    return pl.BlockSpec((1, *tail), lambda h: (h, 0, 0))


def params():
    return pltpu.CompilerParams(vmem_limit_bytes=40 * 1024 * 1024)


def shards(query_rows, key_rows, value_rows, grad_output, block_lists):
    ctx = lax.axis_size("ctx")
    width = query_rows.shape[2]

    def swap(array, step):
        return lax.ppermute(array, "ctx", [(i, i ^ step) for i in range(ctx)])

    def ring(array, low, high):
        pairs = [
            (i, (i + TEAM * (low if i % TEAM < TEAM // 2 else high)) % ctx) for i in range(ctx)
        ]
        return lax.ppermute(array, "ctx", pairs)

    kv = struct(LOCAL, 2 * BLK, DH)
    qg = struct(LOCAL, 2 * BLK + MASK, DH)
    full = struct(LOCAL, 4 * BLK + MASK, DH)
    own, one, kv2, kv3, qg2, qg3, edge = pl.pallas_call(
        pack_kernel,
        out_shape=(full, full, kv, kv, qg, qg, struct(2, LOCAL, 2 * BLK, DH)),
        in_specs=[pl.BlockSpec(memory_space=pltpu.SMEM)] + [VM] * 4,
        out_specs=[VM] * 7,
        compiler_params=params(),
        name="pack",
    )(block_lists, query_rows, key_rows, value_rows, grad_output)

    kv2 = swap(kv2, 2)
    kv3 = swap(kv3, 3)
    edge0 = ring(edge, -1, 1)
    one = swap(one, 1)
    qg2 = swap(qg2, 2)
    qg3 = swap(qg3, 3)
    edge1 = swap(edge0, 1)
    late2 = ring(kv2, 1, -1)
    late3 = ring(kv3, 1, -1)

    block = struct(LOCAL, BLK, DH)
    kept = struct(LOCAL, TEAM * BLK, DH, dtype=f32)
    halo = struct(LOCAL, REACH * BLK, DH)
    piece = per_head(BLK, DH)
    (dq0, dq1, dq2, dq3, dv_own, dk_own, dv_low, dv_high, dk_low, dk_high) = pl.pallas_call(
        attend_kernel,
        grid=(LOCAL,),
        out_shape=(block,) * 4 + (kept,) * 2 + (halo,) * 4,
        in_specs=[per_head(4 * BLK + MASK, DH)] * 2
        + [per_head(2 * BLK, DH)] * 2
        + [per_head(2 * BLK + MASK, DH)] * 2
        + [
            pl.BlockSpec((1, 1, 2 * BLK, DH), lambda h: (0, h, 0, 0)),
            pl.BlockSpec((1, 1, 2 * BLK, DH), lambda h: (1, h, 0, 0)),
        ]
        + [per_head(2 * BLK, DH)] * 2,
        out_specs=[piece] * 4 + [per_head(TEAM * BLK, DH)] * 2 + [per_head(REACH * BLK, DH)] * 4,
        scratch_shapes=[
            pltpu.VMEM((SLOTS * BLK, DH), bf16),
            pltpu.VMEM((SLOTS * BLK, DH), bf16),
            pltpu.VMEM((TEAM * BLK, DH), bf16),
            pltpu.VMEM((TEAM * BLK, DH), bf16),
            pltpu.VMEM((TEAM * MASK, DH), bf16),
            pltpu.VMEM((SLOTS * BLK, TEAM * BLK), bf16),
            pltpu.VMEM((SLOTS * BLK, TEAM * BLK), bf16),
            pltpu.VMEM((TEAM * BLK, DH), bf16),
        ],
        compiler_params=params(),
        name="attend",
    )(own, one, kv2, kv3, qg2, qg3, edge0, edge1, late2, late3)

    def total(mine, low, high):
        below = ring(high, 1, 1)
        above = ring(low, -1, -1)
        return pl.pallas_call(
            total_kernel,
            grid=(LOCAL,),
            out_shape=(block,) * 4,
            in_specs=[per_head(TEAM * BLK, DH)] + [per_head(REACH * BLK, DH)] * 2,
            out_specs=[piece] * 4,
            compiler_params=params(),
            name="total",
        )(mine, below, above)

    def home(parts):
        parts = [parts[0]] + [swap(parts[step], step) for step in range(1, TEAM)]
        return pl.pallas_call(
            unpack_kernel,
            out_shape=struct(1, BLK, width),
            in_specs=[VM] * 4,
            out_specs=VM,
            compiler_params=params(),
            name="unpack",
        )(*parts)

    grad_value = home(total(dv_own, dv_low, dv_high))
    sections = lax.axis_size("section")
    handoff = lax.ppermute(grad_value, "section", [(s + 1, s) for s in range(sections - 1)])
    grad_query = home((dq0, dq1, dq2, dq3))
    grad_key = home(total(dk_own, dk_low, dk_high))
    return (grad_query, grad_key, grad_value, handoff)


def solution(mesh):
    wide = P("section", "ctx", None)
    return jax.shard_map(
        shards,
        mesh=mesh,
        in_specs=(wide, wide, wide, wide, P("ctx", None)),
        out_specs=(wide,) * 4,
        check_vma=False,
    )
```

time: 131 us -> 87.3 us (0.67)
  the two profiles are of different devices: /device:TPU:12 before, /device:TPU:0 now
where the time goes in v1:
time: 87.3 us; the launch traced here: 86.9 us
  waiting for transfers between devices  43.4 us (50%)
  starting transfers between devices  25.9 us (30%)
  Pallas kernels  11.6 us (13%)
  local copies, waits for them, and re-layouts  5.38 us (6%)
    ppermute x7, waiting for transfers between devices, ring(): return lax.ppermute(array, 'ctx', pairs)  29.7 us
    ppermute x7, starting transfers between devices, ring(): return lax.ppermute(array, 'ctx', pairs)  15.6 us
    ppermute x15, waiting for transfers between devices, swap(): return lax.ppermute(array, 'ctx', [(i, i ^ step) for i in range(ctx)])  13.7 us
    ppermute x15, starting transfers between devices, swap(): return lax.ppermute(array, 'ctx', [(i, i ^ step) for i in range(ctx)])  9.05 us
    pallas_call x1, Pallas kernels, shards(): pl.pallas_call(attend_kernel, grid=(LOCAL,), out_shape=(block,) * 4 + (ke...  7.8 us
    unnamed x11, local copies, waits for them, and re-layouts  5.38 us
    pallas_call x3, Pallas kernels, home(): pl.pallas_call(unpack_kernel, out_shape=struct(1, BLK, width), in_specs=[...  2.47 us
  transfers between devices with their start and end apart: 23, of which 13 were waited for; matrix products, arithmetic and copies ran while one was open for 0% of the time, Pallas kernels for 2%

profile of v1, /device:TPU:0, one launch (start us, length us, event | category | flops | bytes accessed | tf_op | source)
XLA Modules:
  0.0 86.9 jit_solution(10283107965742733844)
XLA Ops:
  0.6 1.0 %copy-done = bf16[1,128,1536]{2,1,0:T(8,128)(2,1)S(1)} copy-done((bf16[1,128,1536]{2,1,0:T(8,128)(2,1)S(1)}, bf16[1,128,1536]{2,1,0:T(8,128)(2,1)}, u32[]{:S(2)}) %copy-start) | copy-done | bytes 393240
  1.6 1.0 %copy-done.1 = bf16[1,128,1536]{2,1,0:T(8,128)(2,1)S(1)} copy-done((bf16[1,128,1536]{2,1,0:T(8,128)(2,1)S(1)}, bf16[1,128,1536]{2,1,0:T(8,128)(2,1)}, u32[]{:S(2)}) %copy-start.1) | copy-done | bytes 393240
  2.6 1.0 %copy-done.2 = bf16[1,128,1536]{2,1,0:T(8,128)(2,1)S(1)} copy-done((bf16[1,128,1536]{2,1,0:T(8,128)(2,1)S(1)}, bf16[1,128,1536]{2,1,0:T(8,128)(2,1)}, u32[]{:S(2)}) %copy-start.2) | copy-done | bytes 393240
  3.6 1.0 %copy-done.3 = bf16[1,128,1536]{2,1,0:T(8,128)(2,1)S(1)} copy-done((bf16[1,128,1536]{2,1,0:T(8,128)(2,1)S(1)}, bf16[1,128,1536]{2,1,0:T(8,128)(2,1)}, u32[]{:S(2)}) %copy-start.3) | copy-done | bytes 393240
  5.3 0.9 %pack.1 = (bf16[3,528,128]{2,1,0:T(8,128)(2,1)S(1)}, bf16[3,528,128]{2,1,0:T(8,128)(2,1)S(1)}, bf16[3,256,128]{2,1,0:T(8,128)(2,1)S(1)}, bf16[3,256,128]{2,1,0:T...) custom-call(s32[1,5]{1,0:T(1,128)S(1)} %copy-done.4, ...), custom_call_target="tpu_custom_call" | custom-call | tf_op jit(solution)/shard_map/pack/pallas_call | solution.py:205
  6.2 5.1 %collective-permute-start.5 = (bf16[2,3,256,128]{3,2,1,0:T(8,128)(2,1)S(1)}, bf16[2,3,256,128]{3,2,1,0:T(8,128)(2,1)S(1)}, u32[]{:S(2)}, u32[]{:S(2)}) collective-permute-start(bf16[2,3,256,128]{3,2,1,0:T(8,128)(2,1)S(1)} %get-tuple-element.35), channel_id=1, source_target_pairs={{0,12},{1,13},{2,6},{3,7},{4,0},{5,1},{6,10},{7,11},{8,4},{9,5},{1... | collective-permute-start | bytes 1179656 | tf_op jit(solution)/shard_map/ppermute | solution.py:200
  11.3 2.0 %collective-permute-start.3 = (bf16[3,272,128]{2,1,0:T(8,128)(2,1)S(1)}, bf16[3,272,128]{2,1,0:T(8,128)(2,1)S(1)}, u32[]{:S(2)}, u32[]{:S(2)}) collective-permute-start(bf16[3,272,128]{2,1,0:T(8,128)(2,1)S(1)} %get-tuple-element.33), channel_id=1, source_target_pairs={{0,2},{1,3},{2,0},{3,1},{4,6},{5,7},{6,4},{7,5},{8,10},{9,11},{10,... | collective-permute-start | bytes 626696 | tf_op jit(solution)/shard_map/ppermute | solution.py:194
  13.5 6.2 %collective-permute-done.5.edge0 = bf16[2,3,256,128]{3,2,1,0:T(8,128)(2,1)S(1)} collective-permute-done((bf16[2,3,256,128]{3,2,1,0:T(8,128)(2,1)S(1)}, bf16[2,3,256,128]{3,2,1,0:T(8,128)(2,1)S(1)}, u32[]{:S(2)}, u32[]{:S(2)}) %collective-permute-start.5) | collective-permute-done | bytes 393248 | tf_op jit(solution)/shard_map/ppermute | solution.py:200
  19.7 2.4 %collective-permute-start.4 = (bf16[3,272,128]{2,1,0:T(8,128)(2,1)S(1)}, bf16[3,272,128]{2,1,0:T(8,128)(2,1)S(1)}, u32[]{:S(2)}, u32[]{:S(2)}) collective-permute-start(bf16[3,272,128]{2,1,0:T(8,128)(2,1)S(1)} %get-tuple-element.34), channel_id=1, source_target_pairs={{0,3},{1,2},{2,1},{3,0},{4,7},{5,6},{6,5},{7,4},{8,11},{9,10},{10,... | collective-permute-start | bytes 626696 | tf_op jit(solution)/shard_map/ppermute | solution.py:194
  22.1 3.2 %collective-permute-done.2.kv3 = bf16[3,256,128]{2,1,0:T(8,128)(2,1)S(1)} collective-permute-done((bf16[3,256,128]{2,1,0:T(8,128)(2,1)S(1)}, bf16[3,256,128]{2,1,0:T(8,128)(2,1)S(1)}, u32[]{:S(2)}, u32[]{:S(2)}) %collective-permute-start.2) | collective-permute-done | bytes 196640 | tf_op jit(solution)/shard_map/ppermute | solution.py:194
  25.3 1.1 %collective-permute-start.7 = (bf16[3,256,128]{2,1,0:T(8,128)(2,1)S(1)}, bf16[3,256,128]{2,1,0:T(8,128)(2,1)S(1)}, u32[]{:S(2)}, u32[]{:S(2)}) collective-permute-start(bf16[3,256,128]{2,1,0:T(8,128)(2,1)S(1)} %collective-permute-done.1.kv2), channel_id=1, source_target_pairs={{0,4},{1,5},{2,14},{3,15},{4,8},{5,9},{6,2},{7,3},{8,12},{9,13},{1... | collective-permute-start | bytes 589832 | tf_op jit(solution)/shard_map/ppermute | solution.py:200
  26.4 1.6 %collective-permute-start.8 = (bf16[3,256,128]{2,1,0:T(8,128)(2,1)S(1)}, bf16[3,256,128]{2,1,0:T(8,128)(2,1)S(1)}, u32[]{:S(2)}, u32[]{:S(2)}) collective-permute-start(bf16[3,256,128]{2,1,0:T(8,128)(2,1)S(1)} %collective-permute-done.2.kv3), channel_id=1, source_target_pairs={{0,4},{1,5},{2,14},{3,15},{4,8},{5,9},{6,2},{7,3},{8,12},{9,13},{1... | collective-permute-start | bytes 589832 | tf_op jit(solution)/shard_map/ppermute | solution.py:200
  28.0 1.4 %collective-permute-done.4.qg3 = bf16[3,272,128]{2,1,0:T(8,128)(2,1)S(1)} collective-permute-done((bf16[3,272,128]{2,1,0:T(8,128)(2,1)S(1)}, bf16[3,272,128]{2,1,0:T(8,128)(2,1)S(1)}, u32[]{:S(2)}, u32[]{:S(2)}) %collective-permute-start.4) | collective-permute-done | bytes 208928 | tf_op jit(solution)/shard_map/ppermute | solution.py:194
  29.4 3.8 %collective-permute-done.7.late2 = bf16[3,256,128]{2,1,0:T(8,128)(2,1)S(1)} collective-permute-done((bf16[3,256,128]{2,1,0:T(8,128)(2,1)S(1)}, bf16[3,256,128]{2,1,0:T(8,128)(2,1)S(1)}, u32[]{:S(2)}, u32[]{:S(2)}) %collective-permute-start.7) | collective-permute-done | bytes 196640 | tf_op jit(solution)/shard_map/ppermute | solution.py:200
  33.1 4.2 %collective-permute-done.8.late3 = bf16[3,256,128]{2,1,0:T(8,128)(2,1)S(1)} collective-permute-done((bf16[3,256,128]{2,1,0:T(8,128)(2,1)S(1)}, bf16[3,256,128]{2,1,0:T(8,128)(2,1)S(1)}, u32[]{:S(2)}, u32[]{:S(2)}) %collective-permute-start.8) | collective-permute-done | bytes 196640 | tf_op jit(solution)/shard_map/ppermute | solution.py:200
  37.4 7.8 %attend.1 = (bf16[3,128,128]{2,1,0:T(8,128)(2,1)S(1)}, bf16[3,128,128]{2,1,0:T(8,128)(2,1)S(1)}, bf16[3,128,128]{2,1,0:T(8,128)(2,1)S(1)}, bf16[3,128,128]{2,1,0...) custom-call(bf16[3,528,128]{2,1,0:T(8,128)(2,1)S(1)} %get-tuple-elem, ...), custom_call_target="tpu_custom_call" | custom-call | tf_op jit(solution)/shard_map/attend/pallas_call | solution.py:228
  45.5 3.6 %collective-permute-start.18 = (bf16[3,256,128]{2,1,0:T(8,128)(2,1)S(1)}, bf16[3,256,128]{2,1,0:T(8,128)(2,1)S(1)}, u32[]{:S(2)}, u32[]{:S(2)}) collective-permute-start(bf16[3,256,128]{2,1,0:T(8,128)(2,1)S(1)} %get-tuple-element.49), channel_id=1, source_target_pairs={{0,12},{1,13},{2,14},{3,15},{4,0},{5,1},{6,2},{7,3},{8,4},{9,5},{1... | collective-permute-start | bytes 589832 | tf_op jit(solution)/shard_map/ppermute | solution.py:200
  49.0 5.4 %collective-permute-done.17.from_below = bf16[3,256,128]{2,1,0:T(8,128)(2,1)S(1)} collective-permute-done((bf16[3,256,128]{2,1,0:T(8,128)(2,1)S(1)}, bf16[3,256,128]{2,1,0:T(8,128)(2,1)S(1)}, u32[]{:S(2)}, u32[]{:S(2)}) %collective-permute-start.17) | collective-permute-done | bytes 196640 | tf_op jit(solution)/shard_map/ppermute | solution.py:200
  54.4 2.7 %collective-permute-done.18.from_above = bf16[3,256,128]{2,1,0:T(8,128)(2,1)S(1)} collective-permute-done((bf16[3,256,128]{2,1,0:T(8,128)(2,1)S(1)}, bf16[3,256,128]{2,1,0:T(8,128)(2,1)S(1)}, u32[]{:S(2)}, u32[]{:S(2)}) %collective-permute-start.18) | collective-permute-done | bytes 196640 | tf_op jit(solution)/shard_map/ppermute | solution.py:200
  58.0 1.2 %collective-permute-start.21 = (bf16[3,128,128]{2,1,0:T(8,128)(2,1)S(1)}, bf16[3,128,128]{2,1,0:T(8,128)(2,1)S(1)}, u32[]{:S(2)}, u32[]{:S(2)}) collective-permute-start(bf16[3,128,128]{2,1,0:T(8,128)(2,1)S(1)} %get-tuple-element.53), channel_id=1, source_target_pairs={{0,3},{1,2},{2,1},{3,0},{4,7},{5,6},{6,5},{7,4},{8,11},{9,10},{10,... | collective-permute-start | bytes 294920 | tf_op jit(solution)/shard_map/ppermute | solution.py:194
  59.2 3.9 %collective-permute-done.20.in2 = bf16[3,128,128]{2,1,0:T(8,128)(2,1)S(1)} collective-permute-done((bf16[3,128,128]{2,1,0:T(8,128)(2,1)S(1)}, bf16[3,128,128]{2,1,0:T(8,128)(2,1)S(1)}, u32[]{:S(2)}, u32[]{:S(2)}) %collective-permute-start.20) | collective-permute-done | bytes 98336 | tf_op jit(solution)/shard_map/ppermute | solution.py:194
  63.2 1.0 %collective-permute-done.21.in3 = bf16[3,128,128]{2,1,0:T(8,128)(2,1)S(1)} collective-permute-done((bf16[3,128,128]{2,1,0:T(8,128)(2,1)S(1)}, bf16[3,128,128]{2,1,0:T(8,128)(2,1)S(1)}, u32[]{:S(2)}, u32[]{:S(2)}) %collective-permute-start.21) | collective-permute-done | bytes 98336 | tf_op jit(solution)/shard_map/ppermute | solution.py:194
  64.1 0.8 unpack.5
  65.0 1.3 %collective-permute-start.22 = (bf16[1,128,1536]{2,1,0:T(8,128)(2,1)}, bf16[1,128,1536]{2,1,0:T(8,128)(2,1)S(1)}, u32[]{:S(2)}, u32[]{:S(2)}) collective-permute-start(bf16[1,128,1536]{2,1,0:T(8,128)(2,1)} %unpack.5), channel_id=1, source_target_pairs={{16,0},{17,1},{18,2},{19,3},{20,4},{21,5},{22,6},{23,7},{24,8},{25... | collective-permute-start | bytes 1179656 | tf_op jit(solution)/shard_map/ppermute | solution.py:281
  66.2 1.0 %collective-permute-start.12 = (bf16[3,256,128]{2,1,0:T(8,128)(2,1)S(1)}, bf16[3,256,128]{2,1,0:T(8,128)(2,1)S(1)}, u32[]{:S(2)}, u32[]{:S(2)}) collective-permute-start(bf16[3,256,128]{2,1,0:T(8,128)(2,1)S(1)} %get-tuple-element.41), channel_id=1, source_target_pairs={{0,4},{1,5},{2,6},{3,7},{4,8},{5,9},{6,10},{7,11},{8,12},{9,13},{1... | collective-permute-start | bytes 589832 | tf_op jit(solution)/shard_map/ppermute | solution.py:200
  67.2 2.9 %collective-permute-start.13 = (bf16[3,256,128]{2,1,0:T(8,128)(2,1)S(1)}, bf16[3,256,128]{2,1,0:T(8,128)(2,1)S(1)}, u32[]{:S(2)}, u32[]{:S(2)}) collective-permute-start(bf16[3,256,128]{2,1,0:T(8,128)(2,1)S(1)} %get-tuple-element.42), channel_id=1, source_target_pairs={{0,12},{1,13},{2,14},{3,15},{4,0},{5,1},{6,2},{7,3},{8,4},{9,5},{1... | collective-permute-start | bytes 589832 | tf_op jit(solution)/shard_map/ppermute | solution.py:200
  70.8 5.1 %collective-permute-done.12.from_below = bf16[3,256,128]{2,1,0:T(8,128)(2,1)S(1)} collective-permute-done((bf16[3,256,128]{2,1,0:T(8,128)(2,1)S(1)}, bf16[3,256,128]{2,1,0:T(8,128)(2,1)S(1)}, u32[]{:S(2)}, u32[]{:S(2)}) %collective-permute-start.12) | collective-permute-done | bytes 196640 | tf_op jit(solution)/shard_map/ppermute | solution.py:200
  75.9 2.3 %collective-permute-done.13.from_above = bf16[3,256,128]{2,1,0:T(8,128)(2,1)S(1)} collective-permute-done((bf16[3,256,128]{2,1,0:T(8,128)(2,1)S(1)}, bf16[3,256,128]{2,1,0:T(8,128)(2,1)S(1)}, u32[]{:S(2)}, u32[]{:S(2)}) %collective-permute-start.13) | collective-permute-done | bytes 196640 | tf_op jit(solution)/shard_map/ppermute | solution.py:200
  78.5 1.2 %collective-permute-start.15 = (bf16[3,128,128]{2,1,0:T(8,128)(2,1)S(1)}, bf16[3,128,128]{2,1,0:T(8,128)(2,1)S(1)}, u32[]{:S(2)}, u32[]{:S(2)}) collective-permute-start(bf16[3,128,128]{2,1,0:T(8,128)(2,1)S(1)} %get-tuple-element.45), channel_id=1, source_target_pairs={{0,2},{1,3},{2,0},{3,1},{4,6},{5,7},{6,4},{7,5},{8,10},{9,11},{10,... | collective-permute-start | bytes 294920 | tf_op jit(solution)/shard_map/ppermute | solution.py:194
  80.4 0.8 unpack.3
  81.2 3.0 %collective-permute-done.15.in2 = bf16[3,128,128]{2,1,0:T(8,128)(2,1)S(1)} collective-permute-done((bf16[3,128,128]{2,1,0:T(8,128)(2,1)S(1)}, bf16[3,128,128]{2,1,0:T(8,128)(2,1)S(1)}, u32[]{:S(2)}, u32[]{:S(2)}) %collective-permute-start.15) | collective-permute-done | bytes 98336 | tf_op jit(solution)/shard_map/ppermute | solution.py:194
  84.2 1.2 %collective-permute-done.16.in3 = bf16[3,128,128]{2,1,0:T(8,128)(2,1)S(1)} collective-permute-done((bf16[3,128,128]{2,1,0:T(8,128)(2,1)S(1)}, bf16[3,128,128]{2,1,0:T(8,128)(2,1)S(1)}, u32[]{:S(2)}, u32[]{:S(2)}) %collective-permute-start.16) | collective-permute-done | bytes 98336 | tf_op jit(solution)/shard_map/ppermute | solution.py:194
  (32 shorter events, 5.2 us)
Async XLA Ops:
  0.6 1.0 %copy-start = (bf16[1,128,1536]{2,1,0:T(8,128)(2,1)S(1)}, bf16[1,128,1536]{2,1,0:T(8,128)(2,1)}, u32[]{:S(2)}) copy-start(bf16[1,128,1536]{2,1,0:T(8,128)(2,1)} %q.1) | copy-start | bytes 1179652
  1.6 1.0 %copy-start.1 = (bf16[1,128,1536]{2,1,0:T(8,128)(2,1)S(1)}, bf16[1,128,1536]{2,1,0:T(8,128)(2,1)}, u32[]{:S(2)}) copy-start(bf16[1,128,1536]{2,1,0:T(8,128)(2,1)} %k.1) | copy-start | bytes 1179652
  2.6 1.0 %copy-start.2 = (bf16[1,128,1536]{2,1,0:T(8,128)(2,1)S(1)}, bf16[1,128,1536]{2,1,0:T(8,128)(2,1)}, u32[]{:S(2)}) copy-start(bf16[1,128,1536]{2,1,0:T(8,128)(2,1)} %v.1) | copy-start | bytes 1179652
  3.6 1.0 %copy-start.3 = (bf16[1,128,1536]{2,1,0:T(8,128)(2,1)S(1)}, bf16[1,128,1536]{2,1,0:T(8,128)(2,1)}, u32[]{:S(2)}) copy-start(bf16[1,128,1536]{2,1,0:T(8,128)(2,1)} %g.1) | copy-start | bytes 1179652
  4.6 0.7 copy-start.4
  6.2 13.5 %collective-permute-start.5 = (bf16[2,3,256,128]{3,2,1,0:T(8,128)(2,1)S(1)}, bf16[2,3,256,128]{3,2,1,0:T(8,128)(2,1)S(1)}, u32[]{:S(2)}, u32[]{:S(2)}) collective-permute-start(bf16[2,3,256,128]{3,2,1,0:T(8,128)(2,1)S(1)} %get-tuple-element.35), channel_id=1, source_target_pairs={{0,12},{1,13},{2,6},{3,7},{4,0},{5,1},{6,10},{7,11},{8,4},{9,5},{1... | collective-permute-start | bytes 1179656 | tf_op jit(solution)/shard_map/ppermute | solution.py:200
  11.3 8.4 %collective-permute-start.1 = (bf16[3,256,128]{2,1,0:T(8,128)(2,1)S(1)}, bf16[3,256,128]{2,1,0:T(8,128)(2,1)S(1)}, u32[]{:S(2)}, u32[]{:S(2)}) collective-permute-start(bf16[3,256,128]{2,1,0:T(8,128)(2,1)S(1)} %get-tuple-element.31), channel_id=1, source_target_pairs={{0,2},{1,3},{2,0},{3,1},{4,6},{5,7},{6,4},{7,5},{8,10},{9,11},{10,... | collective-permute-start | bytes 589832 | tf_op jit(solution)/shard_map/ppermute | solution.py:194
  11.3 15.1 %collective-permute-start.3 = (bf16[3,272,128]{2,1,0:T(8,128)(2,1)S(1)}, bf16[3,272,128]{2,1,0:T(8,128)(2,1)S(1)}, u32[]{:S(2)}, u32[]{:S(2)}) collective-permute-start(bf16[3,272,128]{2,1,0:T(8,128)(2,1)S(1)} %get-tuple-element.33), channel_id=1, source_target_pairs={{0,2},{1,3},{2,0},{3,1},{4,6},{5,7},{6,4},{7,5},{8,10},{9,11},{10,... | collective-permute-start | bytes 626696 | tf_op jit(solution)/shard_map/ppermute | solution.py:194
  13.3 24.0 %collective-permute-start = (bf16[3,528,128]{2,1,0:T(8,128)(2,1)S(1)}, bf16[3,528,128]{2,1,0:T(8,128)(2,1)S(1)}, u32[]{:S(2)}, u32[]{:S(2)}) collective-permute-start(bf16[3,528,128]{2,1,0:T(8,128)(2,1)S(1)} %get-tuple-element.30), channel_id=1, source_target_pairs={{0,1},{1,0},{2,3},{3,2},{4,5},{5,4},{6,7},{7,6},{8,9},{9,8},{10,11... | collective-permute-start | bytes 1216520 | tf_op jit(solution)/shard_map/ppermute | solution.py:194
  13.3 12.0 %collective-permute-start.2 = (bf16[3,256,128]{2,1,0:T(8,128)(2,1)S(1)}, bf16[3,256,128]{2,1,0:T(8,128)(2,1)S(1)}, u32[]{:S(2)}, u32[]{:S(2)}) collective-permute-start(bf16[3,256,128]{2,1,0:T(8,128)(2,1)S(1)} %get-tuple-element.32), channel_id=1, source_target_pairs={{0,3},{1,2},{2,1},{3,0},{4,7},{5,6},{6,5},{7,4},{8,11},{9,10},{10,... | collective-permute-start | bytes 589832 | tf_op jit(solution)/shard_map/ppermute | solution.py:194
  19.7 17.7 %collective-permute-start.6 = (bf16[2,3,256,128]{3,2,1,0:T(8,128)(2,1)S(1)}, bf16[2,3,256,128]{3,2,1,0:T(8,128)(2,1)S(1)}, u32[]{:S(2)}, u32[]{:S(2)}) collective-permute-start(bf16[2,3,256,128]{3,2,1,0:T(8,128)(2,1)S(1)} %collective-permute-done.5.edge0), channel_id=1, source_target_pairs={{0,1},{1,0},{2,3},{3,2},{4,5},{5,4},{6,7},{7,6},{8,9},{9,8},{10,11... | collective-permute-start | bytes 1179656 | tf_op jit(solution)/shard_map/ppermute | solution.py:194
  19.7 9.7 %collective-permute-start.4 = (bf16[3,272,128]{2,1,0:T(8,128)(2,1)S(1)}, bf16[3,272,128]{2,1,0:T(8,128)(2,1)S(1)}, u32[]{:S(2)}, u32[]{:S(2)}) collective-permute-start(bf16[3,272,128]{2,1,0:T(8,128)(2,1)S(1)} %get-tuple-element.34), channel_id=1, source_target_pairs={{0,3},{1,2},{2,1},{3,0},{4,7},{5,6},{6,5},{7,4},{8,11},{9,10},{10,... | collective-permute-start | bytes 626696 | tf_op jit(solution)/shard_map/ppermute | solution.py:194
  25.3 7.8 %collective-permute-start.7 = (bf16[3,256,128]{2,1,0:T(8,128)(2,1)S(1)}, bf16[3,256,128]{2,1,0:T(8,128)(2,1)S(1)}, u32[]{:S(2)}, u32[]{:S(2)}) collective-permute-start(bf16[3,256,128]{2,1,0:T(8,128)(2,1)S(1)} %collective-permute-done.1.kv2), channel_id=1, source_target_pairs={{0,4},{1,5},{2,14},{3,15},{4,8},{5,9},{6,2},{7,3},{8,12},{9,13},{1... | collective-permute-start | bytes 589832 | tf_op jit(solution)/shard_map/ppermute | solution.py:200
  26.4 10.9 %collective-permute-start.8 = (bf16[3,256,128]{2,1,0:T(8,128)(2,1)S(1)}, bf16[3,256,128]{2,1,0:T(8,128)(2,1)S(1)}, u32[]{:S(2)}, u32[]{:S(2)}) collective-permute-start(bf16[3,256,128]{2,1,0:T(8,128)(2,1)S(1)} %collective-permute-done.2.kv3), channel_id=1, source_target_pairs={{0,4},{1,5},{2,14},{3,15},{4,8},{5,9},{6,2},{7,3},{8,12},{9,13},{1... | collective-permute-start | bytes 589832 | tf_op jit(solution)/shard_map/ppermute | solution.py:200
  45.2 9.3 %collective-permute-start.17 = (bf16[3,256,128]{2,1,0:T(8,128)(2,1)S(1)}, bf16[3,256,128]{2,1,0:T(8,128)(2,1)S(1)}, u32[]{:S(2)}, u32[]{:S(2)}) collective-permute-start(bf16[3,256,128]{2,1,0:T(8,128)(2,1)S(1)} %get-tuple-element.48), channel_id=1, source_target_pairs={{0,4},{1,5},{2,6},{3,7},{4,8},{5,9},{6,10},{7,11},{8,12},{9,13},{1... | collective-permute-start | bytes 589832 | tf_op jit(solution)/shard_map/ppermute | solution.py:200
  45.5 11.7 %collective-permute-start.18 = (bf16[3,256,128]{2,1,0:T(8,128)(2,1)S(1)}, bf16[3,256,128]{2,1,0:T(8,128)(2,1)S(1)}, u32[]{:S(2)}, u32[]{:S(2)}) collective-permute-start(bf16[3,256,128]{2,1,0:T(8,128)(2,1)S(1)} %get-tuple-element.49), channel_id=1, source_target_pairs={{0,12},{1,13},{2,14},{3,15},{4,0},{5,1},{6,2},{7,3},{8,4},{9,5},{1... | collective-permute-start | bytes 589832 | tf_op jit(solution)/shard_map/ppermute | solution.py:200
  57.3 1.9 %collective-permute-start.19 = (bf16[3,128,128]{2,1,0:T(8,128)(2,1)S(1)}, bf16[3,128,128]{2,1,0:T(8,128)(2,1)S(1)}, u32[]{:S(2)}, u32[]{:S(2)}) collective-permute-start(bf16[3,128,128]{2,1,0:T(8,128)(2,1)S(1)} %get-tuple-element.51), channel_id=1, source_target_pairs={{0,1},{1,0},{2,3},{3,2},{4,5},{5,4},{6,7},{7,6},{8,9},{9,8},{10,11... | collective-permute-start | bytes 294920 | tf_op jit(solution)/shard_map/ppermute | solution.py:194
  57.5 5.6 %collective-permute-start.20 = (bf16[3,128,128]{2,1,0:T(8,128)(2,1)S(1)}, bf16[3,128,128]{2,1,0:T(8,128)(2,1)S(1)}, u32[]{:S(2)}, u32[]{:S(2)}) collective-permute-start(bf16[3,128,128]{2,1,0:T(8,128)(2,1)S(1)} %get-tuple-element.52), channel_id=1, source_target_pairs={{0,2},{1,3},{2,0},{3,1},{4,6},{5,7},{6,4},{7,5},{8,10},{9,11},{10,... | collective-permute-start | bytes 294920 | tf_op jit(solution)/shard_map/ppermute | solution.py:194
  58.0 6.1 %collective-permute-start.21 = (bf16[3,128,128]{2,1,0:T(8,128)(2,1)S(1)}, bf16[3,128,128]{2,1,0:T(8,128)(2,1)S(1)}, u32[]{:S(2)}, u32[]{:S(2)}) collective-permute-start(bf16[3,128,128]{2,1,0:T(8,128)(2,1)S(1)} %get-tuple-element.53), channel_id=1, source_target_pairs={{0,3},{1,2},{2,1},{3,0},{4,7},{5,6},{6,5},{7,4},{8,11},{9,10},{10,... | collective-permute-start | bytes 294920 | tf_op jit(solution)/shard_map/ppermute | solution.py:194
  65.0 21.2 %collective-permute-start.22 = (bf16[1,128,1536]{2,1,0:T(8,128)(2,1)}, bf16[1,128,1536]{2,1,0:T(8,128)(2,1)S(1)}, u32[]{:S(2)}, u32[]{:S(2)}) collective-permute-start(bf16[1,128,1536]{2,1,0:T(8,128)(2,1)} %unpack.5), channel_id=1, source_target_pairs={{16,0},{17,1},{18,2},{19,3},{20,4},{21,5},{22,6},{23,7},{24,8},{25... | collective-permute-start | bytes 1179656 | tf_op jit(solution)/shard_map/ppermute | solution.py:281
  66.2 9.6 %collective-permute-start.12 = (bf16[3,256,128]{2,1,0:T(8,128)(2,1)S(1)}, bf16[3,256,128]{2,1,0:T(8,128)(2,1)S(1)}, u32[]{:S(2)}, u32[]{:S(2)}) collective-permute-start(bf16[3,256,128]{2,1,0:T(8,128)(2,1)S(1)} %get-tuple-element.41), channel_id=1, source_target_pairs={{0,4},{1,5},{2,6},{3,7},{4,8},{5,9},{6,10},{7,11},{8,12},{9,13},{1... | collective-permute-start | bytes 589832 | tf_op jit(solution)/shard_map/ppermute | solution.py:200
  67.2 11.0 %collective-permute-start.13 = (bf16[3,256,128]{2,1,0:T(8,128)(2,1)S(1)}, bf16[3,256,128]{2,1,0:T(8,128)(2,1)S(1)}, u32[]{:S(2)}, u32[]{:S(2)}) collective-permute-start(bf16[3,256,128]{2,1,0:T(8,128)(2,1)S(1)} %get-tuple-element.42), channel_id=1, source_target_pairs={{0,12},{1,13},{2,14},{3,15},{4,0},{5,1},{6,2},{7,3},{8,4},{9,5},{1... | collective-permute-start | bytes 589832 | tf_op jit(solution)/shard_map/ppermute | solution.py:200
  70.2 8.3 %collective-permute-start.9 = (bf16[3,128,128]{2,1,0:T(8,128)(2,1)S(1)}, bf16[3,128,128]{2,1,0:T(8,128)(2,1)S(1)}, u32[]{:S(2)}, u32[]{:S(2)}) collective-permute-start(bf16[3,128,128]{2,1,0:T(8,128)(2,1)S(1)} %get-tuple-element.37), channel_id=1, source_target_pairs={{0,1},{1,0},{2,3},{3,2},{4,5},{5,4},{6,7},{7,6},{8,9},{9,8},{10,11... | collective-permute-start | bytes 294920 | tf_op jit(solution)/shard_map/ppermute | solution.py:194
  70.2 9.5 %collective-permute-start.10 = (bf16[3,128,128]{2,1,0:T(8,128)(2,1)S(1)}, bf16[3,128,128]{2,1,0:T(8,128)(2,1)S(1)}, u32[]{:S(2)}, u32[]{:S(2)}) collective-permute-start(bf16[3,128,128]{2,1,0:T(8,128)(2,1)S(1)} %get-tuple-element.38), channel_id=1, source_target_pairs={{0,2},{1,3},{2,0},{3,1},{4,6},{5,7},{6,4},{7,5},{8,10},{9,11},{10,... | collective-permute-start | bytes 294920 | tf_op jit(solution)/shard_map/ppermute | solution.py:194
  75.9 4.5 %collective-permute-start.11 = (bf16[3,128,128]{2,1,0:T(8,128)(2,1)S(1)}, bf16[3,128,128]{2,1,0:T(8,128)(2,1)S(1)}, u32[]{:S(2)}, u32[]{:S(2)}) collective-permute-start(bf16[3,128,128]{2,1,0:T(8,128)(2,1)S(1)} %get-tuple-element.39), channel_id=1, source_target_pairs={{0,3},{1,2},{2,1},{3,0},{4,7},{5,6},{6,5},{7,4},{8,11},{9,10},{10,... | collective-permute-start | bytes 294920 | tf_op jit(solution)/shard_map/ppermute | solution.py:194
  78.4 2.8 %collective-permute-start.14 = (bf16[3,128,128]{2,1,0:T(8,128)(2,1)S(1)}, bf16[3,128,128]{2,1,0:T(8,128)(2,1)S(1)}, u32[]{:S(2)}, u32[]{:S(2)}) collective-permute-start(bf16[3,128,128]{2,1,0:T(8,128)(2,1)S(1)} %get-tuple-element.44), channel_id=1, source_target_pairs={{0,1},{1,0},{2,3},{3,2},{4,5},{5,4},{6,7},{7,6},{8,9},{9,8},{10,11... | collective-permute-start | bytes 294920 | tf_op jit(solution)/shard_map/ppermute | solution.py:194
  78.5 5.7 %collective-permute-start.15 = (bf16[3,128,128]{2,1,0:T(8,128)(2,1)S(1)}, bf16[3,128,128]{2,1,0:T(8,128)(2,1)S(1)}, u32[]{:S(2)}, u32[]{:S(2)}) collective-permute-start(bf16[3,128,128]{2,1,0:T(8,128)(2,1)S(1)} %get-tuple-element.45), channel_id=1, source_target_pairs={{0,2},{1,3},{2,0},{3,1},{4,6},{5,7},{6,4},{7,5},{8,10},{9,11},{10,... | collective-permute-start | bytes 294920 | tf_op jit(solution)/shard_map/ppermute | solution.py:194
  79.7 5.7 %collective-permute-start.16 = (bf16[3,128,128]{2,1,0:T(8,128)(2,1)S(1)}, bf16[3,128,128]{2,1,0:T(8,128)(2,1)S(1)}, u32[]{:S(2)}, u32[]{:S(2)}) collective-permute-start(bf16[3,128,128]{2,1,0:T(8,128)(2,1)S(1)} %get-tuple-element.46), channel_id=1, source_target_pairs={{0,3},{1,2},{2,1},{3,0},{4,7},{5,6},{6,5},{7,4},{8,11},{9,10},{10,... | collective-permute-start | bytes 294920 | tf_op jit(solution)/shard_map/ppermute | solution.py:194

commit v2 on v0

v2 whole, which is shorter than its diff:
```python
import functools

import jax
import jax.numpy as jnp
from jax import lax
from jax.experimental import pallas as pl
from jax.experimental.pallas import tpu as pltpu
from jax.sharding import PartitionSpec as P

H = 12
DH = 128
BLK = 128
REACH = 2
TEAM = 4
LOCAL = H // TEAM
SPAN = 2 * REACH + 1
SLOTS = TEAM + 2 * REACH
SCALE = DH ** (-0.5)
LOG2E = 1.4426950408889634
OFF = -1e30
MASK = 16
QG = 2 * BLK + MASK

bf16 = jnp.bfloat16
f32 = jnp.float32


def member():
    return lax.rem(lax.axis_index("ctx"), TEAM)


def rows_of(index, count=BLK):
    return pl.ds(pl.multiple_of(index * BLK, BLK), count)


def head_columns(group, h):
    return pl.ds(pl.multiple_of(group * (LOCAL * DH) + h * DH, DH), DH)


def pieces(source, target, sems):
    count = sems.shape[0]
    rows = BLK // count
    return [
        pltpu.make_async_copy(
            source.at[0, n * rows : (n + 1) * rows], target.at[0, n * rows : (n + 1) * rows], sems.at[n]
        )
        for n in range(count)
    ]


def cut(source, targets):
    me = member()
    for step, (target, base) in enumerate(targets):
        group = jnp.bitwise_xor(me, step)
        for h in range(LOCAL):
            target[h, base : base + BLK, :] = source[0, :, head_columns(group, h)]


def keys_kernel(k_hbm, k0, k1, k2, k3, k, sems):
    copies = pieces(k_hbm, k, sems)
    for copy in copies:
        copy.start()
    for copy in copies:
        copy.wait()
    cut(k, ((k0, 0), (k1, 0), (k2, 0), (k3, 0)))


def rest_kernel(
    v_hbm, q_hbm, g_hbm, lists_hbm, v0, qg0, one, v2, v3, qg2, qg3, lists, lists_sem, v, q, g, sems
):
    copies = [
        pieces(source, target, sems.at[n])
        for n, (source, target) in enumerate(((v_hbm, v), (q_hbm, q), (g_hbm, g)))
    ]
    lists_copy = pltpu.make_async_copy(lists_hbm, lists, lists_sem)
    lists_copy.start()
    for group in copies:
        for copy in group:
            copy.start()
    block = lax.axis_index("ctx")
    lists_copy.wait()
    row = lax.broadcasted_iota(jnp.int32, (MASK, DH), 0)
    mask = jnp.full((MASK, DH), OFF, f32)
    for o in range(SPAN):
        wanted = jnp.int32(0)
        for n in range(lists.shape[1]):
            entry = lists[0, n]
            hit = (entry >= 0) & (entry == block + (o - REACH))
            wanted = jnp.maximum(wanted, hit.astype(jnp.int32))
        level = jnp.where(wanted > 0, 0.0, OFF).astype(f32)
        mask = jnp.where(row == o, level, mask)
    mask = mask.astype(bf16)
    for target in (qg0, one, qg2, qg3):
        for h in range(LOCAL):
            target[h, 2 * BLK : QG, :] = mask
    targets = (
        ((v0, 0), (one, QG), (v2, 0), (v3, 0)),
        ((qg0, 0), (one, 0), (qg2, 0), (qg3, 0)),
        ((qg0, BLK), (one, BLK), (qg2, BLK), (qg3, BLK)),
    )
    for group, source, places in zip(copies, (v, q, g), targets):
        for copy in group:
            copy.wait()
        cut(source, places)


def merge_kernel(first, second, both):
    both[0] = first[...]
    both[1] = second[...]


def stage_kernel(base, zero, one, two, three, local, first, second):
    me = member()
    core = lax.rem(me, 2)
    for h in range(LOCAL):
        local[h, rows_of(me), :] = zero[h]
        local[h, rows_of(jnp.bitwise_xor(me, 1)), :] = one[h, base : base + BLK]
        local[h, rows_of(jnp.bitwise_xor(me, 2)), :] = two[h]
        local[h, rows_of(jnp.bitwise_xor(me, 3)), :] = three[h]
    for h in range(LOCAL):
        first[h] = local[h, rows_of(REACH * (1 - core), REACH * BLK), :]
        second[h] = local[h, rows_of(REACH * core, REACH * BLK), :]


def nt(a, b):
    return lax.dot_general(a, b, (((1,), (1,)), ((), ())), preferred_element_type=f32)


def tn(a, b):
    return lax.dot_general(a, b, (((0,), (0,)), ((), ())), preferred_element_type=f32)


def nn(a, b):
    return lax.dot_general(a, b, (((1,), (0,)), ((), ())), preferred_element_type=f32)


def line_up(slots, h, local, first, second):
    core = lax.rem(member(), 2)
    top = REACH + TEAM
    slots[h, REACH * BLK : top * BLK, :] = local[h]
    slots[h, rows_of(core * top, REACH * BLK), :] = first[h]
    slots[h, rows_of((1 - core) * top, REACH * BLK), :] = second[h]


def key_sums(weights, rows, h, mine, ends, scale):
    for j in range(SLOTS):
        there = slice(j * BLK, (j + 1) * BLK)
        seen = slice(max(0, j - SPAN + 1) * BLK, (min(TEAM - 1, j) + 1) * BLK)
        term = nn(weights[h, there, seen], rows[h, seen, :])
        if scale is not None:
            term = term * scale
        if REACH <= j < REACH + TEAM:
            mine[h, (j - REACH) * BLK : (j - REACH + 1) * BLK, :] = term
        else:
            at = j if j < REACH else j - TEAM
            ends[at * BLK : (at + 1) * BLK, :] = term.astype(bf16)


def hand_ends(h, ends, first, second):
    core = lax.rem(member(), 2)
    first[h] = ends[rows_of(REACH * (1 - core), REACH * BLK), :]
    second[h] = ends[rows_of(REACH * core, REACH * BLK), :]


def probs_kernel(
    qg0, one, qg23, local, halo1, halo2, probs, ks, qs, gs, dv_own, dv1, dv2, bs, ends
):
    me = member()
    for h in range(LOCAL):
        line_up(ks, h, local, halo1, halo2)
        for step, source in enumerate((qg0, one, qg23.at[0], qg23.at[1])):
            position = jnp.bitwise_xor(me, step)
            qs[h, rows_of(position), :] = source[h, :BLK]
            gs[h, rows_of(position), :] = source[h, BLK : 2 * BLK]
            if h == 0:
                at = pl.ds(pl.multiple_of(position * MASK, MASK), MASK)
                bs[at, :] = source[h, 2 * BLK : QG]
    for h in range(LOCAL):
        for pair in range(TEAM // 2):
            first = 2 * pair
            keys = ks[h, first * BLK : (first + SPAN + 1) * BLK, :]
            query = qs[h, first * BLK : (first + 2) * BLK, :]
            both = nt(keys, query)
            for n in range(2):
                i = first + n
                here = slice(i * BLK, (i + 1) * BLK)
                reach = slice(i * BLK, (i + SPAN) * BLK)
                bias = bs[i * MASK : (i + 1) * MASK, :].astype(f32)
                lanes = slice(n * BLK, (n + 1) * BLK)
                scores = jnp.concatenate(
                    [
                        both[(n + o) * BLK : (n + o + 1) * BLK, lanes] * (SCALE * LOG2E)
                        + bias[o : o + 1]
                        for o in range(SPAN)
                    ],
                    axis=0,
                )
                highest = jnp.max(scores, axis=0, keepdims=True)
                weights = jnp.exp2(scores - highest)
                scaled = weights * (1.0 / jnp.sum(weights, axis=0, keepdims=True))
                probs[h, reach, here] = scaled.astype(bf16)
        key_sums(probs, gs, h, dv_own, ends, None)
        hand_ends(h, ends, dv1, dv2)


def grads_kernel(
    probs, ks, qs, gs, local, halo1, halo2, dq0, dq1, dq23, dk_own, dk1, dk2, vs, ss, dqs, ends
):
    me = member()
    for h in range(LOCAL):
        line_up(vs, h, local, halo1, halo2)
        for pair in range(TEAM // 2):
            first = 2 * pair
            values = vs[h, first * BLK : (first + SPAN + 1) * BLK, :]
            grad = gs[h, first * BLK : (first + 2) * BLK, :]
            both = nt(values, grad)
            for n in range(2):
                i = first + n
                here = slice(i * BLK, (i + 1) * BLK)
                reach = slice(i * BLK, (i + SPAN) * BLK)
                grad_probs = both[n * BLK : (n + SPAN) * BLK, n * BLK : (n + 1) * BLK]
                weights = probs[h, reach, here].astype(f32)
                delta = jnp.sum(weights * grad_probs, axis=0, keepdims=True)
                scores_low = (weights * (grad_probs - delta)).astype(bf16)
                ss[h, reach, here] = scores_low
                dqs[here, :] = (tn(scores_low, ks[h, reach, :]) * SCALE).astype(bf16)
        for step, target in enumerate((dq0, dq1, dq23.at[0], dq23.at[1])):
            target[h] = dqs[rows_of(jnp.bitwise_xor(me, step)), :]
        key_sums(ss, qs, h, dk_own, ends, SCALE)
        hand_ends(h, ends, dk1, dk2)


def total_kernel(mine, ring1, ring2, out0, out1, out2, out3):
    me = member()
    core = lax.rem(me, 2)
    for step, target in enumerate((out0, out1, out2, out3)):
        block = jnp.bitwise_xor(me, step)
        use1 = block // REACH == core
        at = rows_of(lax.rem(block, REACH))
        for h in range(LOCAL):
            term = jnp.where(use1, ring1[h, at, :].astype(f32), ring2[h, at, :].astype(f32))
            target[h] = (mine[h, rows_of(block), :] + term).astype(bf16)


def unpack_kernel(in0, in1, in2, in3, out_hbm, out, sems):
    me = member()
    for step, source in enumerate((in0, in1, in2, in3)):
        group = jnp.bitwise_xor(me, step)
        for h in range(LOCAL):
            out[0, :, head_columns(group, h)] = source[h]
    copies = pieces(out, out_hbm, sems)
    for copy in copies:
        copy.start()
    for copy in copies:
        copy.wait()


def unpack_pair_kernel(in0, in1, pair, turned, *rest):
    unpack_kernel(in0, in1, pair.at[0], turned.at[1], *rest)


def struct(*shape, dtype=bf16):
    return jax.ShapeDtypeStruct(shape, dtype)


HBM = pltpu.HBM
CUTS = 4


def call(kernel, name, outs, scratch=(), space=pltpu.VMEM, to=pltpu.VMEM):
    def run(*args):
        return pl.pallas_call(
            kernel,
            out_shape=jax.tree.map(lambda out: to(out.shape, out.dtype), outs),
            in_specs=[pl.BlockSpec(memory_space=space)] * len(args),
            out_specs=jax.tree.map(lambda _: pl.BlockSpec(memory_space=to), outs),
            scratch_shapes=scratch,
            compiler_params=pltpu.CompilerParams(vmem_limit_bytes=24 * 1024 * 1024),
            name=name,
        )(*(pltpu.with_memory_space_constraint(arg, space) for arg in args))

    return run


def after(array, *others):
    return lax.optimization_barrier((array, *others))[0]


def shards(query_rows, key_rows, value_rows, grad_output, block_lists):
    ctx = lax.axis_size("ctx")
    layers = ctx // TEAM
    width = query_rows.shape[2]

    def swap(array, step):
        return lax.ppermute(array, "ctx", [(i, i ^ step) for i in range(ctx)])

    def ring(array, flip):
        pairs = []
        for i in range(ctx):
            layer, up = i // TEAM, (i % 2) == flip
            inside = layer < layers - 1 if up else layer > 0
            pairs.append((i, (i + TEAM if up else i - TEAM) if inside else i ^ 1))
        return lax.ppermute(array, "ctx", pairs)

    part = struct(LOCAL, BLK, DH)
    qg = struct(LOCAL, QG, DH)
    team = struct(LOCAL, TEAM * BLK, DH)
    ends = struct(LOCAL, REACH * BLK, DH)
    slots = struct(LOCAL, SLOTS * BLK, DH)
    square = struct(LOCAL, SLOTS * BLK, TEAM * BLK)
    kept = struct(LOCAL, TEAM * BLK, DH, dtype=f32)
    rows_in = pltpu.VMEM((1, BLK, width), bf16)
    sems = pltpu.SemaphoreType.DMA((CUTS,))

    held = (rows_in, sems)
    k0, k1, k2, k3 = call(keys_kernel, "keys", (part,) * 4, held, HBM)(key_rows)
    value_rows = lax.optimization_barrier((value_rows, k0))[0]
    v0, qg0, one, v2, v3, qg2, qg3 = call(
        rest_kernel,
        "rest",
        (part, qg, struct(LOCAL, QG + BLK, DH), part, part, qg, qg),
        [pltpu.SMEM(block_lists.shape, jnp.int32), pltpu.SemaphoreType.DMA]
        + [rows_in] * 3
        + [pltpu.SemaphoreType.DMA((3, CUTS))],
        HBM,
    )(value_rows, query_rows, grad_output, block_lists)

    k2 = swap(k2, 2)
    k3 = swap(k3, 3)
    k1 = swap(k1, 1)
    qg23 = call(merge_kernel, "merge", struct(2, *qg.shape))(qg2, swap(qg3, 1))
    one = swap(one, 1)
    v2 = swap(after(v2, k2, k3), 2)
    v3 = swap(after(v3, k2, k3), 3)
    qg23 = swap(after(qg23, k2, k3), 2)

    def stage(base, *blocks):
        kernel = functools.partial(stage_kernel, base)
        local, first, second = call(kernel, "stage", (team, ends, ends))(*blocks)
        return local, ring(first, 0), ring(second, 1)

    k_local, k_halo1, k_halo2 = stage(0, k0, k1, k2, k3)
    v_local, v_halo1, v_halo2 = stage(QG, v0, one, v2, v3)
    probs, ks, qs, gs, dv_own, dv1, dv2 = call(
        probs_kernel,
        "probs",
        (square, slots, team, team, kept, ends, ends),
        [pltpu.VMEM((TEAM * MASK, DH), bf16), pltpu.VMEM((2 * REACH * BLK, DH), bf16)],
    )(qg0, one, qg23, k_local, k_halo1, k_halo2)

    def total(mine, first, second):
        return call(total_kernel, "total", (part,) * 4)(mine, ring(first, 0), ring(second, 1))

    def unpack(kernel, *parts):
        out = struct(1, BLK, width)
        return call(kernel, "unpack", out, held, to=HBM)(*parts)

    def home(parts):
        return unpack(unpack_kernel, parts[0], *(swap(parts[n], n) for n in range(1, TEAM)))

    grad_value = home(total(dv_own, dv1, dv2))
    sections = lax.axis_size("section")
    handoff = lax.ppermute(grad_value, "section", [(s + 1, s) for s in range(sections - 1)])

    dq0, dq1, dq23, dk_own, dk1, dk2 = call(
        grads_kernel,
        "grads",
        (part, part, struct(2, LOCAL, BLK, DH), kept, ends, ends),
        [
            pltpu.VMEM((LOCAL, SLOTS * BLK, DH), bf16),
            pltpu.VMEM((LOCAL, SLOTS * BLK, TEAM * BLK), bf16),
            pltpu.VMEM((TEAM * BLK, DH), bf16),
            pltpu.VMEM((2 * REACH * BLK, DH), bf16),
        ],
    )(probs, ks, qs, gs, v_local, v_halo1, v_halo2)
    dq23 = swap(dq23, 2)
    grad_query = unpack(unpack_pair_kernel, dq0, swap(dq1, 1), dq23, swap(dq23, 1))
    grad_key = home(total(dk_own, dk1, dk2))
    return (grad_query, grad_key, grad_value, handoff)


def solution(mesh):
    wide = P("section", "ctx", None)
    return jax.shard_map(
        shards,
        mesh=mesh,
        in_specs=(wide, wide, wide, wide, P("ctx", None)),
        out_specs=(wide,) * 4,
        check_vma=False,
    )
```

time: 131 us -> 58.8 us (0.45)
  the two profiles are of different devices: /device:TPU:12 before, /device:TPU:0 now
where the time goes in v2:
time: 58.8 us; the launch traced here: 58.6 us
  waiting for transfers between devices  24.7 us (42%)
  starting transfers between devices  20.1 us (34%)
  Pallas kernels  12.2 us (21%)
  between operations  0.77 us (1%)
  local copies, waits for them, and re-layouts  0.75 us (1%)
    ppermute x17, waiting for transfers between devices, swap(): return lax.ppermute(array, 'ctx', [(i, i ^ step) for i in range(ctx)])  13.7 us
    pallas_call x12, Pallas kernels, run(): pl.pallas_call(kernel, out_shape=jax.tree.map(lambda out: to(out.shape, o...  12.2 us
    ppermute x17, starting transfers between devices, swap(): return lax.ppermute(array, 'ctx', [(i, i ^ step) for i in range(ctx)])  11.5 us
    ppermute x8, waiting for transfers between devices, ring(): return lax.ppermute(array, 'ctx', pairs)  11 us
    ppermute x8, starting transfers between devices, ring(): return lax.ppermute(array, 'ctx', pairs)  7.38 us
    ppermute x1, starting transfers between devices, shards(): lax.ppermute(grad_value, 'section', [(s + 1, s) for s in range(sections -...  1.29 us
  transfers between devices with their start and end apart: 26, of which 13 were waited for; matrix products, arithmetic and copies ran while one was open for 0% of the time, Pallas kernels for 16%

profile of v2, /device:TPU:0, one launch (start us, length us, event | category | flops | bytes accessed | tf_op | source)
XLA Modules:
  0.0 58.6 jit_solution(15131778052076894813)
XLA Ops:
  0.6 1.1 %keys.1 = (bf16[3,128,128]{2,1,0:T(8,128)(2,1)S(1)}, bf16[3,128,128]{2,1,0:T(8,128)(2,1)S(1)}, bf16[3,128,128]{2,1,0:T(8,128)(2,1)S(1)}, bf16[3,128,128]{2,1,0:T(8,128)(2,1)S(1)}) custom-call(bf16[1,128,1536]{2,1,0:T(8,128)(2,1)} %k_hbm.1), custom_call_target="tpu_custom_call" | custom-call | tf_op jit(solution)/shard_map/keys/pallas_call | solution.py:272
  1.8 1.5 %rest.1 = (bf16[3,128,128]{2,1,0:T(8,128)(2,1)S(1)}, bf16[3,272,128]{2,1,0:T(8,128)(2,1)S(1)}, bf16[3,400,128]{2,1,0:T(8,128)(2,1)S(1)}, bf16[3,128,128]{2,1,0:T...) custom-call(bf16[1,128,1536]{2,1,0:T(8,128)(2,1)} %v_hbm, ...), custom_call_target="tpu_custom_call" | custom-call | tf_op jit(solution)/shard_map/rest/pallas_call | solution.py:272
  3.3 0.5 collective-permute-start.1
  3.8 2.6 %collective-permute-start.2 = (bf16[3,128,128]{2,1,0:T(8,128)(2,1)S(1)}, bf16[3,128,128]{2,1,0:T(8,128)(2,1)S(1)}, u32[]{:S(2)}, u32[]{:S(2)}) collective-permute-start(bf16[3,128,128]{2,1,0:T(8,128)(2,1)S(1)} %get-tuple-element.52), channel_id=1, source_target_pairs={{0,2},{1,3},{2,0},{3,1},{4,6},{5,7},{6,4},{7,5},{8,10},{9,11},{10,... | collective-permute-start | bytes 294920 | tf_op jit(solution)/shard_map/ppermute | solution.py:295
  6.5 3.5 %collective-permute-done.2.two = bf16[3,128,128]{2,1,0:T(8,128)(2,1)S(1)} collective-permute-done((bf16[3,128,128]{2,1,0:T(8,128)(2,1)S(1)}, bf16[3,128,128]{2,1,0:T(8,128)(2,1)S(1)}, u32[]{:S(2)}, u32[]{:S(2)}) %collective-permute-start.2) | collective-permute-done | bytes 98336 | tf_op jit(solution)/shard_map/ppermute | solution.py:295
  10.1 1.6 %collective-permute-done.3.three = bf16[3,128,128]{2,1,0:T(8,128)(2,1)S(1)} collective-permute-done((bf16[3,128,128]{2,1,0:T(8,128)(2,1)S(1)}, bf16[3,128,128]{2,1,0:T(8,128)(2,1)S(1)}, u32[]{:S(2)}, u32[]{:S(2)}) %collective-permute-start.3) | collective-permute-done | bytes 98336 | tf_op jit(solution)/shard_map/ppermute | solution.py:295
  11.6 1.6 %collective-permute-start.4 = (bf16[2,3,272,128]{3,2,1,0:T(8,128)(2,1)S(1)}, bf16[2,3,272,128]{3,2,1,0:T(8,128)(2,1)S(1)}, u32[]{:S(2)}, u32[]{:S(2)}) collective-permute-start(bf16[2,3,272,128]{3,2,1,0:T(8,128)(2,1)S(1)} %merge.1), channel_id=1, source_target_pairs={{0,2},{1,3},{2,0},{3,1},{4,6},{5,7},{6,4},{7,5},{8,10},{9,11},{10,... | collective-permute-start | bytes 1253384 | tf_op jit(solution)/shard_map/ppermute | solution.py:295
  13.7 1.2 %collective-permute-done.5.one = bf16[3,128,128]{2,1,0:T(8,128)(2,1)S(1)} collective-permute-done((bf16[3,128,128]{2,1,0:T(8,128)(2,1)S(1)}, bf16[3,128,128]{2,1,0:T(8,128)(2,1)S(1)}, u32[]{:S(2)}, u32[]{:S(2)}) %collective-permute-start.5) | collective-permute-done | bytes 98336 | tf_op jit(solution)/shard_map/ppermute | solution.py:295
  15.0 1.6 %collective-permute-start.6 = (bf16[3,256,128]{2,1,0:T(8,128)(2,1)S(1)}, bf16[3,256,128]{2,1,0:T(8,128)(2,1)S(1)}, u32[]{:S(2)}, u32[]{:S(2)}) collective-permute-start(bf16[3,256,128]{2,1,0:T(8,128)(2,1)S(1)} %get-tuple-element.57), channel_id=1, source_target_pairs={{0,4},{1,0},{2,6},{3,2},{4,8},{5,1},{6,10},{7,3},{8,12},{9,5},{10,... | collective-permute-start | bytes 589832 | tf_op jit(solution)/shard_map/ppermute | solution.py:303
  17.1 4.1 %collective-permute-done.6.halo1 = bf16[3,256,128]{2,1,0:T(8,128)(2,1)S(1)} collective-permute-done((bf16[3,256,128]{2,1,0:T(8,128)(2,1)S(1)}, bf16[3,256,128]{2,1,0:T(8,128)(2,1)S(1)}, u32[]{:S(2)}, u32[]{:S(2)}) %collective-permute-start.6) | collective-permute-done | bytes 196640 | tf_op jit(solution)/shard_map/ppermute | solution.py:303
  21.3 1.0 %collective-permute-done.7.halo2 = bf16[3,256,128]{2,1,0:T(8,128)(2,1)S(1)} collective-permute-done((bf16[3,256,128]{2,1,0:T(8,128)(2,1)S(1)}, bf16[3,256,128]{2,1,0:T(8,128)(2,1)S(1)}, u32[]{:S(2)}, u32[]{:S(2)}) %collective-permute-start.7) | collective-permute-done | bytes 196640 | tf_op jit(solution)/shard_map/ppermute | solution.py:303
  22.3 1.8 %collective-permute-done.4.qg23 = bf16[2,3,272,128]{3,2,1,0:T(8,128)(2,1)S(1)} collective-permute-done((bf16[2,3,272,128]{3,2,1,0:T(8,128)(2,1)S(1)}, bf16[2,3,272,128]{3,2,1,0:T(8,128)(2,1)S(1)}, u32[]{:S(2)}, u32[]{:S(2)}) %collective-permute-start.4) | collective-permute-done | bytes 417824 | tf_op jit(solution)/shard_map/ppermute | solution.py:295
  24.1 2.8 %probs.1 = (bf16[3,1024,512]{2,1,0:T(8,128)(2,1)S(1)}, bf16[3,1024,128]{2,1,0:T(8,128)(2,1)S(1)}, bf16[3,512,128]{2,1,0:T(8,128)(2,1)S(1)}, bf16[3,512,128]{2,1,...) custom-call(bf16[3,272,128]{2,1,0:T(8,128)(2,1)S(1)} %get-tuple-elem, ...), custom_call_target="tpu_custom_call" | custom-call | tf_op jit(solution)/shard_map/probs/pallas_call | solution.py:272
  26.9 1.6 %collective-permute-start.20 = (bf16[3,256,128]{2,1,0:T(8,128)(2,1)S(1)}, bf16[3,256,128]{2,1,0:T(8,128)(2,1)S(1)}, u32[]{:S(2)}, u32[]{:S(2)}) collective-permute-start(bf16[3,256,128]{2,1,0:T(8,128)(2,1)S(1)} %get-tuple-element.82), channel_id=1, source_target_pairs={{0,4},{1,0},{2,6},{3,2},{4,8},{5,1},{6,10},{7,3},{8,12},{9,5},{10,... | collective-permute-start | bytes 589832 | tf_op jit(solution)/shard_map/ppermute | solution.py:303
  28.6 2.0 %collective-permute-start.10 = (bf16[3,256,128]{2,1,0:T(8,128)(2,1)S(1)}, bf16[3,256,128]{2,1,0:T(8,128)(2,1)S(1)}, u32[]{:S(2)}, u32[]{:S(2)}) collective-permute-start(bf16[3,256,128]{2,1,0:T(8,128)(2,1)S(1)} %get-tuple-element.69), channel_id=1, source_target_pairs={{0,4},{1,0},{2,6},{3,2},{4,8},{5,1},{6,10},{7,3},{8,12},{9,5},{10,... | collective-permute-start | bytes 589832 | tf_op jit(solution)/shard_map/ppermute | solution.py:303
  30.6 3.2 %collective-permute-done.20.ring1 = bf16[3,256,128]{2,1,0:T(8,128)(2,1)S(1)} collective-permute-done((bf16[3,256,128]{2,1,0:T(8,128)(2,1)S(1)}, bf16[3,256,128]{2,1,0:T(8,128)(2,1)S(1)}, u32[]{:S(2)}, u32[]{:S(2)}) %collective-permute-start.20) | collective-permute-done | bytes 196640 | tf_op jit(solution)/shard_map/ppermute | solution.py:303
  33.9 0.6 %collective-permute-done.21.ring2 = bf16[3,256,128]{2,1,0:T(8,128)(2,1)S(1)} collective-permute-done((bf16[3,256,128]{2,1,0:T(8,128)(2,1)S(1)}, bf16[3,256,128]{2,1,0:T(8,128)(2,1)S(1)}, u32[]{:S(2)}, u32[]{:S(2)}) %collective-permute-start.21) | collective-permute-done | bytes 196640 | tf_op jit(solution)/shard_map/ppermute | solution.py:303
  34.7 1.7 %collective-permute-start.23 = (bf16[3,128,128]{2,1,0:T(8,128)(2,1)S(1)}, bf16[3,128,128]{2,1,0:T(8,128)(2,1)S(1)}, u32[]{:S(2)}, u32[]{:S(2)}) collective-permute-start(bf16[3,128,128]{2,1,0:T(8,128)(2,1)S(1)} %get-tuple-element.86), channel_id=1, source_target_pairs={{0,2},{1,3},{2,0},{3,1},{4,6},{5,7},{6,4},{7,5},{8,10},{9,11},{10,... | collective-permute-start | bytes 294920 | tf_op jit(solution)/shard_map/ppermute | solution.py:295
  36.6 3.8 %grads.1 = (bf16[3,128,128]{2,1,0:T(8,128)(2,1)S(1)}, bf16[3,128,128]{2,1,0:T(8,128)(2,1)S(1)}, bf16[2,3,128,128]{3,2,1,0:T(8,128)(2,1)S(1)}, f32[3,512,128]{2,1...) custom-call(bf16[3,1024,512]{2,1,0:T(8,128)(2,1)S(1)} %get-tuple-element.59.probs, ...), custom_call_target="tpu_custom_call" | custom-call | tf_op jit(solution)/shard_map/grads/pallas_call | solution.py:272
  40.4 2.1 %collective-permute-start.15 = (bf16[3,256,128]{2,1,0:T(8,128)(2,1)S(1)}, bf16[3,256,128]{2,1,0:T(8,128)(2,1)S(1)}, u32[]{:S(2)}, u32[]{:S(2)}) collective-permute-start(bf16[3,256,128]{2,1,0:T(8,128)(2,1)S(1)} %get-tuple-element.75), channel_id=1, source_target_pairs={{0,4},{1,0},{2,6},{3,2},{4,8},{5,1},{6,10},{7,3},{8,12},{9,5},{10,... | collective-permute-start | bytes 589832 | tf_op jit(solution)/shard_map/ppermute | solution.py:303
  42.5 1.5 %collective-permute-start.13 = (bf16[2,3,128,128]{3,2,1,0:T(8,128)(2,1)S(1)}, bf16[2,3,128,128]{3,2,1,0:T(8,128)(2,1)S(1)}, u32[]{:S(2)}, u32[]{:S(2)}) collective-permute-start(bf16[2,3,128,128]{3,2,1,0:T(8,128)(2,1)S(1)} %get-tuple-element.73), channel_id=1, source_target_pairs={{0,2},{1,3},{2,0},{3,1},{4,6},{5,7},{6,4},{7,5},{8,10},{9,11},{10,... | collective-permute-start | bytes 589832 | tf_op jit(solution)/shard_map/ppermute | solution.py:295
  44.1 0.9 %unpack.5 = bf16[1,128,1536]{2,1,0:T(8,128)(2,1)} custom-call(bf16[3,128,128]{2,1,0:T(8,128)(2,1)S(1)} %get-tuple-element.84.in0, bf16[3,128,128]{2,1,0:T(8,128)(2,1)S(1)} %collective-permute-done.22.in1, bf16[3,128,128]{2,1,0:T(8,128)(2,1)S(1)} %collective-permute-done.23.in2, bf16[3,128,128]{2,1,0:T(8,128)(2,1)S(1)} %collective-permute-done.24.in3), custom_call_target="tpu_custom_call" | custom-call | tf_op jit(solution)/shard_map/unpack/pallas_call | solution.py:272
  44.9 1.3 %collective-permute-start.25 = (bf16[1,128,1536]{2,1,0:T(8,128)(2,1)}, bf16[1,128,1536]{2,1,0:T(8,128)(2,1)S(1)}, u32[]{:S(2)}, u32[]{:S(2)}) collective-permute-start(bf16[1,128,1536]{2,1,0:T(8,128)(2,1)} %unpack.5), channel_id=1, source_target_pairs={{16,0},{17,1},{18,2},{19,3},{20,4},{21,5},{22,6},{23,7},{24,8},{25... | collective-permute-start | bytes 1179656 | tf_op jit(solution)/shard_map/ppermute | solution.py:363
  46.2 0.7 %collective-permute-done.15.ring1 = bf16[3,256,128]{2,1,0:T(8,128)(2,1)S(1)} collective-permute-done((bf16[3,256,128]{2,1,0:T(8,128)(2,1)S(1)}, bf16[3,256,128]{2,1,0:T(8,128)(2,1)S(1)}, u32[]{:S(2)}, u32[]{:S(2)}) %collective-permute-start.15) | collective-permute-done | bytes 196640 | tf_op jit(solution)/shard_map/ppermute | solution.py:303
  46.9 1.3 %collective-permute-done.16.ring2 = bf16[3,256,128]{2,1,0:T(8,128)(2,1)S(1)} collective-permute-done((bf16[3,256,128]{2,1,0:T(8,128)(2,1)S(1)}, bf16[3,256,128]{2,1,0:T(8,128)(2,1)S(1)}, u32[]{:S(2)}, u32[]{:S(2)}) %collective-permute-start.16) | collective-permute-done | bytes 196640 | tf_op jit(solution)/shard_map/ppermute | solution.py:303
  48.4 0.7 %collective-permute-done.13.pair = bf16[2,3,128,128]{3,2,1,0:T(8,128)(2,1)S(1)} collective-permute-done((bf16[2,3,128,128]{3,2,1,0:T(8,128)(2,1)S(1)}, bf16[2,3,128,128]{3,2,1,0:T(8,128)(2,1)S(1)}, u32[]{:S(2)}, u32[]{:S(2)}) %collective-permute-start.13) | collective-permute-done | bytes 196640 | tf_op jit(solution)/shard_map/ppermute | solution.py:295
  49.1 1.6 %collective-permute-start.18 = (bf16[3,128,128]{2,1,0:T(8,128)(2,1)S(1)}, bf16[3,128,128]{2,1,0:T(8,128)(2,1)S(1)}, u32[]{:S(2)}, u32[]{:S(2)}) collective-permute-start(bf16[3,128,128]{2,1,0:T(8,128)(2,1)S(1)} %get-tuple-element.79), channel_id=1, source_target_pairs={{0,2},{1,3},{2,0},{3,1},{4,6},{5,7},{6,4},{7,5},{8,10},{9,11},{10,... | collective-permute-start | bytes 294920 | tf_op jit(solution)/shard_map/ppermute | solution.py:295
  51.3 3.4 %collective-permute-done.18.in2 = bf16[3,128,128]{2,1,0:T(8,128)(2,1)S(1)} collective-permute-done((bf16[3,128,128]{2,1,0:T(8,128)(2,1)S(1)}, bf16[3,128,128]{2,1,0:T(8,128)(2,1)S(1)}, u32[]{:S(2)}, u32[]{:S(2)}) %collective-permute-start.18) | collective-permute-done | bytes 98336 | tf_op jit(solution)/shard_map/ppermute | solution.py:295
  54.7 1.3 %collective-permute-done.19.in3 = bf16[3,128,128]{2,1,0:T(8,128)(2,1)S(1)} collective-permute-done((bf16[3,128,128]{2,1,0:T(8,128)(2,1)S(1)}, bf16[3,128,128]{2,1,0:T(8,128)(2,1)S(1)}, u32[]{:S(2)}, u32[]{:S(2)}) %collective-permute-start.19) | collective-permute-done | bytes 98336 | tf_op jit(solution)/shard_map/ppermute | solution.py:295
  56.1 0.8 %unpack.4 = bf16[1,128,1536]{2,1,0:T(8,128)(2,1)} custom-call(bf16[3,128,128]{2,1,0:T(8,128)(2,1)S(1)} %get-tuple-element.77.in0, bf16[3,128,128]{2,1,0:T(8,128)(2,1)S(1)} %collective-permute-done.17.in1, bf16[3,128,128]{2,1,0:T(8,128)(2,1)S(1)} %collective-permute-done.18.in2, bf16[3,128,128]{2,1,0:T(8,128)(2,1)S(1)} %collective-permute-done.19.in3), custom_call_target="tpu_custom_call" | custom-call | tf_op jit(solution)/shard_map/unpack/pallas_call | solution.py:272
  56.9 0.9 %unpack.3 = bf16[1,128,1536]{2,1,0:T(8,128)(2,1)} custom-call(bf16[3,128,128]{2,1,0:T(8,128)(2,1)S(1)} %get-tuple-element.71.in0, bf16[3,128,128]{2,1,0:T(8,128)(2,1)S(1)} %collective-permute-done.12.in1, bf16[2,3,128,128]{3,2,1,0:T(8,128)(2,1)S(1)} %collective-permute-done.13.pair, bf16[2,3,128,128]{3,2,1,0:T(8,128)(2,1)S(1)} %collective-permute-done.14.turned), custom_call_target="tpu_custom_call" | custom-call | tf_op jit(solution)/shard_map/unpack/pallas_call | solution.py:272
  57.8 0.7 %copy.10 = bf16[1,128,1536]{2,1,0:T(8,128)(2,1)} copy(bf16[1,128,1536]{2,1,0:T(8,128)(2,1)S(1)} %collective-permute-done.25) | data formatting | bytes 786432
  (33 shorter events, 2.4 us)
Async XLA Ops:
  3.3 3.2 %collective-permute-start.1 = (bf16[3,272,128]{2,1,0:T(8,128)(2,1)S(1)}, bf16[3,272,128]{2,1,0:T(8,128)(2,1)S(1)}, u32[]{:S(2)}, u32[]{:S(2)}) collective-permute-start(bf16[3,272,128]{2,1,0:T(8,128)(2,1)S(1)} %get-tuple-element.51), channel_id=1, source_target_pairs={{0,1},{1,0},{2,3},{3,2},{4,5},{5,4},{6,7},{7,6},{8,9},{9,8},{10,11... | collective-permute-start | bytes 626696 | tf_op jit(solution)/shard_map/ppermute | solution.py:295
  3.8 6.2 %collective-permute-start.2 = (bf16[3,128,128]{2,1,0:T(8,128)(2,1)S(1)}, bf16[3,128,128]{2,1,0:T(8,128)(2,1)S(1)}, u32[]{:S(2)}, u32[]{:S(2)}) collective-permute-start(bf16[3,128,128]{2,1,0:T(8,128)(2,1)S(1)} %get-tuple-element.52), channel_id=1, source_target_pairs={{0,2},{1,3},{2,0},{3,1},{4,6},{5,7},{6,4},{7,5},{8,10},{9,11},{10,... | collective-permute-start | bytes 294920 | tf_op jit(solution)/shard_map/ppermute | solution.py:295
  6.4 5.2 %collective-permute-start.3 = (bf16[3,128,128]{2,1,0:T(8,128)(2,1)S(1)}, bf16[3,128,128]{2,1,0:T(8,128)(2,1)S(1)}, u32[]{:S(2)}, u32[]{:S(2)}) collective-permute-start(bf16[3,128,128]{2,1,0:T(8,128)(2,1)S(1)} %get-tuple-element.53), channel_id=1, source_target_pairs={{0,3},{1,2},{2,1},{3,0},{4,7},{5,6},{6,5},{7,4},{8,11},{9,10},{10,... | collective-permute-start | bytes 294920 | tf_op jit(solution)/shard_map/ppermute | solution.py:295
  11.6 12.5 %collective-permute-start.4 = (bf16[2,3,272,128]{3,2,1,0:T(8,128)(2,1)S(1)}, bf16[2,3,272,128]{3,2,1,0:T(8,128)(2,1)S(1)}, u32[]{:S(2)}, u32[]{:S(2)}) collective-permute-start(bf16[2,3,272,128]{3,2,1,0:T(8,128)(2,1)S(1)} %merge.1), channel_id=1, source_target_pairs={{0,2},{1,3},{2,0},{3,1},{4,6},{5,7},{6,4},{7,5},{8,10},{9,11},{10,... | collective-permute-start | bytes 1253384 | tf_op jit(solution)/shard_map/ppermute | solution.py:295
  13.2 9.1 %collective-permute-start = (bf16[3,400,128]{2,1,0:T(8,128)(2,1)S(1)}, bf16[3,400,128]{2,1,0:T(8,128)(2,1)S(1)}, u32[]{:S(2)}, u32[]{:S(2)}) collective-permute-start(bf16[3,400,128]{2,1,0:T(8,128)(2,1)S(1)} %get-tuple-element.49), channel_id=1, source_target_pairs={{0,1},{1,0},{2,3},{3,2},{4,5},{5,4},{6,7},{7,6},{8,9},{9,8},{10,11... | collective-permute-start | bytes 921608 | tf_op jit(solution)/shard_map/ppermute | solution.py:295
  13.2 1.7 %collective-permute-start.5 = (bf16[3,128,128]{2,1,0:T(8,128)(2,1)S(1)}, bf16[3,128,128]{2,1,0:T(8,128)(2,1)S(1)}, u32[]{:S(2)}, u32[]{:S(2)}) collective-permute-start(bf16[3,128,128]{2,1,0:T(8,128)(2,1)S(1)} %get-tuple-element.55), channel_id=1, source_target_pairs={{0,1},{1,0},{2,3},{3,2},{4,5},{5,4},{6,7},{7,6},{8,9},{9,8},{10,11... | collective-permute-start | bytes 294920 | tf_op jit(solution)/shard_map/ppermute | solution.py:295
  15.0 6.2 %collective-permute-start.6 = (bf16[3,256,128]{2,1,0:T(8,128)(2,1)S(1)}, bf16[3,256,128]{2,1,0:T(8,128)(2,1)S(1)}, u32[]{:S(2)}, u32[]{:S(2)}) collective-permute-start(bf16[3,256,128]{2,1,0:T(8,128)(2,1)S(1)} %get-tuple-element.57), channel_id=1, source_target_pairs={{0,4},{1,0},{2,6},{3,2},{4,8},{5,1},{6,10},{7,3},{8,12},{9,5},{10,... | collective-permute-start | bytes 589832 | tf_op jit(solution)/shard_map/ppermute | solution.py:303
  16.6 5.7 %collective-permute-start.7 = (bf16[3,256,128]{2,1,0:T(8,128)(2,1)S(1)}, bf16[3,256,128]{2,1,0:T(8,128)(2,1)S(1)}, u32[]{:S(2)}, u32[]{:S(2)}) collective-permute-start(bf16[3,256,128]{2,1,0:T(8,128)(2,1)S(1)} %get-tuple-element.58), channel_id=1, source_target_pairs={{0,1},{1,5},{2,3},{3,7},{4,0},{5,9},{6,2},{7,11},{8,4},{9,13},{10,... | collective-permute-start | bytes 589832 | tf_op jit(solution)/shard_map/ppermute | solution.py:303
  16.6 11.9 %collective-permute-start.8 = (bf16[3,128,128]{2,1,0:T(8,128)(2,1)S(1)}, bf16[3,128,128]{2,1,0:T(8,128)(2,1)S(1)}, u32[]{:S(2)}, u32[]{:S(2)}) collective-permute-start(bf16[3,128,128]{2,1,0:T(8,128)(2,1)S(1)} %get-tuple-element.65), channel_id=1, source_target_pairs={{0,2},{1,3},{2,0},{3,1},{4,6},{5,7},{6,4},{7,5},{8,10},{9,11},{10,... | collective-permute-start | bytes 294920 | tf_op jit(solution)/shard_map/ppermute | solution.py:295
  21.2 7.3 %collective-permute-start.9 = (bf16[3,128,128]{2,1,0:T(8,128)(2,1)S(1)}, bf16[3,128,128]{2,1,0:T(8,128)(2,1)S(1)}, u32[]{:S(2)}, u32[]{:S(2)}) collective-permute-start(bf16[3,128,128]{2,1,0:T(8,128)(2,1)S(1)} %get-tuple-element.67), channel_id=1, source_target_pairs={{0,3},{1,2},{2,1},{3,0},{4,7},{5,6},{6,5},{7,4},{8,11},{9,10},{10,... | collective-permute-start | bytes 294920 | tf_op jit(solution)/shard_map/ppermute | solution.py:295
  26.9 7.0 %collective-permute-start.20 = (bf16[3,256,128]{2,1,0:T(8,128)(2,1)S(1)}, bf16[3,256,128]{2,1,0:T(8,128)(2,1)S(1)}, u32[]{:S(2)}, u32[]{:S(2)}) collective-permute-start(bf16[3,256,128]{2,1,0:T(8,128)(2,1)S(1)} %get-tuple-element.82), channel_id=1, source_target_pairs={{0,4},{1,0},{2,6},{3,2},{4,8},{5,1},{6,10},{7,3},{8,12},{9,5},{10,... | collective-permute-start | bytes 589832 | tf_op jit(solution)/shard_map/ppermute | solution.py:303
  28.5 6.0 %collective-permute-start.21 = (bf16[3,256,128]{2,1,0:T(8,128)(2,1)S(1)}, bf16[3,256,128]{2,1,0:T(8,128)(2,1)S(1)}, u32[]{:S(2)}, u32[]{:S(2)}) collective-permute-start(bf16[3,256,128]{2,1,0:T(8,128)(2,1)S(1)} %get-tuple-element.83), channel_id=1, source_target_pairs={{0,1},{1,5},{2,3},{3,7},{4,0},{5,9},{6,2},{7,11},{8,4},{9,13},{10,... | collective-permute-start | bytes 589832 | tf_op jit(solution)/shard_map/ppermute | solution.py:303
  28.6 8.0 %collective-permute-start.10 = (bf16[3,256,128]{2,1,0:T(8,128)(2,1)S(1)}, bf16[3,256,128]{2,1,0:T(8,128)(2,1)S(1)}, u32[]{:S(2)}, u32[]{:S(2)}) collective-permute-start(bf16[3,256,128]{2,1,0:T(8,128)(2,1)S(1)} %get-tuple-element.69), channel_id=1, source_target_pairs={{0,4},{1,0},{2,6},{3,2},{4,8},{5,1},{6,10},{7,3},{8,12},{9,5},{10,... | collective-permute-start | bytes 589832 | tf_op jit(solution)/shard_map/ppermute | solution.py:303
  30.6 6.0 %collective-permute-start.11 = (bf16[3,256,128]{2,1,0:T(8,128)(2,1)S(1)}, bf16[3,256,128]{2,1,0:T(8,128)(2,1)S(1)}, u32[]{:S(2)}, u32[]{:S(2)}) collective-permute-start(bf16[3,256,128]{2,1,0:T(8,128)(2,1)S(1)} %get-tuple-element.70), channel_id=1, source_target_pairs={{0,1},{1,5},{2,3},{3,7},{4,0},{5,9},{6,2},{7,11},{8,4},{9,13},{10,... | collective-permute-start | bytes 589832 | tf_op jit(solution)/shard_map/ppermute | solution.py:303
  34.6 7.9 %collective-permute-start.22 = (bf16[3,128,128]{2,1,0:T(8,128)(2,1)S(1)}, bf16[3,128,128]{2,1,0:T(8,128)(2,1)S(1)}, u32[]{:S(2)}, u32[]{:S(2)}) collective-permute-start(bf16[3,128,128]{2,1,0:T(8,128)(2,1)S(1)} %get-tuple-element.85), channel_id=1, source_target_pairs={{0,1},{1,0},{2,3},{3,2},{4,5},{5,4},{6,7},{7,6},{8,9},{9,8},{10,11... | collective-permute-start | bytes 294920 | tf_op jit(solution)/shard_map/ppermute | solution.py:295
  34.7 9.4 %collective-permute-start.23 = (bf16[3,128,128]{2,1,0:T(8,128)(2,1)S(1)}, bf16[3,128,128]{2,1,0:T(8,128)(2,1)S(1)}, u32[]{:S(2)}, u32[]{:S(2)}) collective-permute-start(bf16[3,128,128]{2,1,0:T(8,128)(2,1)S(1)} %get-tuple-element.86), channel_id=1, source_target_pairs={{0,2},{1,3},{2,0},{3,1},{4,6},{5,7},{6,4},{7,5},{8,10},{9,11},{10,... | collective-permute-start | bytes 294920 | tf_op jit(solution)/shard_map/ppermute | solution.py:295
  36.5 7.6 %collective-permute-start.24 = (bf16[3,128,128]{2,1,0:T(8,128)(2,1)S(1)}, bf16[3,128,128]{2,1,0:T(8,128)(2,1)S(1)}, u32[]{:S(2)}, u32[]{:S(2)}) collective-permute-start(bf16[3,128,128]{2,1,0:T(8,128)(2,1)S(1)} %get-tuple-element.87), channel_id=1, source_target_pairs={{0,3},{1,2},{2,1},{3,0},{4,7},{5,6},{6,5},{7,4},{8,11},{9,10},{10,... | collective-permute-start | bytes 294920 | tf_op jit(solution)/shard_map/ppermute | solution.py:295
  40.4 6.6 %collective-permute-start.15 = (bf16[3,256,128]{2,1,0:T(8,128)(2,1)S(1)}, bf16[3,256,128]{2,1,0:T(8,128)(2,1)S(1)}, u32[]{:S(2)}, u32[]{:S(2)}) collective-permute-start(bf16[3,256,128]{2,1,0:T(8,128)(2,1)S(1)} %get-tuple-element.75), channel_id=1, source_target_pairs={{0,4},{1,0},{2,6},{3,2},{4,8},{5,1},{6,10},{7,3},{8,12},{9,5},{10,... | collective-permute-start | bytes 589832 | tf_op jit(solution)/shard_map/ppermute | solution.py:303
  42.5 5.7 %collective-permute-start.16 = (bf16[3,256,128]{2,1,0:T(8,128)(2,1)S(1)}, bf16[3,256,128]{2,1,0:T(8,128)(2,1)S(1)}, u32[]{:S(2)}, u32[]{:S(2)}) collective-permute-start(bf16[3,256,128]{2,1,0:T(8,128)(2,1)S(1)} %get-tuple-element.76), channel_id=1, source_target_pairs={{0,1},{1,5},{2,3},{3,7},{4,0},{5,9},{6,2},{7,11},{8,4},{9,13},{10,... | collective-permute-start | bytes 589832 | tf_op jit(solution)/shard_map/ppermute | solution.py:303
  42.5 6.6 %collective-permute-start.13 = (bf16[2,3,128,128]{3,2,1,0:T(8,128)(2,1)S(1)}, bf16[2,3,128,128]{3,2,1,0:T(8,128)(2,1)S(1)}, u32[]{:S(2)}, u32[]{:S(2)}) collective-permute-start(bf16[2,3,128,128]{3,2,1,0:T(8,128)(2,1)S(1)} %get-tuple-element.73), channel_id=1, source_target_pairs={{0,2},{1,3},{2,0},{3,1},{4,6},{5,7},{6,4},{7,5},{8,10},{9,11},{10,... | collective-permute-start | bytes 589832 | tf_op jit(solution)/shard_map/ppermute | solution.py:295
  44.9 12.9 %collective-permute-start.25 = (bf16[1,128,1536]{2,1,0:T(8,128)(2,1)}, bf16[1,128,1536]{2,1,0:T(8,128)(2,1)S(1)}, u32[]{:S(2)}, u32[]{:S(2)}) collective-permute-start(bf16[1,128,1536]{2,1,0:T(8,128)(2,1)} %unpack.5), channel_id=1, source_target_pairs={{16,0},{17,1},{18,2},{19,3},{20,4},{21,5},{22,6},{23,7},{24,8},{25... | collective-permute-start | bytes 1179656 | tf_op jit(solution)/shard_map/ppermute | solution.py:363
  48.3 2.7 %collective-permute-start.17 = (bf16[3,128,128]{2,1,0:T(8,128)(2,1)S(1)}, bf16[3,128,128]{2,1,0:T(8,128)(2,1)S(1)}, u32[]{:S(2)}, u32[]{:S(2)}) collective-permute-start(bf16[3,128,128]{2,1,0:T(8,128)(2,1)S(1)} %get-tuple-element.78), channel_id=1, source_target_pairs={{0,1},{1,0},{2,3},{3,2},{4,5},{5,4},{6,7},{7,6},{8,9},{9,8},{10,11... | collective-permute-start | bytes 294920 | tf_op jit(solution)/shard_map/ppermute | solution.py:295
  49.1 7.8 %collective-permute-start.14 = (bf16[2,3,128,128]{3,2,1,0:T(8,128)(2,1)S(1)}, bf16[2,3,128,128]{3,2,1,0:T(8,128)(2,1)S(1)}, u32[]{:S(2)}, u32[]{:S(2)}) collective-permute-start(bf16[2,3,128,128]{3,2,1,0:T(8,128)(2,1)S(1)} %collective-permute-done.13.pair), channel_id=1, source_target_pairs={{0,1},{1,0},{2,3},{3,2},{4,5},{5,4},{6,7},{7,6},{8,9},{9,8},{10,11... | collective-permute-start | bytes 589832 | tf_op jit(solution)/shard_map/ppermute | solution.py:295
  49.1 5.6 %collective-permute-start.18 = (bf16[3,128,128]{2,1,0:T(8,128)(2,1)S(1)}, bf16[3,128,128]{2,1,0:T(8,128)(2,1)S(1)}, u32[]{:S(2)}, u32[]{:S(2)}) collective-permute-start(bf16[3,128,128]{2,1,0:T(8,128)(2,1)S(1)} %get-tuple-element.79), channel_id=1, source_target_pairs={{0,2},{1,3},{2,0},{3,1},{4,6},{5,7},{6,4},{7,5},{8,10},{9,11},{10,... | collective-permute-start | bytes 294920 | tf_op jit(solution)/shard_map/ppermute | solution.py:295
  50.7 5.4 %collective-permute-start.19 = (bf16[3,128,128]{2,1,0:T(8,128)(2,1)S(1)}, bf16[3,128,128]{2,1,0:T(8,128)(2,1)S(1)}, u32[]{:S(2)}, u32[]{:S(2)}) collective-permute-start(bf16[3,128,128]{2,1,0:T(8,128)(2,1)S(1)} %get-tuple-element.80), channel_id=1, source_target_pairs={{0,3},{1,2},{2,1},{3,0},{4,7},{5,6},{6,5},{7,4},{8,11},{9,10},{10,... | collective-permute-start | bytes 294920 | tf_op jit(solution)/shard_map/ppermute | solution.py:295
  51.0 5.9 %collective-permute-start.12 = (bf16[3,128,128]{2,1,0:T(8,128)(2,1)S(1)}, bf16[3,128,128]{2,1,0:T(8,128)(2,1)S(1)}, u32[]{:S(2)}, u32[]{:S(2)}) collective-permute-start(bf16[3,128,128]{2,1,0:T(8,128)(2,1)S(1)} %get-tuple-element.72), channel_id=1, source_target_pairs={{0,1},{1,0},{2,3},{3,2},{4,5},{5,4},{6,7},{7,6},{8,9},{9,8},{10,11... | collective-permute-start | bytes 294920 | tf_op jit(solution)/shard_map/ppermute | solution.py:295

commit v3 on v2

--- a/solution.py
+++ b/solution.py
@@ -19,7 +19,9 @@
 LOG2E = 1.4426950408889634
 OFF = -1e30
 MASK = 16
-QG = 2 * BLK + MASK
+K_AT, Q_AT, M_AT, G_AT, V_AT = 0, BLK, 2 * BLK, 2 * BLK + MASK, 3 * BLK + MASK
+ALL = 4 * BLK + MASK
+REST = ALL - BLK
 
 bf16 = jnp.bfloat16
 f32 = jnp.float32
@@ -56,21 +58,12 @@
             target[h, base : base + BLK, :] = source[0, :, head_columns(group, h)]
 
 
-def keys_kernel(k_hbm, k0, k1, k2, k3, k, sems):
-    copies = pieces(k_hbm, k, sems)
-    for copy in copies:
-        copy.start()
-    for copy in copies:
-        copy.wait()
-    cut(k, ((k0, 0), (k1, 0), (k2, 0), (k3, 0)))
-
-
-def rest_kernel(
-    v_hbm, q_hbm, g_hbm, lists_hbm, v0, qg0, one, v2, v3, qg2, qg3, lists, lists_sem, v, q, g, sems
+def pack_kernel(
+    k_hbm, q_hbm, g_hbm, v_hbm, lists_hbm, own, side, k2, k3, cross, lists, lists_sem, k, q, g, v, sems
 ):
     copies = [
         pieces(source, target, sems.at[n])
-        for n, (source, target) in enumerate(((v_hbm, v), (q_hbm, q), (g_hbm, g)))
+        for n, (source, target) in enumerate(((k_hbm, k), (q_hbm, q), (g_hbm, g), (v_hbm, v)))
     ]
     lists_copy = pltpu.make_async_copy(lists_hbm, lists, lists_sem)
     lists_copy.start()
@@ -90,36 +83,39 @@
         level = jnp.where(wanted > 0, 0.0, OFF).astype(f32)
         mask = jnp.where(row == o, level, mask)
     mask = mask.astype(bf16)
-    for target in (qg0, one, qg2, qg3):
+    for target, at in ((own, M_AT), (side, M_AT), (side, ALL + M_AT - BLK), (cross, M_AT - BLK)):
         for h in range(LOCAL):
-            target[h, 2 * BLK : QG, :] = mask
-    targets = (
-        ((v0, 0), (one, QG), (v2, 0), (v3, 0)),
-        ((qg0, 0), (one, 0), (qg2, 0), (qg3, 0)),
-        ((qg0, BLK), (one, BLK), (qg2, BLK), (qg3, BLK)),
-    )
-    for group, source, places in zip(copies, (v, q, g), targets):
+            target[h, at : at + MASK, :] = mask
+    targets = [((own, K_AT), (side, K_AT), (k2, 0), (k3, 0))]
+    for at in (Q_AT, G_AT, V_AT):
+        targets.append(((own, at), (side, at), (cross, at - BLK), (side, ALL + at - BLK)))
+    for group, source, places in zip(copies, (k, q, g, v), targets):
         for copy in group:
             copy.wait()
         cut(source, places)
 
 
-def merge_kernel(first, second, both):
-    both[0] = first[...]
-    both[1] = second[...]
-
-
-def stage_kernel(base, zero, one, two, three, local, first, second):
+def merge_kernel(cross, side, q, g, v):
+    for target, at, rows in ((q, Q_AT, BLK + MASK), (g, G_AT, BLK), (v, V_AT, BLK)):
+        target[0] = cross[:, at - BLK : at - BLK + rows]
+        target[1] = side[:, ALL + at - BLK : ALL + at - BLK + rows]
+
+
+def stage_kernel(at, own, side, two, three, local, first, second):
     me = member()
     core = lax.rem(me, 2)
     for h in range(LOCAL):
-        local[h, rows_of(me), :] = zero[h]
-        local[h, rows_of(jnp.bitwise_xor(me, 1)), :] = one[h, base : base + BLK]
+        local[h, rows_of(me), :] = own[h, at : at + BLK]
+        local[h, rows_of(jnp.bitwise_xor(me, 1)), :] = side[h, at : at + BLK]
         local[h, rows_of(jnp.bitwise_xor(me, 2)), :] = two[h]
         local[h, rows_of(jnp.bitwise_xor(me, 3)), :] = three[h]
     for h in range(LOCAL):
         first[h] = local[h, rows_of(REACH * (1 - core), REACH * BLK), :]
         second[h] = local[h, rows_of(REACH * core, REACH * BLK), :]
+
+
+def stage_pair_kernel(at, own, side, pair, *outs):
+    stage_kernel(at, own, side, pair.at[0], pair.at[1], *outs)
 
 
 def nt(a, b):
@@ -162,19 +158,17 @@
     second[h] = ends[rows_of(REACH * core, REACH * BLK), :]
 
 
-def probs_kernel(
-    qg0, one, qg23, local, halo1, halo2, probs, ks, qs, gs, dv_own, dv1, dv2, bs, ends
-):
-    me = member()
+def probs_kernel(own, side, crossed, local, halo1, halo2, probs, ks, qs, bs):
+    me = member()
+    sources = ((own, Q_AT), (side, Q_AT), (crossed.at[0], 0), (crossed.at[1], 0))
     for h in range(LOCAL):
         line_up(ks, h, local, halo1, halo2)
-        for step, source in enumerate((qg0, one, qg23.at[0], qg23.at[1])):
+        for step, (source, at) in enumerate(sources):
             position = jnp.bitwise_xor(me, step)
-            qs[h, rows_of(position), :] = source[h, :BLK]
-            gs[h, rows_of(position), :] = source[h, BLK : 2 * BLK]
+            qs[h, rows_of(position), :] = source[h, at : at + BLK]
             if h == 0:
-                at = pl.ds(pl.multiple_of(position * MASK, MASK), MASK)
-                bs[at, :] = source[h, 2 * BLK : QG]
+                masks = pl.ds(pl.multiple_of(position * MASK, MASK), MASK)
+                bs[masks, :] = source[h, at + BLK : at + BLK + MASK]
     for h in range(LOCAL):
         for pair in range(TEAM // 2):
             first = 2 * pair
@@ -199,6 +193,14 @@
                 weights = jnp.exp2(scores - highest)
                 scaled = weights * (1.0 / jnp.sum(weights, axis=0, keepdims=True))
                 probs[h, reach, here] = scaled.astype(bf16)
+
+
+def values_kernel(probs, own, side, crossed, gs, dv_own, dv1, dv2, ends):
+    me = member()
+    sources = ((own, G_AT), (side, G_AT), (crossed.at[0], 0), (crossed.at[1], 0))
+    for h in range(LOCAL):
+        for step, (source, at) in enumerate(sources):
+            gs[h, rows_of(jnp.bitwise_xor(me, step)), :] = source[h, at : at + BLK]
         key_sums(probs, gs, h, dv_own, ends, None)
         hand_ends(h, ends, dv1, dv2)
 
@@ -230,22 +232,35 @@
         hand_ends(h, ends, dk1, dk2)
 
 
-def total_kernel(mine, ring1, ring2, out0, out1, out2, out3):
+def total_kernel(mine, ring1, ring2, *outs):
     me = member()
     core = lax.rem(me, 2)
-    for step, target in enumerate((out0, out1, out2, out3)):
+    for step in range(TEAM):
         block = jnp.bitwise_xor(me, step)
         use1 = block // REACH == core
         at = rows_of(lax.rem(block, REACH))
         for h in range(LOCAL):
             term = jnp.where(use1, ring1[h, at, :].astype(f32), ring2[h, at, :].astype(f32))
-            target[h] = (mine[h, rows_of(block), :] + term).astype(bf16)
-
-
-def unpack_kernel(in0, in1, in2, in3, out_hbm, out, sems):
+            outs[step][h] = (mine[h, rows_of(block), :] + term).astype(bf16)
+
+
+def total_pairs_kernel(mine, ring1, ring2, stay, give):
+    total_kernel(mine, ring1, ring2, stay.at[0], give.at[0], stay.at[1], give.at[1])
+
+
+def join_kernel(stay, got, out):
+    out[0] = stay[1]
+    out[1] = got[1]
+
+
+def gather_kernel(in0, in1, in2, in3, groups):
     me = member()
     for step, source in enumerate((in0, in1, in2, in3)):
-        group = jnp.bitwise_xor(me, step)
+        groups[jnp.bitwise_xor(me, step)] = source[...]
+
+
+def write_out(parts, out, out_hbm, sems):
+    for group, source in parts:
         for h in range(LOCAL):
             out[0, :, head_columns(group, h)] = source[h]
     copies = pieces(out, out_hbm, sems)
@@ -255,8 +270,23 @@
         copy.wait()
 
 
-def unpack_pair_kernel(in0, in1, pair, turned, *rest):
-    unpack_kernel(in0, in1, pair.at[0], turned.at[1], *rest)
+def unpack_kernel(in0, in1, in2, in3, out_hbm, out, sems):
+    me = member()
+    sources = (in0, in1, in2, in3)
+    parts = [(jnp.bitwise_xor(me, step), source) for step, source in enumerate(sources)]
+    write_out(parts, out, out_hbm, sems)
+
+
+def unpack_joined_kernel(stay, got, crossed, *rest):
+    unpack_kernel(stay.at[0], got.at[0], crossed.at[0], crossed.at[1], *rest)
+
+
+def unpack_turned_kernel(dq0, dq1, crossed, turned, *rest):
+    unpack_kernel(dq0, dq1, crossed.at[0], turned.at[1], *rest)
+
+
+def unpack_groups_kernel(groups, out_hbm, out, sems):
+    write_out([(group, groups.at[group]) for group in range(TEAM)], out, out_hbm, sems)
 
 
 def struct(*shape, dtype=bf16):
@@ -303,79 +333,88 @@
         return lax.ppermute(array, "ctx", pairs)
 
     part = struct(LOCAL, BLK, DH)
-    qg = struct(LOCAL, QG, DH)
+    pair = struct(2, LOCAL, BLK, DH)
     team = struct(LOCAL, TEAM * BLK, DH)
     ends = struct(LOCAL, REACH * BLK, DH)
     slots = struct(LOCAL, SLOTS * BLK, DH)
     square = struct(LOCAL, SLOTS * BLK, TEAM * BLK)
     kept = struct(LOCAL, TEAM * BLK, DH, dtype=f32)
     rows_in = pltpu.VMEM((1, BLK, width), bf16)
-    sems = pltpu.SemaphoreType.DMA((CUTS,))
-
-    held = (rows_in, sems)
-    k0, k1, k2, k3 = call(keys_kernel, "keys", (part,) * 4, held, HBM)(key_rows)
-    value_rows = lax.optimization_barrier((value_rows, k0))[0]
-    v0, qg0, one, v2, v3, qg2, qg3 = call(
-        rest_kernel,
-        "rest",
-        (part, qg, struct(LOCAL, QG + BLK, DH), part, part, qg, qg),
+    ends_in = pltpu.VMEM((2 * REACH * BLK, DH), bf16)
+
+    own, side, k2, k3, cross = call(
+        pack_kernel,
+        "pack",
+        (struct(LOCAL, ALL, DH), struct(LOCAL, ALL + REST, DH), part, part, struct(LOCAL, REST, DH)),
         [pltpu.SMEM(block_lists.shape, jnp.int32), pltpu.SemaphoreType.DMA]
-        + [rows_in] * 3
-        + [pltpu.SemaphoreType.DMA((3, CUTS))],
+        + [rows_in] * 4
+        + [pltpu.SemaphoreType.DMA((4, CUTS))],
         HBM,
-    )(value_rows, query_rows, grad_output, block_lists)
-
+    )(key_rows, query_rows, grad_output, value_rows, block_lists)
     k2 = swap(k2, 2)
     k3 = swap(k3, 3)
-    k1 = swap(k1, 1)
-    qg23 = call(merge_kernel, "merge", struct(2, *qg.shape))(qg2, swap(qg3, 1))
-    one = swap(one, 1)
-    v2 = swap(after(v2, k2, k3), 2)
-    v3 = swap(after(v3, k2, k3), 3)
-    qg23 = swap(after(qg23, k2, k3), 2)
-
-    def stage(base, *blocks):
-        kernel = functools.partial(stage_kernel, base)
+    side = swap(side, 1)
+    q23, g23, v23 = call(
+        merge_kernel, "merge", (struct(2, LOCAL, BLK + MASK, DH), pair, pair)
+    )(cross, side)
+
+    def stage(kernel, *blocks):
         local, first, second = call(kernel, "stage", (team, ends, ends))(*blocks)
         return local, ring(first, 0), ring(second, 1)
 
-    k_local, k_halo1, k_halo2 = stage(0, k0, k1, k2, k3)
-    v_local, v_halo1, v_halo2 = stage(QG, v0, one, v2, v3)
-    probs, ks, qs, gs, dv_own, dv1, dv2 = call(
-        probs_kernel,
-        "probs",
-        (square, slots, team, team, kept, ends, ends),
-        [pltpu.VMEM((TEAM * MASK, DH), bf16), pltpu.VMEM((2 * REACH * BLK, DH), bf16)],
-    )(qg0, one, qg23, k_local, k_halo1, k_halo2)
-
-    def total(mine, first, second):
-        return call(total_kernel, "total", (part,) * 4)(mine, ring(first, 0), ring(second, 1))
+    k_local, k_halo1, k_halo2 = stage(functools.partial(stage_kernel, K_AT), own, side, k2, k3)
+    q23 = swap(after(q23, k_local), 2)
+    g23 = swap(after(g23, k_local), 2)
+    v23 = swap(v23, 2)
+    v_local, v_halo1, v_halo2 = stage(functools.partial(stage_pair_kernel, V_AT), own, side, v23)
+    probs, ks, qs = call(
+        probs_kernel, "probs", (square, slots, team), [pltpu.VMEM((TEAM * MASK, DH), bf16)]
+    )(own, side, q23, k_local, k_halo1, k_halo2)
+    g23 = after(g23, v_halo1, v_halo2)
+    gs, dv_own, dv1, dv2 = call(values_kernel, "values", (team, kept, ends, ends), [ends_in])(
+        probs, own, side, g23
+    )
+
+    def total(kernel, outs, mine, first, second):
+        return call(kernel, "total", outs)(mine, ring(first, 0), ring(second, 1))
 
     def unpack(kernel, *parts):
         out = struct(1, BLK, width)
-        return call(kernel, "unpack", out, held, to=HBM)(*parts)
-
-    def home(parts):
-        return unpack(unpack_kernel, parts[0], *(swap(parts[n], n) for n in range(1, TEAM)))
-
-    grad_value = home(total(dv_own, dv1, dv2))
-    sections = lax.axis_size("section")
-    handoff = lax.ppermute(grad_value, "section", [(s + 1, s) for s in range(sections - 1)])
+        sems = pltpu.SemaphoreType.DMA((CUTS,))
+        return call(kernel, "unpack", out, [rows_in, sems], to=HBM)(*parts)
 
     dq0, dq1, dq23, dk_own, dk1, dk2 = call(
         grads_kernel,
         "grads",
-        (part, part, struct(2, LOCAL, BLK, DH), kept, ends, ends),
+        (part, part, pair, kept, ends, ends),
         [
             pltpu.VMEM((LOCAL, SLOTS * BLK, DH), bf16),
             pltpu.VMEM((LOCAL, SLOTS * BLK, TEAM * BLK), bf16),
             pltpu.VMEM((TEAM * BLK, DH), bf16),
-            pltpu.VMEM((2 * REACH * BLK, DH), bf16),
+            ends_in,
         ],
     )(probs, ks, qs, gs, v_local, v_halo1, v_halo2)
+    dv_own = after(dv_own, dk_own)
+    dv = total(total_kernel, (part,) * 4, dv_own, dv1, dv2)
+    dv_first = dv[0]
+    dv = [dv[0]] + [swap(dv[step], step) for step in range(1, TEAM)]
+    dv = call(gather_kernel, "gather", struct(TEAM, LOCAL, BLK, DH))(*dv)
+    sections = lax.axis_size("section")
+    passed = lax.ppermute(dv, "section", [(s + 1, s) for s in range(sections - 1)])
+    grad_value = unpack(unpack_groups_kernel, dv)
+
     dq23 = swap(dq23, 2)
-    grad_query = unpack(unpack_pair_kernel, dq0, swap(dq1, 1), dq23, swap(dq23, 1))
-    grad_key = home(total(dk_own, dk1, dk2))
+    dk_own = after(dk_own, dv_first)
+    stay, give = total(total_pairs_kernel, (pair, pair), dk_own, dk1, dk2)
+    got = swap(give, 1)
+    joined = call(join_kernel, "join", pair)(after(stay, dv), got)
+    crossed = swap(joined, 2)
+    dq23 = after(dq23, got)
+    grad_query = unpack(unpack_turned_kernel, dq0, swap(dq1, 1), dq23, swap(dq23, 1))
+    stay = after(stay, grad_query, grad_value)
+    grad_key = unpack(unpack_joined_kernel, stay, got, crossed)
+    passed = after(passed, grad_key)
+    handoff = unpack(unpack_groups_kernel, passed)
     return (grad_query, grad_key, grad_value, handoff)
 
 

time: 58.8 us -> 54.3 us (0.923)
  waiting for transfers between devices: 24.7 us -> 19.9 us
  starting transfers between devices: 20.1 us -> 21.6 us
  local copies, waits for them, and re-layouts: 0.75 us -> 0 us
    ppermute x8, waiting for transfers between devices: 11 us -> 6.28 us  [ring(): return lax.ppermute(array, 'ctx', pairs)]
    ppermute x17 -> x14, starting transfers between devices: 11.5 us -> 12.8 us  [swap(): return lax.ppermute(array, 'ctx', [(i, i ^ step) for i in range(ctx)])]
    ppermute x17 -> x14, waiting for transfers between devices: 13.7 us -> 12.8 us  [swap(): return lax.ppermute(array, 'ctx', [(i, i ^ step) for i in range(ctx)])]
    ppermute x1, waiting for transfers between devices: 0.01 us -> 0.75 us  [shards(): lax.ppermute(dv, 'section', [(s + 1, s) for s in range(sections - 1)])]
    unnamed x1 -> x0, local copies, waits for them, and re-layouts: 0.75 us -> none
    pallas_call x12 -> x15, Pallas kernels: 12.2 us -> 11.9 us  [run(): pl.pallas_call(kernel, out_shape=jax.tree.map(lambda out: to(out.shape, o...]
  transfers between devices with their start and end apart: 26 -> 23, of which waited for: 13 -> 12; matrix products, arithmetic and copies ran while one was open for 0% -> 0% of each run, Pallas kernels for 16% -> 16%
where the time goes in v3:
time: 54.3 us; the launch traced here: 54.2 us
  starting transfers between devices  21.6 us (40%)
  waiting for transfers between devices  19.9 us (37%)
  Pallas kernels  11.9 us (22%)
  between operations  0.76 us (1%)
    ppermute x14, waiting for transfers between devices, swap(): return lax.ppermute(array, 'ctx', [(i, i ^ step) for i in range(ctx)])  12.8 us
    ppermute x14, starting transfers between devices, swap(): return lax.ppermute(array, 'ctx', [(i, i ^ step) for i in range(ctx)])  12.8 us
    pallas_call x15, Pallas kernels, run(): pl.pallas_call(kernel, out_shape=jax.tree.map(lambda out: to(out.shape, o...  11.9 us
    ppermute x8, starting transfers between devices, ring(): return lax.ppermute(array, 'ctx', pairs)  7.54 us
    ppermute x8, waiting for transfers between devices, ring(): return lax.ppermute(array, 'ctx', pairs)  6.28 us
    ppermute x1, starting transfers between devices, shards(): lax.ppermute(dv, 'section', [(s + 1, s) for s in range(sections - 1)])  1.29 us
  transfers between devices with their start and end apart: 23, of which 12 were waited for; matrix products, arithmetic and copies ran while one was open for 0% of the time, Pallas kernels for 16%

profile of v3, /device:TPU:0, one launch (start us, length us, event | category | flops | bytes accessed | tf_op | source)
XLA Modules:
  0.0 54.2 jit_solution(6396239506975687395)
XLA Ops:
  0.6 1.7 %pack.1 = (bf16[3,528,128]{2,1,0:T(8,128)(2,1)S(1)}, bf16[3,928,128]{2,1,0:T(8,128)(2,1)S(1)}, bf16[3,128,128]{2,1,0:T(8,128)(2,1)S(1)}, bf16[3,128,128]{2,1,0:T(8,128)(2,1)S(1)}, bf16[3,400,128]{2,1,0:T(8,128)(2,1)S(1)}) custom-call(bf16[1,128,1536]{2,1,0:T(8,128)(2,1)} %k_hbm.1, bf16[1,128,1536]{2,1,0:T(8,128)(2,1)} %q_hbm.1, bf16[1,128,1536]{2,1,0:T(8,128)(2,1)} %g_hbm.1, ...), custom_call_target="tpu_custom_call" | custom-call | tf_op jit(solution)/shard_map/pack/pallas_call | solution.py:302
  2.3 0.5 collective-permute-start
  2.8 2.6 %collective-permute-start.1 = (bf16[3,128,128]{2,1,0:T(8,128)(2,1)S(1)}, bf16[3,128,128]{2,1,0:T(8,128)(2,1)S(1)}, u32[]{:S(2)}, u32[]{:S(2)}) collective-permute-start(bf16[3,128,128]{2,1,0:T(8,128)(2,1)S(1)} %get-tuple-element.50), channel_id=1, source_target_pairs={{0,2},{1,3},{2,0},{3,1},{4,6},{5,7},{6,4},{7,5},{8,10},{9,11},{10,... | collective-permute-start | bytes 294920 | tf_op jit(solution)/shard_map/ppermute | solution.py:325
  5.5 2.1 %collective-permute-start.7 = (bf16[2,3,128,128]{3,2,1,0:T(8,128)(2,1)S(1)}, bf16[2,3,128,128]{3,2,1,0:T(8,128)(2,1)S(1)}, u32[]{:S(2)}, u32[]{:S(2)}) collective-permute-start(bf16[2,3,128,128]{3,2,1,0:T(8,128)(2,1)S(1)} %get-tuple-element.61), channel_id=1, source_target_pairs={{0,2},{1,3},{2,0},{3,1},{4,6},{5,7},{6,4},{7,5},{8,10},{9,11},{10,... | collective-permute-start | bytes 589832 | tf_op jit(solution)/shard_map/ppermute | solution.py:325
  7.6 1.4 %collective-permute-done.1.two = bf16[3,128,128]{2,1,0:T(8,128)(2,1)S(1)} collective-permute-done((bf16[3,128,128]{2,1,0:T(8,128)(2,1)S(1)}, bf16[3,128,128]{2,1,0:T(8,128)(2,1)S(1)}, u32[]{:S(2)}, u32[]{:S(2)}) %collective-permute-start.1) | collective-permute-done | bytes 98336 | tf_op jit(solution)/shard_map/ppermute | solution.py:325
  9.1 1.6 %collective-permute-done.2.three = bf16[3,128,128]{2,1,0:T(8,128)(2,1)S(1)} collective-permute-done((bf16[3,128,128]{2,1,0:T(8,128)(2,1)S(1)}, bf16[3,128,128]{2,1,0:T(8,128)(2,1)S(1)}, u32[]{:S(2)}, u32[]{:S(2)}) %collective-permute-start.2) | collective-permute-done | bytes 98336 | tf_op jit(solution)/shard_map/ppermute | solution.py:325
  10.7 1.6 %collective-permute-start.4 = (bf16[3,256,128]{2,1,0:T(8,128)(2,1)S(1)}, bf16[3,256,128]{2,1,0:T(8,128)(2,1)S(1)}, u32[]{:S(2)}, u32[]{:S(2)}) collective-permute-start(bf16[3,256,128]{2,1,0:T(8,128)(2,1)S(1)} %get-tuple-element.54), channel_id=1, source_target_pairs={{0,4},{1,0},{2,6},{3,2},{4,8},{5,1},{6,10},{7,3},{8,12},{9,5},{10,... | collective-permute-start | bytes 589832 | tf_op jit(solution)/shard_map/ppermute | solution.py:333
  12.4 1.5 %collective-permute-start.3 = (bf16[2,3,144,128]{3,2,1,0:T(8,128)(2,1)S(1)}, bf16[2,3,144,128]{3,2,1,0:T(8,128)(2,1)S(1)}, u32[]{:S(2)}, u32[]{:S(2)}) collective-permute-start(bf16[2,3,144,128]{3,2,1,0:T(8,128)(2,1)S(1)} %get-tuple-element.53), channel_id=1, source_target_pairs={{0,2},{1,3},{2,0},{3,1},{4,6},{5,7},{6,4},{7,5},{8,10},{9,11},{10,... | collective-permute-start | bytes 663560 | tf_op jit(solution)/shard_map/ppermute | solution.py:325
  13.9 0.5 collective-permute-start.6
  14.4 1.0 %collective-permute-done.7.pair = bf16[2,3,128,128]{3,2,1,0:T(8,128)(2,1)S(1)} collective-permute-done((bf16[2,3,128,128]{3,2,1,0:T(8,128)(2,1)S(1)}, bf16[2,3,128,128]{3,2,1,0:T(8,128)(2,1)S(1)}, u32[]{:S(2)}, u32[]{:S(2)}) %collective-permute-start.7) | collective-permute-done | bytes 196640 | tf_op jit(solution)/shard_map/ppermute | solution.py:325
  15.5 2.0 %collective-permute-start.8 = (bf16[3,256,128]{2,1,0:T(8,128)(2,1)S(1)}, bf16[3,256,128]{2,1,0:T(8,128)(2,1)S(1)}, u32[]{:S(2)}, u32[]{:S(2)}) collective-permute-start(bf16[3,256,128]{2,1,0:T(8,128)(2,1)S(1)} %get-tuple-element.62), channel_id=1, source_target_pairs={{0,4},{1,0},{2,6},{3,2},{4,8},{5,1},{6,10},{7,3},{8,12},{9,5},{10,... | collective-permute-start | bytes 589832 | tf_op jit(solution)/shard_map/ppermute | solution.py:333
  17.5 4.4 %collective-permute-done.5.halo2 = bf16[3,256,128]{2,1,0:T(8,128)(2,1)S(1)} collective-permute-done((bf16[3,256,128]{2,1,0:T(8,128)(2,1)S(1)}, bf16[3,256,128]{2,1,0:T(8,128)(2,1)S(1)}, u32[]{:S(2)}, u32[]{:S(2)}) %collective-permute-start.5) | collective-permute-done | bytes 196640 | tf_op jit(solution)/shard_map/ppermute | solution.py:333
  21.9 1.8 %probs.1 = (bf16[3,1024,512]{2,1,0:T(8,128)(2,1)S(1)}, bf16[3,1024,128]{2,1,0:T(8,128)(2,1)S(1)}, bf16[3,512,128]{2,1,0:T(8,128)(2,1)S(1)}) custom-call(bf16[3,528,128]{2,1,0:T(8,128)(2,1)S(1)} %get-tuple-element.46.own, bf16[3,928,128]{2,1,0:T(8,128)(2,1)S(1)} %collective-permute-done.side, bf16[2,3,144,128]{3,2,1,0:T(8,128)(2,1)S(1)} %collective-permute-done.3.crossed, ...), custom_call_target="tpu_custom_call" | custom-call | tf_op jit(solution)/shard_map/probs/pallas_call | solution.py:302
  23.7 0.4 collective-permute-done.6.crossed
  24.1 0.8 %values.1 = (bf16[3,512,128]{2,1,0:T(8,128)(2,1)S(1)}, f32[3,512,128]{2,1,0:T(8,128)S(1)}, bf16[3,256,128]{2,1,0:T(8,128)(2,1)S(1)}, bf16[3,256,128]{2,1,0:T(8,128)(2,1)S(1)}) custom-call(bf16[3,1024,512]{2,1,0:T(8,128)(2,1)S(1)} %get-tuple-element.56.probs, bf16[3,528,128]{2,1,0:T(8,128)(2,1)S(1)} %get-tuple-element.46.own, ...), custom_call_target="tpu_custom_call" | custom-call | tf_op jit(solution)/shard_map/values/pallas_call | solution.py:302
  24.9 1.8 %collective-permute-start.12 = (bf16[3,256,128]{2,1,0:T(8,128)(2,1)S(1)}, bf16[3,256,128]{2,1,0:T(8,128)(2,1)S(1)}, u32[]{:S(2)}, u32[]{:S(2)}) collective-permute-start(bf16[3,256,128]{2,1,0:T(8,128)(2,1)S(1)} %get-tuple-element.73), channel_id=1, source_target_pairs={{0,4},{1,0},{2,6},{3,2},{4,8},{5,1},{6,10},{7,3},{8,12},{9,5},{10,... | collective-permute-start | bytes 589832 | tf_op jit(solution)/shard_map/ppermute | solution.py:333
  26.7 3.8 %grads.1 = (bf16[3,128,128]{2,1,0:T(8,128)(2,1)S(1)}, bf16[3,128,128]{2,1,0:T(8,128)(2,1)S(1)}, bf16[2,3,128,128]{3,2,1,0:T(8,128)(2,1)S(1)}, f32[3,512,128]{2,1...) custom-call(bf16[3,1024,512]{2,1,0:T(8,128)(2,1)S(1)} %get-tuple-element.56.probs, ...), custom_call_target="tpu_custom_call" | custom-call | tf_op jit(solution)/shard_map/grads/pallas_call | solution.py:302
  30.5 2.0 %collective-permute-start.14 = (bf16[3,256,128]{2,1,0:T(8,128)(2,1)S(1)}, bf16[3,256,128]{2,1,0:T(8,128)(2,1)S(1)}, u32[]{:S(2)}, u32[]{:S(2)}) collective-permute-start(bf16[3,256,128]{2,1,0:T(8,128)(2,1)S(1)} %get-tuple-element.77), channel_id=1, source_target_pairs={{0,4},{1,0},{2,6},{3,2},{4,8},{5,1},{6,10},{7,3},{8,12},{9,5},{10,... | collective-permute-start | bytes 589832 | tf_op jit(solution)/shard_map/ppermute | solution.py:333
  32.8 1.6 %collective-permute-start.19 = (bf16[3,128,128]{2,1,0:T(8,128)(2,1)S(1)}, bf16[3,128,128]{2,1,0:T(8,128)(2,1)S(1)}, u32[]{:S(2)}, u32[]{:S(2)}) collective-permute-start(bf16[3,128,128]{2,1,0:T(8,128)(2,1)S(1)} %get-tuple-element.83), channel_id=1, source_target_pairs={{0,2},{1,3},{2,0},{3,1},{4,6},{5,7},{6,4},{7,5},{8,10},{9,11},{10,... | collective-permute-start | bytes 294920 | tf_op jit(solution)/shard_map/ppermute | solution.py:325
  34.6 1.2 %collective-permute-done.14.ring1 = bf16[3,256,128]{2,1,0:T(8,128)(2,1)S(1)} collective-permute-done((bf16[3,256,128]{2,1,0:T(8,128)(2,1)S(1)}, bf16[3,256,128]{2,1,0:T(8,128)(2,1)S(1)}, u32[]{:S(2)}, u32[]{:S(2)}) %collective-permute-start.14) | collective-permute-done | bytes 196640 | tf_op jit(solution)/shard_map/ppermute | solution.py:333
  35.8 1.7 %collective-permute-start.11 = (bf16[2,3,128,128]{3,2,1,0:T(8,128)(2,1)S(1)}, bf16[2,3,128,128]{3,2,1,0:T(8,128)(2,1)S(1)}, u32[]{:S(2)}, u32[]{:S(2)}) collective-permute-start(bf16[2,3,128,128]{3,2,1,0:T(8,128)(2,1)S(1)} %get-tuple-element.69), channel_id=1, source_target_pairs={{0,2},{1,3},{2,0},{3,1},{4,6},{5,7},{6,4},{7,5},{8,10},{9,11},{10,... | collective-permute-start | bytes 589832 | tf_op jit(solution)/shard_map/ppermute | solution.py:325
  37.5 0.7 %collective-permute-done.15.ring2 = bf16[3,256,128]{2,1,0:T(8,128)(2,1)S(1)} collective-permute-done((bf16[3,256,128]{2,1,0:T(8,128)(2,1)S(1)}, bf16[3,256,128]{2,1,0:T(8,128)(2,1)S(1)}, u32[]{:S(2)}, u32[]{:S(2)}) %collective-permute-start.15) | collective-permute-done | bytes 196640 | tf_op jit(solution)/shard_map/ppermute | solution.py:333
  38.4 1.2 %collective-permute-done.20.in3 = bf16[3,128,128]{2,1,0:T(8,128)(2,1)S(1)} collective-permute-done((bf16[3,128,128]{2,1,0:T(8,128)(2,1)S(1)}, bf16[3,128,128]{2,1,0:T(8,128)(2,1)S(1)}, u32[]{:S(2)}, u32[]{:S(2)}) %collective-permute-start.20) | collective-permute-done | bytes 98336 | tf_op jit(solution)/shard_map/ppermute | solution.py:325
  39.7 1.3 %collective-permute-start.22 = (bf16[4,3,128,128]{3,2,1,0:T(8,128)(2,1)S(1)}, bf16[4,3,128,128]{3,2,1,0:T(8,128)(2,1)S(1)}, u32[]{:S(2)}, u32[]{:S(2)}) collective-permute-start(bf16[4,3,128,128]{3,2,1,0:T(8,128)(2,1)S(1)} %gather.1.groups), channel_id=1, source_target_pairs={{16,0},{17,1},{18,2},{19,3},{20,4},{21,5},{22,6},{23,7},{24,8},{25... | collective-permute-start | bytes 1179656 | tf_op jit(solution)/shard_map/ppermute | solution.py:403
  41.0 3.3 %collective-permute-done.11.crossed = bf16[2,3,128,128]{3,2,1,0:T(8,128)(2,1)S(1)} collective-permute-done((bf16[2,3,128,128]{3,2,1,0:T(8,128)(2,1)S(1)}, bf16[2,3,128,128]{3,2,1,0:T(8,128)(2,1)S(1)}, u32[]{:S(2)}, u32[]{:S(2)}) %collective-permute-start.11) | collective-permute-done | bytes 196640 | tf_op jit(solution)/shard_map/ppermute | solution.py:325
  44.3 1.6 %collective-permute-start.21 = (bf16[2,3,128,128]{3,2,1,0:T(8,128)(2,1)S(1)}, bf16[2,3,128,128]{3,2,1,0:T(8,128)(2,1)S(1)}, u32[]{:S(2)}, u32[]{:S(2)}) collective-permute-start(bf16[2,3,128,128]{3,2,1,0:T(8,128)(2,1)S(1)} %join.1), channel_id=1, source_target_pairs={{0,2},{1,3},{2,0},{3,1},{4,6},{5,7},{6,4},{7,5},{8,10},{9,11},{10,... | collective-permute-start | bytes 589832 | tf_op jit(solution)/shard_map/ppermute | solution.py:325
  46.1 0.8 %unpack.5 = bf16[1,128,1536]{2,1,0:T(8,128)(2,1)} custom-call(bf16[4,3,128,128]{3,2,1,0:T(8,128)(2,1)S(1)} %gather.1.groups), custom_call_target="tpu_custom_call" | custom-call | tf_op jit(solution)/shard_map/unpack/pallas_call | solution.py:302
  47.2 0.9 %unpack.4 = bf16[1,128,1536]{2,1,0:T(8,128)(2,1)} custom-call(bf16[3,128,128]{2,1,0:T(8,128)(2,1)S(1)} %get-tuple-element.67.dq0, bf16[3,128,128]{2,1,0:T(8,128)(2,1)S(1)} %collective-permute-done.10.dq1, bf16[2,3,128,128]{3,2,1,0:T(8,128)(2,1)S(1)} %collective-permute-done.11.crossed, bf16[2,3,128,128]{3,2,1,0:T(8,128)(2,1)S(1)} %collective-permute-done.17.turned), custom_call_target="tpu_custom_call" | custom-call | tf_op jit(solution)/shard_map/unpack/pallas_call | solution.py:302
  48.1 3.6 %collective-permute-done.21.crossed = bf16[2,3,128,128]{3,2,1,0:T(8,128)(2,1)S(1)} collective-permute-done((bf16[2,3,128,128]{3,2,1,0:T(8,128)(2,1)S(1)}, bf16[2,3,128,128]{3,2,1,0:T(8,128)(2,1)S(1)}, u32[]{:S(2)}, u32[]{:S(2)}) %collective-permute-start.21) | collective-permute-done | bytes 196640 | tf_op jit(solution)/shard_map/ppermute | solution.py:325
  51.7 0.8 %unpack.6 = bf16[1,128,1536]{2,1,0:T(8,128)(2,1)} custom-call(bf16[2,3,128,128]{3,2,1,0:T(8,128)(2,1)S(1)} %get-tuple-element.86.stay, bf16[2,3,128,128]{3,2,1,0:T(8,128)(2,1)S(1)} %collective-permute-done.16.got, bf16[2,3,128,128]{3,2,1,0:T(8,128)(2,1)S(1)} %collective-permute-done.21.crossed), custom_call_target="tpu_custom_call" | custom-call | tf_op jit(solution)/shard_map/unpack/pallas_call | solution.py:302
  52.6 0.8 %collective-permute-done.22.groups = bf16[4,3,128,128]{3,2,1,0:T(8,128)(2,1)S(1)} collective-permute-done((bf16[4,3,128,128]{3,2,1,0:T(8,128)(2,1)S(1)}, bf16[4,3,128,128]{3,2,1,0:T(8,128)(2,1)S(1)}, u32[]{:S(2)}, u32[]{:S(2)}) %collective-permute-start.22) | collective-permute-done | bytes 393248 | tf_op jit(solution)/shard_map/ppermute | solution.py:403
  53.3 0.8 %unpack.7 = bf16[1,128,1536]{2,1,0:T(8,128)(2,1)} custom-call(bf16[4,3,128,128]{3,2,1,0:T(8,128)(2,1)S(1)} %collective-permute-done.22.groups), custom_call_target="tpu_custom_call" | custom-call | tf_op jit(solution)/shard_map/unpack/pallas_call | solution.py:302
  (29 shorter events, 1.5 us)
Async XLA Ops:
  2.3 3.2 %collective-permute-start = (bf16[3,928,128]{2,1,0:T(8,128)(2,1)S(1)}, bf16[3,928,128]{2,1,0:T(8,128)(2,1)S(1)}, u32[]{:S(2)}, u32[]{:S(2)}) collective-permute-start(bf16[3,928,128]{2,1,0:T(8,128)(2,1)S(1)} %get-tuple-element.47), channel_id=1, source_target_pairs={{0,1},{1,0},{2,3},{3,2},{4,5},{5,4},{6,7},{7,6},{8,9},{9,8},{10,11... | collective-permute-start | bytes 2138120 | tf_op jit(solution)/shard_map/ppermute | solution.py:325
  2.8 6.2 %collective-permute-start.1 = (bf16[3,128,128]{2,1,0:T(8,128)(2,1)S(1)}, bf16[3,128,128]{2,1,0:T(8,128)(2,1)S(1)}, u32[]{:S(2)}, u32[]{:S(2)}) collective-permute-start(bf16[3,128,128]{2,1,0:T(8,128)(2,1)S(1)} %get-tuple-element.50), channel_id=1, source_target_pairs={{0,2},{1,3},{2,0},{3,1},{4,6},{5,7},{6,4},{7,5},{8,10},{9,11},{10,... | collective-permute-start | bytes 294920 | tf_op jit(solution)/shard_map/ppermute | solution.py:325
  5.4 5.2 %collective-permute-start.2 = (bf16[3,128,128]{2,1,0:T(8,128)(2,1)S(1)}, bf16[3,128,128]{2,1,0:T(8,128)(2,1)S(1)}, u32[]{:S(2)}, u32[]{:S(2)}) collective-permute-start(bf16[3,128,128]{2,1,0:T(8,128)(2,1)S(1)} %get-tuple-element.51), channel_id=1, source_target_pairs={{0,3},{1,2},{2,1},{3,0},{4,7},{5,6},{6,5},{7,4},{8,11},{9,10},{10,... | collective-permute-start | bytes 294920 | tf_op jit(solution)/shard_map/ppermute | solution.py:325
  5.5 9.8 %collective-permute-start.7 = (bf16[2,3,128,128]{3,2,1,0:T(8,128)(2,1)S(1)}, bf16[2,3,128,128]{3,2,1,0:T(8,128)(2,1)S(1)}, u32[]{:S(2)}, u32[]{:S(2)}) collective-permute-start(bf16[2,3,128,128]{3,2,1,0:T(8,128)(2,1)S(1)} %get-tuple-element.61), channel_id=1, source_target_pairs={{0,2},{1,3},{2,0},{3,1},{4,6},{5,7},{6,4},{7,5},{8,10},{9,11},{10,... | collective-permute-start | bytes 589832 | tf_op jit(solution)/shard_map/ppermute | solution.py:325
  10.7 6.8 %collective-permute-start.4 = (bf16[3,256,128]{2,1,0:T(8,128)(2,1)S(1)}, bf16[3,256,128]{2,1,0:T(8,128)(2,1)S(1)}, u32[]{:S(2)}, u32[]{:S(2)}) collective-permute-start(bf16[3,256,128]{2,1,0:T(8,128)(2,1)S(1)} %get-tuple-element.54), channel_id=1, source_target_pairs={{0,4},{1,0},{2,6},{3,2},{4,8},{5,1},{6,10},{7,3},{8,12},{9,5},{10,... | collective-permute-start | bytes 589832 | tf_op jit(solution)/shard_map/ppermute | solution.py:333
  12.4 9.5 %collective-permute-start.3 = (bf16[2,3,144,128]{3,2,1,0:T(8,128)(2,1)S(1)}, bf16[2,3,144,128]{3,2,1,0:T(8,128)(2,1)S(1)}, u32[]{:S(2)}, u32[]{:S(2)}) collective-permute-start(bf16[2,3,144,128]{3,2,1,0:T(8,128)(2,1)S(1)} %get-tuple-element.53), channel_id=1, source_target_pairs={{0,2},{1,3},{2,0},{3,1},{4,6},{5,7},{6,4},{7,5},{8,10},{9,11},{10,... | collective-permute-start | bytes 663560 | tf_op jit(solution)/shard_map/ppermute | solution.py:325
  13.9 10.2 %collective-permute-start.6 = (bf16[2,3,128,128]{3,2,1,0:T(8,128)(2,1)S(1)}, bf16[2,3,128,128]{3,2,1,0:T(8,128)(2,1)S(1)}, u32[]{:S(2)}, u32[]{:S(2)}) collective-permute-start(bf16[2,3,128,128]{3,2,1,0:T(8,128)(2,1)S(1)} %get-tuple-element.60), channel_id=1, source_target_pairs={{0,2},{1,3},{2,0},{3,1},{4,6},{5,7},{6,4},{7,5},{8,10},{9,11},{10,... | collective-permute-start | bytes 589832 | tf_op jit(solution)/shard_map/ppermute | solution.py:325
  14.4 7.5 %collective-permute-start.5 = (bf16[3,256,128]{2,1,0:T(8,128)(2,1)S(1)}, bf16[3,256,128]{2,1,0:T(8,128)(2,1)S(1)}, u32[]{:S(2)}, u32[]{:S(2)}) collective-permute-start(bf16[3,256,128]{2,1,0:T(8,128)(2,1)S(1)} %get-tuple-element.55), channel_id=1, source_target_pairs={{0,1},{1,5},{2,3},{3,7},{4,0},{5,9},{6,2},{7,11},{8,4},{9,13},{10,... | collective-permute-start | bytes 589832 | tf_op jit(solution)/shard_map/ppermute | solution.py:333
  15.5 8.6 %collective-permute-start.8 = (bf16[3,256,128]{2,1,0:T(8,128)(2,1)S(1)}, bf16[3,256,128]{2,1,0:T(8,128)(2,1)S(1)}, u32[]{:S(2)}, u32[]{:S(2)}) collective-permute-start(bf16[3,256,128]{2,1,0:T(8,128)(2,1)S(1)} %get-tuple-element.62), channel_id=1, source_target_pairs={{0,4},{1,0},{2,6},{3,2},{4,8},{5,1},{6,10},{7,3},{8,12},{9,5},{10,... | collective-permute-start | bytes 589832 | tf_op jit(solution)/shard_map/ppermute | solution.py:333
  17.5 6.6 %collective-permute-start.9 = (bf16[3,256,128]{2,1,0:T(8,128)(2,1)S(1)}, bf16[3,256,128]{2,1,0:T(8,128)(2,1)S(1)}, u32[]{:S(2)}, u32[]{:S(2)}) collective-permute-start(bf16[3,256,128]{2,1,0:T(8,128)(2,1)S(1)} %get-tuple-element.63), channel_id=1, source_target_pairs={{0,1},{1,5},{2,3},{3,7},{4,0},{5,9},{6,2},{7,11},{8,4},{9,13},{10,... | collective-permute-start | bytes 589832 | tf_op jit(solution)/shard_map/ppermute | solution.py:333
  24.9 7.7 %collective-permute-start.12 = (bf16[3,256,128]{2,1,0:T(8,128)(2,1)S(1)}, bf16[3,256,128]{2,1,0:T(8,128)(2,1)S(1)}, u32[]{:S(2)}, u32[]{:S(2)}) collective-permute-start(bf16[3,256,128]{2,1,0:T(8,128)(2,1)S(1)} %get-tuple-element.73), channel_id=1, source_target_pairs={{0,4},{1,0},{2,6},{3,2},{4,8},{5,1},{6,10},{7,3},{8,12},{9,5},{10,... | collective-permute-start | bytes 589832 | tf_op jit(solution)/shard_map/ppermute | solution.py:333
  26.7 5.8 %collective-permute-start.13 = (bf16[3,256,128]{2,1,0:T(8,128)(2,1)S(1)}, bf16[3,256,128]{2,1,0:T(8,128)(2,1)S(1)}, u32[]{:S(2)}, u32[]{:S(2)}) collective-permute-start(bf16[3,256,128]{2,1,0:T(8,128)(2,1)S(1)} %get-tuple-element.74), channel_id=1, source_target_pairs={{0,1},{1,5},{2,3},{3,7},{4,0},{5,9},{6,2},{7,11},{8,4},{9,13},{10,... | collective-permute-start | bytes 589832 | tf_op jit(solution)/shard_map/ppermute | solution.py:333
  30.5 5.3 %collective-permute-start.14 = (bf16[3,256,128]{2,1,0:T(8,128)(2,1)S(1)}, bf16[3,256,128]{2,1,0:T(8,128)(2,1)S(1)}, u32[]{:S(2)}, u32[]{:S(2)}) collective-permute-start(bf16[3,256,128]{2,1,0:T(8,128)(2,1)S(1)} %get-tuple-element.77), channel_id=1, source_target_pairs={{0,4},{1,0},{2,6},{3,2},{4,8},{5,1},{6,10},{7,3},{8,12},{9,5},{10,... | collective-permute-start | bytes 589832 | tf_op jit(solution)/shard_map/ppermute | solution.py:333
  32.5 5.7 %collective-permute-start.15 = (bf16[3,256,128]{2,1,0:T(8,128)(2,1)S(1)}, bf16[3,256,128]{2,1,0:T(8,128)(2,1)S(1)}, u32[]{:S(2)}, u32[]{:S(2)}) collective-permute-start(bf16[3,256,128]{2,1,0:T(8,128)(2,1)S(1)} %get-tuple-element.78), channel_id=1, source_target_pairs={{0,1},{1,5},{2,3},{3,7},{4,0},{5,9},{6,2},{7,11},{8,4},{9,13},{10,... | collective-permute-start | bytes 589832 | tf_op jit(solution)/shard_map/ppermute | solution.py:333
  32.7 5.7 %collective-permute-start.18 = (bf16[3,128,128]{2,1,0:T(8,128)(2,1)S(1)}, bf16[3,128,128]{2,1,0:T(8,128)(2,1)S(1)}, u32[]{:S(2)}, u32[]{:S(2)}) collective-permute-start(bf16[3,128,128]{2,1,0:T(8,128)(2,1)S(1)} %get-tuple-element.82), channel_id=1, source_target_pairs={{0,1},{1,0},{2,3},{3,2},{4,5},{5,4},{6,7},{7,6},{8,9},{9,8},{10,11... | collective-permute-start | bytes 294920 | tf_op jit(solution)/shard_map/ppermute | solution.py:325
  32.8 5.7 %collective-permute-start.19 = (bf16[3,128,128]{2,1,0:T(8,128)(2,1)S(1)}, bf16[3,128,128]{2,1,0:T(8,128)(2,1)S(1)}, u32[]{:S(2)}, u32[]{:S(2)}) collective-permute-start(bf16[3,128,128]{2,1,0:T(8,128)(2,1)S(1)} %get-tuple-element.83), channel_id=1, source_target_pairs={{0,2},{1,3},{2,0},{3,1},{4,6},{5,7},{6,4},{7,5},{8,10},{9,11},{10,... | collective-permute-start | bytes 294920 | tf_op jit(solution)/shard_map/ppermute | solution.py:325
  34.4 5.3 %collective-permute-start.20 = (bf16[3,128,128]{2,1,0:T(8,128)(2,1)S(1)}, bf16[3,128,128]{2,1,0:T(8,128)(2,1)S(1)}, u32[]{:S(2)}, u32[]{:S(2)}) collective-permute-start(bf16[3,128,128]{2,1,0:T(8,128)(2,1)S(1)} %get-tuple-element.84), channel_id=1, source_target_pairs={{0,3},{1,2},{2,1},{3,0},{4,7},{5,6},{6,5},{7,4},{8,11},{9,10},{10,... | collective-permute-start | bytes 294920 | tf_op jit(solution)/shard_map/ppermute | solution.py:325
  35.8 8.5 %collective-permute-start.11 = (bf16[2,3,128,128]{3,2,1,0:T(8,128)(2,1)S(1)}, bf16[2,3,128,128]{3,2,1,0:T(8,128)(2,1)S(1)}, u32[]{:S(2)}, u32[]{:S(2)}) collective-permute-start(bf16[2,3,128,128]{3,2,1,0:T(8,128)(2,1)S(1)} %get-tuple-element.69), channel_id=1, source_target_pairs={{0,2},{1,3},{2,0},{3,1},{4,6},{5,7},{6,4},{7,5},{8,10},{9,11},{10,... | collective-permute-start | bytes 589832 | tf_op jit(solution)/shard_map/ppermute | solution.py:325
  38.3 6.0 %collective-permute-start.16 = (bf16[2,3,128,128]{3,2,1,0:T(8,128)(2,1)S(1)}, bf16[2,3,128,128]{3,2,1,0:T(8,128)(2,1)S(1)}, u32[]{:S(2)}, u32[]{:S(2)}) collective-permute-start(bf16[2,3,128,128]{3,2,1,0:T(8,128)(2,1)S(1)} %get-tuple-element.79), channel_id=1, source_target_pairs={{0,1},{1,0},{2,3},{3,2},{4,5},{5,4},{6,7},{7,6},{8,9},{9,8},{10,11... | collective-permute-start | bytes 589832 | tf_op jit(solution)/shard_map/ppermute | solution.py:325
  39.7 13.6 %collective-permute-start.22 = (bf16[4,3,128,128]{3,2,1,0:T(8,128)(2,1)S(1)}, bf16[4,3,128,128]{3,2,1,0:T(8,128)(2,1)S(1)}, u32[]{:S(2)}, u32[]{:S(2)}) collective-permute-start(bf16[4,3,128,128]{3,2,1,0:T(8,128)(2,1)S(1)} %gather.1.groups), channel_id=1, source_target_pairs={{16,0},{17,1},{18,2},{19,3},{20,4},{21,5},{22,6},{23,7},{24,8},{25... | collective-permute-start | bytes 1179656 | tf_op jit(solution)/shard_map/ppermute | solution.py:403
  44.3 2.9 %collective-permute-start.17 = (bf16[2,3,128,128]{3,2,1,0:T(8,128)(2,1)S(1)}, bf16[2,3,128,128]{3,2,1,0:T(8,128)(2,1)S(1)}, u32[]{:S(2)}, u32[]{:S(2)}) collective-permute-start(bf16[2,3,128,128]{3,2,1,0:T(8,128)(2,1)S(1)} %collective-permute-done.11.crossed), channel_id=1, source_target_pairs={{0,1},{1,0},{2,3},{3,2},{4,5},{5,4},{6,7},{7,6},{8,9},{9,8},{10,11... | collective-permute-start | bytes 589832 | tf_op jit(solution)/shard_map/ppermute | solution.py:325
  44.3 7.4 %collective-permute-start.21 = (bf16[2,3,128,128]{3,2,1,0:T(8,128)(2,1)S(1)}, bf16[2,3,128,128]{3,2,1,0:T(8,128)(2,1)S(1)}, u32[]{:S(2)}, u32[]{:S(2)}) collective-permute-start(bf16[2,3,128,128]{3,2,1,0:T(8,128)(2,1)S(1)} %join.1), channel_id=1, source_target_pairs={{0,2},{1,3},{2,0},{3,1},{4,6},{5,7},{6,4},{7,5},{8,10},{9,11},{10,... | collective-permute-start | bytes 589832 | tf_op jit(solution)/shard_map/ppermute | solution.py:325
  45.9 1.3 %collective-permute-start.10 = (bf16[3,128,128]{2,1,0:T(8,128)(2,1)S(1)}, bf16[3,128,128]{2,1,0:T(8,128)(2,1)S(1)}, u32[]{:S(2)}, u32[]{:S(2)}) collective-permute-start(bf16[3,128,128]{2,1,0:T(8,128)(2,1)S(1)} %get-tuple-element.68), channel_id=1, source_target_pairs={{0,1},{1,0},{2,3},{3,2},{4,5},{5,4},{6,7},{7,6},{8,9},{9,8},{10,11... | collective-permute-start | bytes 294920 | tf_op jit(solution)/shard_map/ppermute | solution.py:325

commit v4 on v3

--- a/solution.py
+++ b/solution.py
@@ -205,10 +205,7 @@
         hand_ends(h, ends, dv1, dv2)
 
 
-def grads_kernel(
-    probs, ks, qs, gs, local, halo1, halo2, dq0, dq1, dq23, dk_own, dk1, dk2, vs, ss, dqs, ends
-):
-    me = member()
+def scores_kernel(probs, qs, gs, local, halo1, halo2, ss, dk_own, dk1, dk2, vs, ends):
     for h in range(LOCAL):
         line_up(vs, h, local, halo1, halo2)
         for pair in range(TEAM // 2):
@@ -223,13 +220,20 @@
                 grad_probs = both[n * BLK : (n + SPAN) * BLK, n * BLK : (n + 1) * BLK]
                 weights = probs[h, reach, here].astype(f32)
                 delta = jnp.sum(weights * grad_probs, axis=0, keepdims=True)
-                scores_low = (weights * (grad_probs - delta)).astype(bf16)
-                ss[h, reach, here] = scores_low
-                dqs[here, :] = (tn(scores_low, ks[h, reach, :]) * SCALE).astype(bf16)
+                ss[h, reach, here] = (weights * (grad_probs - delta)).astype(bf16)
+        key_sums(ss, qs, h, dk_own, ends, SCALE)
+        hand_ends(h, ends, dk1, dk2)
+
+
+def queries_kernel(ss, ks, dq0, dq1, dq23, dqs):
+    me = member()
+    for h in range(LOCAL):
+        for i in range(TEAM):
+            here = slice(i * BLK, (i + 1) * BLK)
+            reach = slice(i * BLK, (i + SPAN) * BLK)
+            dqs[here, :] = (tn(ss[h, reach, here], ks[h, reach, :]) * SCALE).astype(bf16)
         for step, target in enumerate((dq0, dq1, dq23.at[0], dq23.at[1])):
             target[h] = dqs[rows_of(jnp.bitwise_xor(me, step)), :]
-        key_sums(ss, qs, h, dk_own, ends, SCALE)
-        hand_ends(h, ends, dk1, dk2)
 
 
 def total_kernel(mine, ring1, ring2, *outs):
@@ -259,10 +263,7 @@
         groups[jnp.bitwise_xor(me, step)] = source[...]
 
 
-def write_out(parts, out, out_hbm, sems):
-    for group, source in parts:
-        for h in range(LOCAL):
-            out[0, :, head_columns(group, h)] = source[h]
+def send_rows(out, out_hbm, sems):
     copies = pieces(out, out_hbm, sems)
     for copy in copies:
         copy.start()
@@ -270,6 +271,13 @@
         copy.wait()
 
 
+def write_out(parts, out, out_hbm, sems):
+    for group, source in parts:
+        for h in range(LOCAL):
+            out[0, :, head_columns(group, h)] = source[h]
+    send_rows(out, out_hbm, sems)
+
+
 def unpack_kernel(in0, in1, in2, in3, out_hbm, out, sems):
     me = member()
     sources = (in0, in1, in2, in3)
@@ -285,8 +293,13 @@
     unpack_kernel(dq0, dq1, crossed.at[0], turned.at[1], *rest)
 
 
-def unpack_groups_kernel(groups, out_hbm, out, sems):
-    write_out([(group, groups.at[group]) for group in range(TEAM)], out, out_hbm, sems)
+def unpack_passed_kernel(groups, out_hbm, out, sems):
+    last = lax.axis_index("section") == lax.axis_size("section") - 1
+    for group in range(TEAM):
+        for h in range(LOCAL):
+            source = groups[group, h]
+            out[0, :, head_columns(group, h)] = jnp.where(last, jnp.zeros_like(source), source)
+    send_rows(out, out_hbm, sems)
 
 
 def struct(*shape, dtype=bf16):
@@ -363,14 +376,15 @@
         return local, ring(first, 0), ring(second, 1)
 
     k_local, k_halo1, k_halo2 = stage(functools.partial(stage_kernel, K_AT), own, side, k2, k3)
-    q23 = swap(after(q23, k_local), 2)
-    g23 = swap(after(g23, k_local), 2)
+    q23 = swap(q23, 2)
+    g23 = swap(after(g23, k2, k3), 2)
     v23 = swap(v23, 2)
     v_local, v_halo1, v_halo2 = stage(functools.partial(stage_pair_kernel, V_AT), own, side, v23)
     probs, ks, qs = call(
         probs_kernel, "probs", (square, slots, team), [pltpu.VMEM((TEAM * MASK, DH), bf16)]
     )(own, side, q23, k_local, k_halo1, k_halo2)
     g23 = after(g23, v_halo1, v_halo2)
+    g23 = after(g23, v_halo1, v_halo2)
     gs, dv_own, dv1, dv2 = call(values_kernel, "values", (team, kept, ends, ends), [ends_in])(
         probs, own, side, g23
     )
@@ -383,38 +397,36 @@
         sems = pltpu.SemaphoreType.DMA((CUTS,))
         return call(kernel, "unpack", out, [rows_in, sems], to=HBM)(*parts)
 
-    dq0, dq1, dq23, dk_own, dk1, dk2 = call(
-        grads_kernel,
-        "grads",
-        (part, part, pair, kept, ends, ends),
-        [
-            pltpu.VMEM((LOCAL, SLOTS * BLK, DH), bf16),
-            pltpu.VMEM((LOCAL, SLOTS * BLK, TEAM * BLK), bf16),
-            pltpu.VMEM((TEAM * BLK, DH), bf16),
-            ends_in,
-        ],
-    )(probs, ks, qs, gs, v_local, v_halo1, v_halo2)
+    ss, dk_own, dk1, dk2 = call(
+        scores_kernel,
+        "scores",
+        (square, kept, ends, ends),
+        [pltpu.VMEM((LOCAL, SLOTS * BLK, DH), bf16), ends_in],
+    )(probs, qs, gs, v_local, v_halo1, v_halo2)
     dv_own = after(dv_own, dk_own)
     dv = total(total_kernel, (part,) * 4, dv_own, dv1, dv2)
     dv_first = dv[0]
     dv = [dv[0]] + [swap(dv[step], step) for step in range(1, TEAM)]
-    dv = call(gather_kernel, "gather", struct(TEAM, LOCAL, BLK, DH))(*dv)
+    late = call(gather_kernel, "gather", struct(TEAM, LOCAL, BLK, DH))(*dv)
     sections = lax.axis_size("section")
-    passed = lax.ppermute(dv, "section", [(s + 1, s) for s in range(sections - 1)])
-    grad_value = unpack(unpack_groups_kernel, dv)
-
+    passed = lax.ppermute(late, "section", [(s, (s - 1) % sections) for s in range(sections)])
+    grad_value = unpack(unpack_kernel, *dv)
+    dq0, dq1, dq23 = call(
+        queries_kernel, "queries", (part, part, pair), [pltpu.VMEM((TEAM * BLK, DH), bf16)]
+    )(ss, ks)
     dq23 = swap(dq23, 2)
     dk_own = after(dk_own, dv_first)
     stay, give = total(total_pairs_kernel, (pair, pair), dk_own, dk1, dk2)
     got = swap(give, 1)
-    joined = call(join_kernel, "join", pair)(after(stay, dv), got)
+    joined = call(join_kernel, "join", pair)(stay, got)
     crossed = swap(joined, 2)
     dq23 = after(dq23, got)
     grad_query = unpack(unpack_turned_kernel, dq0, swap(dq1, 1), dq23, swap(dq23, 1))
-    stay = after(stay, grad_query, grad_value)
+    handoff = passed
+    stay = after(stay, grad_query)
     grad_key = unpack(unpack_joined_kernel, stay, got, crossed)
     passed = after(passed, grad_key)
-    handoff = unpack(unpack_groups_kernel, passed)
+    handoff = unpack(unpack_passed_kernel, passed)
     return (grad_query, grad_key, grad_value, handoff)
 
 

time: 54.3 us -> 54.8 us (level)
  waiting for transfers between devices: 19.9 us -> 21 us
    ppermute x14, waiting for transfers between devices: 12.8 us -> 14.1 us  [swap(): return lax.ppermute(array, 'ctx', [(i, i ^ step) for i in range(ctx)])]
    ppermute x1, waiting for transfers between devices: 0.75 us -> 0.01 us  [shards(): lax.ppermute(late, 'section', [(s, (s - 1) % sections) for s in range(sec...]
    ppermute x8, waiting for transfers between devices: 6.28 us -> 6.89 us  [ring(): return lax.ppermute(array, 'ctx', pairs)]
    pallas_call x15 -> x16, Pallas kernels: 11.9 us -> 11.5 us  [run(): pl.pallas_call(kernel, out_shape=jax.tree.map(lambda out: to(out.shape, o...]
  transfers between devices with their start and end apart: 23 -> 23, of which waited for: 12 -> 11; matrix products, arithmetic and copies ran while one was open for 0% -> 0% of each run, Pallas kernels for 16% -> 15%
where the time goes in v4:
time: 54.8 us; the launch traced here: 54.7 us
  starting transfers between devices  21.4 us (39%)
  waiting for transfers between devices  21 us (38%)
  Pallas kernels  11.5 us (21%)
  between operations  0.75 us (1%)
    ppermute x14, waiting for transfers between devices, swap(): return lax.ppermute(array, 'ctx', [(i, i ^ step) for i in range(ctx)])  14.1 us
    ppermute x14, starting transfers between devices, swap(): return lax.ppermute(array, 'ctx', [(i, i ^ step) for i in range(ctx)])  12.5 us
    pallas_call x16, Pallas kernels, run(): pl.pallas_call(kernel, out_shape=jax.tree.map(lambda out: to(out.shape, o...  11.5 us
    ppermute x8, starting transfers between devices, ring(): return lax.ppermute(array, 'ctx', pairs)  7.53 us
    ppermute x8, waiting for transfers between devices, ring(): return lax.ppermute(array, 'ctx', pairs)  6.89 us
    ppermute x1, starting transfers between devices, shards(): lax.ppermute(late, 'section', [(s, (s - 1) % sections) for s in range(sec...  1.4 us
  transfers between devices with their start and end apart: 23, of which 11 were waited for; matrix products, arithmetic and copies ran while one was open for 0% of the time, Pallas kernels for 15%

profile of v4, /device:TPU:0, one launch (start us, length us, event | category | flops | bytes accessed | tf_op | source)
XLA Modules:
  0.0 54.7 jit_solution(4259988931375760441)
XLA Ops:
  0.6 1.7 %pack.1 = (bf16[3,528,128]{2,1,0:T(8,128)(2,1)S(1)}, bf16[3,928,128]{2,1,0:T(8,128)(2,1)S(1)}, bf16[3,128,128]{2,1,0:T(8,128)(2,1)S(1)}, bf16[3,128,128]{2,1,0:T(8,128)(2,1)S(1)}, bf16[3,400,128]{2,1,0:T(8,128)(2,1)S(1)}) custom-call(bf16[1,128,1536]{2,1,0:T(8,128)(2,1)} %k_hbm.1, bf16[1,128,1536]{2,1,0:T(8,128)(2,1)} %q_hbm.1, bf16[1,128,1536]{2,1,0:T(8,128)(2,1)} %g_hbm.1, ...), custom_call_target="tpu_custom_call" | custom-call | tf_op jit(solution)/shard_map/pack/pallas_call | solution.py:315
  2.3 0.5 collective-permute-start
  2.8 2.6 %collective-permute-start.2 = (bf16[3,128,128]{2,1,0:T(8,128)(2,1)S(1)}, bf16[3,128,128]{2,1,0:T(8,128)(2,1)S(1)}, u32[]{:S(2)}, u32[]{:S(2)}) collective-permute-start(bf16[3,128,128]{2,1,0:T(8,128)(2,1)S(1)} %get-tuple-element.50), channel_id=1, source_target_pairs={{0,2},{1,3},{2,0},{3,1},{4,6},{5,7},{6,4},{7,5},{8,10},{9,11},{10,... | collective-permute-start | bytes 294920 | tf_op jit(solution)/shard_map/ppermute | solution.py:338
  5.5 2.1 %collective-permute-start.7 = (bf16[2,3,128,128]{3,2,1,0:T(8,128)(2,1)S(1)}, bf16[2,3,128,128]{3,2,1,0:T(8,128)(2,1)S(1)}, u32[]{:S(2)}, u32[]{:S(2)}) collective-permute-start(bf16[2,3,128,128]{3,2,1,0:T(8,128)(2,1)S(1)} %get-tuple-element.59), channel_id=1, source_target_pairs={{0,2},{1,3},{2,0},{3,1},{4,6},{5,7},{6,4},{7,5},{8,10},{9,11},{10,... | collective-permute-start | bytes 589832 | tf_op jit(solution)/shard_map/ppermute | solution.py:338
  7.6 1.4 %collective-permute-done.2.two = bf16[3,128,128]{2,1,0:T(8,128)(2,1)S(1)} collective-permute-done((bf16[3,128,128]{2,1,0:T(8,128)(2,1)S(1)}, bf16[3,128,128]{2,1,0:T(8,128)(2,1)S(1)}, u32[]{:S(2)}, u32[]{:S(2)}) %collective-permute-start.2) | collective-permute-done | bytes 98336 | tf_op jit(solution)/shard_map/ppermute | solution.py:338
  9.1 1.6 %collective-permute-done.3.three = bf16[3,128,128]{2,1,0:T(8,128)(2,1)S(1)} collective-permute-done((bf16[3,128,128]{2,1,0:T(8,128)(2,1)S(1)}, bf16[3,128,128]{2,1,0:T(8,128)(2,1)S(1)}, u32[]{:S(2)}, u32[]{:S(2)}) %collective-permute-start.3) | collective-permute-done | bytes 98336 | tf_op jit(solution)/shard_map/ppermute | solution.py:338
  10.7 1.6 %collective-permute-start.4 = (bf16[3,256,128]{2,1,0:T(8,128)(2,1)S(1)}, bf16[3,256,128]{2,1,0:T(8,128)(2,1)S(1)}, u32[]{:S(2)}, u32[]{:S(2)}) collective-permute-start(bf16[3,256,128]{2,1,0:T(8,128)(2,1)S(1)} %get-tuple-element.53), channel_id=1, source_target_pairs={{0,4},{1,0},{2,6},{3,2},{4,8},{5,1},{6,10},{7,3},{8,12},{9,5},{10,... | collective-permute-start | bytes 589832 | tf_op jit(solution)/shard_map/ppermute | solution.py:346
  12.4 1.5 %collective-permute-start.1 = (bf16[2,3,144,128]{3,2,1,0:T(8,128)(2,1)S(1)}, bf16[2,3,144,128]{3,2,1,0:T(8,128)(2,1)S(1)}, u32[]{:S(2)}, u32[]{:S(2)}) collective-permute-start(bf16[2,3,144,128]{3,2,1,0:T(8,128)(2,1)S(1)} %get-tuple-element.49), channel_id=1, source_target_pairs={{0,2},{1,3},{2,0},{3,1},{4,6},{5,7},{6,4},{7,5},{8,10},{9,11},{10,... | collective-permute-start | bytes 663560 | tf_op jit(solution)/shard_map/ppermute | solution.py:338
  13.9 0.5 collective-permute-start.6
  14.4 1.0 %collective-permute-done.7.pair = bf16[2,3,128,128]{3,2,1,0:T(8,128)(2,1)S(1)} collective-permute-done((bf16[2,3,128,128]{3,2,1,0:T(8,128)(2,1)S(1)}, bf16[2,3,128,128]{3,2,1,0:T(8,128)(2,1)S(1)}, u32[]{:S(2)}, u32[]{:S(2)}) %collective-permute-start.7) | collective-permute-done | bytes 196640 | tf_op jit(solution)/shard_map/ppermute | solution.py:338
  15.5 2.0 %collective-permute-start.8 = (bf16[3,256,128]{2,1,0:T(8,128)(2,1)S(1)}, bf16[3,256,128]{2,1,0:T(8,128)(2,1)S(1)}, u32[]{:S(2)}, u32[]{:S(2)}) collective-permute-start(bf16[3,256,128]{2,1,0:T(8,128)(2,1)S(1)} %get-tuple-element.60), channel_id=1, source_target_pairs={{0,4},{1,0},{2,6},{3,2},{4,8},{5,1},{6,10},{7,3},{8,12},{9,5},{10,... | collective-permute-start | bytes 589832 | tf_op jit(solution)/shard_map/ppermute | solution.py:346
  17.5 4.4 %collective-permute-done.5.halo2 = bf16[3,256,128]{2,1,0:T(8,128)(2,1)S(1)} collective-permute-done((bf16[3,256,128]{2,1,0:T(8,128)(2,1)S(1)}, bf16[3,256,128]{2,1,0:T(8,128)(2,1)S(1)}, u32[]{:S(2)}, u32[]{:S(2)}) %collective-permute-start.5) | collective-permute-done | bytes 196640 | tf_op jit(solution)/shard_map/ppermute | solution.py:346
  21.9 1.8 %probs.1 = (bf16[3,1024,512]{2,1,0:T(8,128)(2,1)S(1)}, bf16[3,1024,128]{2,1,0:T(8,128)(2,1)S(1)}, bf16[3,512,128]{2,1,0:T(8,128)(2,1)S(1)}) custom-call(bf16[3,528,128]{2,1,0:T(8,128)(2,1)S(1)} %get-tuple-element.46.own, bf16[3,928,128]{2,1,0:T(8,128)(2,1)S(1)} %collective-permute-done.side, bf16[2,3,144,128]{3,2,1,0:T(8,128)(2,1)S(1)} %collective-permute-done.1.crossed, ...), custom_call_target="tpu_custom_call" | custom-call | tf_op jit(solution)/shard_map/probs/pallas_call | solution.py:315
  24.1 0.8 %values.1 = (bf16[3,512,128]{2,1,0:T(8,128)(2,1)S(1)}, f32[3,512,128]{2,1,0:T(8,128)S(1)}, bf16[3,256,128]{2,1,0:T(8,128)(2,1)S(1)}, bf16[3,256,128]{2,1,0:T(8,128)(2,1)S(1)}) custom-call(bf16[3,1024,512]{2,1,0:T(8,128)(2,1)S(1)} %get-tuple-element.55.probs, bf16[3,528,128]{2,1,0:T(8,128)(2,1)S(1)} %get-tuple-element.46.own, ...), custom_call_target="tpu_custom_call" | custom-call | tf_op jit(solution)/shard_map/values/pallas_call | solution.py:315
  24.9 1.8 %collective-permute-start.12 = (bf16[3,256,128]{2,1,0:T(8,128)(2,1)S(1)}, bf16[3,256,128]{2,1,0:T(8,128)(2,1)S(1)}, u32[]{:S(2)}, u32[]{:S(2)}) collective-permute-start(bf16[3,256,128]{2,1,0:T(8,128)(2,1)S(1)} %get-tuple-element.74), channel_id=1, source_target_pairs={{0,4},{1,0},{2,6},{3,2},{4,8},{5,1},{6,10},{7,3},{8,12},{9,5},{10,... | collective-permute-start | bytes 589832 | tf_op jit(solution)/shard_map/ppermute | solution.py:346
  26.7 2.5 %scores.1 = (bf16[3,1024,512]{2,1,0:T(8,128)(2,1)S(1)}, f32[3,512,128]{2,1,0:T(8,128)S(1)}, bf16[3,256,128]{2,1,0:T(8,128)(2,1)S(1)}, bf16[3,256,128]{2,1,0:T(8,128)(2,1)S(1)}) custom-call(bf16[3,1024,512]{2,1,0:T(8,128)(2,1)S(1)} %get-tuple-element.55.probs, bf16[3,512,128]{2,1,0:T(8,128)(2,1)S(1)} %get-tuple-element.56.qs, ...), custom_call_target="tpu_custom_call" | custom-call | tf_op jit(solution)/shard_map/scores/pallas_call | solution.py:315
  29.2 2.0 %collective-permute-start.14 = (bf16[3,256,128]{2,1,0:T(8,128)(2,1)S(1)}, bf16[3,256,128]{2,1,0:T(8,128)(2,1)S(1)}, u32[]{:S(2)}, u32[]{:S(2)}) collective-permute-start(bf16[3,256,128]{2,1,0:T(8,128)(2,1)S(1)} %get-tuple-element.78), channel_id=1, source_target_pairs={{0,4},{1,0},{2,6},{3,2},{4,8},{5,1},{6,10},{7,3},{8,12},{9,5},{10,... | collective-permute-start | bytes 589832 | tf_op jit(solution)/shard_map/ppermute | solution.py:346
  31.3 2.5 %collective-permute-done.13.ring2 = bf16[3,256,128]{2,1,0:T(8,128)(2,1)S(1)} collective-permute-done((bf16[3,256,128]{2,1,0:T(8,128)(2,1)S(1)}, bf16[3,256,128]{2,1,0:T(8,128)(2,1)S(1)}, u32[]{:S(2)}, u32[]{:S(2)}) %collective-permute-start.13) | collective-permute-done | bytes 196640 | tf_op jit(solution)/shard_map/ppermute | solution.py:346
  34.0 1.4 %collective-permute-start.20 = (bf16[3,128,128]{2,1,0:T(8,128)(2,1)S(1)}, bf16[3,128,128]{2,1,0:T(8,128)(2,1)S(1)}, u32[]{:S(2)}, u32[]{:S(2)}) collective-permute-start(bf16[3,128,128]{2,1,0:T(8,128)(2,1)S(1)} %get-tuple-element.85), channel_id=1, source_target_pairs={{0,2},{1,3},{2,0},{3,1},{4,6},{5,7},{6,4},{7,5},{8,10},{9,11},{10,... | collective-permute-start | bytes 294920 | tf_op jit(solution)/shard_map/ppermute | solution.py:338
  35.4 0.4 collective-permute-start.21
  35.9 0.8 %queries.1 = (bf16[3,128,128]{2,1,0:T(8,128)(2,1)S(1)}, bf16[3,128,128]{2,1,0:T(8,128)(2,1)S(1)}, bf16[2,3,128,128]{3,2,1,0:T(8,128)(2,1)S(1)}) custom-call(bf16[3,1024,512]{2,1,0:T(8,128)(2,1)S(1)} %get-tuple-element.66.ss, bf16[3,1024,128]{2,1,0:T(8,128)(2,1)S(1)} %get-tuple-element.67.ks), custom_call_target="tpu_custom_call" | custom-call | tf_op jit(solution)/shard_map/queries/pallas_call | solution.py:315
  36.7 1.4 %collective-permute-start.11 = (bf16[2,3,128,128]{3,2,1,0:T(8,128)(2,1)S(1)}, bf16[2,3,128,128]{3,2,1,0:T(8,128)(2,1)S(1)}, u32[]{:S(2)}, u32[]{:S(2)}) collective-permute-start(bf16[2,3,128,128]{3,2,1,0:T(8,128)(2,1)S(1)} %get-tuple-element.70), channel_id=1, source_target_pairs={{0,2},{1,3},{2,0},{3,1},{4,6},{5,7},{6,4},{7,5},{8,10},{9,11},{10,... | collective-permute-start | bytes 589832 | tf_op jit(solution)/shard_map/ppermute | solution.py:338
  38.4 1.3 %collective-permute-done.20.in2 = bf16[3,128,128]{2,1,0:T(8,128)(2,1)S(1)} collective-permute-done((bf16[3,128,128]{2,1,0:T(8,128)(2,1)S(1)}, bf16[3,128,128]{2,1,0:T(8,128)(2,1)S(1)}, u32[]{:S(2)}, u32[]{:S(2)}) %collective-permute-start.20) | collective-permute-done | bytes 98336 | tf_op jit(solution)/shard_map/ppermute | solution.py:338
  39.7 1.2 %collective-permute-done.21.in3 = bf16[3,128,128]{2,1,0:T(8,128)(2,1)S(1)} collective-permute-done((bf16[3,128,128]{2,1,0:T(8,128)(2,1)S(1)}, bf16[3,128,128]{2,1,0:T(8,128)(2,1)S(1)}, u32[]{:S(2)}, u32[]{:S(2)}) %collective-permute-start.21) | collective-permute-done | bytes 98336 | tf_op jit(solution)/shard_map/ppermute | solution.py:338
  40.9 1.4 %collective-permute-start.22 = (bf16[4,3,128,128]{3,2,1,0:T(8,128)(2,1)S(1)}, bf16[4,3,128,128]{3,2,1,0:T(8,128)(2,1)S(1)}, u32[]{:S(2)}, u32[]{:S(2)}) collective-permute-start(bf16[4,3,128,128]{3,2,1,0:T(8,128)(2,1)S(1)} %gather.1), channel_id=1, source_target_pairs={{0,16},{16,0},{1,17},{17,1},{2,18},{18,2},{3,19},{19,3},{4,20},{20... | collective-permute-start | bytes 1179656 | tf_op jit(solution)/shard_map/ppermute | solution.py:412
  42.3 3.2 %collective-permute-done.11.crossed = bf16[2,3,128,128]{3,2,1,0:T(8,128)(2,1)S(1)} collective-permute-done((bf16[2,3,128,128]{3,2,1,0:T(8,128)(2,1)S(1)}, bf16[2,3,128,128]{3,2,1,0:T(8,128)(2,1)S(1)}, u32[]{:S(2)}, u32[]{:S(2)}) %collective-permute-start.11) | collective-permute-done | bytes 196640 | tf_op jit(solution)/shard_map/ppermute | solution.py:338
  45.5 1.4 %collective-permute-start.18 = (bf16[2,3,128,128]{3,2,1,0:T(8,128)(2,1)S(1)}, bf16[2,3,128,128]{3,2,1,0:T(8,128)(2,1)S(1)}, u32[]{:S(2)}, u32[]{:S(2)}) collective-permute-start(bf16[2,3,128,128]{3,2,1,0:T(8,128)(2,1)S(1)} %join.1), channel_id=1, source_target_pairs={{0,2},{1,3},{2,0},{3,1},{4,6},{5,7},{6,4},{7,5},{8,10},{9,11},{10,... | collective-permute-start | bytes 589832 | tf_op jit(solution)/shard_map/ppermute | solution.py:338
  47.2 0.8 %unpack.6 = bf16[1,128,1536]{2,1,0:T(8,128)(2,1)} custom-call(bf16[3,128,128]{2,1,0:T(8,128)(2,1)S(1)} %get-tuple-element.76.in0, bf16[3,128,128]{2,1,0:T(8,128)(2,1)S(1)} %collective-permute-done.19.in1, bf16[3,128,128]{2,1,0:T(8,128)(2,1)S(1)} %collective-permute-done.20.in2, bf16[3,128,128]{2,1,0:T(8,128)(2,1)S(1)} %collective-permute-done.21.in3), custom_call_target="tpu_custom_call" | custom-call | tf_op jit(solution)/shard_map/unpack/pallas_call | solution.py:315
  48.3 0.9 %unpack.4 = bf16[1,128,1536]{2,1,0:T(8,128)(2,1)} custom-call(bf16[3,128,128]{2,1,0:T(8,128)(2,1)S(1)} %get-tuple-element.68.dq0, bf16[3,128,128]{2,1,0:T(8,128)(2,1)S(1)} %collective-permute-done.10.dq1, bf16[2,3,128,128]{3,2,1,0:T(8,128)(2,1)S(1)} %collective-permute-done.11.crossed, bf16[2,3,128,128]{3,2,1,0:T(8,128)(2,1)S(1)} %collective-permute-done.17.turned), custom_call_target="tpu_custom_call" | custom-call | tf_op jit(solution)/shard_map/unpack/pallas_call | solution.py:315
  49.1 3.8 %collective-permute-done.18.crossed = bf16[2,3,128,128]{3,2,1,0:T(8,128)(2,1)S(1)} collective-permute-done((bf16[2,3,128,128]{3,2,1,0:T(8,128)(2,1)S(1)}, bf16[2,3,128,128]{3,2,1,0:T(8,128)(2,1)S(1)}, u32[]{:S(2)}, u32[]{:S(2)}) %collective-permute-start.18) | collective-permute-done | bytes 196640 | tf_op jit(solution)/shard_map/ppermute | solution.py:338
  52.9 0.8 %unpack.5 = bf16[1,128,1536]{2,1,0:T(8,128)(2,1)} custom-call(bf16[2,3,128,128]{3,2,1,0:T(8,128)(2,1)S(1)} %get-tuple-element.83.stay, bf16[2,3,128,128]{3,2,1,0:T(8,128)(2,1)S(1)} %collective-permute-done.16.got, bf16[2,3,128,128]{3,2,1,0:T(8,128)(2,1)S(1)} %collective-permute-done.18.crossed), custom_call_target="tpu_custom_call" | custom-call | tf_op jit(solution)/shard_map/unpack/pallas_call | solution.py:315
  53.8 0.9 %unpack.7 = bf16[1,128,1536]{2,1,0:T(8,128)(2,1)} custom-call(bf16[4,3,128,128]{3,2,1,0:T(8,128)(2,1)S(1)} %collective-permute-done.22.groups), custom_call_target="tpu_custom_call" | custom-call | tf_op jit(solution)/shard_map/unpack/pallas_call | solution.py:315
  (30 shorter events, 1.6 us)
Async XLA Ops:
  2.3 3.2 %collective-permute-start = (bf16[3,928,128]{2,1,0:T(8,128)(2,1)S(1)}, bf16[3,928,128]{2,1,0:T(8,128)(2,1)S(1)}, u32[]{:S(2)}, u32[]{:S(2)}) collective-permute-start(bf16[3,928,128]{2,1,0:T(8,128)(2,1)S(1)} %get-tuple-element.47), channel_id=1, source_target_pairs={{0,1},{1,0},{2,3},{3,2},{4,5},{5,4},{6,7},{7,6},{8,9},{9,8},{10,11... | collective-permute-start | bytes 2138120 | tf_op jit(solution)/shard_map/ppermute | solution.py:338
  2.8 6.2 %collective-permute-start.2 = (bf16[3,128,128]{2,1,0:T(8,128)(2,1)S(1)}, bf16[3,128,128]{2,1,0:T(8,128)(2,1)S(1)}, u32[]{:S(2)}, u32[]{:S(2)}) collective-permute-start(bf16[3,128,128]{2,1,0:T(8,128)(2,1)S(1)} %get-tuple-element.50), channel_id=1, source_target_pairs={{0,2},{1,3},{2,0},{3,1},{4,6},{5,7},{6,4},{7,5},{8,10},{9,11},{10,... | collective-permute-start | bytes 294920 | tf_op jit(solution)/shard_map/ppermute | solution.py:338
  5.4 5.2 %collective-permute-start.3 = (bf16[3,128,128]{2,1,0:T(8,128)(2,1)S(1)}, bf16[3,128,128]{2,1,0:T(8,128)(2,1)S(1)}, u32[]{:S(2)}, u32[]{:S(2)}) collective-permute-start(bf16[3,128,128]{2,1,0:T(8,128)(2,1)S(1)} %get-tuple-element.51), channel_id=1, source_target_pairs={{0,3},{1,2},{2,1},{3,0},{4,7},{5,6},{6,5},{7,4},{8,11},{9,10},{10,... | collective-permute-start | bytes 294920 | tf_op jit(solution)/shard_map/ppermute | solution.py:338
  5.5 9.8 %collective-permute-start.7 = (bf16[2,3,128,128]{3,2,1,0:T(8,128)(2,1)S(1)}, bf16[2,3,128,128]{3,2,1,0:T(8,128)(2,1)S(1)}, u32[]{:S(2)}, u32[]{:S(2)}) collective-permute-start(bf16[2,3,128,128]{3,2,1,0:T(8,128)(2,1)S(1)} %get-tuple-element.59), channel_id=1, source_target_pairs={{0,2},{1,3},{2,0},{3,1},{4,6},{5,7},{6,4},{7,5},{8,10},{9,11},{10,... | collective-permute-start | bytes 589832 | tf_op jit(solution)/shard_map/ppermute | solution.py:338
  10.7 6.8 %collective-permute-start.4 = (bf16[3,256,128]{2,1,0:T(8,128)(2,1)S(1)}, bf16[3,256,128]{2,1,0:T(8,128)(2,1)S(1)}, u32[]{:S(2)}, u32[]{:S(2)}) collective-permute-start(bf16[3,256,128]{2,1,0:T(8,128)(2,1)S(1)} %get-tuple-element.53), channel_id=1, source_target_pairs={{0,4},{1,0},{2,6},{3,2},{4,8},{5,1},{6,10},{7,3},{8,12},{9,5},{10,... | collective-permute-start | bytes 589832 | tf_op jit(solution)/shard_map/ppermute | solution.py:346
  12.4 9.5 %collective-permute-start.1 = (bf16[2,3,144,128]{3,2,1,0:T(8,128)(2,1)S(1)}, bf16[2,3,144,128]{3,2,1,0:T(8,128)(2,1)S(1)}, u32[]{:S(2)}, u32[]{:S(2)}) collective-permute-start(bf16[2,3,144,128]{3,2,1,0:T(8,128)(2,1)S(1)} %get-tuple-element.49), channel_id=1, source_target_pairs={{0,2},{1,3},{2,0},{3,1},{4,6},{5,7},{6,4},{7,5},{8,10},{9,11},{10,... | collective-permute-start | bytes 663560 | tf_op jit(solution)/shard_map/ppermute | solution.py:338
  13.9 10.2 %collective-permute-start.6 = (bf16[2,3,128,128]{3,2,1,0:T(8,128)(2,1)S(1)}, bf16[2,3,128,128]{3,2,1,0:T(8,128)(2,1)S(1)}, u32[]{:S(2)}, u32[]{:S(2)}) collective-permute-start(bf16[2,3,128,128]{3,2,1,0:T(8,128)(2,1)S(1)} %get-tuple-element.58), channel_id=1, source_target_pairs={{0,2},{1,3},{2,0},{3,1},{4,6},{5,7},{6,4},{7,5},{8,10},{9,11},{10,... | collective-permute-start | bytes 589832 | tf_op jit(solution)/shard_map/ppermute | solution.py:338
  14.4 7.5 %collective-permute-start.5 = (bf16[3,256,128]{2,1,0:T(8,128)(2,1)S(1)}, bf16[3,256,128]{2,1,0:T(8,128)(2,1)S(1)}, u32[]{:S(2)}, u32[]{:S(2)}) collective-permute-start(bf16[3,256,128]{2,1,0:T(8,128)(2,1)S(1)} %get-tuple-element.54), channel_id=1, source_target_pairs={{0,1},{1,5},{2,3},{3,7},{4,0},{5,9},{6,2},{7,11},{8,4},{9,13},{10,... | collective-permute-start | bytes 589832 | tf_op jit(solution)/shard_map/ppermute | solution.py:346
  15.5 8.6 %collective-permute-start.8 = (bf16[3,256,128]{2,1,0:T(8,128)(2,1)S(1)}, bf16[3,256,128]{2,1,0:T(8,128)(2,1)S(1)}, u32[]{:S(2)}, u32[]{:S(2)}) collective-permute-start(bf16[3,256,128]{2,1,0:T(8,128)(2,1)S(1)} %get-tuple-element.60), channel_id=1, source_target_pairs={{0,4},{1,0},{2,6},{3,2},{4,8},{5,1},{6,10},{7,3},{8,12},{9,5},{10,... | collective-permute-start | bytes 589832 | tf_op jit(solution)/shard_map/ppermute | solution.py:346
  17.5 6.6 %collective-permute-start.9 = (bf16[3,256,128]{2,1,0:T(8,128)(2,1)S(1)}, bf16[3,256,128]{2,1,0:T(8,128)(2,1)S(1)}, u32[]{:S(2)}, u32[]{:S(2)}) collective-permute-start(bf16[3,256,128]{2,1,0:T(8,128)(2,1)S(1)} %get-tuple-element.61), channel_id=1, source_target_pairs={{0,1},{1,5},{2,3},{3,7},{4,0},{5,9},{6,2},{7,11},{8,4},{9,13},{10,... | collective-permute-start | bytes 589832 | tf_op jit(solution)/shard_map/ppermute | solution.py:346
  24.9 6.4 %collective-permute-start.12 = (bf16[3,256,128]{2,1,0:T(8,128)(2,1)S(1)}, bf16[3,256,128]{2,1,0:T(8,128)(2,1)S(1)}, u32[]{:S(2)}, u32[]{:S(2)}) collective-permute-start(bf16[3,256,128]{2,1,0:T(8,128)(2,1)S(1)} %get-tuple-element.74), channel_id=1, source_target_pairs={{0,4},{1,0},{2,6},{3,2},{4,8},{5,1},{6,10},{7,3},{8,12},{9,5},{10,... | collective-permute-start | bytes 589832 | tf_op jit(solution)/shard_map/ppermute | solution.py:346
  26.7 7.0 %collective-permute-start.13 = (bf16[3,256,128]{2,1,0:T(8,128)(2,1)S(1)}, bf16[3,256,128]{2,1,0:T(8,128)(2,1)S(1)}, u32[]{:S(2)}, u32[]{:S(2)}) collective-permute-start(bf16[3,256,128]{2,1,0:T(8,128)(2,1)S(1)} %get-tuple-element.75), channel_id=1, source_target_pairs={{0,1},{1,5},{2,3},{3,7},{4,0},{5,9},{6,2},{7,11},{8,4},{9,13},{10,... | collective-permute-start | bytes 589832 | tf_op jit(solution)/shard_map/ppermute | solution.py:346
  29.2 7.4 %collective-permute-start.14 = (bf16[3,256,128]{2,1,0:T(8,128)(2,1)S(1)}, bf16[3,256,128]{2,1,0:T(8,128)(2,1)S(1)}, u32[]{:S(2)}, u32[]{:S(2)}) collective-permute-start(bf16[3,256,128]{2,1,0:T(8,128)(2,1)S(1)} %get-tuple-element.78), channel_id=1, source_target_pairs={{0,4},{1,0},{2,6},{3,2},{4,8},{5,1},{6,10},{7,3},{8,12},{9,5},{10,... | collective-permute-start | bytes 589832 | tf_op jit(solution)/shard_map/ppermute | solution.py:346
  31.3 6.8 %collective-permute-start.15 = (bf16[3,256,128]{2,1,0:T(8,128)(2,1)S(1)}, bf16[3,256,128]{2,1,0:T(8,128)(2,1)S(1)}, u32[]{:S(2)}, u32[]{:S(2)}) collective-permute-start(bf16[3,256,128]{2,1,0:T(8,128)(2,1)S(1)} %get-tuple-element.79), channel_id=1, source_target_pairs={{0,1},{1,5},{2,3},{3,7},{4,0},{5,9},{6,2},{7,11},{8,4},{9,13},{10,... | collective-permute-start | bytes 589832 | tf_op jit(solution)/shard_map/ppermute | solution.py:346
  33.9 4.4 %collective-permute-start.19 = (bf16[3,128,128]{2,1,0:T(8,128)(2,1)S(1)}, bf16[3,128,128]{2,1,0:T(8,128)(2,1)S(1)}, u32[]{:S(2)}, u32[]{:S(2)}) collective-permute-start(bf16[3,128,128]{2,1,0:T(8,128)(2,1)S(1)} %get-tuple-element.84), channel_id=1, source_target_pairs={{0,1},{1,0},{2,3},{3,2},{4,5},{5,4},{6,7},{7,6},{8,9},{9,8},{10,11... | collective-permute-start | bytes 294920 | tf_op jit(solution)/shard_map/ppermute | solution.py:338
  34.0 5.7 %collective-permute-start.20 = (bf16[3,128,128]{2,1,0:T(8,128)(2,1)S(1)}, bf16[3,128,128]{2,1,0:T(8,128)(2,1)S(1)}, u32[]{:S(2)}, u32[]{:S(2)}) collective-permute-start(bf16[3,128,128]{2,1,0:T(8,128)(2,1)S(1)} %get-tuple-element.85), channel_id=1, source_target_pairs={{0,2},{1,3},{2,0},{3,1},{4,6},{5,7},{6,4},{7,5},{8,10},{9,11},{10,... | collective-permute-start | bytes 294920 | tf_op jit(solution)/shard_map/ppermute | solution.py:338
  35.4 5.4 %collective-permute-start.21 = (bf16[3,128,128]{2,1,0:T(8,128)(2,1)S(1)}, bf16[3,128,128]{2,1,0:T(8,128)(2,1)S(1)}, u32[]{:S(2)}, u32[]{:S(2)}) collective-permute-start(bf16[3,128,128]{2,1,0:T(8,128)(2,1)S(1)} %get-tuple-element.86), channel_id=1, source_target_pairs={{0,3},{1,2},{2,1},{3,0},{4,7},{5,6},{6,5},{7,4},{8,11},{9,10},{10,... | collective-permute-start | bytes 294920 | tf_op jit(solution)/shard_map/ppermute | solution.py:338
  36.7 8.9 %collective-permute-start.11 = (bf16[2,3,128,128]{3,2,1,0:T(8,128)(2,1)S(1)}, bf16[2,3,128,128]{3,2,1,0:T(8,128)(2,1)S(1)}, u32[]{:S(2)}, u32[]{:S(2)}) collective-permute-start(bf16[2,3,128,128]{3,2,1,0:T(8,128)(2,1)S(1)} %get-tuple-element.70), channel_id=1, source_target_pairs={{0,2},{1,3},{2,0},{3,1},{4,6},{5,7},{6,4},{7,5},{8,10},{9,11},{10,... | collective-permute-start | bytes 589832 | tf_op jit(solution)/shard_map/ppermute | solution.py:338
  38.2 7.3 %collective-permute-start.16 = (bf16[2,3,128,128]{3,2,1,0:T(8,128)(2,1)S(1)}, bf16[2,3,128,128]{3,2,1,0:T(8,128)(2,1)S(1)}, u32[]{:S(2)}, u32[]{:S(2)}) collective-permute-start(bf16[2,3,128,128]{3,2,1,0:T(8,128)(2,1)S(1)} %get-tuple-element.80), channel_id=1, source_target_pairs={{0,1},{1,0},{2,3},{3,2},{4,5},{5,4},{6,7},{7,6},{8,9},{9,8},{10,11... | collective-permute-start | bytes 589832 | tf_op jit(solution)/shard_map/ppermute | solution.py:338
  40.9 12.9 %collective-permute-start.22 = (bf16[4,3,128,128]{3,2,1,0:T(8,128)(2,1)S(1)}, bf16[4,3,128,128]{3,2,1,0:T(8,128)(2,1)S(1)}, u32[]{:S(2)}, u32[]{:S(2)}) collective-permute-start(bf16[4,3,128,128]{3,2,1,0:T(8,128)(2,1)S(1)} %gather.1), channel_id=1, source_target_pairs={{0,16},{16,0},{1,17},{17,1},{2,18},{18,2},{3,19},{19,3},{4,20},{20... | collective-permute-start | bytes 1179656 | tf_op jit(solution)/shard_map/ppermute | solution.py:412
  45.5 2.8 %collective-permute-start.17 = (bf16[2,3,128,128]{3,2,1,0:T(8,128)(2,1)S(1)}, bf16[2,3,128,128]{3,2,1,0:T(8,128)(2,1)S(1)}, u32[]{:S(2)}, u32[]{:S(2)}) collective-permute-start(bf16[2,3,128,128]{3,2,1,0:T(8,128)(2,1)S(1)} %collective-permute-done.11.crossed), channel_id=1, source_target_pairs={{0,1},{1,0},{2,3},{3,2},{4,5},{5,4},{6,7},{7,6},{8,9},{9,8},{10,11... | collective-permute-start | bytes 589832 | tf_op jit(solution)/shard_map/ppermute | solution.py:338
  45.5 7.4 %collective-permute-start.18 = (bf16[2,3,128,128]{3,2,1,0:T(8,128)(2,1)S(1)}, bf16[2,3,128,128]{3,2,1,0:T(8,128)(2,1)S(1)}, u32[]{:S(2)}, u32[]{:S(2)}) collective-permute-start(bf16[2,3,128,128]{3,2,1,0:T(8,128)(2,1)S(1)} %join.1), channel_id=1, source_target_pairs={{0,2},{1,3},{2,0},{3,1},{4,6},{5,7},{6,4},{7,5},{8,10},{9,11},{10,... | collective-permute-start | bytes 589832 | tf_op jit(solution)/shard_map/ppermute | solution.py:338
  47.0 1.3 %collective-permute-start.10 = (bf16[3,128,128]{2,1,0:T(8,128)(2,1)S(1)}, bf16[3,128,128]{2,1,0:T(8,128)(2,1)S(1)}, u32[]{:S(2)}, u32[]{:S(2)}) collective-permute-start(bf16[3,128,128]{2,1,0:T(8,128)(2,1)S(1)} %get-tuple-element.69), channel_id=1, source_target_pairs={{0,1},{1,0},{2,3},{3,2},{4,5},{5,4},{6,7},{7,6},{8,9},{9,8},{10,11... | collective-permute-start | bytes 294920 | tf_op jit(solution)/shard_map/ppermute | solution.py:338

commit v5 on v4

--- a/solution.py
+++ b/solution.py
@@ -384,7 +384,6 @@
         probs_kernel, "probs", (square, slots, team), [pltpu.VMEM((TEAM * MASK, DH), bf16)]
     )(own, side, q23, k_local, k_halo1, k_halo2)
     g23 = after(g23, v_halo1, v_halo2)
-    g23 = after(g23, v_halo1, v_halo2)
     gs, dv_own, dv1, dv2 = call(values_kernel, "values", (team, kept, ends, ends), [ends_in])(
         probs, own, side, g23
     )
@@ -410,20 +409,19 @@
     late = call(gather_kernel, "gather", struct(TEAM, LOCAL, BLK, DH))(*dv)
     sections = lax.axis_size("section")
     passed = lax.ppermute(late, "section", [(s, (s - 1) % sections) for s in range(sections)])
-    grad_value = unpack(unpack_kernel, *dv)
     dq0, dq1, dq23 = call(
         queries_kernel, "queries", (part, part, pair), [pltpu.VMEM((TEAM * BLK, DH), bf16)]
-    )(ss, ks)
+    )(after(ss, dv_first), ks)
     dq23 = swap(dq23, 2)
-    dk_own = after(dk_own, dv_first)
     stay, give = total(total_pairs_kernel, (pair, pair), dk_own, dk1, dk2)
     got = swap(give, 1)
-    joined = call(join_kernel, "join", pair)(stay, got)
+    joined = call(join_kernel, "join", pair)(after(stay, late), got)
     crossed = swap(joined, 2)
+    dv[0] = after(dv[0], joined)
+    grad_value = unpack(unpack_kernel, *dv)
     dq23 = after(dq23, got)
     grad_query = unpack(unpack_turned_kernel, dq0, swap(dq1, 1), dq23, swap(dq23, 1))
     handoff = passed
-    stay = after(stay, grad_query)
     grad_key = unpack(unpack_joined_kernel, stay, got, crossed)
     passed = after(passed, grad_key)
     handoff = unpack(unpack_passed_kernel, passed)

time: 54.8 us -> 53.4 us (0.974)
  waiting for transfers between devices: 21 us -> 19.1 us
    ppermute x14, waiting for transfers between devices: 14.1 us -> 10.2 us  [swap(): return lax.ppermute(array, 'ctx', [(i, i ^ step) for i in range(ctx)])]
    ppermute x8, waiting for transfers between devices: 6.89 us -> 7.98 us  [ring(): return lax.ppermute(array, 'ctx', pairs)]
    ppermute x1, waiting for transfers between devices: 0.01 us -> 0.95 us  [shards(): lax.ppermute(late, 'section', [(s, (s - 1) % sections) for s in range(sec...]
  transfers between devices with their start and end apart: 23 -> 23, of which waited for: 11 -> 12; matrix products, arithmetic and copies ran while one was open for 0% -> 0% of each run, Pallas kernels for 15% -> 15%
where the time goes in v5:
time: 53.4 us; the launch traced here: 53.3 us
  starting transfers between devices  21.9 us (41%)
  waiting for transfers between devices  19.1 us (36%)
  Pallas kernels  11.5 us (22%)
  between operations  0.76 us (1%)
    ppermute x14, starting transfers between devices, swap(): return lax.ppermute(array, 'ctx', [(i, i ^ step) for i in range(ctx)])  13 us
    pallas_call x16, Pallas kernels, run(): pl.pallas_call(kernel, out_shape=jax.tree.map(lambda out: to(out.shape, o...  11.5 us
    ppermute x14, waiting for transfers between devices, swap(): return lax.ppermute(array, 'ctx', [(i, i ^ step) for i in range(ctx)])  10.2 us
    ppermute x8, waiting for transfers between devices, ring(): return lax.ppermute(array, 'ctx', pairs)  7.98 us
    ppermute x8, starting transfers between devices, ring(): return lax.ppermute(array, 'ctx', pairs)  7.53 us
    ppermute x1, starting transfers between devices, shards(): lax.ppermute(late, 'section', [(s, (s - 1) % sections) for s in range(sec...  1.4 us
  transfers between devices with their start and end apart: 23, of which 12 were waited for; matrix products, arithmetic and copies ran while one was open for 0% of the time, Pallas kernels for 15%

profile of v5, /device:TPU:0, one launch (start us, length us, event | category | flops | bytes accessed | tf_op | source)
XLA Modules:
  0.0 53.3 jit_solution(15517287749436462465)
XLA Ops:
  0.6 1.7 %pack.1 = (bf16[3,528,128]{2,1,0:T(8,128)(2,1)S(1)}, bf16[3,928,128]{2,1,0:T(8,128)(2,1)S(1)}, bf16[3,128,128]{2,1,0:T(8,128)(2,1)S(1)}, bf16[3,128,128]{2,1,0:T(8,128)(2,1)S(1)}, bf16[3,400,128]{2,1,0:T(8,128)(2,1)S(1)}) custom-call(bf16[1,128,1536]{2,1,0:T(8,128)(2,1)} %k_hbm.1, bf16[1,128,1536]{2,1,0:T(8,128)(2,1)} %q_hbm.1, bf16[1,128,1536]{2,1,0:T(8,128)(2,1)} %g_hbm.1, ...), custom_call_target="tpu_custom_call" | custom-call | tf_op jit(solution)/shard_map/pack/pallas_call | solution.py:315
  2.3 0.5 collective-permute-start
  2.8 2.6 %collective-permute-start.2 = (bf16[3,128,128]{2,1,0:T(8,128)(2,1)S(1)}, bf16[3,128,128]{2,1,0:T(8,128)(2,1)S(1)}, u32[]{:S(2)}, u32[]{:S(2)}) collective-permute-start(bf16[3,128,128]{2,1,0:T(8,128)(2,1)S(1)} %get-tuple-element.50), channel_id=1, source_target_pairs={{0,2},{1,3},{2,0},{3,1},{4,6},{5,7},{6,4},{7,5},{8,10},{9,11},{10,... | collective-permute-start | bytes 294920 | tf_op jit(solution)/shard_map/ppermute | solution.py:338
  5.5 2.1 %collective-permute-start.7 = (bf16[2,3,128,128]{3,2,1,0:T(8,128)(2,1)S(1)}, bf16[2,3,128,128]{3,2,1,0:T(8,128)(2,1)S(1)}, u32[]{:S(2)}, u32[]{:S(2)}) collective-permute-start(bf16[2,3,128,128]{3,2,1,0:T(8,128)(2,1)S(1)} %get-tuple-element.59), channel_id=1, source_target_pairs={{0,2},{1,3},{2,0},{3,1},{4,6},{5,7},{6,4},{7,5},{8,10},{9,11},{10,... | collective-permute-start | bytes 589832 | tf_op jit(solution)/shard_map/ppermute | solution.py:338
  7.6 1.4 %collective-permute-done.2.two = bf16[3,128,128]{2,1,0:T(8,128)(2,1)S(1)} collective-permute-done((bf16[3,128,128]{2,1,0:T(8,128)(2,1)S(1)}, bf16[3,128,128]{2,1,0:T(8,128)(2,1)S(1)}, u32[]{:S(2)}, u32[]{:S(2)}) %collective-permute-start.2) | collective-permute-done | bytes 98336 | tf_op jit(solution)/shard_map/ppermute | solution.py:338
  9.1 1.6 %collective-permute-done.3.three = bf16[3,128,128]{2,1,0:T(8,128)(2,1)S(1)} collective-permute-done((bf16[3,128,128]{2,1,0:T(8,128)(2,1)S(1)}, bf16[3,128,128]{2,1,0:T(8,128)(2,1)S(1)}, u32[]{:S(2)}, u32[]{:S(2)}) %collective-permute-start.3) | collective-permute-done | bytes 98336 | tf_op jit(solution)/shard_map/ppermute | solution.py:338
  10.7 1.6 %collective-permute-start.4 = (bf16[3,256,128]{2,1,0:T(8,128)(2,1)S(1)}, bf16[3,256,128]{2,1,0:T(8,128)(2,1)S(1)}, u32[]{:S(2)}, u32[]{:S(2)}) collective-permute-start(bf16[3,256,128]{2,1,0:T(8,128)(2,1)S(1)} %get-tuple-element.53), channel_id=1, source_target_pairs={{0,4},{1,0},{2,6},{3,2},{4,8},{5,1},{6,10},{7,3},{8,12},{9,5},{10,... | collective-permute-start | bytes 589832 | tf_op jit(solution)/shard_map/ppermute | solution.py:346
  12.4 1.5 %collective-permute-start.1 = (bf16[2,3,144,128]{3,2,1,0:T(8,128)(2,1)S(1)}, bf16[2,3,144,128]{3,2,1,0:T(8,128)(2,1)S(1)}, u32[]{:S(2)}, u32[]{:S(2)}) collective-permute-start(bf16[2,3,144,128]{3,2,1,0:T(8,128)(2,1)S(1)} %get-tuple-element.49), channel_id=1, source_target_pairs={{0,2},{1,3},{2,0},{3,1},{4,6},{5,7},{6,4},{7,5},{8,10},{9,11},{10,... | collective-permute-start | bytes 663560 | tf_op jit(solution)/shard_map/ppermute | solution.py:338
  14.4 1.0 %collective-permute-done.7.pair = bf16[2,3,128,128]{3,2,1,0:T(8,128)(2,1)S(1)} collective-permute-done((bf16[2,3,128,128]{3,2,1,0:T(8,128)(2,1)S(1)}, bf16[2,3,128,128]{3,2,1,0:T(8,128)(2,1)S(1)}, u32[]{:S(2)}, u32[]{:S(2)}) %collective-permute-start.7) | collective-permute-done | bytes 196640 | tf_op jit(solution)/shard_map/ppermute | solution.py:338
  15.5 2.0 %collective-permute-start.8 = (bf16[3,256,128]{2,1,0:T(8,128)(2,1)S(1)}, bf16[3,256,128]{2,1,0:T(8,128)(2,1)S(1)}, u32[]{:S(2)}, u32[]{:S(2)}) collective-permute-start(bf16[3,256,128]{2,1,0:T(8,128)(2,1)S(1)} %get-tuple-element.60), channel_id=1, source_target_pairs={{0,4},{1,0},{2,6},{3,2},{4,8},{5,1},{6,10},{7,3},{8,12},{9,5},{10,... | collective-permute-start | bytes 589832 | tf_op jit(solution)/shard_map/ppermute | solution.py:346
  17.5 4.4 %collective-permute-done.5.halo2 = bf16[3,256,128]{2,1,0:T(8,128)(2,1)S(1)} collective-permute-done((bf16[3,256,128]{2,1,0:T(8,128)(2,1)S(1)}, bf16[3,256,128]{2,1,0:T(8,128)(2,1)S(1)}, u32[]{:S(2)}, u32[]{:S(2)}) %collective-permute-start.5) | collective-permute-done | bytes 196640 | tf_op jit(solution)/shard_map/ppermute | solution.py:346
  21.9 1.8 %probs.1 = (bf16[3,1024,512]{2,1,0:T(8,128)(2,1)S(1)}, bf16[3,1024,128]{2,1,0:T(8,128)(2,1)S(1)}, bf16[3,512,128]{2,1,0:T(8,128)(2,1)S(1)}) custom-call(bf16[3,528,128]{2,1,0:T(8,128)(2,1)S(1)} %get-tuple-element.46.own, bf16[3,928,128]{2,1,0:T(8,128)(2,1)S(1)} %collective-permute-done.side, bf16[2,3,144,128]{3,2,1,0:T(8,128)(2,1)S(1)} %collective-permute-done.1.crossed, ...), custom_call_target="tpu_custom_call" | custom-call | tf_op jit(solution)/shard_map/probs/pallas_call | solution.py:315
  24.1 0.8 %values.1 = (bf16[3,512,128]{2,1,0:T(8,128)(2,1)S(1)}, f32[3,512,128]{2,1,0:T(8,128)S(1)}, bf16[3,256,128]{2,1,0:T(8,128)(2,1)S(1)}, bf16[3,256,128]{2,1,0:T(8,128)(2,1)S(1)}) custom-call(bf16[3,1024,512]{2,1,0:T(8,128)(2,1)S(1)} %get-tuple-element.55.probs, bf16[3,528,128]{2,1,0:T(8,128)(2,1)S(1)} %get-tuple-element.46.own, ...), custom_call_target="tpu_custom_call" | custom-call | tf_op jit(solution)/shard_map/values/pallas_call | solution.py:315
  24.9 1.8 %collective-permute-start.10 = (bf16[3,256,128]{2,1,0:T(8,128)(2,1)S(1)}, bf16[3,256,128]{2,1,0:T(8,128)(2,1)S(1)}, u32[]{:S(2)}, u32[]{:S(2)}) collective-permute-start(bf16[3,256,128]{2,1,0:T(8,128)(2,1)S(1)} %get-tuple-element.69), channel_id=1, source_target_pairs={{0,4},{1,0},{2,6},{3,2},{4,8},{5,1},{6,10},{7,3},{8,12},{9,5},{10,... | collective-permute-start | bytes 589832 | tf_op jit(solution)/shard_map/ppermute | solution.py:346
  26.7 2.5 %scores.1 = (bf16[3,1024,512]{2,1,0:T(8,128)(2,1)S(1)}, f32[3,512,128]{2,1,0:T(8,128)S(1)}, bf16[3,256,128]{2,1,0:T(8,128)(2,1)S(1)}, bf16[3,256,128]{2,1,0:T(8,128)(2,1)S(1)}) custom-call(bf16[3,1024,512]{2,1,0:T(8,128)(2,1)S(1)} %get-tuple-element.55.probs, bf16[3,512,128]{2,1,0:T(8,128)(2,1)S(1)} %get-tuple-element.56.qs, ...), custom_call_target="tpu_custom_call" | custom-call | tf_op jit(solution)/shard_map/scores/pallas_call | solution.py:315
  29.2 2.0 %collective-permute-start.14 = (bf16[3,256,128]{2,1,0:T(8,128)(2,1)S(1)}, bf16[3,256,128]{2,1,0:T(8,128)(2,1)S(1)}, u32[]{:S(2)}, u32[]{:S(2)}) collective-permute-start(bf16[3,256,128]{2,1,0:T(8,128)(2,1)S(1)} %get-tuple-element.77), channel_id=1, source_target_pairs={{0,4},{1,0},{2,6},{3,2},{4,8},{5,1},{6,10},{7,3},{8,12},{9,5},{10,... | collective-permute-start | bytes 589832 | tf_op jit(solution)/shard_map/ppermute | solution.py:346
  31.3 2.5 %collective-permute-done.11.ring2 = bf16[3,256,128]{2,1,0:T(8,128)(2,1)S(1)} collective-permute-done((bf16[3,256,128]{2,1,0:T(8,128)(2,1)S(1)}, bf16[3,256,128]{2,1,0:T(8,128)(2,1)S(1)}, u32[]{:S(2)}, u32[]{:S(2)}) %collective-permute-start.11) | collective-permute-done | bytes 196640 | tf_op jit(solution)/shard_map/ppermute | solution.py:346
  34.0 1.4 %collective-permute-start.19 = (bf16[3,128,128]{2,1,0:T(8,128)(2,1)S(1)}, bf16[3,128,128]{2,1,0:T(8,128)(2,1)S(1)}, u32[]{:S(2)}, u32[]{:S(2)}) collective-permute-start(bf16[3,128,128]{2,1,0:T(8,128)(2,1)S(1)} %get-tuple-element.83), channel_id=1, source_target_pairs={{0,2},{1,3},{2,0},{3,1},{4,6},{5,7},{6,4},{7,5},{8,10},{9,11},{10,... | collective-permute-start | bytes 294920 | tf_op jit(solution)/shard_map/ppermute | solution.py:338
  35.9 1.1 %collective-permute-done.15.ring2 = bf16[3,256,128]{2,1,0:T(8,128)(2,1)S(1)} collective-permute-done((bf16[3,256,128]{2,1,0:T(8,128)(2,1)S(1)}, bf16[3,256,128]{2,1,0:T(8,128)(2,1)S(1)}, u32[]{:S(2)}, u32[]{:S(2)}) %collective-permute-start.15) | collective-permute-done | bytes 196640 | tf_op jit(solution)/shard_map/ppermute | solution.py:346
  37.1 0.8 %queries.1 = (bf16[3,128,128]{2,1,0:T(8,128)(2,1)S(1)}, bf16[3,128,128]{2,1,0:T(8,128)(2,1)S(1)}, bf16[2,3,128,128]{3,2,1,0:T(8,128)(2,1)S(1)}) custom-call(bf16[3,1024,512]{2,1,0:T(8,128)(2,1)S(1)} %get-tuple-element.72.ss, bf16[3,1024,128]{2,1,0:T(8,128)(2,1)S(1)} %get-tuple-element.73.ks), custom_call_target="tpu_custom_call" | custom-call | tf_op jit(solution)/shard_map/queries/pallas_call | solution.py:315
  37.9 1.6 %collective-permute-start.13 = (bf16[2,3,128,128]{3,2,1,0:T(8,128)(2,1)S(1)}, bf16[2,3,128,128]{3,2,1,0:T(8,128)(2,1)S(1)}, u32[]{:S(2)}, u32[]{:S(2)}) collective-permute-start(bf16[2,3,128,128]{3,2,1,0:T(8,128)(2,1)S(1)} %get-tuple-element.76), channel_id=1, source_target_pairs={{0,2},{1,3},{2,0},{3,1},{4,6},{5,7},{6,4},{7,5},{8,10},{9,11},{10,... | collective-permute-start | bytes 589832 | tf_op jit(solution)/shard_map/ppermute | solution.py:338
  39.7 1.2 %collective-permute-done.20.in3 = bf16[3,128,128]{2,1,0:T(8,128)(2,1)S(1)} collective-permute-done((bf16[3,128,128]{2,1,0:T(8,128)(2,1)S(1)}, bf16[3,128,128]{2,1,0:T(8,128)(2,1)S(1)}, u32[]{:S(2)}, u32[]{:S(2)}) %collective-permute-start.20) | collective-permute-done | bytes 98336 | tf_op jit(solution)/shard_map/ppermute | solution.py:338
  40.9 1.4 %collective-permute-start.22 = (bf16[4,3,128,128]{3,2,1,0:T(8,128)(2,1)S(1)}, bf16[4,3,128,128]{3,2,1,0:T(8,128)(2,1)S(1)}, u32[]{:S(2)}, u32[]{:S(2)}) collective-permute-start(bf16[4,3,128,128]{3,2,1,0:T(8,128)(2,1)S(1)} %gather.1), channel_id=1, source_target_pairs={{0,16},{16,0},{1,17},{17,1},{2,18},{18,2},{3,19},{19,3},{4,20},{20... | collective-permute-start | bytes 1179656 | tf_op jit(solution)/shard_map/ppermute | solution.py:411
  42.3 1.6 %collective-permute-start.21 = (bf16[2,3,128,128]{3,2,1,0:T(8,128)(2,1)S(1)}, bf16[2,3,128,128]{3,2,1,0:T(8,128)(2,1)S(1)}, u32[]{:S(2)}, u32[]{:S(2)}) collective-permute-start(bf16[2,3,128,128]{3,2,1,0:T(8,128)(2,1)S(1)} %join.1), channel_id=1, source_target_pairs={{0,2},{1,3},{2,0},{3,1},{4,6},{5,7},{6,4},{7,5},{8,10},{9,11},{10,... | collective-permute-start | bytes 589832 | tf_op jit(solution)/shard_map/ppermute | solution.py:338
  43.9 1.9 %collective-permute-done.13.crossed = bf16[2,3,128,128]{3,2,1,0:T(8,128)(2,1)S(1)} collective-permute-done((bf16[2,3,128,128]{3,2,1,0:T(8,128)(2,1)S(1)}, bf16[2,3,128,128]{3,2,1,0:T(8,128)(2,1)S(1)}, u32[]{:S(2)}, u32[]{:S(2)}) %collective-permute-start.13) | collective-permute-done | bytes 196640 | tf_op jit(solution)/shard_map/ppermute | solution.py:338
  45.8 0.5 collective-permute-start.12
  46.3 0.8 %unpack.6 = bf16[1,128,1536]{2,1,0:T(8,128)(2,1)} custom-call(bf16[3,128,128]{2,1,0:T(8,128)(2,1)S(1)} %get-tuple-element.86.in0, bf16[3,128,128]{2,1,0:T(8,128)(2,1)S(1)} %collective-permute-done.18.in1, bf16[3,128,128]{2,1,0:T(8,128)(2,1)S(1)} %collective-permute-done.19.in2, bf16[3,128,128]{2,1,0:T(8,128)(2,1)S(1)} %collective-permute-done.20.in3), custom_call_target="tpu_custom_call" | custom-call | tf_op jit(solution)/shard_map/unpack/pallas_call | solution.py:315
  47.1 2.6 %collective-permute-done.21.crossed = bf16[2,3,128,128]{3,2,1,0:T(8,128)(2,1)S(1)} collective-permute-done((bf16[2,3,128,128]{3,2,1,0:T(8,128)(2,1)S(1)}, bf16[2,3,128,128]{3,2,1,0:T(8,128)(2,1)S(1)}, u32[]{:S(2)}, u32[]{:S(2)}) %collective-permute-start.21) | collective-permute-done | bytes 196640 | tf_op jit(solution)/shard_map/ppermute | solution.py:338
  49.7 0.8 %unpack.5 = bf16[1,128,1536]{2,1,0:T(8,128)(2,1)} custom-call(bf16[2,3,128,128]{3,2,1,0:T(8,128)(2,1)S(1)} %get-tuple-element.85.stay, bf16[2,3,128,128]{3,2,1,0:T(8,128)(2,1)S(1)} %collective-permute-done.16.got, bf16[2,3,128,128]{3,2,1,0:T(8,128)(2,1)S(1)} %collective-permute-done.21.crossed), custom_call_target="tpu_custom_call" | custom-call | tf_op jit(solution)/shard_map/unpack/pallas_call | solution.py:315
  50.6 0.9 %unpack.4 = bf16[1,128,1536]{2,1,0:T(8,128)(2,1)} custom-call(bf16[3,128,128]{2,1,0:T(8,128)(2,1)S(1)} %get-tuple-element.74.dq0, bf16[3,128,128]{2,1,0:T(8,128)(2,1)S(1)} %collective-permute-done.12.dq1, bf16[2,3,128,128]{3,2,1,0:T(8,128)(2,1)S(1)} %collective-permute-done.13.crossed, bf16[2,3,128,128]{3,2,1,0:T(8,128)(2,1)S(1)} %collective-permute-done.17.turned), custom_call_target="tpu_custom_call" | custom-call | tf_op jit(solution)/shard_map/unpack/pallas_call | solution.py:315
  51.5 0.9 %collective-permute-done.22.groups = bf16[4,3,128,128]{3,2,1,0:T(8,128)(2,1)S(1)} collective-permute-done((bf16[4,3,128,128]{3,2,1,0:T(8,128)(2,1)S(1)}, bf16[4,3,128,128]{3,2,1,0:T(8,128)(2,1)S(1)}, u32[]{:S(2)}, u32[]{:S(2)}) %collective-permute-start.22) | collective-permute-done | bytes 393248 | tf_op jit(solution)/shard_map/ppermute | solution.py:411
  52.4 0.9 %unpack.7 = bf16[1,128,1536]{2,1,0:T(8,128)(2,1)} custom-call(bf16[4,3,128,128]{3,2,1,0:T(8,128)(2,1)S(1)} %collective-permute-done.22.groups), custom_call_target="tpu_custom_call" | custom-call | tf_op jit(solution)/shard_map/unpack/pallas_call | solution.py:315
  (30 shorter events, 2.2 us)
Async XLA Ops:
  2.3 3.2 %collective-permute-start = (bf16[3,928,128]{2,1,0:T(8,128)(2,1)S(1)}, bf16[3,928,128]{2,1,0:T(8,128)(2,1)S(1)}, u32[]{:S(2)}, u32[]{:S(2)}) collective-permute-start(bf16[3,928,128]{2,1,0:T(8,128)(2,1)S(1)} %get-tuple-element.47), channel_id=1, source_target_pairs={{0,1},{1,0},{2,3},{3,2},{4,5},{5,4},{6,7},{7,6},{8,9},{9,8},{10,11... | collective-permute-start | bytes 2138120 | tf_op jit(solution)/shard_map/ppermute | solution.py:338
  2.8 6.2 %collective-permute-start.2 = (bf16[3,128,128]{2,1,0:T(8,128)(2,1)S(1)}, bf16[3,128,128]{2,1,0:T(8,128)(2,1)S(1)}, u32[]{:S(2)}, u32[]{:S(2)}) collective-permute-start(bf16[3,128,128]{2,1,0:T(8,128)(2,1)S(1)} %get-tuple-element.50), channel_id=1, source_target_pairs={{0,2},{1,3},{2,0},{3,1},{4,6},{5,7},{6,4},{7,5},{8,10},{9,11},{10,... | collective-permute-start | bytes 294920 | tf_op jit(solution)/shard_map/ppermute | solution.py:338
  5.4 5.2 %collective-permute-start.3 = (bf16[3,128,128]{2,1,0:T(8,128)(2,1)S(1)}, bf16[3,128,128]{2,1,0:T(8,128)(2,1)S(1)}, u32[]{:S(2)}, u32[]{:S(2)}) collective-permute-start(bf16[3,128,128]{2,1,0:T(8,128)(2,1)S(1)} %get-tuple-element.51), channel_id=1, source_target_pairs={{0,3},{1,2},{2,1},{3,0},{4,7},{5,6},{6,5},{7,4},{8,11},{9,10},{10,... | collective-permute-start | bytes 294920 | tf_op jit(solution)/shard_map/ppermute | solution.py:338
  5.5 9.8 %collective-permute-start.7 = (bf16[2,3,128,128]{3,2,1,0:T(8,128)(2,1)S(1)}, bf16[2,3,128,128]{3,2,1,0:T(8,128)(2,1)S(1)}, u32[]{:S(2)}, u32[]{:S(2)}) collective-permute-start(bf16[2,3,128,128]{3,2,1,0:T(8,128)(2,1)S(1)} %get-tuple-element.59), channel_id=1, source_target_pairs={{0,2},{1,3},{2,0},{3,1},{4,6},{5,7},{6,4},{7,5},{8,10},{9,11},{10,... | collective-permute-start | bytes 589832 | tf_op jit(solution)/shard_map/ppermute | solution.py:338
  10.7 6.8 %collective-permute-start.4 = (bf16[3,256,128]{2,1,0:T(8,128)(2,1)S(1)}, bf16[3,256,128]{2,1,0:T(8,128)(2,1)S(1)}, u32[]{:S(2)}, u32[]{:S(2)}) collective-permute-start(bf16[3,256,128]{2,1,0:T(8,128)(2,1)S(1)} %get-tuple-element.53), channel_id=1, source_target_pairs={{0,4},{1,0},{2,6},{3,2},{4,8},{5,1},{6,10},{7,3},{8,12},{9,5},{10,... | collective-permute-start | bytes 589832 | tf_op jit(solution)/shard_map/ppermute | solution.py:346
  12.4 9.5 %collective-permute-start.1 = (bf16[2,3,144,128]{3,2,1,0:T(8,128)(2,1)S(1)}, bf16[2,3,144,128]{3,2,1,0:T(8,128)(2,1)S(1)}, u32[]{:S(2)}, u32[]{:S(2)}) collective-permute-start(bf16[2,3,144,128]{3,2,1,0:T(8,128)(2,1)S(1)} %get-tuple-element.49), channel_id=1, source_target_pairs={{0,2},{1,3},{2,0},{3,1},{4,6},{5,7},{6,4},{7,5},{8,10},{9,11},{10,... | collective-permute-start | bytes 663560 | tf_op jit(solution)/shard_map/ppermute | solution.py:338
  13.9 10.2 %collective-permute-start.6 = (bf16[2,3,128,128]{3,2,1,0:T(8,128)(2,1)S(1)}, bf16[2,3,128,128]{3,2,1,0:T(8,128)(2,1)S(1)}, u32[]{:S(2)}, u32[]{:S(2)}) collective-permute-start(bf16[2,3,128,128]{3,2,1,0:T(8,128)(2,1)S(1)} %get-tuple-element.58), channel_id=1, source_target_pairs={{0,2},{1,3},{2,0},{3,1},{4,6},{5,7},{6,4},{7,5},{8,10},{9,11},{10,... | collective-permute-start | bytes 589832 | tf_op jit(solution)/shard_map/ppermute | solution.py:338
  14.4 7.5 %collective-permute-start.5 = (bf16[3,256,128]{2,1,0:T(8,128)(2,1)S(1)}, bf16[3,256,128]{2,1,0:T(8,128)(2,1)S(1)}, u32[]{:S(2)}, u32[]{:S(2)}) collective-permute-start(bf16[3,256,128]{2,1,0:T(8,128)(2,1)S(1)} %get-tuple-element.54), channel_id=1, source_target_pairs={{0,1},{1,5},{2,3},{3,7},{4,0},{5,9},{6,2},{7,11},{8,4},{9,13},{10,... | collective-permute-start | bytes 589832 | tf_op jit(solution)/shard_map/ppermute | solution.py:346
  15.5 8.6 %collective-permute-start.8 = (bf16[3,256,128]{2,1,0:T(8,128)(2,1)S(1)}, bf16[3,256,128]{2,1,0:T(8,128)(2,1)S(1)}, u32[]{:S(2)}, u32[]{:S(2)}) collective-permute-start(bf16[3,256,128]{2,1,0:T(8,128)(2,1)S(1)} %get-tuple-element.60), channel_id=1, source_target_pairs={{0,4},{1,0},{2,6},{3,2},{4,8},{5,1},{6,10},{7,3},{8,12},{9,5},{10,... | collective-permute-start | bytes 589832 | tf_op jit(solution)/shard_map/ppermute | solution.py:346
  17.5 6.6 %collective-permute-start.9 = (bf16[3,256,128]{2,1,0:T(8,128)(2,1)S(1)}, bf16[3,256,128]{2,1,0:T(8,128)(2,1)S(1)}, u32[]{:S(2)}, u32[]{:S(2)}) collective-permute-start(bf16[3,256,128]{2,1,0:T(8,128)(2,1)S(1)} %get-tuple-element.61), channel_id=1, source_target_pairs={{0,1},{1,5},{2,3},{3,7},{4,0},{5,9},{6,2},{7,11},{8,4},{9,13},{10,... | collective-permute-start | bytes 589832 | tf_op jit(solution)/shard_map/ppermute | solution.py:346
  24.9 6.4 %collective-permute-start.10 = (bf16[3,256,128]{2,1,0:T(8,128)(2,1)S(1)}, bf16[3,256,128]{2,1,0:T(8,128)(2,1)S(1)}, u32[]{:S(2)}, u32[]{:S(2)}) collective-permute-start(bf16[3,256,128]{2,1,0:T(8,128)(2,1)S(1)} %get-tuple-element.69), channel_id=1, source_target_pairs={{0,4},{1,0},{2,6},{3,2},{4,8},{5,1},{6,10},{7,3},{8,12},{9,5},{10,... | collective-permute-start | bytes 589832 | tf_op jit(solution)/shard_map/ppermute | solution.py:346
  26.7 7.0 %collective-permute-start.11 = (bf16[3,256,128]{2,1,0:T(8,128)(2,1)S(1)}, bf16[3,256,128]{2,1,0:T(8,128)(2,1)S(1)}, u32[]{:S(2)}, u32[]{:S(2)}) collective-permute-start(bf16[3,256,128]{2,1,0:T(8,128)(2,1)S(1)} %get-tuple-element.70), channel_id=1, source_target_pairs={{0,1},{1,5},{2,3},{3,7},{4,0},{5,9},{6,2},{7,11},{8,4},{9,13},{10,... | collective-permute-start | bytes 589832 | tf_op jit(solution)/shard_map/ppermute | solution.py:346
  29.2 6.6 %collective-permute-start.14 = (bf16[3,256,128]{2,1,0:T(8,128)(2,1)S(1)}, bf16[3,256,128]{2,1,0:T(8,128)(2,1)S(1)}, u32[]{:S(2)}, u32[]{:S(2)}) collective-permute-start(bf16[3,256,128]{2,1,0:T(8,128)(2,1)S(1)} %get-tuple-element.77), channel_id=1, source_target_pairs={{0,4},{1,0},{2,6},{3,2},{4,8},{5,1},{6,10},{7,3},{8,12},{9,5},{10,... | collective-permute-start | bytes 589832 | tf_op jit(solution)/shard_map/ppermute | solution.py:346
  31.3 5.7 %collective-permute-start.15 = (bf16[3,256,128]{2,1,0:T(8,128)(2,1)S(1)}, bf16[3,256,128]{2,1,0:T(8,128)(2,1)S(1)}, u32[]{:S(2)}, u32[]{:S(2)}) collective-permute-start(bf16[3,256,128]{2,1,0:T(8,128)(2,1)S(1)} %get-tuple-element.78), channel_id=1, source_target_pairs={{0,1},{1,5},{2,3},{3,7},{4,0},{5,9},{6,2},{7,11},{8,4},{9,13},{10,... | collective-permute-start | bytes 589832 | tf_op jit(solution)/shard_map/ppermute | solution.py:346
  33.9 5.6 %collective-permute-start.18 = (bf16[3,128,128]{2,1,0:T(8,128)(2,1)S(1)}, bf16[3,128,128]{2,1,0:T(8,128)(2,1)S(1)}, u32[]{:S(2)}, u32[]{:S(2)}) collective-permute-start(bf16[3,128,128]{2,1,0:T(8,128)(2,1)S(1)} %get-tuple-element.82), channel_id=1, source_target_pairs={{0,1},{1,0},{2,3},{3,2},{4,5},{5,4},{6,7},{7,6},{8,9},{9,8},{10,11... | collective-permute-start | bytes 294920 | tf_op jit(solution)/shard_map/ppermute | solution.py:338
  34.0 5.7 %collective-permute-start.19 = (bf16[3,128,128]{2,1,0:T(8,128)(2,1)S(1)}, bf16[3,128,128]{2,1,0:T(8,128)(2,1)S(1)}, u32[]{:S(2)}, u32[]{:S(2)}) collective-permute-start(bf16[3,128,128]{2,1,0:T(8,128)(2,1)S(1)} %get-tuple-element.83), channel_id=1, source_target_pairs={{0,2},{1,3},{2,0},{3,1},{4,6},{5,7},{6,4},{7,5},{8,10},{9,11},{10,... | collective-permute-start | bytes 294920 | tf_op jit(solution)/shard_map/ppermute | solution.py:338
  35.4 5.4 %collective-permute-start.20 = (bf16[3,128,128]{2,1,0:T(8,128)(2,1)S(1)}, bf16[3,128,128]{2,1,0:T(8,128)(2,1)S(1)}, u32[]{:S(2)}, u32[]{:S(2)}) collective-permute-start(bf16[3,128,128]{2,1,0:T(8,128)(2,1)S(1)} %get-tuple-element.84), channel_id=1, source_target_pairs={{0,3},{1,2},{2,1},{3,0},{4,7},{5,6},{6,5},{7,4},{8,11},{9,10},{10,... | collective-permute-start | bytes 294920 | tf_op jit(solution)/shard_map/ppermute | solution.py:338
  37.1 5.2 %collective-permute-start.16 = (bf16[2,3,128,128]{3,2,1,0:T(8,128)(2,1)S(1)}, bf16[2,3,128,128]{3,2,1,0:T(8,128)(2,1)S(1)}, u32[]{:S(2)}, u32[]{:S(2)}) collective-permute-start(bf16[2,3,128,128]{3,2,1,0:T(8,128)(2,1)S(1)} %get-tuple-element.79), channel_id=1, source_target_pairs={{0,1},{1,0},{2,3},{3,2},{4,5},{5,4},{6,7},{7,6},{8,9},{9,8},{10,11... | collective-permute-start | bytes 589832 | tf_op jit(solution)/shard_map/ppermute | solution.py:338
  37.9 7.8 %collective-permute-start.13 = (bf16[2,3,128,128]{3,2,1,0:T(8,128)(2,1)S(1)}, bf16[2,3,128,128]{3,2,1,0:T(8,128)(2,1)S(1)}, u32[]{:S(2)}, u32[]{:S(2)}) collective-permute-start(bf16[2,3,128,128]{3,2,1,0:T(8,128)(2,1)S(1)} %get-tuple-element.76), channel_id=1, source_target_pairs={{0,2},{1,3},{2,0},{3,1},{4,6},{5,7},{6,4},{7,5},{8,10},{9,11},{10,... | collective-permute-start | bytes 589832 | tf_op jit(solution)/shard_map/ppermute | solution.py:338
  40.9 11.5 %collective-permute-start.22 = (bf16[4,3,128,128]{3,2,1,0:T(8,128)(2,1)S(1)}, bf16[4,3,128,128]{3,2,1,0:T(8,128)(2,1)S(1)}, u32[]{:S(2)}, u32[]{:S(2)}) collective-permute-start(bf16[4,3,128,128]{3,2,1,0:T(8,128)(2,1)S(1)} %gather.1), channel_id=1, source_target_pairs={{0,16},{16,0},{1,17},{17,1},{2,18},{18,2},{3,19},{19,3},{4,20},{20... | collective-permute-start | bytes 1179656 | tf_op jit(solution)/shard_map/ppermute | solution.py:411
  42.3 7.4 %collective-permute-start.21 = (bf16[2,3,128,128]{3,2,1,0:T(8,128)(2,1)S(1)}, bf16[2,3,128,128]{3,2,1,0:T(8,128)(2,1)S(1)}, u32[]{:S(2)}, u32[]{:S(2)}) collective-permute-start(bf16[2,3,128,128]{3,2,1,0:T(8,128)(2,1)S(1)} %join.1), channel_id=1, source_target_pairs={{0,2},{1,3},{2,0},{3,1},{4,6},{5,7},{6,4},{7,5},{8,10},{9,11},{10,... | collective-permute-start | bytes 589832 | tf_op jit(solution)/shard_map/ppermute | solution.py:338
  45.8 4.8 %collective-permute-start.17 = (bf16[2,3,128,128]{3,2,1,0:T(8,128)(2,1)S(1)}, bf16[2,3,128,128]{3,2,1,0:T(8,128)(2,1)S(1)}, u32[]{:S(2)}, u32[]{:S(2)}) collective-permute-start(bf16[2,3,128,128]{3,2,1,0:T(8,128)(2,1)S(1)} %collective-permute-done.13.crossed), channel_id=1, source_target_pairs={{0,1},{1,0},{2,3},{3,2},{4,5},{5,4},{6,7},{7,6},{8,9},{9,8},{10,11... | collective-permute-start | bytes 589832 | tf_op jit(solution)/shard_map/ppermute | solution.py:338
  45.8 4.8 %collective-permute-start.12 = (bf16[3,128,128]{2,1,0:T(8,128)(2,1)S(1)}, bf16[3,128,128]{2,1,0:T(8,128)(2,1)S(1)}, u32[]{:S(2)}, u32[]{:S(2)}) collective-permute-start(bf16[3,128,128]{2,1,0:T(8,128)(2,1)S(1)} %get-tuple-element.75), channel_id=1, source_target_pairs={{0,1},{1,0},{2,3},{3,2},{4,5},{5,4},{6,7},{7,6},{8,9},{9,8},{10,11... | collective-permute-start | bytes 294920 | tf_op jit(solution)/shard_map/ppermute | solution.py:338

commit v6 on v5

--- a/solution.py
+++ b/solution.py
@@ -263,21 +263,22 @@
         groups[jnp.bitwise_xor(me, step)] = source[...]
 
 
-def send_rows(out, out_hbm, sems):
+def write_out(parts, out, out_hbm, sems, wanted=None):
     copies = pieces(out, out_hbm, sems)
-    for copy in copies:
+    count = BLK // len(copies)
+    for n, copy in enumerate(copies):
+        rows = slice(n * count, (n + 1) * count)
+        for group, source in parts:
+            for h in range(LOCAL):
+                value = source[h, rows]
+                if wanted is not None:
+                    value = jnp.where(wanted, value, jnp.zeros_like(value))
+                out[0, rows, head_columns(group, h)] = value
         copy.start()
     for copy in copies:
         copy.wait()
 
 
-def write_out(parts, out, out_hbm, sems):
-    for group, source in parts:
-        for h in range(LOCAL):
-            out[0, :, head_columns(group, h)] = source[h]
-    send_rows(out, out_hbm, sems)
-
-
 def unpack_kernel(in0, in1, in2, in3, out_hbm, out, sems):
     me = member()
     sources = (in0, in1, in2, in3)
@@ -294,12 +295,9 @@
 
 
 def unpack_passed_kernel(groups, out_hbm, out, sems):
-    last = lax.axis_index("section") == lax.axis_size("section") - 1
-    for group in range(TEAM):
-        for h in range(LOCAL):
-            source = groups[group, h]
-            out[0, :, head_columns(group, h)] = jnp.where(last, jnp.zeros_like(source), source)
-    send_rows(out, out_hbm, sems)
+    wanted = lax.axis_index("section") < lax.axis_size("section") - 1
+    parts = [(group, groups.at[group]) for group in range(TEAM)]
+    write_out(parts, out, out_hbm, sems, wanted)
 
 
 def struct(*shape, dtype=bf16):
@@ -411,7 +409,8 @@
     passed = lax.ppermute(late, "section", [(s, (s - 1) % sections) for s in range(sections)])
     dq0, dq1, dq23 = call(
         queries_kernel, "queries", (part, part, pair), [pltpu.VMEM((TEAM * BLK, DH), bf16)]
-    )(after(ss, dv_first), ks)
+    )(ss, ks)
+    dq23 = after(dq23, dv_first)
     dq23 = swap(dq23, 2)
     stay, give = total(total_pairs_kernel, (pair, pair), dk_own, dk1, dk2)
     got = swap(give, 1)
@@ -421,9 +420,7 @@
     grad_value = unpack(unpack_kernel, *dv)
     dq23 = after(dq23, got)
     grad_query = unpack(unpack_turned_kernel, dq0, swap(dq1, 1), dq23, swap(dq23, 1))
-    handoff = passed
     grad_key = unpack(unpack_joined_kernel, stay, got, crossed)
-    passed = after(passed, grad_key)
     handoff = unpack(unpack_passed_kernel, passed)
     return (grad_query, grad_key, grad_value, handoff)
 

time: 53.4 us -> 53.7 us (level)
    ppermute x14, waiting for transfers between devices: 10.2 us -> 11 us  [swap(): return lax.ppermute(array, 'ctx', [(i, i ^ step) for i in range(ctx)])]
    ppermute x8, waiting for transfers between devices: 7.98 us -> 7.18 us  [ring(): return lax.ppermute(array, 'ctx', pairs)]
where the time goes in v6:
time: 53.7 us; the launch traced here: 53.5 us
  starting transfers between devices  21.9 us (41%)
  waiting for transfers between devices  19.6 us (36%)
  Pallas kernels  11.3 us (21%)
  between operations  0.76 us (1%)
    ppermute x14, starting transfers between devices, swap(): return lax.ppermute(array, 'ctx', [(i, i ^ step) for i in range(ctx)])  13 us
    pallas_call x16, Pallas kernels, run(): pl.pallas_call(kernel, out_shape=jax.tree.map(lambda out: to(out.shape, o...  11.3 us
    ppermute x14, waiting for transfers between devices, swap(): return lax.ppermute(array, 'ctx', [(i, i ^ step) for i in range(ctx)])  11 us
    ppermute x8, starting transfers between devices, ring(): return lax.ppermute(array, 'ctx', pairs)  7.53 us
    ppermute x8, waiting for transfers between devices, ring(): return lax.ppermute(array, 'ctx', pairs)  7.18 us
    ppermute x1, starting transfers between devices, shards(): lax.ppermute(late, 'section', [(s, (s - 1) % sections) for s in range(sec...  1.4 us
    ppermute x1, waiting for transfers between devices, shards(): lax.ppermute(late, 'section', [(s, (s - 1) % sections) for s in range(sec...  1.33 us
  transfers between devices with their start and end apart: 23, of which 12 were waited for; matrix products, arithmetic and copies ran while one was open for 0% of the time, Pallas kernels for 15%

profile of v6, /device:TPU:0, one launch (start us, length us, event | category | flops | bytes accessed | tf_op | source)
XLA Modules:
  0.0 53.5 jit_solution(5760043629835841089)
XLA Ops:
  0.6 1.7 %pack.1 = (bf16[3,528,128]{2,1,0:T(8,128)(2,1)S(1)}, bf16[3,928,128]{2,1,0:T(8,128)(2,1)S(1)}, bf16[3,128,128]{2,1,0:T(8,128)(2,1)S(1)}, bf16[3,128,128]{2,1,0:T(8,128)(2,1)S(1)}, bf16[3,400,128]{2,1,0:T(8,128)(2,1)S(1)}) custom-call(bf16[1,128,1536]{2,1,0:T(8,128)(2,1)} %k_hbm.1, bf16[1,128,1536]{2,1,0:T(8,128)(2,1)} %q_hbm.1, bf16[1,128,1536]{2,1,0:T(8,128)(2,1)} %g_hbm.1, ...), custom_call_target="tpu_custom_call" | custom-call | tf_op jit(solution)/shard_map/pack/pallas_call | solution.py:313
  2.3 0.5 collective-permute-start
  2.8 2.6 %collective-permute-start.2 = (bf16[3,128,128]{2,1,0:T(8,128)(2,1)S(1)}, bf16[3,128,128]{2,1,0:T(8,128)(2,1)S(1)}, u32[]{:S(2)}, u32[]{:S(2)}) collective-permute-start(bf16[3,128,128]{2,1,0:T(8,128)(2,1)S(1)} %get-tuple-element.49), channel_id=1, source_target_pairs={{0,2},{1,3},{2,0},{3,1},{4,6},{5,7},{6,4},{7,5},{8,10},{9,11},{10,... | collective-permute-start | bytes 294920 | tf_op jit(solution)/shard_map/ppermute | solution.py:336
  5.5 2.1 %collective-permute-start.7 = (bf16[2,3,128,128]{3,2,1,0:T(8,128)(2,1)S(1)}, bf16[2,3,128,128]{3,2,1,0:T(8,128)(2,1)S(1)}, u32[]{:S(2)}, u32[]{:S(2)}) collective-permute-start(bf16[2,3,128,128]{3,2,1,0:T(8,128)(2,1)S(1)} %get-tuple-element.58), channel_id=1, source_target_pairs={{0,2},{1,3},{2,0},{3,1},{4,6},{5,7},{6,4},{7,5},{8,10},{9,11},{10,... | collective-permute-start | bytes 589832 | tf_op jit(solution)/shard_map/ppermute | solution.py:336
  7.6 1.4 %collective-permute-done.2.two = bf16[3,128,128]{2,1,0:T(8,128)(2,1)S(1)} collective-permute-done((bf16[3,128,128]{2,1,0:T(8,128)(2,1)S(1)}, bf16[3,128,128]{2,1,0:T(8,128)(2,1)S(1)}, u32[]{:S(2)}, u32[]{:S(2)}) %collective-permute-start.2) | collective-permute-done | bytes 98336 | tf_op jit(solution)/shard_map/ppermute | solution.py:336
  9.1 1.6 %collective-permute-done.3.three = bf16[3,128,128]{2,1,0:T(8,128)(2,1)S(1)} collective-permute-done((bf16[3,128,128]{2,1,0:T(8,128)(2,1)S(1)}, bf16[3,128,128]{2,1,0:T(8,128)(2,1)S(1)}, u32[]{:S(2)}, u32[]{:S(2)}) %collective-permute-start.3) | collective-permute-done | bytes 98336 | tf_op jit(solution)/shard_map/ppermute | solution.py:336
  10.7 1.6 %collective-permute-start.4 = (bf16[3,256,128]{2,1,0:T(8,128)(2,1)S(1)}, bf16[3,256,128]{2,1,0:T(8,128)(2,1)S(1)}, u32[]{:S(2)}, u32[]{:S(2)}) collective-permute-start(bf16[3,256,128]{2,1,0:T(8,128)(2,1)S(1)} %get-tuple-element.52), channel_id=1, source_target_pairs={{0,4},{1,0},{2,6},{3,2},{4,8},{5,1},{6,10},{7,3},{8,12},{9,5},{10,... | collective-permute-start | bytes 589832 | tf_op jit(solution)/shard_map/ppermute | solution.py:344
  12.4 1.5 %collective-permute-start.1 = (bf16[2,3,144,128]{3,2,1,0:T(8,128)(2,1)S(1)}, bf16[2,3,144,128]{3,2,1,0:T(8,128)(2,1)S(1)}, u32[]{:S(2)}, u32[]{:S(2)}) collective-permute-start(bf16[2,3,144,128]{3,2,1,0:T(8,128)(2,1)S(1)} %get-tuple-element.48), channel_id=1, source_target_pairs={{0,2},{1,3},{2,0},{3,1},{4,6},{5,7},{6,4},{7,5},{8,10},{9,11},{10,... | collective-permute-start | bytes 663560 | tf_op jit(solution)/shard_map/ppermute | solution.py:336
  14.4 1.0 %collective-permute-done.7.pair = bf16[2,3,128,128]{3,2,1,0:T(8,128)(2,1)S(1)} collective-permute-done((bf16[2,3,128,128]{3,2,1,0:T(8,128)(2,1)S(1)}, bf16[2,3,128,128]{3,2,1,0:T(8,128)(2,1)S(1)}, u32[]{:S(2)}, u32[]{:S(2)}) %collective-permute-start.7) | collective-permute-done | bytes 196640 | tf_op jit(solution)/shard_map/ppermute | solution.py:336
  15.5 2.0 %collective-permute-start.8 = (bf16[3,256,128]{2,1,0:T(8,128)(2,1)S(1)}, bf16[3,256,128]{2,1,0:T(8,128)(2,1)S(1)}, u32[]{:S(2)}, u32[]{:S(2)}) collective-permute-start(bf16[3,256,128]{2,1,0:T(8,128)(2,1)S(1)} %get-tuple-element.59), channel_id=1, source_target_pairs={{0,4},{1,0},{2,6},{3,2},{4,8},{5,1},{6,10},{7,3},{8,12},{9,5},{10,... | collective-permute-start | bytes 589832 | tf_op jit(solution)/shard_map/ppermute | solution.py:344
  17.5 4.4 %collective-permute-done.5.halo2 = bf16[3,256,128]{2,1,0:T(8,128)(2,1)S(1)} collective-permute-done((bf16[3,256,128]{2,1,0:T(8,128)(2,1)S(1)}, bf16[3,256,128]{2,1,0:T(8,128)(2,1)S(1)}, u32[]{:S(2)}, u32[]{:S(2)}) %collective-permute-start.5) | collective-permute-done | bytes 196640 | tf_op jit(solution)/shard_map/ppermute | solution.py:344
  21.9 1.8 %probs.1 = (bf16[3,1024,512]{2,1,0:T(8,128)(2,1)S(1)}, bf16[3,1024,128]{2,1,0:T(8,128)(2,1)S(1)}, bf16[3,512,128]{2,1,0:T(8,128)(2,1)S(1)}) custom-call(bf16[3,528,128]{2,1,0:T(8,128)(2,1)S(1)} %get-tuple-element.45.own, bf16[3,928,128]{2,1,0:T(8,128)(2,1)S(1)} %collective-permute-done.side, bf16[2,3,144,128]{3,2,1,0:T(8,128)(2,1)S(1)} %collective-permute-done.1.crossed, ...), custom_call_target="tpu_custom_call" | custom-call | tf_op jit(solution)/shard_map/probs/pallas_call | solution.py:313
  24.1 0.8 %values.1 = (bf16[3,512,128]{2,1,0:T(8,128)(2,1)S(1)}, f32[3,512,128]{2,1,0:T(8,128)S(1)}, bf16[3,256,128]{2,1,0:T(8,128)(2,1)S(1)}, bf16[3,256,128]{2,1,0:T(8,128)(2,1)S(1)}) custom-call(bf16[3,1024,512]{2,1,0:T(8,128)(2,1)S(1)} %get-tuple-element.54.probs, bf16[3,528,128]{2,1,0:T(8,128)(2,1)S(1)} %get-tuple-element.45.own, ...), custom_call_target="tpu_custom_call" | custom-call | tf_op jit(solution)/shard_map/values/pallas_call | solution.py:313
  24.9 1.8 %collective-permute-start.11 = (bf16[3,256,128]{2,1,0:T(8,128)(2,1)S(1)}, bf16[3,256,128]{2,1,0:T(8,128)(2,1)S(1)}, u32[]{:S(2)}, u32[]{:S(2)}) collective-permute-start(bf16[3,256,128]{2,1,0:T(8,128)(2,1)S(1)} %get-tuple-element.72), channel_id=1, source_target_pairs={{0,4},{1,0},{2,6},{3,2},{4,8},{5,1},{6,10},{7,3},{8,12},{9,5},{10,... | collective-permute-start | bytes 589832 | tf_op jit(solution)/shard_map/ppermute | solution.py:344
  26.7 2.5 %scores.1 = (bf16[3,1024,512]{2,1,0:T(8,128)(2,1)S(1)}, f32[3,512,128]{2,1,0:T(8,128)S(1)}, bf16[3,256,128]{2,1,0:T(8,128)(2,1)S(1)}, bf16[3,256,128]{2,1,0:T(8,128)(2,1)S(1)}) custom-call(bf16[3,1024,512]{2,1,0:T(8,128)(2,1)S(1)} %get-tuple-element.54.probs, bf16[3,512,128]{2,1,0:T(8,128)(2,1)S(1)} %get-tuple-element.55.qs, ...), custom_call_target="tpu_custom_call" | custom-call | tf_op jit(solution)/shard_map/scores/pallas_call | solution.py:313
  29.2 2.0 %collective-permute-start.14 = (bf16[3,256,128]{2,1,0:T(8,128)(2,1)S(1)}, bf16[3,256,128]{2,1,0:T(8,128)(2,1)S(1)}, u32[]{:S(2)}, u32[]{:S(2)}) collective-permute-start(bf16[3,256,128]{2,1,0:T(8,128)(2,1)S(1)} %get-tuple-element.76), channel_id=1, source_target_pairs={{0,4},{1,0},{2,6},{3,2},{4,8},{5,1},{6,10},{7,3},{8,12},{9,5},{10,... | collective-permute-start | bytes 589832 | tf_op jit(solution)/shard_map/ppermute | solution.py:344
  31.3 2.5 %collective-permute-done.12.ring2 = bf16[3,256,128]{2,1,0:T(8,128)(2,1)S(1)} collective-permute-done((bf16[3,256,128]{2,1,0:T(8,128)(2,1)S(1)}, bf16[3,256,128]{2,1,0:T(8,128)(2,1)S(1)}, u32[]{:S(2)}, u32[]{:S(2)}) %collective-permute-start.12) | collective-permute-done | bytes 196640 | tf_op jit(solution)/shard_map/ppermute | solution.py:344
  34.0 1.4 %collective-permute-start.19 = (bf16[3,128,128]{2,1,0:T(8,128)(2,1)S(1)}, bf16[3,128,128]{2,1,0:T(8,128)(2,1)S(1)}, u32[]{:S(2)}, u32[]{:S(2)}) collective-permute-start(bf16[3,128,128]{2,1,0:T(8,128)(2,1)S(1)} %get-tuple-element.82), channel_id=1, source_target_pairs={{0,2},{1,3},{2,0},{3,1},{4,6},{5,7},{6,4},{7,5},{8,10},{9,11},{10,... | collective-permute-start | bytes 294920 | tf_op jit(solution)/shard_map/ppermute | solution.py:336
  35.9 0.8 %queries.1 = (bf16[3,128,128]{2,1,0:T(8,128)(2,1)S(1)}, bf16[3,128,128]{2,1,0:T(8,128)(2,1)S(1)}, bf16[2,3,128,128]{3,2,1,0:T(8,128)(2,1)S(1)}) custom-call(bf16[3,1024,512]{2,1,0:T(8,128)(2,1)S(1)} %get-tuple-element.64.ss, bf16[3,1024,128]{2,1,0:T(8,128)(2,1)S(1)} %get-tuple-element.65.ks), custom_call_target="tpu_custom_call" | custom-call | tf_op jit(solution)/shard_map/queries/pallas_call | solution.py:313
  37.2 1.5 %collective-permute-start.13 = (bf16[2,3,128,128]{3,2,1,0:T(8,128)(2,1)S(1)}, bf16[2,3,128,128]{3,2,1,0:T(8,128)(2,1)S(1)}, u32[]{:S(2)}, u32[]{:S(2)}) collective-permute-start(bf16[2,3,128,128]{3,2,1,0:T(8,128)(2,1)S(1)} %get-tuple-element.75), channel_id=1, source_target_pairs={{0,2},{1,3},{2,0},{3,1},{4,6},{5,7},{6,4},{7,5},{8,10},{9,11},{10,... | collective-permute-start | bytes 589832 | tf_op jit(solution)/shard_map/ppermute | solution.py:336
  38.7 0.9 %collective-permute-done.19.in2 = bf16[3,128,128]{2,1,0:T(8,128)(2,1)S(1)} collective-permute-done((bf16[3,128,128]{2,1,0:T(8,128)(2,1)S(1)}, bf16[3,128,128]{2,1,0:T(8,128)(2,1)S(1)}, u32[]{:S(2)}, u32[]{:S(2)}) %collective-permute-start.19) | collective-permute-done | bytes 98336 | tf_op jit(solution)/shard_map/ppermute | solution.py:336
  39.7 1.2 %collective-permute-done.20.in3 = bf16[3,128,128]{2,1,0:T(8,128)(2,1)S(1)} collective-permute-done((bf16[3,128,128]{2,1,0:T(8,128)(2,1)S(1)}, bf16[3,128,128]{2,1,0:T(8,128)(2,1)S(1)}, u32[]{:S(2)}, u32[]{:S(2)}) %collective-permute-start.20) | collective-permute-done | bytes 98336 | tf_op jit(solution)/shard_map/ppermute | solution.py:336
  40.9 1.4 %collective-permute-start.22 = (bf16[4,3,128,128]{3,2,1,0:T(8,128)(2,1)S(1)}, bf16[4,3,128,128]{3,2,1,0:T(8,128)(2,1)S(1)}, u32[]{:S(2)}, u32[]{:S(2)}) collective-permute-start(bf16[4,3,128,128]{3,2,1,0:T(8,128)(2,1)S(1)} %gather.1), channel_id=1, source_target_pairs={{0,16},{16,0},{1,17},{17,1},{2,18},{18,2},{3,19},{19,3},{4,20},{20... | collective-permute-start | bytes 1179656 | tf_op jit(solution)/shard_map/ppermute | solution.py:409
  42.3 1.6 %collective-permute-start.21 = (bf16[2,3,128,128]{3,2,1,0:T(8,128)(2,1)S(1)}, bf16[2,3,128,128]{3,2,1,0:T(8,128)(2,1)S(1)}, u32[]{:S(2)}, u32[]{:S(2)}) collective-permute-start(bf16[2,3,128,128]{3,2,1,0:T(8,128)(2,1)S(1)} %join.1), channel_id=1, source_target_pairs={{0,2},{1,3},{2,0},{3,1},{4,6},{5,7},{6,4},{7,5},{8,10},{9,11},{10,... | collective-permute-start | bytes 589832 | tf_op jit(solution)/shard_map/ppermute | solution.py:336
  43.9 1.7 %collective-permute-done.13.crossed = bf16[2,3,128,128]{3,2,1,0:T(8,128)(2,1)S(1)} collective-permute-done((bf16[2,3,128,128]{3,2,1,0:T(8,128)(2,1)S(1)}, bf16[2,3,128,128]{3,2,1,0:T(8,128)(2,1)S(1)}, u32[]{:S(2)}, u32[]{:S(2)}) %collective-permute-start.13) | collective-permute-done | bytes 196640 | tf_op jit(solution)/shard_map/ppermute | solution.py:336
  45.6 0.5 collective-permute-start.10
  46.1 0.8 %unpack.6 = bf16[1,128,1536]{2,1,0:T(8,128)(2,1)} custom-call(bf16[3,128,128]{2,1,0:T(8,128)(2,1)S(1)} %get-tuple-element.85.in0, bf16[3,128,128]{2,1,0:T(8,128)(2,1)S(1)} %collective-permute-done.18.in1, bf16[3,128,128]{2,1,0:T(8,128)(2,1)S(1)} %collective-permute-done.19.in2, bf16[3,128,128]{2,1,0:T(8,128)(2,1)S(1)} %collective-permute-done.20.in3), custom_call_target="tpu_custom_call" | custom-call | tf_op jit(solution)/shard_map/unpack/pallas_call | solution.py:313
  46.9 2.9 %collective-permute-done.21.crossed = bf16[2,3,128,128]{3,2,1,0:T(8,128)(2,1)S(1)} collective-permute-done((bf16[2,3,128,128]{3,2,1,0:T(8,128)(2,1)S(1)}, bf16[2,3,128,128]{3,2,1,0:T(8,128)(2,1)S(1)}, u32[]{:S(2)}, u32[]{:S(2)}) %collective-permute-start.21) | collective-permute-done | bytes 196640 | tf_op jit(solution)/shard_map/ppermute | solution.py:336
  49.7 0.8 %unpack.5 = bf16[1,128,1536]{2,1,0:T(8,128)(2,1)} custom-call(bf16[2,3,128,128]{3,2,1,0:T(8,128)(2,1)S(1)} %get-tuple-element.84.stay, bf16[2,3,128,128]{3,2,1,0:T(8,128)(2,1)S(1)} %collective-permute-done.16.got, bf16[2,3,128,128]{3,2,1,0:T(8,128)(2,1)S(1)} %collective-permute-done.21.crossed), custom_call_target="tpu_custom_call" | custom-call | tf_op jit(solution)/shard_map/unpack/pallas_call | solution.py:313
  50.6 0.8 %unpack.4 = bf16[1,128,1536]{2,1,0:T(8,128)(2,1)} custom-call(bf16[3,128,128]{2,1,0:T(8,128)(2,1)S(1)} %get-tuple-element.66.dq0, bf16[3,128,128]{2,1,0:T(8,128)(2,1)S(1)} %collective-permute-done.10.dq1, bf16[2,3,128,128]{3,2,1,0:T(8,128)(2,1)S(1)} %collective-permute-done.13.crossed, bf16[2,3,128,128]{3,2,1,0:T(8,128)(2,1)S(1)} %collective-permute-done.17.turned), custom_call_target="tpu_custom_call" | custom-call | tf_op jit(solution)/shard_map/unpack/pallas_call | solution.py:313
  51.4 1.3 %collective-permute-done.22.groups = bf16[4,3,128,128]{3,2,1,0:T(8,128)(2,1)S(1)} collective-permute-done((bf16[4,3,128,128]{3,2,1,0:T(8,128)(2,1)S(1)}, bf16[4,3,128,128]{3,2,1,0:T(8,128)(2,1)S(1)}, u32[]{:S(2)}, u32[]{:S(2)}) %collective-permute-start.22) | collective-permute-done | bytes 393248 | tf_op jit(solution)/shard_map/ppermute | solution.py:409
  52.7 0.8 %unpack.7 = bf16[1,128,1536]{2,1,0:T(8,128)(2,1)} custom-call(bf16[4,3,128,128]{3,2,1,0:T(8,128)(2,1)S(1)} %collective-permute-done.22.groups), custom_call_target="tpu_custom_call" | custom-call | tf_op jit(solution)/shard_map/unpack/pallas_call | solution.py:313
  (30 shorter events, 2.4 us)
Async XLA Ops:
  2.3 3.2 %collective-permute-start = (bf16[3,928,128]{2,1,0:T(8,128)(2,1)S(1)}, bf16[3,928,128]{2,1,0:T(8,128)(2,1)S(1)}, u32[]{:S(2)}, u32[]{:S(2)}) collective-permute-start(bf16[3,928,128]{2,1,0:T(8,128)(2,1)S(1)} %get-tuple-element.46), channel_id=1, source_target_pairs={{0,1},{1,0},{2,3},{3,2},{4,5},{5,4},{6,7},{7,6},{8,9},{9,8},{10,11... | collective-permute-start | bytes 2138120 | tf_op jit(solution)/shard_map/ppermute | solution.py:336
  2.8 6.2 %collective-permute-start.2 = (bf16[3,128,128]{2,1,0:T(8,128)(2,1)S(1)}, bf16[3,128,128]{2,1,0:T(8,128)(2,1)S(1)}, u32[]{:S(2)}, u32[]{:S(2)}) collective-permute-start(bf16[3,128,128]{2,1,0:T(8,128)(2,1)S(1)} %get-tuple-element.49), channel_id=1, source_target_pairs={{0,2},{1,3},{2,0},{3,1},{4,6},{5,7},{6,4},{7,5},{8,10},{9,11},{10,... | collective-permute-start | bytes 294920 | tf_op jit(solution)/shard_map/ppermute | solution.py:336
  5.4 5.2 %collective-permute-start.3 = (bf16[3,128,128]{2,1,0:T(8,128)(2,1)S(1)}, bf16[3,128,128]{2,1,0:T(8,128)(2,1)S(1)}, u32[]{:S(2)}, u32[]{:S(2)}) collective-permute-start(bf16[3,128,128]{2,1,0:T(8,128)(2,1)S(1)} %get-tuple-element.50), channel_id=1, source_target_pairs={{0,3},{1,2},{2,1},{3,0},{4,7},{5,6},{6,5},{7,4},{8,11},{9,10},{10,... | collective-permute-start | bytes 294920 | tf_op jit(solution)/shard_map/ppermute | solution.py:336
  5.5 9.8 %collective-permute-start.7 = (bf16[2,3,128,128]{3,2,1,0:T(8,128)(2,1)S(1)}, bf16[2,3,128,128]{3,2,1,0:T(8,128)(2,1)S(1)}, u32[]{:S(2)}, u32[]{:S(2)}) collective-permute-start(bf16[2,3,128,128]{3,2,1,0:T(8,128)(2,1)S(1)} %get-tuple-element.58), channel_id=1, source_target_pairs={{0,2},{1,3},{2,0},{3,1},{4,6},{5,7},{6,4},{7,5},{8,10},{9,11},{10,... | collective-permute-start | bytes 589832 | tf_op jit(solution)/shard_map/ppermute | solution.py:336
  10.7 6.8 %collective-permute-start.4 = (bf16[3,256,128]{2,1,0:T(8,128)(2,1)S(1)}, bf16[3,256,128]{2,1,0:T(8,128)(2,1)S(1)}, u32[]{:S(2)}, u32[]{:S(2)}) collective-permute-start(bf16[3,256,128]{2,1,0:T(8,128)(2,1)S(1)} %get-tuple-element.52), channel_id=1, source_target_pairs={{0,4},{1,0},{2,6},{3,2},{4,8},{5,1},{6,10},{7,3},{8,12},{9,5},{10,... | collective-permute-start | bytes 589832 | tf_op jit(solution)/shard_map/ppermute | solution.py:344
  12.4 9.5 %collective-permute-start.1 = (bf16[2,3,144,128]{3,2,1,0:T(8,128)(2,1)S(1)}, bf16[2,3,144,128]{3,2,1,0:T(8,128)(2,1)S(1)}, u32[]{:S(2)}, u32[]{:S(2)}) collective-permute-start(bf16[2,3,144,128]{3,2,1,0:T(8,128)(2,1)S(1)} %get-tuple-element.48), channel_id=1, source_target_pairs={{0,2},{1,3},{2,0},{3,1},{4,6},{5,7},{6,4},{7,5},{8,10},{9,11},{10,... | collective-permute-start | bytes 663560 | tf_op jit(solution)/shard_map/ppermute | solution.py:336
  13.9 10.2 %collective-permute-start.6 = (bf16[2,3,128,128]{3,2,1,0:T(8,128)(2,1)S(1)}, bf16[2,3,128,128]{3,2,1,0:T(8,128)(2,1)S(1)}, u32[]{:S(2)}, u32[]{:S(2)}) collective-permute-start(bf16[2,3,128,128]{3,2,1,0:T(8,128)(2,1)S(1)} %get-tuple-element.57), channel_id=1, source_target_pairs={{0,2},{1,3},{2,0},{3,1},{4,6},{5,7},{6,4},{7,5},{8,10},{9,11},{10,... | collective-permute-start | bytes 589832 | tf_op jit(solution)/shard_map/ppermute | solution.py:336
  14.4 7.5 %collective-permute-start.5 = (bf16[3,256,128]{2,1,0:T(8,128)(2,1)S(1)}, bf16[3,256,128]{2,1,0:T(8,128)(2,1)S(1)}, u32[]{:S(2)}, u32[]{:S(2)}) collective-permute-start(bf16[3,256,128]{2,1,0:T(8,128)(2,1)S(1)} %get-tuple-element.53), channel_id=1, source_target_pairs={{0,1},{1,5},{2,3},{3,7},{4,0},{5,9},{6,2},{7,11},{8,4},{9,13},{10,... | collective-permute-start | bytes 589832 | tf_op jit(solution)/shard_map/ppermute | solution.py:344
  15.5 8.6 %collective-permute-start.8 = (bf16[3,256,128]{2,1,0:T(8,128)(2,1)S(1)}, bf16[3,256,128]{2,1,0:T(8,128)(2,1)S(1)}, u32[]{:S(2)}, u32[]{:S(2)}) collective-permute-start(bf16[3,256,128]{2,1,0:T(8,128)(2,1)S(1)} %get-tuple-element.59), channel_id=1, source_target_pairs={{0,4},{1,0},{2,6},{3,2},{4,8},{5,1},{6,10},{7,3},{8,12},{9,5},{10,... | collective-permute-start | bytes 589832 | tf_op jit(solution)/shard_map/ppermute | solution.py:344
  17.5 6.6 %collective-permute-start.9 = (bf16[3,256,128]{2,1,0:T(8,128)(2,1)S(1)}, bf16[3,256,128]{2,1,0:T(8,128)(2,1)S(1)}, u32[]{:S(2)}, u32[]{:S(2)}) collective-permute-start(bf16[3,256,128]{2,1,0:T(8,128)(2,1)S(1)} %get-tuple-element.60), channel_id=1, source_target_pairs={{0,1},{1,5},{2,3},{3,7},{4,0},{5,9},{6,2},{7,11},{8,4},{9,13},{10,... | collective-permute-start | bytes 589832 | tf_op jit(solution)/shard_map/ppermute | solution.py:344
  24.9 6.4 %collective-permute-start.11 = (bf16[3,256,128]{2,1,0:T(8,128)(2,1)S(1)}, bf16[3,256,128]{2,1,0:T(8,128)(2,1)S(1)}, u32[]{:S(2)}, u32[]{:S(2)}) collective-permute-start(bf16[3,256,128]{2,1,0:T(8,128)(2,1)S(1)} %get-tuple-element.72), channel_id=1, source_target_pairs={{0,4},{1,0},{2,6},{3,2},{4,8},{5,1},{6,10},{7,3},{8,12},{9,5},{10,... | collective-permute-start | bytes 589832 | tf_op jit(solution)/shard_map/ppermute | solution.py:344
  26.7 7.0 %collective-permute-start.12 = (bf16[3,256,128]{2,1,0:T(8,128)(2,1)S(1)}, bf16[3,256,128]{2,1,0:T(8,128)(2,1)S(1)}, u32[]{:S(2)}, u32[]{:S(2)}) collective-permute-start(bf16[3,256,128]{2,1,0:T(8,128)(2,1)S(1)} %get-tuple-element.73), channel_id=1, source_target_pairs={{0,1},{1,5},{2,3},{3,7},{4,0},{5,9},{6,2},{7,11},{8,4},{9,13},{10,... | collective-permute-start | bytes 589832 | tf_op jit(solution)/shard_map/ppermute | solution.py:344
  29.2 7.4 %collective-permute-start.14 = (bf16[3,256,128]{2,1,0:T(8,128)(2,1)S(1)}, bf16[3,256,128]{2,1,0:T(8,128)(2,1)S(1)}, u32[]{:S(2)}, u32[]{:S(2)}) collective-permute-start(bf16[3,256,128]{2,1,0:T(8,128)(2,1)S(1)} %get-tuple-element.76), channel_id=1, source_target_pairs={{0,4},{1,0},{2,6},{3,2},{4,8},{5,1},{6,10},{7,3},{8,12},{9,5},{10,... | collective-permute-start | bytes 589832 | tf_op jit(solution)/shard_map/ppermute | solution.py:344
  31.3 5.7 %collective-permute-start.15 = (bf16[3,256,128]{2,1,0:T(8,128)(2,1)S(1)}, bf16[3,256,128]{2,1,0:T(8,128)(2,1)S(1)}, u32[]{:S(2)}, u32[]{:S(2)}) collective-permute-start(bf16[3,256,128]{2,1,0:T(8,128)(2,1)S(1)} %get-tuple-element.77), channel_id=1, source_target_pairs={{0,1},{1,5},{2,3},{3,7},{4,0},{5,9},{6,2},{7,11},{8,4},{9,13},{10,... | collective-permute-start | bytes 589832 | tf_op jit(solution)/shard_map/ppermute | solution.py:344
  33.9 4.8 %collective-permute-start.18 = (bf16[3,128,128]{2,1,0:T(8,128)(2,1)S(1)}, bf16[3,128,128]{2,1,0:T(8,128)(2,1)S(1)}, u32[]{:S(2)}, u32[]{:S(2)}) collective-permute-start(bf16[3,128,128]{2,1,0:T(8,128)(2,1)S(1)} %get-tuple-element.81), channel_id=1, source_target_pairs={{0,1},{1,0},{2,3},{3,2},{4,5},{5,4},{6,7},{7,6},{8,9},{9,8},{10,11... | collective-permute-start | bytes 294920 | tf_op jit(solution)/shard_map/ppermute | solution.py:336
  34.0 5.7 %collective-permute-start.19 = (bf16[3,128,128]{2,1,0:T(8,128)(2,1)S(1)}, bf16[3,128,128]{2,1,0:T(8,128)(2,1)S(1)}, u32[]{:S(2)}, u32[]{:S(2)}) collective-permute-start(bf16[3,128,128]{2,1,0:T(8,128)(2,1)S(1)} %get-tuple-element.82), channel_id=1, source_target_pairs={{0,2},{1,3},{2,0},{3,1},{4,6},{5,7},{6,4},{7,5},{8,10},{9,11},{10,... | collective-permute-start | bytes 294920 | tf_op jit(solution)/shard_map/ppermute | solution.py:336
  35.4 5.4 %collective-permute-start.20 = (bf16[3,128,128]{2,1,0:T(8,128)(2,1)S(1)}, bf16[3,128,128]{2,1,0:T(8,128)(2,1)S(1)}, u32[]{:S(2)}, u32[]{:S(2)}) collective-permute-start(bf16[3,128,128]{2,1,0:T(8,128)(2,1)S(1)} %get-tuple-element.83), channel_id=1, source_target_pairs={{0,3},{1,2},{2,1},{3,0},{4,7},{5,6},{6,5},{7,4},{8,11},{9,10},{10,... | collective-permute-start | bytes 294920 | tf_op jit(solution)/shard_map/ppermute | solution.py:336
  37.1 5.2 %collective-permute-start.16 = (bf16[2,3,128,128]{3,2,1,0:T(8,128)(2,1)S(1)}, bf16[2,3,128,128]{3,2,1,0:T(8,128)(2,1)S(1)}, u32[]{:S(2)}, u32[]{:S(2)}) collective-permute-start(bf16[2,3,128,128]{3,2,1,0:T(8,128)(2,1)S(1)} %get-tuple-element.78), channel_id=1, source_target_pairs={{0,1},{1,0},{2,3},{3,2},{4,5},{5,4},{6,7},{7,6},{8,9},{9,8},{10,11... | collective-permute-start | bytes 589832 | tf_op jit(solution)/shard_map/ppermute | solution.py:336
  37.2 8.3 %collective-permute-start.13 = (bf16[2,3,128,128]{3,2,1,0:T(8,128)(2,1)S(1)}, bf16[2,3,128,128]{3,2,1,0:T(8,128)(2,1)S(1)}, u32[]{:S(2)}, u32[]{:S(2)}) collective-permute-start(bf16[2,3,128,128]{3,2,1,0:T(8,128)(2,1)S(1)} %get-tuple-element.75), channel_id=1, source_target_pairs={{0,2},{1,3},{2,0},{3,1},{4,6},{5,7},{6,4},{7,5},{8,10},{9,11},{10,... | collective-permute-start | bytes 589832 | tf_op jit(solution)/shard_map/ppermute | solution.py:336
  40.9 11.8 %collective-permute-start.22 = (bf16[4,3,128,128]{3,2,1,0:T(8,128)(2,1)S(1)}, bf16[4,3,128,128]{3,2,1,0:T(8,128)(2,1)S(1)}, u32[]{:S(2)}, u32[]{:S(2)}) collective-permute-start(bf16[4,3,128,128]{3,2,1,0:T(8,128)(2,1)S(1)} %gather.1), channel_id=1, source_target_pairs={{0,16},{16,0},{1,17},{17,1},{2,18},{18,2},{3,19},{19,3},{4,20},{20... | collective-permute-start | bytes 1179656 | tf_op jit(solution)/shard_map/ppermute | solution.py:409
  42.3 7.4 %collective-permute-start.21 = (bf16[2,3,128,128]{3,2,1,0:T(8,128)(2,1)S(1)}, bf16[2,3,128,128]{3,2,1,0:T(8,128)(2,1)S(1)}, u32[]{:S(2)}, u32[]{:S(2)}) collective-permute-start(bf16[2,3,128,128]{3,2,1,0:T(8,128)(2,1)S(1)} %join.1), channel_id=1, source_target_pairs={{0,2},{1,3},{2,0},{3,1},{4,6},{5,7},{6,4},{7,5},{8,10},{9,11},{10,... | collective-permute-start | bytes 589832 | tf_op jit(solution)/shard_map/ppermute | solution.py:336
  45.6 5.0 %collective-permute-start.17 = (bf16[2,3,128,128]{3,2,1,0:T(8,128)(2,1)S(1)}, bf16[2,3,128,128]{3,2,1,0:T(8,128)(2,1)S(1)}, u32[]{:S(2)}, u32[]{:S(2)}) collective-permute-start(bf16[2,3,128,128]{3,2,1,0:T(8,128)(2,1)S(1)} %collective-permute-done.13.crossed), channel_id=1, source_target_pairs={{0,1},{1,0},{2,3},{3,2},{4,5},{5,4},{6,7},{7,6},{8,9},{9,8},{10,11... | collective-permute-start | bytes 589832 | tf_op jit(solution)/shard_map/ppermute | solution.py:336
  45.6 5.0 %collective-permute-start.10 = (bf16[3,128,128]{2,1,0:T(8,128)(2,1)S(1)}, bf16[3,128,128]{2,1,0:T(8,128)(2,1)S(1)}, u32[]{:S(2)}, u32[]{:S(2)}) collective-permute-start(bf16[3,128,128]{2,1,0:T(8,128)(2,1)S(1)} %get-tuple-element.67), channel_id=1, source_target_pairs={{0,1},{1,0},{2,3},{3,2},{4,5},{5,4},{6,7},{7,6},{8,9},{9,8},{10,11... | collective-permute-start | bytes 294920 | tf_op jit(solution)/shard_map/ppermute | solution.py:336

commit v7 on v6

--- a/solution.py
+++ b/solution.py
@@ -400,7 +400,6 @@
         (square, kept, ends, ends),
         [pltpu.VMEM((LOCAL, SLOTS * BLK, DH), bf16), ends_in],
     )(probs, qs, gs, v_local, v_halo1, v_halo2)
-    dv_own = after(dv_own, dk_own)
     dv = total(total_kernel, (part,) * 4, dv_own, dv1, dv2)
     dv_first = dv[0]
     dv = [dv[0]] + [swap(dv[step], step) for step in range(1, TEAM)]
@@ -412,6 +411,8 @@
     )(ss, ks)
     dq23 = after(dq23, dv_first)
     dq23 = swap(dq23, 2)
+    dk1 = after(dk1, dq0)
+    dk2 = after(dk2, dq0)
     stay, give = total(total_pairs_kernel, (pair, pair), dk_own, dk1, dk2)
     got = swap(give, 1)
     joined = call(join_kernel, "join", pair)(after(stay, late), got)
@@ -421,6 +422,7 @@
     dq23 = after(dq23, got)
     grad_query = unpack(unpack_turned_kernel, dq0, swap(dq1, 1), dq23, swap(dq23, 1))
     grad_key = unpack(unpack_joined_kernel, stay, got, crossed)
+    passed = after(passed, grad_key)
     handoff = unpack(unpack_passed_kernel, passed)
     return (grad_query, grad_key, grad_value, handoff)
 

time: 53.7 us -> 51.8 us (0.965)
  waiting for transfers between devices: 19.6 us -> 17.6 us
    ppermute x1, waiting for transfers between devices: 1.33 us -> 0.03 us  [shards(): lax.ppermute(late, 'section', [(s, (s - 1) % sections) for s in range(sec...]
    ppermute x14, waiting for transfers between devices: 11 us -> 10.3 us  [swap(): return lax.ppermute(array, 'ctx', [(i, i ^ step) for i in range(ctx)])]
  transfers between devices with their start and end apart: 23 -> 23, of which waited for: 12 -> 10; matrix products, arithmetic and copies ran while one was open for 0% -> 0% of each run, Pallas kernels for 15% -> 15%
where the time goes in v7:
time: 51.8 us; the launch traced here: 51.7 us
  starting transfers between devices  22.1 us (43%)
  waiting for transfers between devices  17.6 us (34%)
  Pallas kernels  11.2 us (22%)
  between operations  0.77 us (1%)
    ppermute x14, starting transfers between devices, swap(): return lax.ppermute(array, 'ctx', [(i, i ^ step) for i in range(ctx)])  13 us
    pallas_call x16, Pallas kernels, run(): pl.pallas_call(kernel, out_shape=jax.tree.map(lambda out: to(out.shape, o...  11.2 us
    ppermute x14, waiting for transfers between devices, swap(): return lax.ppermute(array, 'ctx', [(i, i ^ step) for i in range(ctx)])  10.3 us
    ppermute x8, starting transfers between devices, ring(): return lax.ppermute(array, 'ctx', pairs)  7.55 us
    ppermute x8, waiting for transfers between devices, ring(): return lax.ppermute(array, 'ctx', pairs)  7.31 us
    ppermute x1, starting transfers between devices, shards(): lax.ppermute(late, 'section', [(s, (s - 1) % sections) for s in range(sec...  1.55 us
  transfers between devices with their start and end apart: 23, of which 10 were waited for; matrix products, arithmetic and copies ran while one was open for 0% of the time, Pallas kernels for 15%

profile of v7, /device:TPU:0, one launch (start us, length us, event | category | flops | bytes accessed | tf_op | source)
XLA Modules:
  0.0 51.7 jit_solution(18283831752249800900)
XLA Ops:
  0.6 1.7 %pack.1 = (bf16[3,528,128]{2,1,0:T(8,128)(2,1)S(1)}, bf16[3,928,128]{2,1,0:T(8,128)(2,1)S(1)}, bf16[3,128,128]{2,1,0:T(8,128)(2,1)S(1)}, bf16[3,128,128]{2,1,0:T(8,128)(2,1)S(1)}, bf16[3,400,128]{2,1,0:T(8,128)(2,1)S(1)}) custom-call(bf16[1,128,1536]{2,1,0:T(8,128)(2,1)} %k_hbm.1, bf16[1,128,1536]{2,1,0:T(8,128)(2,1)} %q_hbm.1, bf16[1,128,1536]{2,1,0:T(8,128)(2,1)} %g_hbm.1, ...), custom_call_target="tpu_custom_call" | custom-call | tf_op jit(solution)/shard_map/pack/pallas_call | solution.py:313
  2.3 0.5 %collective-permute-start = (bf16[3,928,128]{2,1,0:T(8,128)(2,1)S(1)}, bf16[3,928,128]{2,1,0:T(8,128)(2,1)S(1)}, u32[]{:S(2)}, u32[]{:S(2)}) collective-permute-start(bf16[3,928,128]{2,1,0:T(8,128)(2,1)S(1)} %get-tuple-element.48), channel_id=1, source_target_pairs={{0,1},{1,0},{2,3},{3,2},{4,5},{5,4},{6,7},{7,6},{8,9},{9,8},{10,11... | collective-permute-start | bytes 2138120 | tf_op jit(solution)/shard_map/ppermute | solution.py:336
  2.8 2.6 %collective-permute-start.2 = (bf16[3,128,128]{2,1,0:T(8,128)(2,1)S(1)}, bf16[3,128,128]{2,1,0:T(8,128)(2,1)S(1)}, u32[]{:S(2)}, u32[]{:S(2)}) collective-permute-start(bf16[3,128,128]{2,1,0:T(8,128)(2,1)S(1)} %get-tuple-element.51), channel_id=1, source_target_pairs={{0,2},{1,3},{2,0},{3,1},{4,6},{5,7},{6,4},{7,5},{8,10},{9,11},{10,... | collective-permute-start | bytes 294920 | tf_op jit(solution)/shard_map/ppermute | solution.py:336
  5.5 2.1 %collective-permute-start.7 = (bf16[2,3,128,128]{3,2,1,0:T(8,128)(2,1)S(1)}, bf16[2,3,128,128]{3,2,1,0:T(8,128)(2,1)S(1)}, u32[]{:S(2)}, u32[]{:S(2)}) collective-permute-start(bf16[2,3,128,128]{3,2,1,0:T(8,128)(2,1)S(1)} %get-tuple-element.60), channel_id=1, source_target_pairs={{0,2},{1,3},{2,0},{3,1},{4,6},{5,7},{6,4},{7,5},{8,10},{9,11},{10,... | collective-permute-start | bytes 589832 | tf_op jit(solution)/shard_map/ppermute | solution.py:336
  7.6 1.4 %collective-permute-done.2.two = bf16[3,128,128]{2,1,0:T(8,128)(2,1)S(1)} collective-permute-done((bf16[3,128,128]{2,1,0:T(8,128)(2,1)S(1)}, bf16[3,128,128]{2,1,0:T(8,128)(2,1)S(1)}, u32[]{:S(2)}, u32[]{:S(2)}) %collective-permute-start.2) | collective-permute-done | bytes 98336 | tf_op jit(solution)/shard_map/ppermute | solution.py:336
  9.1 1.6 %collective-permute-done.3.three = bf16[3,128,128]{2,1,0:T(8,128)(2,1)S(1)} collective-permute-done((bf16[3,128,128]{2,1,0:T(8,128)(2,1)S(1)}, bf16[3,128,128]{2,1,0:T(8,128)(2,1)S(1)}, u32[]{:S(2)}, u32[]{:S(2)}) %collective-permute-start.3) | collective-permute-done | bytes 98336 | tf_op jit(solution)/shard_map/ppermute | solution.py:336
  10.7 1.6 %collective-permute-start.4 = (bf16[3,256,128]{2,1,0:T(8,128)(2,1)S(1)}, bf16[3,256,128]{2,1,0:T(8,128)(2,1)S(1)}, u32[]{:S(2)}, u32[]{:S(2)}) collective-permute-start(bf16[3,256,128]{2,1,0:T(8,128)(2,1)S(1)} %get-tuple-element.54), channel_id=1, source_target_pairs={{0,4},{1,0},{2,6},{3,2},{4,8},{5,1},{6,10},{7,3},{8,12},{9,5},{10,... | collective-permute-start | bytes 589832 | tf_op jit(solution)/shard_map/ppermute | solution.py:344
  12.4 1.5 %collective-permute-start.1 = (bf16[2,3,144,128]{3,2,1,0:T(8,128)(2,1)S(1)}, bf16[2,3,144,128]{3,2,1,0:T(8,128)(2,1)S(1)}, u32[]{:S(2)}, u32[]{:S(2)}) collective-permute-start(bf16[2,3,144,128]{3,2,1,0:T(8,128)(2,1)S(1)} %get-tuple-element.50), channel_id=1, source_target_pairs={{0,2},{1,3},{2,0},{3,1},{4,6},{5,7},{6,4},{7,5},{8,10},{9,11},{10,... | collective-permute-start | bytes 663560 | tf_op jit(solution)/shard_map/ppermute | solution.py:336
  13.9 0.5 collective-permute-start.6
  14.4 1.0 %collective-permute-done.7.pair = bf16[2,3,128,128]{3,2,1,0:T(8,128)(2,1)S(1)} collective-permute-done((bf16[2,3,128,128]{3,2,1,0:T(8,128)(2,1)S(1)}, bf16[2,3,128,128]{3,2,1,0:T(8,128)(2,1)S(1)}, u32[]{:S(2)}, u32[]{:S(2)}) %collective-permute-start.7) | collective-permute-done | bytes 196640 | tf_op jit(solution)/shard_map/ppermute | solution.py:336
  15.5 2.0 %collective-permute-start.8 = (bf16[3,256,128]{2,1,0:T(8,128)(2,1)S(1)}, bf16[3,256,128]{2,1,0:T(8,128)(2,1)S(1)}, u32[]{:S(2)}, u32[]{:S(2)}) collective-permute-start(bf16[3,256,128]{2,1,0:T(8,128)(2,1)S(1)} %get-tuple-element.61), channel_id=1, source_target_pairs={{0,4},{1,0},{2,6},{3,2},{4,8},{5,1},{6,10},{7,3},{8,12},{9,5},{10,... | collective-permute-start | bytes 589832 | tf_op jit(solution)/shard_map/ppermute | solution.py:344
  17.5 4.0 %collective-permute-done.5.halo2 = bf16[3,256,128]{2,1,0:T(8,128)(2,1)S(1)} collective-permute-done((bf16[3,256,128]{2,1,0:T(8,128)(2,1)S(1)}, bf16[3,256,128]{2,1,0:T(8,128)(2,1)S(1)}, u32[]{:S(2)}, u32[]{:S(2)}) %collective-permute-start.5) | collective-permute-done | bytes 196640 | tf_op jit(solution)/shard_map/ppermute | solution.py:344
  21.4 1.8 %probs.1 = (bf16[3,1024,512]{2,1,0:T(8,128)(2,1)S(1)}, bf16[3,1024,128]{2,1,0:T(8,128)(2,1)S(1)}, bf16[3,512,128]{2,1,0:T(8,128)(2,1)S(1)}) custom-call(bf16[3,528,128]{2,1,0:T(8,128)(2,1)S(1)} %get-tuple-element.47.own, bf16[3,928,128]{2,1,0:T(8,128)(2,1)S(1)} %collective-permute-done.side, bf16[2,3,144,128]{3,2,1,0:T(8,128)(2,1)S(1)} %collective-permute-done.1.crossed, ...), custom_call_target="tpu_custom_call" | custom-call | tf_op jit(solution)/shard_map/probs/pallas_call | solution.py:313
  23.2 0.8 %collective-permute-done.6.crossed = bf16[2,3,128,128]{3,2,1,0:T(8,128)(2,1)S(1)} collective-permute-done((bf16[2,3,128,128]{3,2,1,0:T(8,128)(2,1)S(1)}, bf16[2,3,128,128]{3,2,1,0:T(8,128)(2,1)S(1)}, u32[]{:S(2)}, u32[]{:S(2)}) %collective-permute-start.6) | collective-permute-done | bytes 196640 | tf_op jit(solution)/shard_map/ppermute | solution.py:336
  24.1 0.8 %values.1 = (bf16[3,512,128]{2,1,0:T(8,128)(2,1)S(1)}, f32[3,512,128]{2,1,0:T(8,128)S(1)}, bf16[3,256,128]{2,1,0:T(8,128)(2,1)S(1)}, bf16[3,256,128]{2,1,0:T(8,128)(2,1)S(1)}) custom-call(bf16[3,1024,512]{2,1,0:T(8,128)(2,1)S(1)} %get-tuple-element.56.probs, bf16[3,528,128]{2,1,0:T(8,128)(2,1)S(1)} %get-tuple-element.47.own, ...), custom_call_target="tpu_custom_call" | custom-call | tf_op jit(solution)/shard_map/values/pallas_call | solution.py:313
  24.9 1.8 %collective-permute-start.11 = (bf16[3,256,128]{2,1,0:T(8,128)(2,1)S(1)}, bf16[3,256,128]{2,1,0:T(8,128)(2,1)S(1)}, u32[]{:S(2)}, u32[]{:S(2)}) collective-permute-start(bf16[3,256,128]{2,1,0:T(8,128)(2,1)S(1)} %get-tuple-element.72), channel_id=1, source_target_pairs={{0,4},{1,0},{2,6},{3,2},{4,8},{5,1},{6,10},{7,3},{8,12},{9,5},{10,... | collective-permute-start | bytes 589832 | tf_op jit(solution)/shard_map/ppermute | solution.py:344
  26.7 2.5 %scores.1 = (bf16[3,1024,512]{2,1,0:T(8,128)(2,1)S(1)}, f32[3,512,128]{2,1,0:T(8,128)S(1)}, bf16[3,256,128]{2,1,0:T(8,128)(2,1)S(1)}, bf16[3,256,128]{2,1,0:T(8,128)(2,1)S(1)}) custom-call(bf16[3,1024,512]{2,1,0:T(8,128)(2,1)S(1)} %get-tuple-element.56.probs, bf16[3,512,128]{2,1,0:T(8,128)(2,1)S(1)} %get-tuple-element.57.qs, ...), custom_call_target="tpu_custom_call" | custom-call | tf_op jit(solution)/shard_map/scores/pallas_call | solution.py:313
  29.2 0.8 %queries.1 = (bf16[3,128,128]{2,1,0:T(8,128)(2,1)S(1)}, bf16[3,128,128]{2,1,0:T(8,128)(2,1)S(1)}, bf16[2,3,128,128]{3,2,1,0:T(8,128)(2,1)S(1)}) custom-call(bf16[3,1024,512]{2,1,0:T(8,128)(2,1)S(1)} %get-tuple-element.66.ss, bf16[3,1024,128]{2,1,0:T(8,128)(2,1)S(1)} %get-tuple-element.67.ks), custom_call_target="tpu_custom_call" | custom-call | tf_op jit(solution)/shard_map/queries/pallas_call | solution.py:313
  30.0 2.0 %collective-permute-start.14 = (bf16[3,256,128]{2,1,0:T(8,128)(2,1)S(1)}, bf16[3,256,128]{2,1,0:T(8,128)(2,1)S(1)}, u32[]{:S(2)}, u32[]{:S(2)}) collective-permute-start(bf16[3,256,128]{2,1,0:T(8,128)(2,1)S(1)} %get-tuple-element.78), channel_id=1, source_target_pairs={{0,4},{1,0},{2,6},{3,2},{4,8},{5,1},{6,10},{7,3},{8,12},{9,5},{10,... | collective-permute-start | bytes 589832 | tf_op jit(solution)/shard_map/ppermute | solution.py:344
  32.0 0.3 collective-permute-done.12.ring2
  32.6 1.6 %collective-permute-start.19 = (bf16[3,128,128]{2,1,0:T(8,128)(2,1)S(1)}, bf16[3,128,128]{2,1,0:T(8,128)(2,1)S(1)}, u32[]{:S(2)}, u32[]{:S(2)}) collective-permute-start(bf16[3,128,128]{2,1,0:T(8,128)(2,1)S(1)} %get-tuple-element.85), channel_id=1, source_target_pairs={{0,2},{1,3},{2,0},{3,1},{4,6},{5,7},{6,4},{7,5},{8,10},{9,11},{10,... | collective-permute-start | bytes 294920 | tf_op jit(solution)/shard_map/ppermute | solution.py:336
  34.5 3.0 %collective-permute-done.15.ring2 = bf16[3,256,128]{2,1,0:T(8,128)(2,1)S(1)} collective-permute-done((bf16[3,256,128]{2,1,0:T(8,128)(2,1)S(1)}, bf16[3,256,128]{2,1,0:T(8,128)(2,1)S(1)}, u32[]{:S(2)}, u32[]{:S(2)}) %collective-permute-start.15) | collective-permute-done | bytes 196640 | tf_op jit(solution)/shard_map/ppermute | solution.py:344
  37.7 1.6 %collective-permute-start.13 = (bf16[2,3,128,128]{3,2,1,0:T(8,128)(2,1)S(1)}, bf16[2,3,128,128]{3,2,1,0:T(8,128)(2,1)S(1)}, u32[]{:S(2)}, u32[]{:S(2)}) collective-permute-start(bf16[2,3,128,128]{3,2,1,0:T(8,128)(2,1)S(1)} %get-tuple-element.75), channel_id=1, source_target_pairs={{0,2},{1,3},{2,0},{3,1},{4,6},{5,7},{6,4},{7,5},{8,10},{9,11},{10,... | collective-permute-start | bytes 589832 | tf_op jit(solution)/shard_map/ppermute | solution.py:336
  39.5 1.6 %collective-permute-start.22 = (bf16[4,3,128,128]{3,2,1,0:T(8,128)(2,1)S(1)}, bf16[4,3,128,128]{3,2,1,0:T(8,128)(2,1)S(1)}, u32[]{:S(2)}, u32[]{:S(2)}) collective-permute-start(bf16[4,3,128,128]{3,2,1,0:T(8,128)(2,1)S(1)} %gather.1), channel_id=1, source_target_pairs={{0,16},{16,0},{1,17},{17,1},{2,18},{18,2},{3,19},{19,3},{4,20},{20... | collective-permute-start | bytes 1179656 | tf_op jit(solution)/shard_map/ppermute | solution.py:408
  41.1 1.6 %collective-permute-start.21 = (bf16[2,3,128,128]{3,2,1,0:T(8,128)(2,1)S(1)}, bf16[2,3,128,128]{3,2,1,0:T(8,128)(2,1)S(1)}, u32[]{:S(2)}, u32[]{:S(2)}) collective-permute-start(bf16[2,3,128,128]{3,2,1,0:T(8,128)(2,1)S(1)} %join.1), channel_id=1, source_target_pairs={{0,2},{1,3},{2,0},{3,1},{4,6},{5,7},{6,4},{7,5},{8,10},{9,11},{10,... | collective-permute-start | bytes 589832 | tf_op jit(solution)/shard_map/ppermute | solution.py:336
  42.7 2.8 %collective-permute-done.13.crossed = bf16[2,3,128,128]{3,2,1,0:T(8,128)(2,1)S(1)} collective-permute-done((bf16[2,3,128,128]{3,2,1,0:T(8,128)(2,1)S(1)}, bf16[2,3,128,128]{3,2,1,0:T(8,128)(2,1)S(1)}, u32[]{:S(2)}, u32[]{:S(2)}) %collective-permute-start.13) | collective-permute-done | bytes 196640 | tf_op jit(solution)/shard_map/ppermute | solution.py:336
  45.4 0.5 collective-permute-start.10
  45.9 0.8 %unpack.6 = bf16[1,128,1536]{2,1,0:T(8,128)(2,1)} custom-call(bf16[3,128,128]{2,1,0:T(8,128)(2,1)S(1)} %get-tuple-element.88.in0, bf16[3,128,128]{2,1,0:T(8,128)(2,1)S(1)} %collective-permute-done.18.in1, bf16[3,128,128]{2,1,0:T(8,128)(2,1)S(1)} %collective-permute-done.19.in2, bf16[3,128,128]{2,1,0:T(8,128)(2,1)S(1)} %collective-permute-done.20.in3), custom_call_target="tpu_custom_call" | custom-call | tf_op jit(solution)/shard_map/unpack/pallas_call | solution.py:313
  46.7 2.4 %collective-permute-done.21.crossed = bf16[2,3,128,128]{3,2,1,0:T(8,128)(2,1)S(1)} collective-permute-done((bf16[2,3,128,128]{3,2,1,0:T(8,128)(2,1)S(1)}, bf16[2,3,128,128]{3,2,1,0:T(8,128)(2,1)S(1)}, u32[]{:S(2)}, u32[]{:S(2)}) %collective-permute-start.21) | collective-permute-done | bytes 196640 | tf_op jit(solution)/shard_map/ppermute | solution.py:336
  49.2 0.8 %unpack.5 = bf16[1,128,1536]{2,1,0:T(8,128)(2,1)} custom-call(bf16[2,3,128,128]{3,2,1,0:T(8,128)(2,1)S(1)} %get-tuple-element.87.stay, bf16[2,3,128,128]{3,2,1,0:T(8,128)(2,1)S(1)} %collective-permute-done.16.got, bf16[2,3,128,128]{3,2,1,0:T(8,128)(2,1)S(1)} %collective-permute-done.21.crossed), custom_call_target="tpu_custom_call" | custom-call | tf_op jit(solution)/shard_map/unpack/pallas_call | solution.py:313
  50.0 0.8 %unpack.4 = bf16[1,128,1536]{2,1,0:T(8,128)(2,1)} custom-call(bf16[3,128,128]{2,1,0:T(8,128)(2,1)S(1)} %get-tuple-element.68.dq0, bf16[3,128,128]{2,1,0:T(8,128)(2,1)S(1)} %collective-permute-done.10.dq1, bf16[2,3,128,128]{3,2,1,0:T(8,128)(2,1)S(1)} %collective-permute-done.13.crossed, bf16[2,3,128,128]{3,2,1,0:T(8,128)(2,1)S(1)} %collective-permute-done.17.turned), custom_call_target="tpu_custom_call" | custom-call | tf_op jit(solution)/shard_map/unpack/pallas_call | solution.py:313
  50.9 0.8 %unpack.7 = bf16[1,128,1536]{2,1,0:T(8,128)(2,1)} custom-call(bf16[4,3,128,128]{3,2,1,0:T(8,128)(2,1)S(1)} %collective-permute-done.22.groups), custom_call_target="tpu_custom_call" | custom-call | tf_op jit(solution)/shard_map/unpack/pallas_call | solution.py:313
  (30 shorter events, 1.2 us)
Async XLA Ops:
  2.3 3.2 %collective-permute-start = (bf16[3,928,128]{2,1,0:T(8,128)(2,1)S(1)}, bf16[3,928,128]{2,1,0:T(8,128)(2,1)S(1)}, u32[]{:S(2)}, u32[]{:S(2)}) collective-permute-start(bf16[3,928,128]{2,1,0:T(8,128)(2,1)S(1)} %get-tuple-element.48), channel_id=1, source_target_pairs={{0,1},{1,0},{2,3},{3,2},{4,5},{5,4},{6,7},{7,6},{8,9},{9,8},{10,11... | collective-permute-start | bytes 2138120 | tf_op jit(solution)/shard_map/ppermute | solution.py:336
  2.8 6.2 %collective-permute-start.2 = (bf16[3,128,128]{2,1,0:T(8,128)(2,1)S(1)}, bf16[3,128,128]{2,1,0:T(8,128)(2,1)S(1)}, u32[]{:S(2)}, u32[]{:S(2)}) collective-permute-start(bf16[3,128,128]{2,1,0:T(8,128)(2,1)S(1)} %get-tuple-element.51), channel_id=1, source_target_pairs={{0,2},{1,3},{2,0},{3,1},{4,6},{5,7},{6,4},{7,5},{8,10},{9,11},{10,... | collective-permute-start | bytes 294920 | tf_op jit(solution)/shard_map/ppermute | solution.py:336
  5.4 5.2 %collective-permute-start.3 = (bf16[3,128,128]{2,1,0:T(8,128)(2,1)S(1)}, bf16[3,128,128]{2,1,0:T(8,128)(2,1)S(1)}, u32[]{:S(2)}, u32[]{:S(2)}) collective-permute-start(bf16[3,128,128]{2,1,0:T(8,128)(2,1)S(1)} %get-tuple-element.52), channel_id=1, source_target_pairs={{0,3},{1,2},{2,1},{3,0},{4,7},{5,6},{6,5},{7,4},{8,11},{9,10},{10,... | collective-permute-start | bytes 294920 | tf_op jit(solution)/shard_map/ppermute | solution.py:336
  5.5 9.8 %collective-permute-start.7 = (bf16[2,3,128,128]{3,2,1,0:T(8,128)(2,1)S(1)}, bf16[2,3,128,128]{3,2,1,0:T(8,128)(2,1)S(1)}, u32[]{:S(2)}, u32[]{:S(2)}) collective-permute-start(bf16[2,3,128,128]{3,2,1,0:T(8,128)(2,1)S(1)} %get-tuple-element.60), channel_id=1, source_target_pairs={{0,2},{1,3},{2,0},{3,1},{4,6},{5,7},{6,4},{7,5},{8,10},{9,11},{10,... | collective-permute-start | bytes 589832 | tf_op jit(solution)/shard_map/ppermute | solution.py:336
  10.7 6.8 %collective-permute-start.4 = (bf16[3,256,128]{2,1,0:T(8,128)(2,1)S(1)}, bf16[3,256,128]{2,1,0:T(8,128)(2,1)S(1)}, u32[]{:S(2)}, u32[]{:S(2)}) collective-permute-start(bf16[3,256,128]{2,1,0:T(8,128)(2,1)S(1)} %get-tuple-element.54), channel_id=1, source_target_pairs={{0,4},{1,0},{2,6},{3,2},{4,8},{5,1},{6,10},{7,3},{8,12},{9,5},{10,... | collective-permute-start | bytes 589832 | tf_op jit(solution)/shard_map/ppermute | solution.py:344
  12.4 9.1 %collective-permute-start.1 = (bf16[2,3,144,128]{3,2,1,0:T(8,128)(2,1)S(1)}, bf16[2,3,144,128]{3,2,1,0:T(8,128)(2,1)S(1)}, u32[]{:S(2)}, u32[]{:S(2)}) collective-permute-start(bf16[2,3,144,128]{3,2,1,0:T(8,128)(2,1)S(1)} %get-tuple-element.50), channel_id=1, source_target_pairs={{0,2},{1,3},{2,0},{3,1},{4,6},{5,7},{6,4},{7,5},{8,10},{9,11},{10,... | collective-permute-start | bytes 663560 | tf_op jit(solution)/shard_map/ppermute | solution.py:336
  13.9 7.6 %collective-permute-start.5 = (bf16[3,256,128]{2,1,0:T(8,128)(2,1)S(1)}, bf16[3,256,128]{2,1,0:T(8,128)(2,1)S(1)}, u32[]{:S(2)}, u32[]{:S(2)}) collective-permute-start(bf16[3,256,128]{2,1,0:T(8,128)(2,1)S(1)} %get-tuple-element.55), channel_id=1, source_target_pairs={{0,1},{1,5},{2,3},{3,7},{4,0},{5,9},{6,2},{7,11},{8,4},{9,13},{10,... | collective-permute-start | bytes 589832 | tf_op jit(solution)/shard_map/ppermute | solution.py:344
  13.9 10.2 %collective-permute-start.6 = (bf16[2,3,128,128]{3,2,1,0:T(8,128)(2,1)S(1)}, bf16[2,3,128,128]{3,2,1,0:T(8,128)(2,1)S(1)}, u32[]{:S(2)}, u32[]{:S(2)}) collective-permute-start(bf16[2,3,128,128]{3,2,1,0:T(8,128)(2,1)S(1)} %get-tuple-element.59), channel_id=1, source_target_pairs={{0,2},{1,3},{2,0},{3,1},{4,6},{5,7},{6,4},{7,5},{8,10},{9,11},{10,... | collective-permute-start | bytes 589832 | tf_op jit(solution)/shard_map/ppermute | solution.py:336
  15.5 8.6 %collective-permute-start.8 = (bf16[3,256,128]{2,1,0:T(8,128)(2,1)S(1)}, bf16[3,256,128]{2,1,0:T(8,128)(2,1)S(1)}, u32[]{:S(2)}, u32[]{:S(2)}) collective-permute-start(bf16[3,256,128]{2,1,0:T(8,128)(2,1)S(1)} %get-tuple-element.61), channel_id=1, source_target_pairs={{0,4},{1,0},{2,6},{3,2},{4,8},{5,1},{6,10},{7,3},{8,12},{9,5},{10,... | collective-permute-start | bytes 589832 | tf_op jit(solution)/shard_map/ppermute | solution.py:344
  17.5 6.6 %collective-permute-start.9 = (bf16[3,256,128]{2,1,0:T(8,128)(2,1)S(1)}, bf16[3,256,128]{2,1,0:T(8,128)(2,1)S(1)}, u32[]{:S(2)}, u32[]{:S(2)}) collective-permute-start(bf16[3,256,128]{2,1,0:T(8,128)(2,1)S(1)} %get-tuple-element.62), channel_id=1, source_target_pairs={{0,1},{1,5},{2,3},{3,7},{4,0},{5,9},{6,2},{7,11},{8,4},{9,13},{10,... | collective-permute-start | bytes 589832 | tf_op jit(solution)/shard_map/ppermute | solution.py:344
  24.9 7.1 %collective-permute-start.11 = (bf16[3,256,128]{2,1,0:T(8,128)(2,1)S(1)}, bf16[3,256,128]{2,1,0:T(8,128)(2,1)S(1)}, u32[]{:S(2)}, u32[]{:S(2)}) collective-permute-start(bf16[3,256,128]{2,1,0:T(8,128)(2,1)S(1)} %get-tuple-element.72), channel_id=1, source_target_pairs={{0,4},{1,0},{2,6},{3,2},{4,8},{5,1},{6,10},{7,3},{8,12},{9,5},{10,... | collective-permute-start | bytes 589832 | tf_op jit(solution)/shard_map/ppermute | solution.py:344
  26.7 5.7 %collective-permute-start.12 = (bf16[3,256,128]{2,1,0:T(8,128)(2,1)S(1)}, bf16[3,256,128]{2,1,0:T(8,128)(2,1)S(1)}, u32[]{:S(2)}, u32[]{:S(2)}) collective-permute-start(bf16[3,256,128]{2,1,0:T(8,128)(2,1)S(1)} %get-tuple-element.73), channel_id=1, source_target_pairs={{0,1},{1,5},{2,3},{3,7},{4,0},{5,9},{6,2},{7,11},{8,4},{9,13},{10,... | collective-permute-start | bytes 589832 | tf_op jit(solution)/shard_map/ppermute | solution.py:344
  30.0 7.5 %collective-permute-start.15 = (bf16[3,256,128]{2,1,0:T(8,128)(2,1)S(1)}, bf16[3,256,128]{2,1,0:T(8,128)(2,1)S(1)}, u32[]{:S(2)}, u32[]{:S(2)}) collective-permute-start(bf16[3,256,128]{2,1,0:T(8,128)(2,1)S(1)} %get-tuple-element.80), channel_id=1, source_target_pairs={{0,1},{1,5},{2,3},{3,7},{4,0},{5,9},{6,2},{7,11},{8,4},{9,13},{10,... | collective-permute-start | bytes 589832 | tf_op jit(solution)/shard_map/ppermute | solution.py:344
  30.0 7.5 %collective-permute-start.14 = (bf16[3,256,128]{2,1,0:T(8,128)(2,1)S(1)}, bf16[3,256,128]{2,1,0:T(8,128)(2,1)S(1)}, u32[]{:S(2)}, u32[]{:S(2)}) collective-permute-start(bf16[3,256,128]{2,1,0:T(8,128)(2,1)S(1)} %get-tuple-element.78), channel_id=1, source_target_pairs={{0,4},{1,0},{2,6},{3,2},{4,8},{5,1},{6,10},{7,3},{8,12},{9,5},{10,... | collective-permute-start | bytes 589832 | tf_op jit(solution)/shard_map/ppermute | solution.py:344
  32.5 6.8 %collective-permute-start.18 = (bf16[3,128,128]{2,1,0:T(8,128)(2,1)S(1)}, bf16[3,128,128]{2,1,0:T(8,128)(2,1)S(1)}, u32[]{:S(2)}, u32[]{:S(2)}) collective-permute-start(bf16[3,128,128]{2,1,0:T(8,128)(2,1)S(1)} %get-tuple-element.84), channel_id=1, source_target_pairs={{0,1},{1,0},{2,3},{3,2},{4,5},{5,4},{6,7},{7,6},{8,9},{9,8},{10,11... | collective-permute-start | bytes 294920 | tf_op jit(solution)/shard_map/ppermute | solution.py:336
  32.6 6.7 %collective-permute-start.19 = (bf16[3,128,128]{2,1,0:T(8,128)(2,1)S(1)}, bf16[3,128,128]{2,1,0:T(8,128)(2,1)S(1)}, u32[]{:S(2)}, u32[]{:S(2)}) collective-permute-start(bf16[3,128,128]{2,1,0:T(8,128)(2,1)S(1)} %get-tuple-element.85), channel_id=1, source_target_pairs={{0,2},{1,3},{2,0},{3,1},{4,6},{5,7},{6,4},{7,5},{8,10},{9,11},{10,... | collective-permute-start | bytes 294920 | tf_op jit(solution)/shard_map/ppermute | solution.py:336
  34.2 5.3 %collective-permute-start.20 = (bf16[3,128,128]{2,1,0:T(8,128)(2,1)S(1)}, bf16[3,128,128]{2,1,0:T(8,128)(2,1)S(1)}, u32[]{:S(2)}, u32[]{:S(2)}) collective-permute-start(bf16[3,128,128]{2,1,0:T(8,128)(2,1)S(1)} %get-tuple-element.86), channel_id=1, source_target_pairs={{0,3},{1,2},{2,1},{3,0},{4,7},{5,6},{6,5},{7,4},{8,11},{9,10},{10,... | collective-permute-start | bytes 294920 | tf_op jit(solution)/shard_map/ppermute | solution.py:336
  37.6 3.5 %collective-permute-start.16 = (bf16[2,3,128,128]{3,2,1,0:T(8,128)(2,1)S(1)}, bf16[2,3,128,128]{3,2,1,0:T(8,128)(2,1)S(1)}, u32[]{:S(2)}, u32[]{:S(2)}) collective-permute-start(bf16[2,3,128,128]{3,2,1,0:T(8,128)(2,1)S(1)} %get-tuple-element.81), channel_id=1, source_target_pairs={{0,1},{1,0},{2,3},{3,2},{4,5},{5,4},{6,7},{7,6},{8,9},{9,8},{10,11... | collective-permute-start | bytes 589832 | tf_op jit(solution)/shard_map/ppermute | solution.py:336
  37.7 7.8 %collective-permute-start.13 = (bf16[2,3,128,128]{3,2,1,0:T(8,128)(2,1)S(1)}, bf16[2,3,128,128]{3,2,1,0:T(8,128)(2,1)S(1)}, u32[]{:S(2)}, u32[]{:S(2)}) collective-permute-start(bf16[2,3,128,128]{3,2,1,0:T(8,128)(2,1)S(1)} %get-tuple-element.75), channel_id=1, source_target_pairs={{0,2},{1,3},{2,0},{3,1},{4,6},{5,7},{6,4},{7,5},{8,10},{9,11},{10,... | collective-permute-start | bytes 589832 | tf_op jit(solution)/shard_map/ppermute | solution.py:336
  39.5 11.4 %collective-permute-start.22 = (bf16[4,3,128,128]{3,2,1,0:T(8,128)(2,1)S(1)}, bf16[4,3,128,128]{3,2,1,0:T(8,128)(2,1)S(1)}, u32[]{:S(2)}, u32[]{:S(2)}) collective-permute-start(bf16[4,3,128,128]{3,2,1,0:T(8,128)(2,1)S(1)} %gather.1), channel_id=1, source_target_pairs={{0,16},{16,0},{1,17},{17,1},{2,18},{18,2},{3,19},{19,3},{4,20},{20... | collective-permute-start | bytes 1179656 | tf_op jit(solution)/shard_map/ppermute | solution.py:408
  41.1 8.1 %collective-permute-start.21 = (bf16[2,3,128,128]{3,2,1,0:T(8,128)(2,1)S(1)}, bf16[2,3,128,128]{3,2,1,0:T(8,128)(2,1)S(1)}, u32[]{:S(2)}, u32[]{:S(2)}) collective-permute-start(bf16[2,3,128,128]{3,2,1,0:T(8,128)(2,1)S(1)} %join.1), channel_id=1, source_target_pairs={{0,2},{1,3},{2,0},{3,1},{4,6},{5,7},{6,4},{7,5},{8,10},{9,11},{10,... | collective-permute-start | bytes 589832 | tf_op jit(solution)/shard_map/ppermute | solution.py:336
  45.4 4.6 %collective-permute-start.17 = (bf16[2,3,128,128]{3,2,1,0:T(8,128)(2,1)S(1)}, bf16[2,3,128,128]{3,2,1,0:T(8,128)(2,1)S(1)}, u32[]{:S(2)}, u32[]{:S(2)}) collective-permute-start(bf16[2,3,128,128]{3,2,1,0:T(8,128)(2,1)S(1)} %collective-permute-done.13.crossed), channel_id=1, source_target_pairs={{0,1},{1,0},{2,3},{3,2},{4,5},{5,4},{6,7},{7,6},{8,9},{9,8},{10,11... | collective-permute-start | bytes 589832 | tf_op jit(solution)/shard_map/ppermute | solution.py:336
  45.4 4.6 %collective-permute-start.10 = (bf16[3,128,128]{2,1,0:T(8,128)(2,1)S(1)}, bf16[3,128,128]{2,1,0:T(8,128)(2,1)S(1)}, u32[]{:S(2)}, u32[]{:S(2)}) collective-permute-start(bf16[3,128,128]{2,1,0:T(8,128)(2,1)S(1)} %get-tuple-element.69), channel_id=1, source_target_pairs={{0,1},{1,0},{2,3},{3,2},{4,5},{5,4},{6,7},{7,6},{8,9},{9,8},{10,11... | collective-permute-start | bytes 294920 | tf_op jit(solution)/shard_map/ppermute | solution.py:336

commit v8 on v7

--- a/solution.py
+++ b/solution.py
@@ -263,7 +263,7 @@
         groups[jnp.bitwise_xor(me, step)] = source[...]
 
 
-def write_out(parts, out, out_hbm, sems, wanted=None):
+def fill_out(parts, out, out_hbm, sems, wanted=None):
     copies = pieces(out, out_hbm, sems)
     count = BLK // len(copies)
     for n, copy in enumerate(copies):
@@ -275,29 +275,31 @@
                     value = jnp.where(wanted, value, jnp.zeros_like(value))
                 out[0, rows, head_columns(group, h)] = value
         copy.start()
+    return copies
+
+
+def by_step(*sources):
+    me = member()
+    return [(jnp.bitwise_xor(me, step), source) for step, source in enumerate(sources)]
+
+
+def unpack_kernel(in0, in1, in2, in3, out_hbm, out, sems):
+    for copy in fill_out(by_step(in0, in1, in2, in3), out, out_hbm, sems):
+        copy.wait()
+
+
+def unpack_last_kernel(
+    dq0, dq1, dq23, turned, stay, got, crossed, groups,
+    dq_hbm, dk_hbm, passed_hbm, dq, dk, passed, sems,
+):
+    copies = fill_out(by_step(dq0, dq1, dq23.at[0], turned.at[1]), dq, dq_hbm, sems.at[0])
+    sources = by_step(stay.at[0], got.at[0], crossed.at[0], crossed.at[1])
+    copies += fill_out(sources, dk, dk_hbm, sems.at[1])
+    wanted = lax.axis_index("section") < lax.axis_size("section") - 1
+    sources = [(group, groups.at[group]) for group in range(TEAM)]
+    copies += fill_out(sources, passed, passed_hbm, sems.at[2], wanted)
     for copy in copies:
         copy.wait()
-
-
-def unpack_kernel(in0, in1, in2, in3, out_hbm, out, sems):
-    me = member()
-    sources = (in0, in1, in2, in3)
-    parts = [(jnp.bitwise_xor(me, step), source) for step, source in enumerate(sources)]
-    write_out(parts, out, out_hbm, sems)
-
-
-def unpack_joined_kernel(stay, got, crossed, *rest):
-    unpack_kernel(stay.at[0], got.at[0], crossed.at[0], crossed.at[1], *rest)
-
-
-def unpack_turned_kernel(dq0, dq1, crossed, turned, *rest):
-    unpack_kernel(dq0, dq1, crossed.at[0], turned.at[1], *rest)
-
-
-def unpack_passed_kernel(groups, out_hbm, out, sems):
-    wanted = lax.axis_index("section") < lax.axis_size("section") - 1
-    parts = [(group, groups.at[group]) for group in range(TEAM)]
-    write_out(parts, out, out_hbm, sems, wanted)
 
 
 def struct(*shape, dtype=bf16):
@@ -420,10 +422,14 @@
     dv[0] = after(dv[0], joined)
     grad_value = unpack(unpack_kernel, *dv)
     dq23 = after(dq23, got)
-    grad_query = unpack(unpack_turned_kernel, dq0, swap(dq1, 1), dq23, swap(dq23, 1))
-    grad_key = unpack(unpack_joined_kernel, stay, got, crossed)
-    passed = after(passed, grad_key)
-    handoff = unpack(unpack_passed_kernel, passed)
+    out = struct(1, BLK, width)
+    grad_query, grad_key, handoff = call(
+        unpack_last_kernel,
+        "unpack",
+        (out,) * 3,
+        [rows_in] * 3 + [pltpu.SemaphoreType.DMA((3, CUTS))],
+        to=HBM,
+    )(dq0, swap(dq1, 1), dq23, swap(dq23, 1), stay, got, crossed, passed)
     return (grad_query, grad_key, grad_value, handoff)
 
 

time: 51.8 us -> 52.2 us (level)
  waiting for transfers between devices: 17.6 us -> 19.2 us
  Pallas kernels: 11.2 us -> 9.89 us
    ppermute x1, waiting for transfers between devices: 0.03 us -> 1.67 us  [shards(): lax.ppermute(late, 'section', [(s, (s - 1) % sections) for s in range(sec...]
    pallas_call x16 -> x14, Pallas kernels: 11.2 us -> 9.89 us  [run(): pl.pallas_call(kernel, out_shape=jax.tree.map(lambda out: to(out.shape, o...]
  transfers between devices with their start and end apart: 23 -> 23, of which waited for: 10 -> 12; matrix products, arithmetic and copies ran while one was open for 0% -> 0% of each run, Pallas kernels for 15% -> 12%
where the time goes in v8:
time: 52.2 us; the launch traced here: 52 us
  starting transfers between devices  22.1 us (42%)
  waiting for transfers between devices  19.2 us (37%)
  Pallas kernels  9.89 us (19%)
  between operations  0.74 us (1%)
    ppermute x14, starting transfers between devices, swap(): return lax.ppermute(array, 'ctx', [(i, i ^ step) for i in range(ctx)])  13 us
    ppermute x14, waiting for transfers between devices, swap(): return lax.ppermute(array, 'ctx', [(i, i ^ step) for i in range(ctx)])  10.3 us
    pallas_call x14, Pallas kernels, run(): pl.pallas_call(kernel, out_shape=jax.tree.map(lambda out: to(out.shape, o...  9.89 us
    ppermute x8, starting transfers between devices, ring(): return lax.ppermute(array, 'ctx', pairs)  7.56 us
    ppermute x8, waiting for transfers between devices, ring(): return lax.ppermute(array, 'ctx', pairs)  7.31 us
    ppermute x1, waiting for transfers between devices, shards(): lax.ppermute(late, 'section', [(s, (s - 1) % sections) for s in range(sec...  1.67 us
    ppermute x1, starting transfers between devices, shards(): lax.ppermute(late, 'section', [(s, (s - 1) % sections) for s in range(sec...  1.55 us
  transfers between devices with their start and end apart: 23, of which 12 were waited for; matrix products, arithmetic and copies ran while one was open for 0% of the time, Pallas kernels for 12%

profile of v8, /device:TPU:0, one launch (start us, length us, event | category | flops | bytes accessed | tf_op | source)
XLA Modules:
  0.0 52.0 jit_solution(1448228536771574248)
XLA Ops:
  0.6 1.7 %pack.1 = (bf16[3,528,128]{2,1,0:T(8,128)(2,1)S(1)}, bf16[3,928,128]{2,1,0:T(8,128)(2,1)S(1)}, bf16[3,128,128]{2,1,0:T(8,128)(2,1)S(1)}, bf16[3,128,128]{2,1,0:T(8,128)(2,1)S(1)}, bf16[3,400,128]{2,1,0:T(8,128)(2,1)S(1)}) custom-call(bf16[1,128,1536]{2,1,0:T(8,128)(2,1)} %k_hbm.1, bf16[1,128,1536]{2,1,0:T(8,128)(2,1)} %q_hbm.1, bf16[1,128,1536]{2,1,0:T(8,128)(2,1)} %g_hbm.1, ...), custom_call_target="tpu_custom_call" | custom-call | tf_op jit(solution)/shard_map/pack/pallas_call | solution.py:315
  2.3 0.5 collective-permute-start
  2.8 2.6 %collective-permute-start.2 = (bf16[3,128,128]{2,1,0:T(8,128)(2,1)S(1)}, bf16[3,128,128]{2,1,0:T(8,128)(2,1)S(1)}, u32[]{:S(2)}, u32[]{:S(2)}) collective-permute-start(bf16[3,128,128]{2,1,0:T(8,128)(2,1)S(1)} %get-tuple-element.53), channel_id=1, source_target_pairs={{0,2},{1,3},{2,0},{3,1},{4,6},{5,7},{6,4},{7,5},{8,10},{9,11},{10,... | collective-permute-start | bytes 294920 | tf_op jit(solution)/shard_map/ppermute | solution.py:338
  5.5 2.1 %collective-permute-start.7 = (bf16[2,3,128,128]{3,2,1,0:T(8,128)(2,1)S(1)}, bf16[2,3,128,128]{3,2,1,0:T(8,128)(2,1)S(1)}, u32[]{:S(2)}, u32[]{:S(2)}) collective-permute-start(bf16[2,3,128,128]{3,2,1,0:T(8,128)(2,1)S(1)} %get-tuple-element.62), channel_id=1, source_target_pairs={{0,2},{1,3},{2,0},{3,1},{4,6},{5,7},{6,4},{7,5},{8,10},{9,11},{10,... | collective-permute-start | bytes 589832 | tf_op jit(solution)/shard_map/ppermute | solution.py:338
  7.6 1.4 %collective-permute-done.2.two = bf16[3,128,128]{2,1,0:T(8,128)(2,1)S(1)} collective-permute-done((bf16[3,128,128]{2,1,0:T(8,128)(2,1)S(1)}, bf16[3,128,128]{2,1,0:T(8,128)(2,1)S(1)}, u32[]{:S(2)}, u32[]{:S(2)}) %collective-permute-start.2) | collective-permute-done | bytes 98336 | tf_op jit(solution)/shard_map/ppermute | solution.py:338
  9.1 1.6 %collective-permute-done.3.three = bf16[3,128,128]{2,1,0:T(8,128)(2,1)S(1)} collective-permute-done((bf16[3,128,128]{2,1,0:T(8,128)(2,1)S(1)}, bf16[3,128,128]{2,1,0:T(8,128)(2,1)S(1)}, u32[]{:S(2)}, u32[]{:S(2)}) %collective-permute-start.3) | collective-permute-done | bytes 98336 | tf_op jit(solution)/shard_map/ppermute | solution.py:338
  10.7 1.6 %collective-permute-start.4 = (bf16[3,256,128]{2,1,0:T(8,128)(2,1)S(1)}, bf16[3,256,128]{2,1,0:T(8,128)(2,1)S(1)}, u32[]{:S(2)}, u32[]{:S(2)}) collective-permute-start(bf16[3,256,128]{2,1,0:T(8,128)(2,1)S(1)} %get-tuple-element.56), channel_id=1, source_target_pairs={{0,4},{1,0},{2,6},{3,2},{4,8},{5,1},{6,10},{7,3},{8,12},{9,5},{10,... | collective-permute-start | bytes 589832 | tf_op jit(solution)/shard_map/ppermute | solution.py:346
  12.4 1.5 %collective-permute-start.1 = (bf16[2,3,144,128]{3,2,1,0:T(8,128)(2,1)S(1)}, bf16[2,3,144,128]{3,2,1,0:T(8,128)(2,1)S(1)}, u32[]{:S(2)}, u32[]{:S(2)}) collective-permute-start(bf16[2,3,144,128]{3,2,1,0:T(8,128)(2,1)S(1)} %get-tuple-element.52), channel_id=1, source_target_pairs={{0,2},{1,3},{2,0},{3,1},{4,6},{5,7},{6,4},{7,5},{8,10},{9,11},{10,... | collective-permute-start | bytes 663560 | tf_op jit(solution)/shard_map/ppermute | solution.py:338
  13.9 0.5 collective-permute-start.6
  14.4 1.0 %collective-permute-done.7.pair = bf16[2,3,128,128]{3,2,1,0:T(8,128)(2,1)S(1)} collective-permute-done((bf16[2,3,128,128]{3,2,1,0:T(8,128)(2,1)S(1)}, bf16[2,3,128,128]{3,2,1,0:T(8,128)(2,1)S(1)}, u32[]{:S(2)}, u32[]{:S(2)}) %collective-permute-start.7) | collective-permute-done | bytes 196640 | tf_op jit(solution)/shard_map/ppermute | solution.py:338
  15.5 2.0 %collective-permute-start.8 = (bf16[3,256,128]{2,1,0:T(8,128)(2,1)S(1)}, bf16[3,256,128]{2,1,0:T(8,128)(2,1)S(1)}, u32[]{:S(2)}, u32[]{:S(2)}) collective-permute-start(bf16[3,256,128]{2,1,0:T(8,128)(2,1)S(1)} %get-tuple-element.63), channel_id=1, source_target_pairs={{0,4},{1,0},{2,6},{3,2},{4,8},{5,1},{6,10},{7,3},{8,12},{9,5},{10,... | collective-permute-start | bytes 589832 | tf_op jit(solution)/shard_map/ppermute | solution.py:346
  17.5 4.0 %collective-permute-done.5.halo2 = bf16[3,256,128]{2,1,0:T(8,128)(2,1)S(1)} collective-permute-done((bf16[3,256,128]{2,1,0:T(8,128)(2,1)S(1)}, bf16[3,256,128]{2,1,0:T(8,128)(2,1)S(1)}, u32[]{:S(2)}, u32[]{:S(2)}) %collective-permute-start.5) | collective-permute-done | bytes 196640 | tf_op jit(solution)/shard_map/ppermute | solution.py:346
  21.4 1.8 %probs.1 = (bf16[3,1024,512]{2,1,0:T(8,128)(2,1)S(1)}, bf16[3,1024,128]{2,1,0:T(8,128)(2,1)S(1)}, bf16[3,512,128]{2,1,0:T(8,128)(2,1)S(1)}) custom-call(bf16[3,528,128]{2,1,0:T(8,128)(2,1)S(1)} %get-tuple-element.49.own, bf16[3,928,128]{2,1,0:T(8,128)(2,1)S(1)} %collective-permute-done.side, bf16[2,3,144,128]{3,2,1,0:T(8,128)(2,1)S(1)} %collective-permute-done.1.crossed, ...), custom_call_target="tpu_custom_call" | custom-call | tf_op jit(solution)/shard_map/probs/pallas_call | solution.py:315
  23.2 0.8 %collective-permute-done.6.crossed = bf16[2,3,128,128]{3,2,1,0:T(8,128)(2,1)S(1)} collective-permute-done((bf16[2,3,128,128]{3,2,1,0:T(8,128)(2,1)S(1)}, bf16[2,3,128,128]{3,2,1,0:T(8,128)(2,1)S(1)}, u32[]{:S(2)}, u32[]{:S(2)}) %collective-permute-start.6) | collective-permute-done | bytes 196640 | tf_op jit(solution)/shard_map/ppermute | solution.py:338
  24.1 0.8 %values.1 = (bf16[3,512,128]{2,1,0:T(8,128)(2,1)S(1)}, f32[3,512,128]{2,1,0:T(8,128)S(1)}, bf16[3,256,128]{2,1,0:T(8,128)(2,1)S(1)}, bf16[3,256,128]{2,1,0:T(8,128)(2,1)S(1)}) custom-call(bf16[3,1024,512]{2,1,0:T(8,128)(2,1)S(1)} %get-tuple-element.58.probs, bf16[3,528,128]{2,1,0:T(8,128)(2,1)S(1)} %get-tuple-element.49.own, ...), custom_call_target="tpu_custom_call" | custom-call | tf_op jit(solution)/shard_map/values/pallas_call | solution.py:315
  24.9 1.8 %collective-permute-start.11 = (bf16[3,256,128]{2,1,0:T(8,128)(2,1)S(1)}, bf16[3,256,128]{2,1,0:T(8,128)(2,1)S(1)}, u32[]{:S(2)}, u32[]{:S(2)}) collective-permute-start(bf16[3,256,128]{2,1,0:T(8,128)(2,1)S(1)} %get-tuple-element.74), channel_id=1, source_target_pairs={{0,4},{1,0},{2,6},{3,2},{4,8},{5,1},{6,10},{7,3},{8,12},{9,5},{10,... | collective-permute-start | bytes 589832 | tf_op jit(solution)/shard_map/ppermute | solution.py:346
  26.7 2.5 %scores.1 = (bf16[3,1024,512]{2,1,0:T(8,128)(2,1)S(1)}, f32[3,512,128]{2,1,0:T(8,128)S(1)}, bf16[3,256,128]{2,1,0:T(8,128)(2,1)S(1)}, bf16[3,256,128]{2,1,0:T(8,128)(2,1)S(1)}) custom-call(bf16[3,1024,512]{2,1,0:T(8,128)(2,1)S(1)} %get-tuple-element.58.probs, bf16[3,512,128]{2,1,0:T(8,128)(2,1)S(1)} %get-tuple-element.59.qs, ...), custom_call_target="tpu_custom_call" | custom-call | tf_op jit(solution)/shard_map/scores/pallas_call | solution.py:315
  29.2 0.8 %queries.1 = (bf16[3,128,128]{2,1,0:T(8,128)(2,1)S(1)}, bf16[3,128,128]{2,1,0:T(8,128)(2,1)S(1)}, bf16[2,3,128,128]{3,2,1,0:T(8,128)(2,1)S(1)}) custom-call(bf16[3,1024,512]{2,1,0:T(8,128)(2,1)S(1)} %get-tuple-element.68.ss, bf16[3,1024,128]{2,1,0:T(8,128)(2,1)S(1)} %get-tuple-element.69.ks), custom_call_target="tpu_custom_call" | custom-call | tf_op jit(solution)/shard_map/queries/pallas_call | solution.py:315
  30.0 2.0 %collective-permute-start.14 = (bf16[3,256,128]{2,1,0:T(8,128)(2,1)S(1)}, bf16[3,256,128]{2,1,0:T(8,128)(2,1)S(1)}, u32[]{:S(2)}, u32[]{:S(2)}) collective-permute-start(bf16[3,256,128]{2,1,0:T(8,128)(2,1)S(1)} %get-tuple-element.80), channel_id=1, source_target_pairs={{0,4},{1,0},{2,6},{3,2},{4,8},{5,1},{6,10},{7,3},{8,12},{9,5},{10,... | collective-permute-start | bytes 589832 | tf_op jit(solution)/shard_map/ppermute | solution.py:346
  32.0 0.3 collective-permute-done.12.ring2
  32.6 1.6 %collective-permute-start.19 = (bf16[3,128,128]{2,1,0:T(8,128)(2,1)S(1)}, bf16[3,128,128]{2,1,0:T(8,128)(2,1)S(1)}, u32[]{:S(2)}, u32[]{:S(2)}) collective-permute-start(bf16[3,128,128]{2,1,0:T(8,128)(2,1)S(1)} %get-tuple-element.87), channel_id=1, source_target_pairs={{0,2},{1,3},{2,0},{3,1},{4,6},{5,7},{6,4},{7,5},{8,10},{9,11},{10,... | collective-permute-start | bytes 294920 | tf_op jit(solution)/shard_map/ppermute | solution.py:338
  34.2 0.3 collective-permute-start.20
  34.5 3.0 %collective-permute-done.15.ring2 = bf16[3,256,128]{2,1,0:T(8,128)(2,1)S(1)} collective-permute-done((bf16[3,256,128]{2,1,0:T(8,128)(2,1)S(1)}, bf16[3,256,128]{2,1,0:T(8,128)(2,1)S(1)}, u32[]{:S(2)}, u32[]{:S(2)}) %collective-permute-start.15) | collective-permute-done | bytes 196640 | tf_op jit(solution)/shard_map/ppermute | solution.py:346
  37.7 1.6 %collective-permute-start.13 = (bf16[2,3,128,128]{3,2,1,0:T(8,128)(2,1)S(1)}, bf16[2,3,128,128]{3,2,1,0:T(8,128)(2,1)S(1)}, u32[]{:S(2)}, u32[]{:S(2)}) collective-permute-start(bf16[2,3,128,128]{3,2,1,0:T(8,128)(2,1)S(1)} %get-tuple-element.77), channel_id=1, source_target_pairs={{0,2},{1,3},{2,0},{3,1},{4,6},{5,7},{6,4},{7,5},{8,10},{9,11},{10,... | collective-permute-start | bytes 589832 | tf_op jit(solution)/shard_map/ppermute | solution.py:338
  39.5 1.6 %collective-permute-start.22 = (bf16[4,3,128,128]{3,2,1,0:T(8,128)(2,1)S(1)}, bf16[4,3,128,128]{3,2,1,0:T(8,128)(2,1)S(1)}, u32[]{:S(2)}, u32[]{:S(2)}) collective-permute-start(bf16[4,3,128,128]{3,2,1,0:T(8,128)(2,1)S(1)} %gather.1), channel_id=1, source_target_pairs={{0,16},{16,0},{1,17},{17,1},{2,18},{18,2},{3,19},{19,3},{4,20},{20... | collective-permute-start | bytes 1179656 | tf_op jit(solution)/shard_map/ppermute | solution.py:410
  41.1 1.6 %collective-permute-start.21 = (bf16[2,3,128,128]{3,2,1,0:T(8,128)(2,1)S(1)}, bf16[2,3,128,128]{3,2,1,0:T(8,128)(2,1)S(1)}, u32[]{:S(2)}, u32[]{:S(2)}) collective-permute-start(bf16[2,3,128,128]{3,2,1,0:T(8,128)(2,1)S(1)} %join.1), channel_id=1, source_target_pairs={{0,2},{1,3},{2,0},{3,1},{4,6},{5,7},{6,4},{7,5},{8,10},{9,11},{10,... | collective-permute-start | bytes 589832 | tf_op jit(solution)/shard_map/ppermute | solution.py:338
  42.7 2.8 %collective-permute-done.13.dq23 = bf16[2,3,128,128]{3,2,1,0:T(8,128)(2,1)S(1)} collective-permute-done((bf16[2,3,128,128]{3,2,1,0:T(8,128)(2,1)S(1)}, bf16[2,3,128,128]{3,2,1,0:T(8,128)(2,1)S(1)}, u32[]{:S(2)}, u32[]{:S(2)}) %collective-permute-start.13) | collective-permute-done | bytes 196640 | tf_op jit(solution)/shard_map/ppermute | solution.py:338
  45.4 0.5 collective-permute-start.10
  45.9 0.8 %unpack.3 = bf16[1,128,1536]{2,1,0:T(8,128)(2,1)} custom-call(bf16[3,128,128]{2,1,0:T(8,128)(2,1)S(1)} %get-tuple-element.92.in0, bf16[3,128,128]{2,1,0:T(8,128)(2,1)S(1)} %collective-permute-done.18.in1, bf16[3,128,128]{2,1,0:T(8,128)(2,1)S(1)} %collective-permute-done.19.in2, bf16[3,128,128]{2,1,0:T(8,128)(2,1)S(1)} %collective-permute-done.20.in3), custom_call_target="tpu_custom_call" | custom-call | tf_op jit(solution)/shard_map/unpack/pallas_call | solution.py:315
  47.0 2.2 %collective-permute-done.21.crossed = bf16[2,3,128,128]{3,2,1,0:T(8,128)(2,1)S(1)} collective-permute-done((bf16[2,3,128,128]{3,2,1,0:T(8,128)(2,1)S(1)}, bf16[2,3,128,128]{3,2,1,0:T(8,128)(2,1)S(1)}, u32[]{:S(2)}, u32[]{:S(2)}) %collective-permute-start.21) | collective-permute-done | bytes 196640 | tf_op jit(solution)/shard_map/ppermute | solution.py:338
  49.2 1.7 %collective-permute-done.22.groups = bf16[4,3,128,128]{3,2,1,0:T(8,128)(2,1)S(1)} collective-permute-done((bf16[4,3,128,128]{3,2,1,0:T(8,128)(2,1)S(1)}, bf16[4,3,128,128]{3,2,1,0:T(8,128)(2,1)S(1)}, u32[]{:S(2)}, u32[]{:S(2)}) %collective-permute-start.22) | collective-permute-done | bytes 393248 | tf_op jit(solution)/shard_map/ppermute | solution.py:410
  50.9 1.1 %unpack.2 = (bf16[1,128,1536]{2,1,0:T(8,128)(2,1)}, bf16[1,128,1536]{2,1,0:T(8,128)(2,1)}, bf16[1,128,1536]{2,1,0:T(8,128)(2,1)}) custom-call(bf16[3,128,128]{2,1,0:T(8,128)(2,1)S(1)} %get-tuple-element.70.dq0, bf16[3,128,128]{2,1,0:T(8,128)(2,1)S(1)} %collective-permute-done.10.dq1, bf16[2,3,128,128]{3,2,1,0:T(8,128)(2,1)S(1)} %collective-permute-done.13.dq23, ...), custom_call_target="tpu_custom_call" | custom-call | tf_op jit(solution)/shard_map/unpack/pallas_call | solution.py:315
  (28 shorter events, 1.2 us)
Async XLA Ops:
  2.3 3.2 %collective-permute-start = (bf16[3,928,128]{2,1,0:T(8,128)(2,1)S(1)}, bf16[3,928,128]{2,1,0:T(8,128)(2,1)S(1)}, u32[]{:S(2)}, u32[]{:S(2)}) collective-permute-start(bf16[3,928,128]{2,1,0:T(8,128)(2,1)S(1)} %get-tuple-element.50), channel_id=1, source_target_pairs={{0,1},{1,0},{2,3},{3,2},{4,5},{5,4},{6,7},{7,6},{8,9},{9,8},{10,11... | collective-permute-start | bytes 2138120 | tf_op jit(solution)/shard_map/ppermute | solution.py:338
  2.8 6.2 %collective-permute-start.2 = (bf16[3,128,128]{2,1,0:T(8,128)(2,1)S(1)}, bf16[3,128,128]{2,1,0:T(8,128)(2,1)S(1)}, u32[]{:S(2)}, u32[]{:S(2)}) collective-permute-start(bf16[3,128,128]{2,1,0:T(8,128)(2,1)S(1)} %get-tuple-element.53), channel_id=1, source_target_pairs={{0,2},{1,3},{2,0},{3,1},{4,6},{5,7},{6,4},{7,5},{8,10},{9,11},{10,... | collective-permute-start | bytes 294920 | tf_op jit(solution)/shard_map/ppermute | solution.py:338
  5.4 5.2 %collective-permute-start.3 = (bf16[3,128,128]{2,1,0:T(8,128)(2,1)S(1)}, bf16[3,128,128]{2,1,0:T(8,128)(2,1)S(1)}, u32[]{:S(2)}, u32[]{:S(2)}) collective-permute-start(bf16[3,128,128]{2,1,0:T(8,128)(2,1)S(1)} %get-tuple-element.54), channel_id=1, source_target_pairs={{0,3},{1,2},{2,1},{3,0},{4,7},{5,6},{6,5},{7,4},{8,11},{9,10},{10,... | collective-permute-start | bytes 294920 | tf_op jit(solution)/shard_map/ppermute | solution.py:338
  5.5 9.8 %collective-permute-start.7 = (bf16[2,3,128,128]{3,2,1,0:T(8,128)(2,1)S(1)}, bf16[2,3,128,128]{3,2,1,0:T(8,128)(2,1)S(1)}, u32[]{:S(2)}, u32[]{:S(2)}) collective-permute-start(bf16[2,3,128,128]{3,2,1,0:T(8,128)(2,1)S(1)} %get-tuple-element.62), channel_id=1, source_target_pairs={{0,2},{1,3},{2,0},{3,1},{4,6},{5,7},{6,4},{7,5},{8,10},{9,11},{10,... | collective-permute-start | bytes 589832 | tf_op jit(solution)/shard_map/ppermute | solution.py:338
  10.7 6.8 %collective-permute-start.4 = (bf16[3,256,128]{2,1,0:T(8,128)(2,1)S(1)}, bf16[3,256,128]{2,1,0:T(8,128)(2,1)S(1)}, u32[]{:S(2)}, u32[]{:S(2)}) collective-permute-start(bf16[3,256,128]{2,1,0:T(8,128)(2,1)S(1)} %get-tuple-element.56), channel_id=1, source_target_pairs={{0,4},{1,0},{2,6},{3,2},{4,8},{5,1},{6,10},{7,3},{8,12},{9,5},{10,... | collective-permute-start | bytes 589832 | tf_op jit(solution)/shard_map/ppermute | solution.py:346
  12.4 9.1 %collective-permute-start.1 = (bf16[2,3,144,128]{3,2,1,0:T(8,128)(2,1)S(1)}, bf16[2,3,144,128]{3,2,1,0:T(8,128)(2,1)S(1)}, u32[]{:S(2)}, u32[]{:S(2)}) collective-permute-start(bf16[2,3,144,128]{3,2,1,0:T(8,128)(2,1)S(1)} %get-tuple-element.52), channel_id=1, source_target_pairs={{0,2},{1,3},{2,0},{3,1},{4,6},{5,7},{6,4},{7,5},{8,10},{9,11},{10,... | collective-permute-start | bytes 663560 | tf_op jit(solution)/shard_map/ppermute | solution.py:338
  13.9 7.6 %collective-permute-start.5 = (bf16[3,256,128]{2,1,0:T(8,128)(2,1)S(1)}, bf16[3,256,128]{2,1,0:T(8,128)(2,1)S(1)}, u32[]{:S(2)}, u32[]{:S(2)}) collective-permute-start(bf16[3,256,128]{2,1,0:T(8,128)(2,1)S(1)} %get-tuple-element.57), channel_id=1, source_target_pairs={{0,1},{1,5},{2,3},{3,7},{4,0},{5,9},{6,2},{7,11},{8,4},{9,13},{10,... | collective-permute-start | bytes 589832 | tf_op jit(solution)/shard_map/ppermute | solution.py:346
  13.9 10.2 %collective-permute-start.6 = (bf16[2,3,128,128]{3,2,1,0:T(8,128)(2,1)S(1)}, bf16[2,3,128,128]{3,2,1,0:T(8,128)(2,1)S(1)}, u32[]{:S(2)}, u32[]{:S(2)}) collective-permute-start(bf16[2,3,128,128]{3,2,1,0:T(8,128)(2,1)S(1)} %get-tuple-element.61), channel_id=1, source_target_pairs={{0,2},{1,3},{2,0},{3,1},{4,6},{5,7},{6,4},{7,5},{8,10},{9,11},{10,... | collective-permute-start | bytes 589832 | tf_op jit(solution)/shard_map/ppermute | solution.py:338
  15.5 8.6 %collective-permute-start.8 = (bf16[3,256,128]{2,1,0:T(8,128)(2,1)S(1)}, bf16[3,256,128]{2,1,0:T(8,128)(2,1)S(1)}, u32[]{:S(2)}, u32[]{:S(2)}) collective-permute-start(bf16[3,256,128]{2,1,0:T(8,128)(2,1)S(1)} %get-tuple-element.63), channel_id=1, source_target_pairs={{0,4},{1,0},{2,6},{3,2},{4,8},{5,1},{6,10},{7,3},{8,12},{9,5},{10,... | collective-permute-start | bytes 589832 | tf_op jit(solution)/shard_map/ppermute | solution.py:346
  17.5 6.6 %collective-permute-start.9 = (bf16[3,256,128]{2,1,0:T(8,128)(2,1)S(1)}, bf16[3,256,128]{2,1,0:T(8,128)(2,1)S(1)}, u32[]{:S(2)}, u32[]{:S(2)}) collective-permute-start(bf16[3,256,128]{2,1,0:T(8,128)(2,1)S(1)} %get-tuple-element.64), channel_id=1, source_target_pairs={{0,1},{1,5},{2,3},{3,7},{4,0},{5,9},{6,2},{7,11},{8,4},{9,13},{10,... | collective-permute-start | bytes 589832 | tf_op jit(solution)/shard_map/ppermute | solution.py:346
  24.9 7.2 %collective-permute-start.11 = (bf16[3,256,128]{2,1,0:T(8,128)(2,1)S(1)}, bf16[3,256,128]{2,1,0:T(8,128)(2,1)S(1)}, u32[]{:S(2)}, u32[]{:S(2)}) collective-permute-start(bf16[3,256,128]{2,1,0:T(8,128)(2,1)S(1)} %get-tuple-element.74), channel_id=1, source_target_pairs={{0,4},{1,0},{2,6},{3,2},{4,8},{5,1},{6,10},{7,3},{8,12},{9,5},{10,... | collective-permute-start | bytes 589832 | tf_op jit(solution)/shard_map/ppermute | solution.py:346
  26.7 5.7 %collective-permute-start.12 = (bf16[3,256,128]{2,1,0:T(8,128)(2,1)S(1)}, bf16[3,256,128]{2,1,0:T(8,128)(2,1)S(1)}, u32[]{:S(2)}, u32[]{:S(2)}) collective-permute-start(bf16[3,256,128]{2,1,0:T(8,128)(2,1)S(1)} %get-tuple-element.75), channel_id=1, source_target_pairs={{0,1},{1,5},{2,3},{3,7},{4,0},{5,9},{6,2},{7,11},{8,4},{9,13},{10,... | collective-permute-start | bytes 589832 | tf_op jit(solution)/shard_map/ppermute | solution.py:346
  30.0 7.5 %collective-permute-start.15 = (bf16[3,256,128]{2,1,0:T(8,128)(2,1)S(1)}, bf16[3,256,128]{2,1,0:T(8,128)(2,1)S(1)}, u32[]{:S(2)}, u32[]{:S(2)}) collective-permute-start(bf16[3,256,128]{2,1,0:T(8,128)(2,1)S(1)} %get-tuple-element.82), channel_id=1, source_target_pairs={{0,1},{1,5},{2,3},{3,7},{4,0},{5,9},{6,2},{7,11},{8,4},{9,13},{10,... | collective-permute-start | bytes 589832 | tf_op jit(solution)/shard_map/ppermute | solution.py:346
  30.0 7.5 %collective-permute-start.14 = (bf16[3,256,128]{2,1,0:T(8,128)(2,1)S(1)}, bf16[3,256,128]{2,1,0:T(8,128)(2,1)S(1)}, u32[]{:S(2)}, u32[]{:S(2)}) collective-permute-start(bf16[3,256,128]{2,1,0:T(8,128)(2,1)S(1)} %get-tuple-element.80), channel_id=1, source_target_pairs={{0,4},{1,0},{2,6},{3,2},{4,8},{5,1},{6,10},{7,3},{8,12},{9,5},{10,... | collective-permute-start | bytes 589832 | tf_op jit(solution)/shard_map/ppermute | solution.py:346
  32.5 6.7 %collective-permute-start.18 = (bf16[3,128,128]{2,1,0:T(8,128)(2,1)S(1)}, bf16[3,128,128]{2,1,0:T(8,128)(2,1)S(1)}, u32[]{:S(2)}, u32[]{:S(2)}) collective-permute-start(bf16[3,128,128]{2,1,0:T(8,128)(2,1)S(1)} %get-tuple-element.86), channel_id=1, source_target_pairs={{0,1},{1,0},{2,3},{3,2},{4,5},{5,4},{6,7},{7,6},{8,9},{9,8},{10,11... | collective-permute-start | bytes 294920 | tf_op jit(solution)/shard_map/ppermute | solution.py:338
  32.6 6.7 %collective-permute-start.19 = (bf16[3,128,128]{2,1,0:T(8,128)(2,1)S(1)}, bf16[3,128,128]{2,1,0:T(8,128)(2,1)S(1)}, u32[]{:S(2)}, u32[]{:S(2)}) collective-permute-start(bf16[3,128,128]{2,1,0:T(8,128)(2,1)S(1)} %get-tuple-element.87), channel_id=1, source_target_pairs={{0,2},{1,3},{2,0},{3,1},{4,6},{5,7},{6,4},{7,5},{8,10},{9,11},{10,... | collective-permute-start | bytes 294920 | tf_op jit(solution)/shard_map/ppermute | solution.py:338
  34.2 5.3 %collective-permute-start.20 = (bf16[3,128,128]{2,1,0:T(8,128)(2,1)S(1)}, bf16[3,128,128]{2,1,0:T(8,128)(2,1)S(1)}, u32[]{:S(2)}, u32[]{:S(2)}) collective-permute-start(bf16[3,128,128]{2,1,0:T(8,128)(2,1)S(1)} %get-tuple-element.88), channel_id=1, source_target_pairs={{0,3},{1,2},{2,1},{3,0},{4,7},{5,6},{6,5},{7,4},{8,11},{9,10},{10,... | collective-permute-start | bytes 294920 | tf_op jit(solution)/shard_map/ppermute | solution.py:338
  37.6 3.5 %collective-permute-start.16 = (bf16[2,3,128,128]{3,2,1,0:T(8,128)(2,1)S(1)}, bf16[2,3,128,128]{3,2,1,0:T(8,128)(2,1)S(1)}, u32[]{:S(2)}, u32[]{:S(2)}) collective-permute-start(bf16[2,3,128,128]{3,2,1,0:T(8,128)(2,1)S(1)} %get-tuple-element.83), channel_id=1, source_target_pairs={{0,1},{1,0},{2,3},{3,2},{4,5},{5,4},{6,7},{7,6},{8,9},{9,8},{10,11... | collective-permute-start | bytes 589832 | tf_op jit(solution)/shard_map/ppermute | solution.py:338
  37.7 7.8 %collective-permute-start.13 = (bf16[2,3,128,128]{3,2,1,0:T(8,128)(2,1)S(1)}, bf16[2,3,128,128]{3,2,1,0:T(8,128)(2,1)S(1)}, u32[]{:S(2)}, u32[]{:S(2)}) collective-permute-start(bf16[2,3,128,128]{3,2,1,0:T(8,128)(2,1)S(1)} %get-tuple-element.77), channel_id=1, source_target_pairs={{0,2},{1,3},{2,0},{3,1},{4,6},{5,7},{6,4},{7,5},{8,10},{9,11},{10,... | collective-permute-start | bytes 589832 | tf_op jit(solution)/shard_map/ppermute | solution.py:338
  39.5 11.4 %collective-permute-start.22 = (bf16[4,3,128,128]{3,2,1,0:T(8,128)(2,1)S(1)}, bf16[4,3,128,128]{3,2,1,0:T(8,128)(2,1)S(1)}, u32[]{:S(2)}, u32[]{:S(2)}) collective-permute-start(bf16[4,3,128,128]{3,2,1,0:T(8,128)(2,1)S(1)} %gather.1), channel_id=1, source_target_pairs={{0,16},{16,0},{1,17},{17,1},{2,18},{18,2},{3,19},{19,3},{4,20},{20... | collective-permute-start | bytes 1179656 | tf_op jit(solution)/shard_map/ppermute | solution.py:410
  41.1 8.1 %collective-permute-start.21 = (bf16[2,3,128,128]{3,2,1,0:T(8,128)(2,1)S(1)}, bf16[2,3,128,128]{3,2,1,0:T(8,128)(2,1)S(1)}, u32[]{:S(2)}, u32[]{:S(2)}) collective-permute-start(bf16[2,3,128,128]{3,2,1,0:T(8,128)(2,1)S(1)} %join.1), channel_id=1, source_target_pairs={{0,2},{1,3},{2,0},{3,1},{4,6},{5,7},{6,4},{7,5},{8,10},{9,11},{10,... | collective-permute-start | bytes 589832 | tf_op jit(solution)/shard_map/ppermute | solution.py:338
  45.4 3.8 %collective-permute-start.17 = (bf16[2,3,128,128]{3,2,1,0:T(8,128)(2,1)S(1)}, bf16[2,3,128,128]{3,2,1,0:T(8,128)(2,1)S(1)}, u32[]{:S(2)}, u32[]{:S(2)}) collective-permute-start(bf16[2,3,128,128]{3,2,1,0:T(8,128)(2,1)S(1)} %collective-permute-done.13.dq23), channel_id=1, source_target_pairs={{0,1},{1,0},{2,3},{3,2},{4,5},{5,4},{6,7},{7,6},{8,9},{9,8},{10,11... | collective-permute-start | bytes 589832 | tf_op jit(solution)/shard_map/ppermute | solution.py:338
  45.4 1.6 %collective-permute-start.10 = (bf16[3,128,128]{2,1,0:T(8,128)(2,1)S(1)}, bf16[3,128,128]{2,1,0:T(8,128)(2,1)S(1)}, u32[]{:S(2)}, u32[]{:S(2)}) collective-permute-start(bf16[3,128,128]{2,1,0:T(8,128)(2,1)S(1)} %get-tuple-element.71), channel_id=1, source_target_pairs={{0,1},{1,0},{2,3},{3,2},{4,5},{5,4},{6,7},{7,6},{8,9},{9,8},{10,11... | collective-permute-start | bytes 294920 | tf_op jit(solution)/shard_map/ppermute | solution.py:338

commit v9 on v7

--- a/solution.py
+++ b/solution.py
@@ -305,7 +305,7 @@
 
 
 HBM = pltpu.HBM
-CUTS = 4
+CUTS = 8
 
 
 def call(kernel, name, outs, scratch=(), space=pltpu.VMEM, to=pltpu.VMEM):

time: 51.8 us -> 52 us (level)
  no operation moved by 1% of the time
where the time goes in v9:
time: 52 us; the launch traced here: 51.8 us
  starting transfers between devices  22.1 us (42%)
  waiting for transfers between devices  17.6 us (34%)
  Pallas kernels  11.3 us (22%)
  between operations  0.78 us (2%)
    ppermute x14, starting transfers between devices, swap(): return lax.ppermute(array, 'ctx', [(i, i ^ step) for i in range(ctx)])  13 us
    pallas_call x16, Pallas kernels, run(): pl.pallas_call(kernel, out_shape=jax.tree.map(lambda out: to(out.shape, o...  11.3 us
    ppermute x14, waiting for transfers between devices, swap(): return lax.ppermute(array, 'ctx', [(i, i ^ step) for i in range(ctx)])  10.2 us
    ppermute x8, starting transfers between devices, ring(): return lax.ppermute(array, 'ctx', pairs)  7.56 us
    ppermute x8, waiting for transfers between devices, ring(): return lax.ppermute(array, 'ctx', pairs)  7.31 us
    ppermute x1, starting transfers between devices, shards(): lax.ppermute(late, 'section', [(s, (s - 1) % sections) for s in range(sec...  1.56 us
  transfers between devices with their start and end apart: 23, of which 10 were waited for; matrix products, arithmetic and copies ran while one was open for 0% of the time, Pallas kernels for 15%

profile of v9, /device:TPU:0, one launch (start us, length us, event | category | flops | bytes accessed | tf_op | source)
XLA Modules:
  0.0 51.8 jit_solution(8818594804011255771)
XLA Ops:
  0.6 1.7 %pack.1 = (bf16[3,528,128]{2,1,0:T(8,128)(2,1)S(1)}, bf16[3,928,128]{2,1,0:T(8,128)(2,1)S(1)}, bf16[3,128,128]{2,1,0:T(8,128)(2,1)S(1)}, bf16[3,128,128]{2,1,0:T(8,128)(2,1)S(1)}, bf16[3,400,128]{2,1,0:T(8,128)(2,1)S(1)}) custom-call(bf16[1,128,1536]{2,1,0:T(8,128)(2,1)} %k_hbm.1, bf16[1,128,1536]{2,1,0:T(8,128)(2,1)} %q_hbm.1, bf16[1,128,1536]{2,1,0:T(8,128)(2,1)} %g_hbm.1, ...), custom_call_target="tpu_custom_call" | custom-call | tf_op jit(solution)/shard_map/pack/pallas_call | solution.py:313
  2.4 0.5 %collective-permute-start = (bf16[3,928,128]{2,1,0:T(8,128)(2,1)S(1)}, bf16[3,928,128]{2,1,0:T(8,128)(2,1)S(1)}, u32[]{:S(2)}, u32[]{:S(2)}) collective-permute-start(bf16[3,928,128]{2,1,0:T(8,128)(2,1)S(1)} %get-tuple-element.48), channel_id=1, source_target_pairs={{0,1},{1,0},{2,3},{3,2},{4,5},{5,4},{6,7},{7,6},{8,9},{9,8},{10,11... | collective-permute-start | bytes 2138120 | tf_op jit(solution)/shard_map/ppermute | solution.py:336
  2.9 2.6 %collective-permute-start.2 = (bf16[3,128,128]{2,1,0:T(8,128)(2,1)S(1)}, bf16[3,128,128]{2,1,0:T(8,128)(2,1)S(1)}, u32[]{:S(2)}, u32[]{:S(2)}) collective-permute-start(bf16[3,128,128]{2,1,0:T(8,128)(2,1)S(1)} %get-tuple-element.51), channel_id=1, source_target_pairs={{0,2},{1,3},{2,0},{3,1},{4,6},{5,7},{6,4},{7,5},{8,10},{9,11},{10,... | collective-permute-start | bytes 294920 | tf_op jit(solution)/shard_map/ppermute | solution.py:336
  5.6 2.1 %collective-permute-start.7 = (bf16[2,3,128,128]{3,2,1,0:T(8,128)(2,1)S(1)}, bf16[2,3,128,128]{3,2,1,0:T(8,128)(2,1)S(1)}, u32[]{:S(2)}, u32[]{:S(2)}) collective-permute-start(bf16[2,3,128,128]{3,2,1,0:T(8,128)(2,1)S(1)} %get-tuple-element.60), channel_id=1, source_target_pairs={{0,2},{1,3},{2,0},{3,1},{4,6},{5,7},{6,4},{7,5},{8,10},{9,11},{10,... | collective-permute-start | bytes 589832 | tf_op jit(solution)/shard_map/ppermute | solution.py:336
  7.7 1.4 %collective-permute-done.2.two = bf16[3,128,128]{2,1,0:T(8,128)(2,1)S(1)} collective-permute-done((bf16[3,128,128]{2,1,0:T(8,128)(2,1)S(1)}, bf16[3,128,128]{2,1,0:T(8,128)(2,1)S(1)}, u32[]{:S(2)}, u32[]{:S(2)}) %collective-permute-start.2) | collective-permute-done | bytes 98336 | tf_op jit(solution)/shard_map/ppermute | solution.py:336
  9.1 1.6 %collective-permute-done.3.three = bf16[3,128,128]{2,1,0:T(8,128)(2,1)S(1)} collective-permute-done((bf16[3,128,128]{2,1,0:T(8,128)(2,1)S(1)}, bf16[3,128,128]{2,1,0:T(8,128)(2,1)S(1)}, u32[]{:S(2)}, u32[]{:S(2)}) %collective-permute-start.3) | collective-permute-done | bytes 98336 | tf_op jit(solution)/shard_map/ppermute | solution.py:336
  10.8 1.6 %collective-permute-start.4 = (bf16[3,256,128]{2,1,0:T(8,128)(2,1)S(1)}, bf16[3,256,128]{2,1,0:T(8,128)(2,1)S(1)}, u32[]{:S(2)}, u32[]{:S(2)}) collective-permute-start(bf16[3,256,128]{2,1,0:T(8,128)(2,1)S(1)} %get-tuple-element.54), channel_id=1, source_target_pairs={{0,4},{1,0},{2,6},{3,2},{4,8},{5,1},{6,10},{7,3},{8,12},{9,5},{10,... | collective-permute-start | bytes 589832 | tf_op jit(solution)/shard_map/ppermute | solution.py:344
  12.4 1.5 %collective-permute-start.1 = (bf16[2,3,144,128]{3,2,1,0:T(8,128)(2,1)S(1)}, bf16[2,3,144,128]{3,2,1,0:T(8,128)(2,1)S(1)}, u32[]{:S(2)}, u32[]{:S(2)}) collective-permute-start(bf16[2,3,144,128]{3,2,1,0:T(8,128)(2,1)S(1)} %get-tuple-element.50), channel_id=1, source_target_pairs={{0,2},{1,3},{2,0},{3,1},{4,6},{5,7},{6,4},{7,5},{8,10},{9,11},{10,... | collective-permute-start | bytes 663560 | tf_op jit(solution)/shard_map/ppermute | solution.py:336
  13.9 0.5 collective-permute-start.6
  14.4 1.0 %collective-permute-done.7.pair = bf16[2,3,128,128]{3,2,1,0:T(8,128)(2,1)S(1)} collective-permute-done((bf16[2,3,128,128]{3,2,1,0:T(8,128)(2,1)S(1)}, bf16[2,3,128,128]{3,2,1,0:T(8,128)(2,1)S(1)}, u32[]{:S(2)}, u32[]{:S(2)}) %collective-permute-start.7) | collective-permute-done | bytes 196640 | tf_op jit(solution)/shard_map/ppermute | solution.py:336
  15.5 2.0 %collective-permute-start.8 = (bf16[3,256,128]{2,1,0:T(8,128)(2,1)S(1)}, bf16[3,256,128]{2,1,0:T(8,128)(2,1)S(1)}, u32[]{:S(2)}, u32[]{:S(2)}) collective-permute-start(bf16[3,256,128]{2,1,0:T(8,128)(2,1)S(1)} %get-tuple-element.61), channel_id=1, source_target_pairs={{0,4},{1,0},{2,6},{3,2},{4,8},{5,1},{6,10},{7,3},{8,12},{9,5},{10,... | collective-permute-start | bytes 589832 | tf_op jit(solution)/shard_map/ppermute | solution.py:344
  17.5 4.0 %collective-permute-done.5.halo2 = bf16[3,256,128]{2,1,0:T(8,128)(2,1)S(1)} collective-permute-done((bf16[3,256,128]{2,1,0:T(8,128)(2,1)S(1)}, bf16[3,256,128]{2,1,0:T(8,128)(2,1)S(1)}, u32[]{:S(2)}, u32[]{:S(2)}) %collective-permute-start.5) | collective-permute-done | bytes 196640 | tf_op jit(solution)/shard_map/ppermute | solution.py:344
  21.5 1.8 %probs.1 = (bf16[3,1024,512]{2,1,0:T(8,128)(2,1)S(1)}, bf16[3,1024,128]{2,1,0:T(8,128)(2,1)S(1)}, bf16[3,512,128]{2,1,0:T(8,128)(2,1)S(1)}) custom-call(bf16[3,528,128]{2,1,0:T(8,128)(2,1)S(1)} %get-tuple-element.47.own, bf16[3,928,128]{2,1,0:T(8,128)(2,1)S(1)} %collective-permute-done.side, bf16[2,3,144,128]{3,2,1,0:T(8,128)(2,1)S(1)} %collective-permute-done.1.crossed, ...), custom_call_target="tpu_custom_call" | custom-call | tf_op jit(solution)/shard_map/probs/pallas_call | solution.py:313
  23.3 0.8 %collective-permute-done.6.crossed = bf16[2,3,128,128]{3,2,1,0:T(8,128)(2,1)S(1)} collective-permute-done((bf16[2,3,128,128]{3,2,1,0:T(8,128)(2,1)S(1)}, bf16[2,3,128,128]{3,2,1,0:T(8,128)(2,1)S(1)}, u32[]{:S(2)}, u32[]{:S(2)}) %collective-permute-start.6) | collective-permute-done | bytes 196640 | tf_op jit(solution)/shard_map/ppermute | solution.py:336
  24.1 0.8 %values.1 = (bf16[3,512,128]{2,1,0:T(8,128)(2,1)S(1)}, f32[3,512,128]{2,1,0:T(8,128)S(1)}, bf16[3,256,128]{2,1,0:T(8,128)(2,1)S(1)}, bf16[3,256,128]{2,1,0:T(8,128)(2,1)S(1)}) custom-call(bf16[3,1024,512]{2,1,0:T(8,128)(2,1)S(1)} %get-tuple-element.56.probs, bf16[3,528,128]{2,1,0:T(8,128)(2,1)S(1)} %get-tuple-element.47.own, ...), custom_call_target="tpu_custom_call" | custom-call | tf_op jit(solution)/shard_map/values/pallas_call | solution.py:313
  25.0 1.8 %collective-permute-start.11 = (bf16[3,256,128]{2,1,0:T(8,128)(2,1)S(1)}, bf16[3,256,128]{2,1,0:T(8,128)(2,1)S(1)}, u32[]{:S(2)}, u32[]{:S(2)}) collective-permute-start(bf16[3,256,128]{2,1,0:T(8,128)(2,1)S(1)} %get-tuple-element.72), channel_id=1, source_target_pairs={{0,4},{1,0},{2,6},{3,2},{4,8},{5,1},{6,10},{7,3},{8,12},{9,5},{10,... | collective-permute-start | bytes 589832 | tf_op jit(solution)/shard_map/ppermute | solution.py:344
  26.8 2.5 %scores.1 = (bf16[3,1024,512]{2,1,0:T(8,128)(2,1)S(1)}, f32[3,512,128]{2,1,0:T(8,128)S(1)}, bf16[3,256,128]{2,1,0:T(8,128)(2,1)S(1)}, bf16[3,256,128]{2,1,0:T(8,128)(2,1)S(1)}) custom-call(bf16[3,1024,512]{2,1,0:T(8,128)(2,1)S(1)} %get-tuple-element.56.probs, bf16[3,512,128]{2,1,0:T(8,128)(2,1)S(1)} %get-tuple-element.57.qs, ...), custom_call_target="tpu_custom_call" | custom-call | tf_op jit(solution)/shard_map/scores/pallas_call | solution.py:313
  29.3 0.8 %queries.1 = (bf16[3,128,128]{2,1,0:T(8,128)(2,1)S(1)}, bf16[3,128,128]{2,1,0:T(8,128)(2,1)S(1)}, bf16[2,3,128,128]{3,2,1,0:T(8,128)(2,1)S(1)}) custom-call(bf16[3,1024,512]{2,1,0:T(8,128)(2,1)S(1)} %get-tuple-element.66.ss, bf16[3,1024,128]{2,1,0:T(8,128)(2,1)S(1)} %get-tuple-element.67.ks), custom_call_target="tpu_custom_call" | custom-call | tf_op jit(solution)/shard_map/queries/pallas_call | solution.py:313
  30.1 2.0 %collective-permute-start.14 = (bf16[3,256,128]{2,1,0:T(8,128)(2,1)S(1)}, bf16[3,256,128]{2,1,0:T(8,128)(2,1)S(1)}, u32[]{:S(2)}, u32[]{:S(2)}) collective-permute-start(bf16[3,256,128]{2,1,0:T(8,128)(2,1)S(1)} %get-tuple-element.78), channel_id=1, source_target_pairs={{0,4},{1,0},{2,6},{3,2},{4,8},{5,1},{6,10},{7,3},{8,12},{9,5},{10,... | collective-permute-start | bytes 589832 | tf_op jit(solution)/shard_map/ppermute | solution.py:344
  32.1 0.3 collective-permute-done.12.ring2
  32.7 1.6 %collective-permute-start.19 = (bf16[3,128,128]{2,1,0:T(8,128)(2,1)S(1)}, bf16[3,128,128]{2,1,0:T(8,128)(2,1)S(1)}, u32[]{:S(2)}, u32[]{:S(2)}) collective-permute-start(bf16[3,128,128]{2,1,0:T(8,128)(2,1)S(1)} %get-tuple-element.85), channel_id=1, source_target_pairs={{0,2},{1,3},{2,0},{3,1},{4,6},{5,7},{6,4},{7,5},{8,10},{9,11},{10,... | collective-permute-start | bytes 294920 | tf_op jit(solution)/shard_map/ppermute | solution.py:336
  34.5 3.0 %collective-permute-done.15.ring2 = bf16[3,256,128]{2,1,0:T(8,128)(2,1)S(1)} collective-permute-done((bf16[3,256,128]{2,1,0:T(8,128)(2,1)S(1)}, bf16[3,256,128]{2,1,0:T(8,128)(2,1)S(1)}, u32[]{:S(2)}, u32[]{:S(2)}) %collective-permute-start.15) | collective-permute-done | bytes 196640 | tf_op jit(solution)/shard_map/ppermute | solution.py:344
  37.7 1.6 %collective-permute-start.13 = (bf16[2,3,128,128]{3,2,1,0:T(8,128)(2,1)S(1)}, bf16[2,3,128,128]{3,2,1,0:T(8,128)(2,1)S(1)}, u32[]{:S(2)}, u32[]{:S(2)}) collective-permute-start(bf16[2,3,128,128]{3,2,1,0:T(8,128)(2,1)S(1)} %get-tuple-element.75), channel_id=1, source_target_pairs={{0,2},{1,3},{2,0},{3,1},{4,6},{5,7},{6,4},{7,5},{8,10},{9,11},{10,... | collective-permute-start | bytes 589832 | tf_op jit(solution)/shard_map/ppermute | solution.py:336
  39.6 1.6 %collective-permute-start.22 = (bf16[4,3,128,128]{3,2,1,0:T(8,128)(2,1)S(1)}, bf16[4,3,128,128]{3,2,1,0:T(8,128)(2,1)S(1)}, u32[]{:S(2)}, u32[]{:S(2)}) collective-permute-start(bf16[4,3,128,128]{3,2,1,0:T(8,128)(2,1)S(1)} %gather.1), channel_id=1, source_target_pairs={{0,16},{16,0},{1,17},{17,1},{2,18},{18,2},{3,19},{19,3},{4,20},{20... | collective-permute-start | bytes 1179656 | tf_op jit(solution)/shard_map/ppermute | solution.py:408
  41.1 1.6 %collective-permute-start.21 = (bf16[2,3,128,128]{3,2,1,0:T(8,128)(2,1)S(1)}, bf16[2,3,128,128]{3,2,1,0:T(8,128)(2,1)S(1)}, u32[]{:S(2)}, u32[]{:S(2)}) collective-permute-start(bf16[2,3,128,128]{3,2,1,0:T(8,128)(2,1)S(1)} %join.1), channel_id=1, source_target_pairs={{0,2},{1,3},{2,0},{3,1},{4,6},{5,7},{6,4},{7,5},{8,10},{9,11},{10,... | collective-permute-start | bytes 589832 | tf_op jit(solution)/shard_map/ppermute | solution.py:336
  42.7 2.8 %collective-permute-done.13.crossed = bf16[2,3,128,128]{3,2,1,0:T(8,128)(2,1)S(1)} collective-permute-done((bf16[2,3,128,128]{3,2,1,0:T(8,128)(2,1)S(1)}, bf16[2,3,128,128]{3,2,1,0:T(8,128)(2,1)S(1)}, u32[]{:S(2)}, u32[]{:S(2)}) %collective-permute-start.13) | collective-permute-done | bytes 196640 | tf_op jit(solution)/shard_map/ppermute | solution.py:336
  45.5 0.5 collective-permute-start.10
  46.0 0.8 %unpack.6 = bf16[1,128,1536]{2,1,0:T(8,128)(2,1)} custom-call(bf16[3,128,128]{2,1,0:T(8,128)(2,1)S(1)} %get-tuple-element.88.in0, bf16[3,128,128]{2,1,0:T(8,128)(2,1)S(1)} %collective-permute-done.18.in1, bf16[3,128,128]{2,1,0:T(8,128)(2,1)S(1)} %collective-permute-done.19.in2, bf16[3,128,128]{2,1,0:T(8,128)(2,1)S(1)} %collective-permute-done.20.in3), custom_call_target="tpu_custom_call" | custom-call | tf_op jit(solution)/shard_map/unpack/pallas_call | solution.py:313
  46.8 2.4 %collective-permute-done.21.crossed = bf16[2,3,128,128]{3,2,1,0:T(8,128)(2,1)S(1)} collective-permute-done((bf16[2,3,128,128]{3,2,1,0:T(8,128)(2,1)S(1)}, bf16[2,3,128,128]{3,2,1,0:T(8,128)(2,1)S(1)}, u32[]{:S(2)}, u32[]{:S(2)}) %collective-permute-start.21) | collective-permute-done | bytes 196640 | tf_op jit(solution)/shard_map/ppermute | solution.py:336
  49.2 0.8 %unpack.5 = bf16[1,128,1536]{2,1,0:T(8,128)(2,1)} custom-call(bf16[2,3,128,128]{3,2,1,0:T(8,128)(2,1)S(1)} %get-tuple-element.87.stay, bf16[2,3,128,128]{3,2,1,0:T(8,128)(2,1)S(1)} %collective-permute-done.16.got, bf16[2,3,128,128]{3,2,1,0:T(8,128)(2,1)S(1)} %collective-permute-done.21.crossed), custom_call_target="tpu_custom_call" | custom-call | tf_op jit(solution)/shard_map/unpack/pallas_call | solution.py:313
  50.1 0.8 %unpack.4 = bf16[1,128,1536]{2,1,0:T(8,128)(2,1)} custom-call(bf16[3,128,128]{2,1,0:T(8,128)(2,1)S(1)} %get-tuple-element.68.dq0, bf16[3,128,128]{2,1,0:T(8,128)(2,1)S(1)} %collective-permute-done.10.dq1, bf16[2,3,128,128]{3,2,1,0:T(8,128)(2,1)S(1)} %collective-permute-done.13.crossed, bf16[2,3,128,128]{3,2,1,0:T(8,128)(2,1)S(1)} %collective-permute-done.17.turned), custom_call_target="tpu_custom_call" | custom-call | tf_op jit(solution)/shard_map/unpack/pallas_call | solution.py:313
  50.9 0.8 %unpack.7 = bf16[1,128,1536]{2,1,0:T(8,128)(2,1)} custom-call(bf16[4,3,128,128]{3,2,1,0:T(8,128)(2,1)S(1)} %collective-permute-done.22.groups), custom_call_target="tpu_custom_call" | custom-call | tf_op jit(solution)/shard_map/unpack/pallas_call | solution.py:313
  (30 shorter events, 1.2 us)
Async XLA Ops:
  2.4 3.2 %collective-permute-start = (bf16[3,928,128]{2,1,0:T(8,128)(2,1)S(1)}, bf16[3,928,128]{2,1,0:T(8,128)(2,1)S(1)}, u32[]{:S(2)}, u32[]{:S(2)}) collective-permute-start(bf16[3,928,128]{2,1,0:T(8,128)(2,1)S(1)} %get-tuple-element.48), channel_id=1, source_target_pairs={{0,1},{1,0},{2,3},{3,2},{4,5},{5,4},{6,7},{7,6},{8,9},{9,8},{10,11... | collective-permute-start | bytes 2138120 | tf_op jit(solution)/shard_map/ppermute | solution.py:336
  2.9 6.2 %collective-permute-start.2 = (bf16[3,128,128]{2,1,0:T(8,128)(2,1)S(1)}, bf16[3,128,128]{2,1,0:T(8,128)(2,1)S(1)}, u32[]{:S(2)}, u32[]{:S(2)}) collective-permute-start(bf16[3,128,128]{2,1,0:T(8,128)(2,1)S(1)} %get-tuple-element.51), channel_id=1, source_target_pairs={{0,2},{1,3},{2,0},{3,1},{4,6},{5,7},{6,4},{7,5},{8,10},{9,11},{10,... | collective-permute-start | bytes 294920 | tf_op jit(solution)/shard_map/ppermute | solution.py:336
  5.5 5.2 %collective-permute-start.3 = (bf16[3,128,128]{2,1,0:T(8,128)(2,1)S(1)}, bf16[3,128,128]{2,1,0:T(8,128)(2,1)S(1)}, u32[]{:S(2)}, u32[]{:S(2)}) collective-permute-start(bf16[3,128,128]{2,1,0:T(8,128)(2,1)S(1)} %get-tuple-element.52), channel_id=1, source_target_pairs={{0,3},{1,2},{2,1},{3,0},{4,7},{5,6},{6,5},{7,4},{8,11},{9,10},{10,... | collective-permute-start | bytes 294920 | tf_op jit(solution)/shard_map/ppermute | solution.py:336
  5.6 9.8 %collective-permute-start.7 = (bf16[2,3,128,128]{3,2,1,0:T(8,128)(2,1)S(1)}, bf16[2,3,128,128]{3,2,1,0:T(8,128)(2,1)S(1)}, u32[]{:S(2)}, u32[]{:S(2)}) collective-permute-start(bf16[2,3,128,128]{3,2,1,0:T(8,128)(2,1)S(1)} %get-tuple-element.60), channel_id=1, source_target_pairs={{0,2},{1,3},{2,0},{3,1},{4,6},{5,7},{6,4},{7,5},{8,10},{9,11},{10,... | collective-permute-start | bytes 589832 | tf_op jit(solution)/shard_map/ppermute | solution.py:336
  10.8 6.8 %collective-permute-start.4 = (bf16[3,256,128]{2,1,0:T(8,128)(2,1)S(1)}, bf16[3,256,128]{2,1,0:T(8,128)(2,1)S(1)}, u32[]{:S(2)}, u32[]{:S(2)}) collective-permute-start(bf16[3,256,128]{2,1,0:T(8,128)(2,1)S(1)} %get-tuple-element.54), channel_id=1, source_target_pairs={{0,4},{1,0},{2,6},{3,2},{4,8},{5,1},{6,10},{7,3},{8,12},{9,5},{10,... | collective-permute-start | bytes 589832 | tf_op jit(solution)/shard_map/ppermute | solution.py:344
  12.4 9.1 %collective-permute-start.1 = (bf16[2,3,144,128]{3,2,1,0:T(8,128)(2,1)S(1)}, bf16[2,3,144,128]{3,2,1,0:T(8,128)(2,1)S(1)}, u32[]{:S(2)}, u32[]{:S(2)}) collective-permute-start(bf16[2,3,144,128]{3,2,1,0:T(8,128)(2,1)S(1)} %get-tuple-element.50), channel_id=1, source_target_pairs={{0,2},{1,3},{2,0},{3,1},{4,6},{5,7},{6,4},{7,5},{8,10},{9,11},{10,... | collective-permute-start | bytes 663560 | tf_op jit(solution)/shard_map/ppermute | solution.py:336
  13.9 7.6 %collective-permute-start.5 = (bf16[3,256,128]{2,1,0:T(8,128)(2,1)S(1)}, bf16[3,256,128]{2,1,0:T(8,128)(2,1)S(1)}, u32[]{:S(2)}, u32[]{:S(2)}) collective-permute-start(bf16[3,256,128]{2,1,0:T(8,128)(2,1)S(1)} %get-tuple-element.55), channel_id=1, source_target_pairs={{0,1},{1,5},{2,3},{3,7},{4,0},{5,9},{6,2},{7,11},{8,4},{9,13},{10,... | collective-permute-start | bytes 589832 | tf_op jit(solution)/shard_map/ppermute | solution.py:344
  13.9 10.2 %collective-permute-start.6 = (bf16[2,3,128,128]{3,2,1,0:T(8,128)(2,1)S(1)}, bf16[2,3,128,128]{3,2,1,0:T(8,128)(2,1)S(1)}, u32[]{:S(2)}, u32[]{:S(2)}) collective-permute-start(bf16[2,3,128,128]{3,2,1,0:T(8,128)(2,1)S(1)} %get-tuple-element.59), channel_id=1, source_target_pairs={{0,2},{1,3},{2,0},{3,1},{4,6},{5,7},{6,4},{7,5},{8,10},{9,11},{10,... | collective-permute-start | bytes 589832 | tf_op jit(solution)/shard_map/ppermute | solution.py:336
  15.5 8.6 %collective-permute-start.8 = (bf16[3,256,128]{2,1,0:T(8,128)(2,1)S(1)}, bf16[3,256,128]{2,1,0:T(8,128)(2,1)S(1)}, u32[]{:S(2)}, u32[]{:S(2)}) collective-permute-start(bf16[3,256,128]{2,1,0:T(8,128)(2,1)S(1)} %get-tuple-element.61), channel_id=1, source_target_pairs={{0,4},{1,0},{2,6},{3,2},{4,8},{5,1},{6,10},{7,3},{8,12},{9,5},{10,... | collective-permute-start | bytes 589832 | tf_op jit(solution)/shard_map/ppermute | solution.py:344
  17.5 6.6 %collective-permute-start.9 = (bf16[3,256,128]{2,1,0:T(8,128)(2,1)S(1)}, bf16[3,256,128]{2,1,0:T(8,128)(2,1)S(1)}, u32[]{:S(2)}, u32[]{:S(2)}) collective-permute-start(bf16[3,256,128]{2,1,0:T(8,128)(2,1)S(1)} %get-tuple-element.62), channel_id=1, source_target_pairs={{0,1},{1,5},{2,3},{3,7},{4,0},{5,9},{6,2},{7,11},{8,4},{9,13},{10,... | collective-permute-start | bytes 589832 | tf_op jit(solution)/shard_map/ppermute | solution.py:344
  25.0 7.1 %collective-permute-start.11 = (bf16[3,256,128]{2,1,0:T(8,128)(2,1)S(1)}, bf16[3,256,128]{2,1,0:T(8,128)(2,1)S(1)}, u32[]{:S(2)}, u32[]{:S(2)}) collective-permute-start(bf16[3,256,128]{2,1,0:T(8,128)(2,1)S(1)} %get-tuple-element.72), channel_id=1, source_target_pairs={{0,4},{1,0},{2,6},{3,2},{4,8},{5,1},{6,10},{7,3},{8,12},{9,5},{10,... | collective-permute-start | bytes 589832 | tf_op jit(solution)/shard_map/ppermute | solution.py:344
  26.8 5.7 %collective-permute-start.12 = (bf16[3,256,128]{2,1,0:T(8,128)(2,1)S(1)}, bf16[3,256,128]{2,1,0:T(8,128)(2,1)S(1)}, u32[]{:S(2)}, u32[]{:S(2)}) collective-permute-start(bf16[3,256,128]{2,1,0:T(8,128)(2,1)S(1)} %get-tuple-element.73), channel_id=1, source_target_pairs={{0,1},{1,5},{2,3},{3,7},{4,0},{5,9},{6,2},{7,11},{8,4},{9,13},{10,... | collective-permute-start | bytes 589832 | tf_op jit(solution)/shard_map/ppermute | solution.py:344
  30.0 7.5 %collective-permute-start.15 = (bf16[3,256,128]{2,1,0:T(8,128)(2,1)S(1)}, bf16[3,256,128]{2,1,0:T(8,128)(2,1)S(1)}, u32[]{:S(2)}, u32[]{:S(2)}) collective-permute-start(bf16[3,256,128]{2,1,0:T(8,128)(2,1)S(1)} %get-tuple-element.80), channel_id=1, source_target_pairs={{0,1},{1,5},{2,3},{3,7},{4,0},{5,9},{6,2},{7,11},{8,4},{9,13},{10,... | collective-permute-start | bytes 589832 | tf_op jit(solution)/shard_map/ppermute | solution.py:344
  30.1 7.5 %collective-permute-start.14 = (bf16[3,256,128]{2,1,0:T(8,128)(2,1)S(1)}, bf16[3,256,128]{2,1,0:T(8,128)(2,1)S(1)}, u32[]{:S(2)}, u32[]{:S(2)}) collective-permute-start(bf16[3,256,128]{2,1,0:T(8,128)(2,1)S(1)} %get-tuple-element.78), channel_id=1, source_target_pairs={{0,4},{1,0},{2,6},{3,2},{4,8},{5,1},{6,10},{7,3},{8,12},{9,5},{10,... | collective-permute-start | bytes 589832 | tf_op jit(solution)/shard_map/ppermute | solution.py:344
  32.6 6.8 %collective-permute-start.18 = (bf16[3,128,128]{2,1,0:T(8,128)(2,1)S(1)}, bf16[3,128,128]{2,1,0:T(8,128)(2,1)S(1)}, u32[]{:S(2)}, u32[]{:S(2)}) collective-permute-start(bf16[3,128,128]{2,1,0:T(8,128)(2,1)S(1)} %get-tuple-element.84), channel_id=1, source_target_pairs={{0,1},{1,0},{2,3},{3,2},{4,5},{5,4},{6,7},{7,6},{8,9},{9,8},{10,11... | collective-permute-start | bytes 294920 | tf_op jit(solution)/shard_map/ppermute | solution.py:336
  32.7 6.7 %collective-permute-start.19 = (bf16[3,128,128]{2,1,0:T(8,128)(2,1)S(1)}, bf16[3,128,128]{2,1,0:T(8,128)(2,1)S(1)}, u32[]{:S(2)}, u32[]{:S(2)}) collective-permute-start(bf16[3,128,128]{2,1,0:T(8,128)(2,1)S(1)} %get-tuple-element.85), channel_id=1, source_target_pairs={{0,2},{1,3},{2,0},{3,1},{4,6},{5,7},{6,4},{7,5},{8,10},{9,11},{10,... | collective-permute-start | bytes 294920 | tf_op jit(solution)/shard_map/ppermute | solution.py:336
  34.2 5.3 %collective-permute-start.20 = (bf16[3,128,128]{2,1,0:T(8,128)(2,1)S(1)}, bf16[3,128,128]{2,1,0:T(8,128)(2,1)S(1)}, u32[]{:S(2)}, u32[]{:S(2)}) collective-permute-start(bf16[3,128,128]{2,1,0:T(8,128)(2,1)S(1)} %get-tuple-element.86), channel_id=1, source_target_pairs={{0,3},{1,2},{2,1},{3,0},{4,7},{5,6},{6,5},{7,4},{8,11},{9,10},{10,... | collective-permute-start | bytes 294920 | tf_op jit(solution)/shard_map/ppermute | solution.py:336
  37.6 3.5 %collective-permute-start.16 = (bf16[2,3,128,128]{3,2,1,0:T(8,128)(2,1)S(1)}, bf16[2,3,128,128]{3,2,1,0:T(8,128)(2,1)S(1)}, u32[]{:S(2)}, u32[]{:S(2)}) collective-permute-start(bf16[2,3,128,128]{3,2,1,0:T(8,128)(2,1)S(1)} %get-tuple-element.81), channel_id=1, source_target_pairs={{0,1},{1,0},{2,3},{3,2},{4,5},{5,4},{6,7},{7,6},{8,9},{9,8},{10,11... | collective-permute-start | bytes 589832 | tf_op jit(solution)/shard_map/ppermute | solution.py:336
  37.7 7.8 %collective-permute-start.13 = (bf16[2,3,128,128]{3,2,1,0:T(8,128)(2,1)S(1)}, bf16[2,3,128,128]{3,2,1,0:T(8,128)(2,1)S(1)}, u32[]{:S(2)}, u32[]{:S(2)}) collective-permute-start(bf16[2,3,128,128]{3,2,1,0:T(8,128)(2,1)S(1)} %get-tuple-element.75), channel_id=1, source_target_pairs={{0,2},{1,3},{2,0},{3,1},{4,6},{5,7},{6,4},{7,5},{8,10},{9,11},{10,... | collective-permute-start | bytes 589832 | tf_op jit(solution)/shard_map/ppermute | solution.py:336
  39.6 11.4 %collective-permute-start.22 = (bf16[4,3,128,128]{3,2,1,0:T(8,128)(2,1)S(1)}, bf16[4,3,128,128]{3,2,1,0:T(8,128)(2,1)S(1)}, u32[]{:S(2)}, u32[]{:S(2)}) collective-permute-start(bf16[4,3,128,128]{3,2,1,0:T(8,128)(2,1)S(1)} %gather.1), channel_id=1, source_target_pairs={{0,16},{16,0},{1,17},{17,1},{2,18},{18,2},{3,19},{19,3},{4,20},{20... | collective-permute-start | bytes 1179656 | tf_op jit(solution)/shard_map/ppermute | solution.py:408
  41.1 8.1 %collective-permute-start.21 = (bf16[2,3,128,128]{3,2,1,0:T(8,128)(2,1)S(1)}, bf16[2,3,128,128]{3,2,1,0:T(8,128)(2,1)S(1)}, u32[]{:S(2)}, u32[]{:S(2)}) collective-permute-start(bf16[2,3,128,128]{3,2,1,0:T(8,128)(2,1)S(1)} %join.1), channel_id=1, source_target_pairs={{0,2},{1,3},{2,0},{3,1},{4,6},{5,7},{6,4},{7,5},{8,10},{9,11},{10,... | collective-permute-start | bytes 589832 | tf_op jit(solution)/shard_map/ppermute | solution.py:336
  45.5 4.6 %collective-permute-start.17 = (bf16[2,3,128,128]{3,2,1,0:T(8,128)(2,1)S(1)}, bf16[2,3,128,128]{3,2,1,0:T(8,128)(2,1)S(1)}, u32[]{:S(2)}, u32[]{:S(2)}) collective-permute-start(bf16[2,3,128,128]{3,2,1,0:T(8,128)(2,1)S(1)} %collective-permute-done.13.crossed), channel_id=1, source_target_pairs={{0,1},{1,0},{2,3},{3,2},{4,5},{5,4},{6,7},{7,6},{8,9},{9,8},{10,11... | collective-permute-start | bytes 589832 | tf_op jit(solution)/shard_map/ppermute | solution.py:336
  45.5 4.6 %collective-permute-start.10 = (bf16[3,128,128]{2,1,0:T(8,128)(2,1)S(1)}, bf16[3,128,128]{2,1,0:T(8,128)(2,1)S(1)}, u32[]{:S(2)}, u32[]{:S(2)}) collective-permute-start(bf16[3,128,128]{2,1,0:T(8,128)(2,1)S(1)} %get-tuple-element.69), channel_id=1, source_target_pairs={{0,1},{1,0},{2,3},{3,2},{4,5},{5,4},{6,7},{7,6},{8,9},{9,8},{10,11... | collective-permute-start | bytes 294920 | tf_op jit(solution)/shard_map/ppermute | solution.py:336
